TPU v7x, 32 devices: a whole 2x2x4 slice. The times are simulated.
32 devices in a mesh: group: 2 (over y), seq: 4 (over z), tp: 2 (over x), role: 2 (over core).
Axes of the slice: x: 2, y: 2, z: 4, core: 2. Of those that a mesh axis runs over, the one named last changes fastest.
Arguments:
- queries: bfloat16 [2, 3072, 4096], P('role', ('group', 'seq'), 'tp'), parts along dimension 1, may hold values from -6 to 6
- new_kv: bfloat16 [2, 3072, 2, 512], P('role', ('group', 'seq'), None, 'tp'), parts along dimension 1, may hold values from -6 to 6
- pool: bfloat16 [2, 2048, 2, 16, 512], P('role', ('group', 'seq'), None, None, 'tp'), parts along dimension 1, may hold values from -6 to 6
- out_weight: bfloat16 [4096, 4096], P('tp', 'seq'), may hold values from -0.5 to 0.5
- tok_conv: int32 [2, 3072], P('role', ('group', 'seq')), parts along dimension 1, may hold values from 0 to 95, as said below
- page_conv: int32 [2, 1024], P('role', ('group', 'seq')), parts along dimension 1, may hold values from 0 to 95, as said below
- page_fill: int32 [2, 1024], P('role', ('group', 'seq')), parts along dimension 1, may hold values from 1 to 16, as said below
- page_owner: int32 [2, 1024], P('role', ('group', 'seq')), parts along dimension 1, may hold values from 0 to 3, as said below
- page_index: int32 [2, 1024], P('role', ('group', 'seq')), parts along dimension 1, may hold values from 0 to 255, as said below
Outputs:
- projected: bfloat16 [2, 3072, 4096], P('role', ('group', 'seq', 'tp')), parts along dimension 1
There are 2 independent parts, one for each index of `group`. A program takes and returns all parts, laid end to end along the dimension named above; an argument that names none is the same for every part. Nothing has to cross between parts.
Inputs may be any that keep to these rules, and one draw needn't show every extreme that they name: `tok_conv`: in each device's block of 384 tokens conversation numbers never fall and each present number holds one or more tokens; in half 0 a block holds 8 conversations, in half 1 it holds 96 conversations of 4 tokens each. `page_conv`: in each device's block of 128 slots conversation numbers never fall, and every conversation of the matching token block has one or more slots. `page_fill`: every slot of a conversation but its last holds 16 live positions. `page_owner`: no owner is named by more than 64 slots of one device's block; in each half one owner is named by exactly 64 slots of every device's block. `page_index`: within a half, no two slots name the same owner and page number.
All inputs are finite; a program needn't handle non-finite values.
Results may differ from a plain program's by a relative error of at most 0.0066.
Values may be sent and summed in bfloat16 or wider, within the bound.
No kernel may reach another device: no remote copies, remote signals or barrier semaphores. Data moves between devices by JAX's collectives and lax.ppermute only.
A program may use at most 128 MiB of HBM per device.

v0:
```python
import math

import jax
import jax.numpy as jnp
from jax import lax
from jax.sharding import PartitionSpec as P

HD = 128


def bucket_ranks(slot_owner, owner_count):
    one_hot = (slot_owner[..., None] == jnp.arange(owner_count)).astype(jnp.int32)
    before = jnp.cumsum(one_hot, axis=-2) - one_hot
    return jnp.sum(before * one_hot, axis=-1)


def shards(
    queries, new_kv, pool, out_weight, tok_conv, page_conv, page_fill, page_owner, page_index
):
    row_count = queries.shape[1]
    channels = pool.shape[4]
    kv_local = channels // HD
    heads_local = queries.shape[2] // HD
    group_size = heads_local // kv_local
    page_len = pool.shape[3]
    slot_count = page_owner.shape[1]
    owner_count = lax.axis_size("seq")
    bucket = 2 * slot_count // owner_count
    slot_owner = page_owner[0]
    slot_page = page_index[0]
    slot_rank = bucket_ranks(slot_owner, owner_count)
    position = slot_owner * bucket + slot_rank
    local_pool = pool[0]
    wanted = (
        jnp.zeros((owner_count * bucket,), jnp.int32)
        .at[position]
        .set(slot_page)
        .reshape(owner_count, bucket)
    )
    found_pages = jnp.take(
        local_pool, lax.all_to_all(wanted, "seq", split_axis=0, concat_axis=0, tiled=True), axis=0
    )
    fetched = lax.all_to_all(found_pages, "seq", split_axis=0, concat_axis=0, tiled=True)
    flat_pages = fetched.reshape(owner_count * bucket, 2, page_len, channels)
    history = jnp.take(flat_pages, position, axis=0)
    key_rows = jnp.concatenate(
        [
            history[:, 0].reshape(slot_count * page_len, kv_local, HD),
            new_kv[0, :, 0].reshape(row_count, kv_local, HD),
        ],
        axis=0,
    )
    value_rows = jnp.concatenate(
        [
            history[:, 1].reshape(slot_count * page_len, kv_local, HD),
            new_kv[0, :, 1].reshape(row_count, kv_local, HD),
        ],
        axis=0,
    )
    key_heads = jnp.transpose(key_rows, (1, 0, 2))
    value_heads = jnp.transpose(value_rows, (1, 0, 2))
    token_conv = tok_conv[0]
    slot_range = jnp.arange(page_len)
    history_ok = (page_conv[0][:, None, None] == token_conv[None, None, :]) & (
        slot_range[None, :, None] < page_fill[0][:, None, None]
    )
    history_ok = history_ok.reshape(slot_count * page_len, row_count).T
    row_range = jnp.arange(row_count)
    fresh_ok = (token_conv[:, None] == token_conv[None, :]) & (
        row_range[None, :] <= row_range[:, None]
    )
    allowed = jnp.concatenate([history_ok, fresh_ok], axis=1)
    allowed_pair = jnp.concatenate([allowed, allowed], axis=0)
    pair_count = heads_local // 2
    query_pairs = (
        queries[0]
        .reshape(row_count, pair_count, 2, HD)
        .transpose(1, 2, 0, 3)
        .reshape(pair_count, 2 * row_count, HD)
    )
    score_scale = 1.0 / math.sqrt(HD)

    def attend(pair_index):
        kv_at = pair_index // (group_size // 2)
        key_block = lax.dynamic_index_in_dim(key_heads, kv_at, 0, keepdims=False)
        value_block = lax.dynamic_index_in_dim(value_heads, kv_at, 0, keepdims=False)
        query_block = lax.dynamic_index_in_dim(query_pairs, pair_index, 0, keepdims=False)
        scores = (
            jnp.einsum("qd,kd->qk", query_block, key_block, preferred_element_type=jnp.float32)
            * score_scale
        )
        scores = jnp.where(allowed_pair, scores, -jnp.inf)
        row_max = jnp.max(scores, axis=-1, keepdims=True)
        expanded = jnp.exp(scores - row_max)
        weights_bf = (expanded / jnp.sum(expanded, axis=-1, keepdims=True)).astype(jnp.bfloat16)
        return jnp.dot(weights_bf, value_block, preferred_element_type=jnp.float32).astype(
            jnp.bfloat16
        )

    attended_pairs = lax.map(attend, jnp.arange(pair_count))
    attended = (
        attended_pairs.reshape(pair_count, 2, row_count, HD)
        .transpose(2, 0, 1, 3)
        .reshape(row_count, heads_local * HD)
    )
    partial_sum = jnp.dot(
        attended,
        lax.all_gather(out_weight, "seq", axis=1, tiled=True),
        preferred_element_type=jnp.float32,
    ).astype(jnp.bfloat16)
    reduced = lax.psum_scatter(
        partial_sum.astype(jnp.float32).astype(jnp.bfloat16), "tp", scatter_dimension=0, tiled=True
    )
    return reduced[None]


def solution(mesh):
    return jax.shard_map(
        shards,
        mesh=mesh,
        in_specs=(
            P("role", ("group", "seq"), "tp"),
            P("role", ("group", "seq"), None, "tp"),
            P("role", ("group", "seq"), None, None, "tp"),
            P("tp", "seq"),
            P("role", ("group", "seq")),
            P("role", ("group", "seq")),
            P("role", ("group", "seq")),
            P("role", ("group", "seq")),
            P("role", ("group", "seq")),
        ),
        out_specs=P("role", ("group", "seq", "tp"), None),
        check_vma=False,
    )
```

profile of v0, /device:TPU:16, one launch (start us, length us, event | category | flops | bytes accessed | tf_op | source)
XLA Modules:
  0.0 446.5 jit_solution(7798305791847149548)
XLA Ops:
  7.7 1.1 scatter_custom_fusion
  8.9 8.2 %all_to_all.20 = s32[4,1,64]{2,1,0:T(1,128)S(1)} all-to-all(s32[4,1,64]{2,1,0:T(1,128)S(1)} %all_to_all.13), channel_id=1, replica_groups=mesh['group'=2,'seq'=4,'tp'=2,'role'=2] {'seq'}, dimensions={0} | all-to-all | bytes 2048 | tf_op jit(solution)/shard_map/all_to_all | solution.py:41
  17.2 5.8 %gather_fusion = bf16[256,2,16,256]{3,2,1,0:T(8,128)(2,1)} fusion(bf16[256,2,16,256]{3,2,1,0:T(8,128)(2,1)} %bitcast.72, s32[1024]{0:T(1024)S(1)} %pad_clamp_fusion.1), kind=kCustom, calls=%fused_computation | custom fusion | bytes 8389632 | tf_op jit(solution)/shard_map/jit(_take)/gather | solution.py:40
  23.0 4.2 broadcast_select_fusion
  27.2 7.3 %all-to-all-start.1 = ((bf16[4,64,2,16,256]{4,3,2,1,0:T(8,128)(2,1)}), bf16[4,64,2,16,256]{4,3,2,1,0:T(8,128)(2,1)}, u32[]{:S(2)}, u32[]{:S(2)}) async-start(bf16[4,64,2,16,256]{4,3,2,1,0:T(8,128)(2,1)} %broadcast_select_fusion), calls=%async_computation.1 | async-start | bytes 8388608 | tf_op jit(solution)/shard_map/all_to_all | solution.py:43
  37.1 0.9 copy.32
  39.0 4.3 add_add_fusion
  43.3 2.0 copy.34
  45.3 2.8 reshape_squeeze.15
  48.1 1.6 copy.28
  49.8 176.2 %all-to-all-done.1 = bf16[4,64,2,16,256]{4,3,2,1,0:T(8,128)(2,1)} async-done(((bf16[4,64,2,16,256]{4,3,2,1,0:T(8,128)(2,1)}), bf16[4,64,2,16,256]{4,3,2,1,0:T(8,128)(2,1)}, u32[]{:S(2)}, u32[]{:S(2)}) %all-to-all-start.1) | async-done | bytes 4194336 | tf_op jit(solution)/shard_map/all_to_all | solution.py:43
  226.0 4.2 gather_fusion.1
  230.2 1.9 broadcast_select_fusion.1
  232.1 1.5 fusion.19
  233.6 1.4 reshape_squeeze.16
  235.0 9.6 %maximum_bitcast_fusion = bf16[2,2432,128]{2,0,1:T(2,128)(2,1)S(1)} fusion(bf16[384,2,128]{2,1,0:T(2,128)(2,1)S(1)} %copy-done.3, bf16[2048,2,128]{2,1,0:T(2,128)(2,1)S(1)} %reshape_squeeze.16), kind=kLoop, calls=%fused_computation.24 | loop fusion | flops 622592 | bytes 2490368 | tf_op jit(solution)/shard_map/transpose | solution.py:60
  244.7 2.2 reshape_squeeze.18
  246.9 8.4 %maximum_bitcast_fusion.1 = bf16[2,2432,128]{2,0,1:T(2,128)(2,1)S(1)} fusion(bf16[384,2,128]{2,1,0:T(2,128)(2,1)S(1)} %copy-done.2, bf16[2048,2,128]{2,1,0:T(2,128)(2,1)} %reshape_squeeze.18), kind=kLoop, calls=%fused_computation.25 | loop fusion | flops 622592 | bytes 2490368 | tf_op jit(solution)/shard_map/transpose | solution.py:61
  255.3 1.2 copy.35
  256.6 81.5 %while.12 = (s32[]{:T(128)}, bf16[8,768,128]{2,1,0:T(8,128)(2,1)}, s32[8]{0:T(128)S(1)}, bf16[8,768,128]{2,1,0:T(8,128)(2,1)}, bf16[2,2432,128]{2,1,0:T(8,128)(2...) while((s32[]{:T(128)}, bf16[8,768,128]{2,1,0:T(8,128)(2,1)}, ...), condition=%wide.region_6.7_spmd, body=%wide.region_3.6_spmd.sunk | while | flops 971340288 | bytes 30918528 | solution.py:100
  260.4 2.7 fusion.28
  263.1 1.2 fusion.29
  264.4 2.4 fusion.30
  270.6 2.7 fusion.28
  273.3 1.2 fusion.29
  274.6 2.4 fusion.30
  280.8 2.7 fusion.28
  283.5 1.2 fusion.29
  284.7 2.4 fusion.30
  291.0 2.7 fusion.28
  293.6 1.2 fusion.29
  294.9 2.4 fusion.30
  301.2 2.7 fusion.28
  303.8 1.2 fusion.29
  305.1 2.4 fusion.30
  311.4 2.7 fusion.28
  314.0 1.2 fusion.29
  315.3 2.4 fusion.30
  321.5 2.7 fusion.28
  324.2 1.2 fusion.29
  325.5 2.4 fusion.30
  331.7 2.7 fusion.28
  334.4 1.2 fusion.29
  335.7 2.4 fusion.30
  338.1 1.9 copy.36
  340.0 43.4 %all-gather.2.cloned.1.call-done = bf16[2048,4096]{1,0:T(8,128)(2,1)} async-done(((bf16[2048,1024]{1,0:T(8,128)(2,1)}), bf16[2048,4096]{1,0:T(8,128)(2,1)}) %all-gather.2.cloned.1.call-update) | async-done | bytes 16777232 | tf_op jit(solution)/shard_map/all_gather | solution.py:108
  383.3 11.6 %convolution_convert_fusion = bf16[384,4096]{1,0:T(8,128)(2,1)} fusion(bf16[384,2048]{0,1:T(8,128)(2,1)S(1)} %bitcast.75, bf16[2048,4096]{1,0:T(8,128)(2,1)} %all-gather.2.cloned.1.call-done), kind=kOutput, calls=%fused_computation.20 | convolution fusion | flops 6444023808 | bytes 21495808 | tf_op jit(solution)/shard_map/dot_general | solution.py:106
  395.0 44.7 %reduce-scatter.2.cloned.1.call-done = bf16[192,4096]{1,0:T(8,128)(2,1)} async-done(((bf16[384,4096]{1,0:T(8,128)(2,1)}), bf16[192,4096]{1,0:T(8,128)(2,1)}) %reduce-scatter.2.cloned.1.call-update) | async-done | bytes 1572880 | tf_op jit(solution)/shard_map/reduce_scatter | solution.py:111
  (66 shorter events, 10.6 us)
Async XLA Ops:
  6.5 0.7 copy-start.4
  6.5 376.8 %all-gather.2.cloned.1.call-start = ((), (), s32[]{:S(2)}) async-start(), calls=%async_computation.3 | async-start | bytes 20971520 | tf_op jit(solution)/shard_map/all_gather | solution.py:108
  27.2 7.4 %copy-start = (bf16[1,384,2,256]{3,2,1,0:T(2,128)(2,1)S(1)}, bf16[1,384,2,256]{3,2,1,0:T(2,128)(2,1)}, u32[]{:S(2)}) copy-start(bf16[1,384,2,256]{3,2,1,0:T(2,128)(2,1)} %param.12) | copy-start | bytes 1179652
  27.2 198.8 %all-to-all-start.1 = ((bf16[4,64,2,16,256]{4,3,2,1,0:T(8,128)(2,1)}), bf16[4,64,2,16,256]{4,3,2,1,0:T(8,128)(2,1)}, u32[]{:S(2)}, u32[]{:S(2)}) async-start(bf16[4,64,2,16,256]{4,3,2,1,0:T(8,128)(2,1)} %broadcast_select_fusion), calls=%async_computation.1 | async-start | bytes 8388608 | tf_op jit(solution)/shard_map/all_to_all | solution.py:43
  34.5 3.5 copy-start.5
  34.5 3.5 copy-start.7
  34.5 3.7 copy-start.6
  34.5 405.2 %reduce-scatter.2.cloned.1.call-start = ((), (), s32[]{:S(2)}) async-start(), calls=%async_computation.4 | async-start | bytes 4718592 | tf_op jit(solution)/shard_map/reduce_scatter | solution.py:111
  233.6 1.4 copy-start.3
  244.5 2.4 copy-start.2
  263.1 1.3 copy-start.1
  273.3 1.3 copy-start.1
  283.4 1.3 copy-start.1
  293.6 1.3 copy-start.1
  303.8 1.3 copy-start.1
  314.0 1.3 copy-start.1
  324.2 1.3 copy-start.1
  334.4 1.3 copy-start.1
Sparse Core Ops, SparseCore 0:
  8.9 374.3 all-gather.1
  395.1 44.5 reduce-scatter.1
where the time goes:
time: 449 us; the launch traced here: 446 us
  waiting for transfers between devices  265 us (59%)
  matrix products  52 us (12%)
  other arithmetic  38.9 us (9%)
  local copies, waits for them, and re-layouts  35 us (8%)
  loops' own time  26.4 us (6%)
  between operations  13.6 us (3%)
  blocking collectives  8.19 us (2%)
  starting transfers between devices  7.33 us (2%)
    all_to_all x1, waiting for transfers between devices, shards(): lax.all_to_all(found_pages, 'seq', split_axis=0, concat_axis=0, tiled=True)  176 us
    reduce_scatter x1, waiting for transfers between devices, shards(): lax.psum_scatter(partial_sum.astype(jnp.float32).astype(jnp.bfloat16), 't...  44.7 us
    all_gather x1, waiting for transfers between devices, shards(): lax.all_gather(out_weight, 'seq', axis=1, tiled=True)  43.4 us
    another operation x1, loops' own time, shards(): attended_pairs = lax.map(attend, jnp.arange(pair_count))  26.4 us
    dot_general x8, matrix products, attend(): jnp.einsum('qd,kd->qk', query_block, key_block, preferred_element_type=jn...  21.3 us
    dot_general x8, matrix products, attend(): jnp.dot(weights_bf, value_block, preferred_element_type=jnp.float32)  19.1 us
    dot_general x1, matrix products, shards(): jnp.dot(attended, lax.all_gather(out_weight, 'seq', axis=1, tiled=True),...  11.6 us
    transpose x1, other arithmetic, shards(): key_heads = jnp.transpose(key_rows, (1, 0, 2))  9.55 us
  transfers between devices with their start and end apart: 3, of which 3 were waited for; matrix products, arithmetic and copies ran while one was open for 25% of the time, Pallas kernels for 0%

commit v1 on v0

v1 whole, which is shorter than its diff:
```python
import functools
import math

import jax
import jax.numpy as jnp
from jax import lax
from jax.experimental import pallas as pl
from jax.experimental.pallas import tpu as pltpu
from jax.sharding import PartitionSpec as P

HD = 128
TILE = 32
KEYS = 256
LANES = 128
HIDDEN = -1e30
PARTS = 2
VMEM = 56 * 1024 * 1024


def bucket_ranks(slot_owner, owner_count):
    one_hot = (slot_owner[..., None] == jnp.arange(owner_count)).astype(jnp.int32)
    before = jnp.cumsum(one_hot, axis=-2) - one_hot
    return jnp.sum(before * one_hot, axis=-1)


def attend_kernel(
    spec, position, hist_at, hist_steps, fresh_at, fresh_steps,
    query, pages, fresh, key_conv, key_row, tok_conv, out, keys, values, scores, sums,
):
    kv_local, group_size, slots, page_len, rows, fresh_base, key_total = spec
    channels = kv_local * HD
    hist = slots * page_len
    for head in range(kv_local):
        values[head, :, HD:] = jnp.ones((key_total, HD), jnp.bfloat16)
        for first, last in ((hist, fresh_base), (fresh_base + rows, key_total)):
            keys[head, first:last] = jnp.zeros((last - first, HD), jnp.bfloat16)
            values[head, first:last, :HD] = jnp.zeros((last - first, HD), jnp.bfloat16)
        at = head * HD
        keys[head, fresh_base : fresh_base + rows] = fresh[:, at : at + HD]
        values[head, fresh_base : fresh_base + rows, :HD] = fresh[:, channels + at : channels + at + HD]

    def place(slot, carry):
        page = position[slot]
        row = pl.ds(pl.multiple_of(slot * page_len, page_len), page_len)
        for head in range(kv_local):
            at = head * HD
            keys[head, row] = pages[page, 0, :, at : at + HD]
            values[head, row, :HD] = pages[page, 1, :, at : at + HD]
        return carry

    lax.fori_loop(0, slots, place, 0, unroll=8)
    to_exp2 = math.log2(math.e) / math.sqrt(HD)
    wide = group_size * TILE

    def tile(index, carry):
        first = pl.multiple_of(index * TILE, TILE)
        tokens = pl.ds(first, TILE)
        conv = tok_conv[tokens]
        number = first + lax.broadcasted_iota(jnp.int32, (TILE, 1), 0)
        steps_h, steps_f = hist_steps[index], fresh_steps[index]
        at_h, at_f = hist_at[index], fresh_at[index]
        heads = [
            jnp.concatenate(
                [
                    query[tokens, (head * group_size + g) * HD : (head * group_size + g + 1) * HD]
                    for g in range(group_size)
                ],
                axis=0,
            )
            for head in range(kv_local)
        ]

        def key_range(step):
            start = jnp.where(
                step < steps_h, at_h + step * KEYS, fresh_base + at_f + (step - steps_h) * KEYS
            )
            return pl.ds(pl.multiple_of(start, LANES), KEYS)

        def score(step, tops):
            where = key_range(step)
            ok = (key_conv[:, where] == conv) & (key_row[:, where] <= number)
            held = pl.ds(pl.multiple_of(step * KEYS, KEYS), KEYS)
            new = []
            for head in range(kv_local):
                s = lax.dot_general(
                    heads[head], keys[head, where], (((1,), (1,)), ((), ())),
                    preferred_element_type=jnp.float32,
                ).reshape(group_size, TILE, KEYS)
                s = jnp.where(ok[None], s, HIDDEN).reshape(wide, KEYS)
                scores[head, :, held] = s
                top = tops[head]
                for k in range(0, KEYS, LANES):
                    top = jnp.maximum(top, s[:, k : k + LANES])
                new.append(top)
            return tuple(new)

        low = jnp.full((wide, LANES), HIDDEN, jnp.float32)
        tops = lax.fori_loop(0, steps_h + steps_f, score, (low,) * kv_local)
        tops = [jnp.max(top, axis=1, keepdims=True) * to_exp2 for top in tops]
        sums[...] = jnp.zeros_like(sums)

        def gather(step, carry):
            where = key_range(step)
            held = pl.ds(pl.multiple_of(step * KEYS, KEYS), KEYS)
            for head in range(kv_local):
                w = jnp.exp2(scores[head, :, held] * to_exp2 - tops[head]).astype(jnp.bfloat16)
                sums[head] += jnp.dot(w, values[head, where], preferred_element_type=jnp.float32)
            return carry

        lax.fori_loop(0, steps_h + steps_f, gather, 0)
        for head in range(kv_local):
            done = (sums[head, :, :HD] / sums[head, :, HD:]).astype(jnp.bfloat16)
            for g in range(group_size):
                at = (head * group_size + g) * HD
                out[tokens, at : at + HD] = done[g * TILE : (g + 1) * TILE]
        return carry

    lax.fori_loop(0, rows // TILE, tile, 0)


def attend(queries, pages, new_kv, position, tok_conv, page_conv, page_fill):
    rows, width = queries.shape
    page_len, channels = pages.shape[2], pages.shape[3]
    slots = position.shape[0]
    kv_local = channels // HD
    group_size = width // channels
    hist = slots * page_len
    fresh_base = hist + KEYS
    key_total = fresh_base + pl.cdiv(rows, KEYS) * KEYS + KEYS
    live = jnp.arange(page_len)[None, :] < page_fill[:, None]
    hist_conv = jnp.where(live, page_conv[:, None], -1).reshape(hist)
    tail = key_total - fresh_base - rows
    key_conv = jnp.concatenate(
        [hist_conv, jnp.full((KEYS,), -1, jnp.int32), tok_conv, jnp.full((tail,), -1, jnp.int32)]
    )[None]
    key_row = jnp.maximum(jnp.arange(key_total, dtype=jnp.int32) - fresh_base, -1)[None]
    lowest, highest = tok_conv[::TILE], tok_conv[TILE - 1 :: TILE]
    hist_at = jnp.sum(page_conv[None] < lowest[:, None], axis=1, dtype=jnp.int32) * page_len
    hist_at = hist_at // LANES * LANES
    hist_end = jnp.sum(page_conv[None] <= highest[:, None], axis=1, dtype=jnp.int32) * page_len
    hist_steps = (hist_end - hist_at + KEYS - 1) // KEYS
    fresh_at = jnp.sum(tok_conv[None] < lowest[:, None], axis=1, dtype=jnp.int32) // LANES * LANES
    fresh_end = (jnp.arange(rows // TILE, dtype=jnp.int32) + 1) * TILE
    fresh_steps = (fresh_end - fresh_at + KEYS - 1) // KEYS
    most = (hist // KEYS + 1 + pl.cdiv(rows, KEYS) + 1) * KEYS
    spec = (kv_local, group_size, slots, page_len, rows, fresh_base, key_total)
    smem = pl.BlockSpec(memory_space=pltpu.SMEM)
    vmem = pl.BlockSpec(memory_space=pltpu.VMEM)
    return pl.pallas_call(
        functools.partial(attend_kernel, spec),
        out_shape=jax.ShapeDtypeStruct((rows, width), jnp.bfloat16),
        in_specs=[smem] * 5 + [vmem] * 6,
        out_specs=vmem,
        scratch_shapes=[
            pltpu.VMEM((kv_local, key_total, HD), jnp.bfloat16),
            pltpu.VMEM((kv_local, key_total, 2 * HD), jnp.bfloat16),
            pltpu.VMEM((kv_local, group_size * TILE, most), jnp.float32),
            pltpu.VMEM((kv_local, group_size * TILE, 2 * HD), jnp.float32),
        ],
        compiler_params=pltpu.CompilerParams(vmem_limit_bytes=VMEM),
        cost_estimate=pl.CostEstimate(
            flops=rows * width * 800 * 4, bytes_accessed=8 << 20, transcendentals=rows * width // HD * 800
        ),
        name="attend",
    )(
        position, hist_at, hist_steps, fresh_at, fresh_steps,
        queries, pages, new_kv, key_conv, key_row, tok_conv[:, None],
    )


def project_kernel(places, attended, *refs):
    pieces, (kept, sent) = refs[:-2], refs[-2:]
    depth = pieces[0].shape[1]
    half = kept.shape[1]
    for row, out in ((places[0], kept), (places[1], sent)):
        total = None
        for n, piece in enumerate(pieces):
            at = pl.ds(pl.multiple_of(places[2 + n] * depth, depth), depth)
            term = jnp.dot(
                attended[pl.ds(pl.multiple_of(row * half, 16), half), at],
                piece[0],
                preferred_element_type=jnp.float32,
            )
            total = term if total is None else total + term
        out[0] = total.astype(jnp.bfloat16)


def project(attended, pieces, places):
    rows, width = attended.shape
    owners, depth, columns = pieces[0].shape
    half = rows // 2
    shape = jax.ShapeDtypeStruct((owners, half, columns), jnp.bfloat16)
    block = pl.BlockSpec((1, half, columns), lambda z, places: (z, 0, 0))
    return pl.pallas_call(
        project_kernel,
        out_shape=(shape, shape),
        grid_spec=pltpu.PrefetchScalarGridSpec(
            num_scalar_prefetch=1,
            grid=(owners,),
            in_specs=[pl.BlockSpec((rows, width), lambda z, places: (0, 0))]
            + [pl.BlockSpec((1, depth, columns), lambda z, places: (z, 0, 0))] * len(pieces),
            out_specs=(block, block),
        ),
        compiler_params=pltpu.CompilerParams(vmem_limit_bytes=VMEM),
        cost_estimate=pl.CostEstimate(
            flops=2 * rows * width * owners * columns,
            bytes_accessed=2 * (rows * width + (width + rows) * owners * columns),
            transcendentals=0,
        ),
        name="project",
    )(places, attended, *pieces)


def join_kernel(*refs):
    out = refs[-1]
    count = (len(refs) - 1) // 2
    columns = refs[0].shape[2]
    for n in range(count):
        total = refs[n][0].astype(jnp.float32) + refs[count + n][0].astype(jnp.float32)
        out[0, :, n * columns : (n + 1) * columns] = total.astype(jnp.bfloat16)


def join(kept, came):
    owners, half, columns = kept[0].shape
    count = len(kept)
    return pl.pallas_call(
        join_kernel,
        out_shape=jax.ShapeDtypeStruct((1, half, owners * columns * count), jnp.bfloat16),
        grid=(owners,),
        in_specs=[pl.BlockSpec((1, half, columns), lambda z: (z, 0, 0))] * (2 * count),
        out_specs=pl.BlockSpec((1, half, columns * count), lambda z: (0, 0, z)),
        compiler_params=pltpu.CompilerParams(vmem_limit_bytes=VMEM),
        name="join",
    )(*kept, *came)


SWAP = [(0, 1), (1, 0)]


def shards(
    queries, new_kv, pool, out_weight, tok_conv, page_conv, page_fill, page_owner, page_index
):
    row_count = queries.shape[1]
    slot_count = page_owner.shape[1]
    owner_count = lax.axis_size("seq")
    tp_count = lax.axis_size("tp")
    bucket = 2 * slot_count // owner_count
    group, role, tp = lax.axis_index("group"), lax.axis_index("role"), lax.axis_index("tp")

    depth = out_weight.shape[0] // 4
    columns = out_weight.shape[1]
    parts = PARTS if columns % (PARTS * LANES) == 0 else 1
    part = columns // parts
    quarter = lax.dynamic_slice_in_dim(out_weight, (2 * group + role) * depth, depth, 0)
    gathered = [
        lax.all_gather(quarter[:, n * part : (n + 1) * part], "seq", axis=0) for n in range(parts)
    ]
    weights = []
    for own in gathered:
        across = lax.ppermute(own, "group", SWAP)
        weights.append((own, across, lax.ppermute(own, "role", SWAP), lax.ppermute(across, "role", SWAP)))

    slot_owner = page_owner[0]
    position = slot_owner * bucket + bucket_ranks(slot_owner, owner_count)
    wanted = (
        jnp.zeros((owner_count * bucket,), jnp.int32)
        .at[position]
        .set(page_index[0], mode="promise_in_bounds", unique_indices=True)
        .reshape(owner_count, bucket)
    )
    asked = lax.all_to_all(wanted, "seq", split_axis=0, concat_axis=0, tiled=True)
    found = pool[0].at[asked].get(mode="promise_in_bounds")
    fetched = lax.all_to_all(found, "seq", split_axis=0, concat_axis=0, tiled=True)
    pages = fetched.reshape((owner_count * bucket,) + pool.shape[2:])

    attended = attend(
        queries[0], pages, new_kv[0].reshape(row_count, -1), position,
        tok_conv[0], page_conv[0], page_fill[0],
    )

    if tp_count != 2:
        partial = []
        places = jnp.stack(
            [0, 1, 2 * group + role, 2 * (1 - group) + role, 2 * group + 1 - role,
             2 * (1 - group) + 1 - role]
        ).astype(jnp.int32)
        for pieces in weights:
            partial.append(jnp.concatenate(project(attended, pieces, places), axis=1))
        partial = jnp.stack(partial, axis=2).transpose(1, 0, 2, 3).reshape(row_count, -1)
        return lax.psum_scatter(partial, "tp", scatter_dimension=0, tiled=True)[None]

    places = jnp.stack(
        [tp, 1 - tp, 2 * group + role, 2 * (1 - group) + role, 2 * group + 1 - role,
         2 * (1 - group) + 1 - role]
    ).astype(jnp.int32)
    kept, came = [], []
    for pieces in weights:
        mine, theirs = project(attended, pieces, places)
        kept.append(mine)
        came.append(lax.ppermute(theirs, "tp", SWAP))
    return join(kept, came)


def solution(mesh):
    return jax.shard_map(
        shards,
        mesh=mesh,
        in_specs=(
            P("role", ("group", "seq"), "tp"),
            P("role", ("group", "seq"), None, "tp"),
            P("role", ("group", "seq"), None, None, "tp"),
            P("tp", "seq"),
            P("role", ("group", "seq")),
            P("role", ("group", "seq")),
            P("role", ("group", "seq")),
            P("role", ("group", "seq")),
            P("role", ("group", "seq")),
        ),
        out_specs=P("role", ("group", "seq", "tp"), None),
        check_vma=False,
    )
```

time: 449 us -> 307 us (0.68)
  waiting for transfers between devices: 265 us -> 203 us
  matrix products: 52 us -> 0 us
  Pallas kernels: 0 us -> 48.1 us
  other arithmetic: 38.9 us -> 3.26 us
  loops' own time: 26.4 us -> 0 us
  local copies, waits for them, and re-layouts: 35 us -> 12.2 us
  starting transfers between devices: 7.33 us -> 12.8 us
    all_to_all x1, waiting for transfers between devices: 176 us -> 0.01 us  [shards(): lax.all_to_all(found, 'seq', split_axis=0, concat_axis=0, tiled=True)]
    all_gather x1 -> x2, waiting for transfers between devices: 43.4 us -> 137 us  [shards(): lax.all_gather(quarter[:, n * part:(n + 1) * part], 'seq', axis=0)]
    ppermute x0 -> x8, waiting for transfers between devices: none -> 65.2 us  [the longest x2 45.8 us: shards(): across = lax.ppermute(own, 'group', SWAP)]
    dot_general x17 -> x0, matrix products: 52 us -> none  [the longest x8 21.3 us: attend(): jnp.einsum('qd,kd->qk', query_block, key_block, preferred_element_type=jn...]
    pallas_call x0 -> x4, Pallas kernels: none -> 48.1 us  [the longest x1 27.1 us: attend(): pl.pallas_call(functools.partial(attend_kernel, spec), out_shape=jax.Shap...]
    reduce_scatter x1 -> x0, waiting for transfers between devices: 44.7 us -> none  [shards(): lax.psum_scatter(partial_sum.astype(jnp.float32).astype(jnp.bfloat16), 't...]
    another operation x1 -> x0, loops' own time: 26.4 us -> none  [shards(): attended_pairs = lax.map(attend, jnp.arange(pair_count))]
    transpose x2 -> x0, other arithmetic: 18 us -> none  [the longest x1 9.55 us: shards(): key_heads = jnp.transpose(key_rows, (1, 0, 2))]
  transfers between devices with their start and end apart: 3 -> 11, of which waited for: 3 -> 5; matrix products, arithmetic and copies ran while one was open for 25% -> 4% of each run, Pallas kernels for 0% -> 15%
where the time goes in v1:
time: 307 us; the launch traced here: 301 us
  waiting for transfers between devices  203 us (66%)
  Pallas kernels  48.1 us (16%)
  between operations  13.5 us (4%)
  starting transfers between devices  12.8 us (4%)
  local copies, waits for them, and re-layouts  12.2 us (4%)
  blocking collectives  8.19 us (3%)
  other arithmetic  3.26 us (1%)
    all_gather x2, waiting for transfers between devices, shards(): lax.all_gather(quarter[:, n * part:(n + 1) * part], 'seq', axis=0)  137 us
    ppermute x2, waiting for transfers between devices, shards(): across = lax.ppermute(own, 'group', SWAP)  45.8 us
    pallas_call x1, Pallas kernels, attend(): pl.pallas_call(functools.partial(attend_kernel, spec), out_shape=jax.Shap...  27.1 us
    ppermute x2, waiting for transfers between devices, shards(): came.append(lax.ppermute(theirs, 'tp', SWAP))  19.4 us
    pallas_call x2, Pallas kernels, project(): pl.pallas_call(project_kernel, out_shape=(shape, shape), grid_spec=pltpu....  16.9 us
    all_to_all x1, blocking collectives, shards(): lax.all_to_all(wanted, 'seq', split_axis=0, concat_axis=0, tiled=True)  8.19 us
    all_to_all x1, starting transfers between devices, shards(): lax.all_to_all(found, 'seq', split_axis=0, concat_axis=0, tiled=True)  7.3 us
  transfers between devices with their start and end apart: 11, of which 5 were waited for; matrix products, arithmetic and copies ran while one was open for 4% of the time, Pallas kernels for 15%

profile of v1, /device:TPU:16, one launch (start us, length us, event | category | flops | bytes accessed | tf_op | source)
XLA Modules:
  0.0 301.5 jit_solution(9293854024302959045)
XLA Ops:
  6.5 2.3 fusion.9
  8.8 0.0 all-gather.7.cloned.1.call-update
  8.8 0.0 all-gather.5.cloned.1.call-start
  8.9 0.7 all-gather.5.cloned.1.call-update
  9.6 0.1 fusion
  9.7 0.2 reduce_window_sum.11
  9.9 0.2 select_reduce_fusion
  10.0 1.1 scatter_custom_fusion
  11.2 0.1 all_to_all.11
  11.2 8.2 %all_to_all.17 = s32[4,1,64]{2,1,0:T(1,128)S(1)} all-to-all(s32[4,1,64]{2,1,0:T(1,128)S(1)} %all_to_all.11), channel_id=1, replica_groups=mesh['group'=2,'seq'=4,'tp'=2,'role'=2] {'seq'}, dimensions={0} | all-to-all | bytes 2048 | tf_op jit(solution)/shard_map/all_to_all | solution.py:271
  19.4 0.1 reshape.88
  19.5 5.0 %gather_fusion = bf16[256,2,16,256]{3,2,1,0:T(8,128)(2,1)} fusion(bf16[256,2,16,256]{3,2,1,0:T(8,128)(2,1)} %bitcast.34, s32[1024]{0:T(1024)S(1)} %pad_clamp_fusion), kind=kCustom, calls=%fused_computation | custom fusion | bytes 8389632 | tf_op jit(solution)/shard_map/gather | solution.py:272
  24.5 7.3 %all-to-all-start.1 = ((bf16[4,64,2,16,256]{4,3,2,1,0:T(8,128)(2,1)}), bf16[4,64,2,16,256]{4,3,2,1,0:T(8,128)(2,1)}, u32[]{:S(2)}, u32[]{:S(2)}) async-start(bf16[4,64,2,16,256]{4,3,2,1,0:T(8,128)(2,1)} %bitcast.33), calls=%async_computation.1 | async-start | bytes 8388608 | tf_op jit(solution)/shard_map/all_to_all | solution.py:273
  31.8 54.3 %all-gather.7.cloned.1.call-done = bf16[2048,512]{1,0:T(8,128)(2,1)} async-done(((bf16[512,512]{1,0:T(8,128)(2,1)}), bf16[2048,512]{1,0:T(8,128)(2,1)}) %all-gather.7.cloned.1.call-update) | async-done | bytes 2097168 | tf_op jit(solution)/shard_map/all_gather | solution.py:256
  86.1 1.4 collective-permute-start.3
  87.5 83.2 %all-gather.5.cloned.1.call-done = bf16[2048,512]{1,0:T(8,128)(2,1)} async-done(((bf16[512,512]{1,0:T(8,128)(2,1)}), bf16[2048,512]{1,0:T(8,128)(2,1)}) %all-gather.5.cloned.1.call-update) | async-done | bytes 2097168 | tf_op jit(solution)/shard_map/all_gather | solution.py:256
  170.8 1.5 collective-permute-start
  172.2 0.0 collective-permute-start.4
  172.2 0.0 collective-permute-done.3.refs_1_
  172.2 0.5 collective-permute-start.5
  172.8 0.0 collective-permute-start.1
  172.8 45.8 %collective-permute-done.refs_1_ = bf16[4,512,512]{2,1,0:T(8,128)(2,1)S(1)} collective-permute-done((bf16[4,512,512]{2,1,0:T(8,128)(2,1)}, bf16[4,512,512]{2,1,0:T(8,128)(2,1)S(1)}, u32[]{:S(2)}, u32[]{:S(2)}) %collective-permute-start) | collective-permute-done | bytes 2097184 | tf_op jit(solution)/shard_map/ppermute | solution.py:260
  218.6 0.1 slice.12
  218.7 0.1 slice.13
  218.8 0.1 fusion.1
  219.0 0.1 select_n.52
  219.0 1.0 copy.12
  220.1 0.8 copy.11.tok_conv
  220.9 0.6 stack.27.places
  221.5 0.6 pad_add_fusion
  222.1 0.2 convert_reduce_fusion
  222.3 0.2 convert_reduce_fusion.1
  222.5 0.5 multiply_add_fusion.position
  223.0 0.6 and_select_fusion
  223.6 0.6 add_maximum_fusion.key_row
  224.2 0.0 all-to-all-done.1
  224.2 27.1 %attend.1.attended = bf16[384,2048]{1,0:T(8,128)(2,1)} custom-call(s32[128]{0:T(128)} %multiply_add_fusion.position, s32[12]{0:T(128)} %get-tuple-element.22.hist_at, s32[12]{0:T(128)} %get-tuple-element.21.hist_steps, s32[12]{0:T(128)} %get-tuple-element.16.fresh_at, s32[12]{0:T(128)} %get-tuple-element.15.fresh_steps, bf16[384,2048]{1,0:T(8,128)(2,1)} %bitcast.51, ...), custom_call_target="tpu_custom_call" | custom-call | flops 2516582400 | bytes 8388608 | tf_op jit(solution)/shard_map/attend/pallas_call | solution.py:149
  251.3 0.0 collective-permute-done.4.refs_2_
  251.3 0.0 collective-permute-done.5.refs_3_
  251.4 8.5 %project.3 = (bf16[4,192,512]{2,1,0:T(8,128)(2,1)}, bf16[4,192,512]{2,1,0:T(8,128)(2,1)}) custom-call(s32[6]{0:T(128)} %stack.27.places, bf16[384,2048]{1,0:T(8,128)(2,1)} %attend.1.attended, bf16[4,512,512]{2,1,0:T(8,128)(2,1)} %bitcast.50, bf16[4,512,512]{2,1,0:T(8,128)(2,1)} %collective-permute-done.3.refs_1_, ...), custom_call_target="tpu_custom_call" | custom-call | flops 3221225472 | bytes 11534336 | tf_op jit(solution)/shard_map/project/pallas_call | solution.py:194
  259.8 1.5 collective-permute-start.7
  261.3 0.0 collective-permute-done.1.refs_2_
  261.3 8.5 %project.2 = (bf16[4,192,512]{2,1,0:T(8,128)(2,1)}, bf16[4,192,512]{2,1,0:T(8,128)(2,1)}) custom-call(s32[6]{0:T(128)} %stack.27.places, bf16[384,2048]{1,0:T(8,128)(2,1)} %attend.1.attended, bf16[4,512,512]{2,1,0:T(8,128)(2,1)} %bitcast.47, bf16[4,512,512]{2,1,0:T(8,128)(2,1)} %copy-done.7, bf16[4,512,512]{2,1,0:T(8,128)(2,1)} %collective-permute-done.1.refs_2_, ...), custom_call_target="tpu_custom_call" | custom-call | flops 3221225472 | bytes 11534336 | tf_op jit(solution)/shard_map/project/pallas_call | solution.py:194
  269.7 0.6 collective-permute-start.6
  270.3 9.7 %collective-permute-done.7.refs_3_ = bf16[4,192,512]{2,1,0:T(8,128)(2,1)S(1)} collective-permute-done((bf16[4,192,512]{2,1,0:T(8,128)(2,1)}, bf16[4,192,512]{2,1,0:T(8,128)(2,1)S(1)}, u32[]{:S(2)}, u32[]{:S(2)}) %collective-permute-start.7) | collective-permute-done | bytes 786464 | tf_op jit(solution)/shard_map/ppermute | solution.py:300
  280.0 9.7 %collective-permute-done.6.refs_2_ = bf16[4,192,512]{2,1,0:T(8,128)(2,1)S(1)} collective-permute-done((bf16[4,192,512]{2,1,0:T(8,128)(2,1)}, bf16[4,192,512]{2,1,0:T(8,128)(2,1)S(1)}, u32[]{:S(2)}, u32[]{:S(2)}) %collective-permute-start.6) | collective-permute-done | bytes 786464 | tf_op jit(solution)/shard_map/ppermute | solution.py:300
  289.7 0.9 copy-done.1
  290.6 4.1 %join.1 = bf16[1,192,4096]{2,1,0:T(8,128)(2,1)} custom-call(bf16[4,192,512]{2,1,0:T(8,128)(2,1)} %get-tuple-element.9.refs_0_, bf16[4,192,512]{2,1,0:T(8,128)(2,1)} %get-tuple-element.10.refs_1_, bf16[4,192,512]{2,1,0:T(8,128)(2,1)} %copy-done.1, bf16[4,192,512]{2,1,0:T(8,128)(2,1)} %copy-done), custom_call_target="tpu_custom_call" | custom-call | tf_op jit(solution)/shard_map/join/pallas_call | solution.py:226
  (24 shorter events, 0.1 us)
Async XLA Ops:
  6.5 3.0 %copy-start.4 = (s32[1,128]{1,0:T(1,128)S(1)}, s32[1,128]{1,0:T(1,128)}, u32[]{:S(2)}) copy-start(s32[1,128]{1,0:T(1,128)} %param.16) | copy-start | bytes 1540
  6.5 79.6 %all-gather.7.cloned.1.call-start = ((), (), s32[]{:S(2)}) async-start(), calls=%async_computation.3 | async-start | bytes 2621440 | tf_op jit(solution)/shard_map/all_gather | solution.py:256
  8.8 161.9 %all-gather.5.cloned.1.call-start = ((), (), s32[]{:S(2)}) async-start(), calls=%async_computation.2 | async-start | bytes 2621440 | tf_op jit(solution)/shard_map/all_gather | solution.py:256
  24.5 194.1 %copy-start.3 = (s32[1,384]{1,0:T(1,128)S(1)}, s32[1,384]{1,0:T(1,128)}, u32[]{:S(2)}) copy-start(s32[1,384]{1,0:T(1,128)} %param.13) | copy-start | bytes 4612
  24.5 194.3 %copy-start.5 = (s32[1,128]{1,0:T(1,128)S(1)}, s32[1,128]{1,0:T(1,128)}, u32[]{:S(2)}) copy-start(s32[1,128]{1,0:T(1,128)} %param.14) | copy-start | bytes 1540
  24.5 194.3 %copy-start.6 = (s32[1,128]{1,0:T(1,128)S(1)}, s32[1,128]{1,0:T(1,128)}, u32[]{:S(2)}) copy-start(s32[1,128]{1,0:T(1,128)} %param.15) | copy-start | bytes 1540
  24.5 194.5 %copy-start.2 = (bf16[1,384,2,256]{3,2,1,0:T(2,128)(2,1)S(1)}, bf16[1,384,2,256]{3,2,1,0:T(2,128)(2,1)}, u32[]{:S(2)}) copy-start(bf16[1,384,2,256]{3,2,1,0:T(2,128)(2,1)} %param.10) | copy-start | bytes 1179652
  24.5 199.7 %all-to-all-start.1 = ((bf16[4,64,2,16,256]{4,3,2,1,0:T(8,128)(2,1)}), bf16[4,64,2,16,256]{4,3,2,1,0:T(8,128)(2,1)}, u32[]{:S(2)}, u32[]{:S(2)}) async-start(bf16[4,64,2,16,256]{4,3,2,1,0:T(8,128)(2,1)} %bitcast.33), calls=%async_computation.1 | async-start | bytes 8388608 | tf_op jit(solution)/shard_map/all_to_all | solution.py:273
  86.1 86.1 %collective-permute-start.3 = (bf16[4,512,512]{2,1,0:T(8,128)(2,1)}, bf16[4,512,512]{2,1,0:T(8,128)(2,1)}, u32[]{:S(2)}, u32[]{:S(2)}) collective-permute-start(bf16[4,512,512]{2,1,0:T(8,128)(2,1)} %bitcast.48), channel_id=1, source_target_pairs={{0,16},{16,0},{1,17},{17,1},{2,18},{18,2},{3,19},{19,3},{4,20},{20... | collective-permute-start | bytes 6291464 | tf_op jit(solution)/shard_map/ppermute | solution.py:260
  170.8 47.8 %collective-permute-start = (bf16[4,512,512]{2,1,0:T(8,128)(2,1)}, bf16[4,512,512]{2,1,0:T(8,128)(2,1)S(1)}, u32[]{:S(2)}, u32[]{:S(2)}) collective-permute-start(bf16[4,512,512]{2,1,0:T(8,128)(2,1)} %bitcast.45), channel_id=1, source_target_pairs={{0,16},{16,0},{1,17},{17,1},{2,18},{18,2},{3,19},{19,3},{4,20},{20... | collective-permute-start | bytes 6291464 | tf_op jit(solution)/shard_map/ppermute | solution.py:260
  172.2 79.1 %collective-permute-start.4 = (bf16[4,512,512]{2,1,0:T(8,128)(2,1)}, bf16[4,512,512]{2,1,0:T(8,128)(2,1)}, u32[]{:S(2)}, u32[]{:S(2)}) collective-permute-start(bf16[4,512,512]{2,1,0:T(8,128)(2,1)} %bitcast.49), channel_id=1, source_target_pairs={{0,1},{1,0},{2,3},{3,2},{4,5},{5,4},{6,7},{7,6},{8,9},{9,8},{10,11... | collective-permute-start | bytes 6291464 | tf_op jit(solution)/shard_map/ppermute | solution.py:261
  172.2 79.1 %collective-permute-start.5 = (bf16[4,512,512]{2,1,0:T(8,128)(2,1)}, bf16[4,512,512]{2,1,0:T(8,128)(2,1)}, u32[]{:S(2)}, u32[]{:S(2)}) collective-permute-start(bf16[4,512,512]{2,1,0:T(8,128)(2,1)} %collective-permute-done.3.refs_1_), channel_id=1, source_target_pairs={{0,1},{1,0},{2,3},{3,2},{4,5},{5,4},{6,7},{7,6},{8,9},{9,8},{10,11... | collective-permute-start | bytes 6291464 | tf_op jit(solution)/shard_map/ppermute | solution.py:261
  172.8 88.5 %collective-permute-start.1 = (bf16[4,512,512]{2,1,0:T(8,128)(2,1)}, bf16[4,512,512]{2,1,0:T(8,128)(2,1)}, u32[]{:S(2)}, u32[]{:S(2)}) collective-permute-start(bf16[4,512,512]{2,1,0:T(8,128)(2,1)} %bitcast.46), channel_id=1, source_target_pairs={{0,1},{1,0},{2,3},{3,2},{4,5},{5,4},{6,7},{7,6},{8,9},{9,8},{10,11... | collective-permute-start | bytes 6291464 | tf_op jit(solution)/shard_map/ppermute | solution.py:261
  218.6 32.7 %copy-start.7 = (bf16[4,512,512]{2,1,0:T(8,128)(2,1)}, bf16[4,512,512]{2,1,0:T(8,128)(2,1)S(1)}, u32[]{:S(2)}) copy-start(bf16[4,512,512]{2,1,0:T(8,128)(2,1)S(1)} %collective-permute-done.refs_1_) | copy-start | bytes 6291460
  218.6 42.7 %collective-permute-start.2 = (bf16[4,512,512]{2,1,0:T(8,128)(2,1)S(1)}, bf16[4,512,512]{2,1,0:T(8,128)(2,1)}, u32[]{:S(2)}, u32[]{:S(2)}) collective-permute-start(bf16[4,512,512]{2,1,0:T(8,128)(2,1)S(1)} %collective-permute-done.refs_1_), channel_id=1, source_target_pairs={{0,1},{1,0},{2,3},{3,2},{4,5},{5,4},{6,7},{7,6},{8,9},{9,8},{10,11... | collective-permute-start | bytes 6291464 | tf_op jit(solution)/shard_map/ppermute | solution.py:261
  259.8 20.1 %collective-permute-start.7 = (bf16[4,192,512]{2,1,0:T(8,128)(2,1)}, bf16[4,192,512]{2,1,0:T(8,128)(2,1)S(1)}, u32[]{:S(2)}, u32[]{:S(2)}) collective-permute-start(bf16[4,192,512]{2,1,0:T(8,128)(2,1)} %get-tuple-element.12), channel_id=1, source_target_pairs={{0,2},{2,0},{1,3},{3,1},{4,6},{6,4},{5,7},{7,5},{8,10},{10,8},{9,1... | collective-permute-start | bytes 2359304 | tf_op jit(solution)/shard_map/ppermute | solution.py:300
  269.7 19.9 %collective-permute-start.6 = (bf16[4,192,512]{2,1,0:T(8,128)(2,1)}, bf16[4,192,512]{2,1,0:T(8,128)(2,1)S(1)}, u32[]{:S(2)}, u32[]{:S(2)}) collective-permute-start(bf16[4,192,512]{2,1,0:T(8,128)(2,1)} %get-tuple-element.11), channel_id=1, source_target_pairs={{0,2},{2,0},{1,3},{3,1},{4,6},{6,4},{5,7},{7,5},{8,10},{10,8},{9,1... | collective-permute-start | bytes 2359304 | tf_op jit(solution)/shard_map/ppermute | solution.py:300
  280.0 9.7 %copy-start = (bf16[4,192,512]{2,1,0:T(8,128)(2,1)}, bf16[4,192,512]{2,1,0:T(8,128)(2,1)S(1)}, u32[]{:S(2)}) copy-start(bf16[4,192,512]{2,1,0:T(8,128)(2,1)S(1)} %collective-permute-done.7.refs_3_) | copy-start | bytes 2359300
  289.7 0.9 copy-start.1
Sparse Core Ops, SparseCore 0:
  8.9 77.1 all-gather.6
  87.7 83.0 all-gather.4

commit v2 on v1

--- a/solution.py
+++ b/solution.py
@@ -9,11 +9,11 @@
 from jax.sharding import PartitionSpec as P
 
 HD = 128
-TILE = 32
+TILE = 64
 KEYS = 256
 LANES = 128
 HIDDEN = -1e30
-PARTS = 2
+PARTS = 4
 VMEM = 56 * 1024 * 1024
 
 
@@ -168,47 +168,58 @@
     )
 
 
-def project_kernel(places, attended, *refs):
-    pieces, (kept, sent) = refs[:-2], refs[-2:]
+def project_kernel(kv_local, places, *refs):
+    heads, pieces = refs[:kv_local], refs[kv_local:-3]
+    kept, sent, left = refs[-3:]
     depth = pieces[0].shape[1]
     half = kept.shape[1]
-    for row, out in ((places[0], kept), (places[1], sent)):
-        total = None
-        for n, piece in enumerate(pieces):
-            at = pl.ds(pl.multiple_of(places[2 + n] * depth, depth), depth)
-            term = jnp.dot(
-                attended[pl.ds(pl.multiple_of(row * half, 16), half), at],
-                piece[0],
-                preferred_element_type=jnp.float32,
-            )
-            total = term if total is None else total + term
-        out[0] = total.astype(jnp.bfloat16)
-
-
-def project(attended, pieces, places):
-    rows, width = attended.shape
+
+    @pl.when(pl.program_id(0) == 0)
+    def _():
+        per_head = len(pieces) // kv_local
+        for n in range(len(pieces)):
+            at = (n % per_head) * depth
+            for side in range(2):
+                row = pl.multiple_of(places[side] * half, 16)
+                left[places[2 + n], side * half : (side + 1) * half] = heads[n // per_head][
+                    pl.ds(row, half), at : at + depth
+                ]
+
+    total = None
+    for n, piece in enumerate(pieces):
+        term = jnp.dot(left[n], piece[0], preferred_element_type=jnp.float32)
+        total = term if total is None else total + term
+    total = total.astype(jnp.bfloat16)
+    kept[0] = total[:half]
+    sent[0] = total[half:]
+
+
+def project(heads, pieces, places):
+    rows, width = heads[0].shape
     owners, depth, columns = pieces[0].shape
     half = rows // 2
     shape = jax.ShapeDtypeStruct((owners, half, columns), jnp.bfloat16)
     block = pl.BlockSpec((1, half, columns), lambda z, places: (z, 0, 0))
+    total = width * len(heads)
     return pl.pallas_call(
-        project_kernel,
+        functools.partial(project_kernel, len(heads)),
         out_shape=(shape, shape),
         grid_spec=pltpu.PrefetchScalarGridSpec(
             num_scalar_prefetch=1,
             grid=(owners,),
-            in_specs=[pl.BlockSpec((rows, width), lambda z, places: (0, 0))]
+            in_specs=[pl.BlockSpec((rows, width), lambda z, places: (0, 0))] * len(heads)
             + [pl.BlockSpec((1, depth, columns), lambda z, places: (z, 0, 0))] * len(pieces),
             out_specs=(block, block),
+            scratch_shapes=[pltpu.VMEM((len(pieces), rows, depth), jnp.bfloat16)],
         ),
         compiler_params=pltpu.CompilerParams(vmem_limit_bytes=VMEM),
         cost_estimate=pl.CostEstimate(
-            flops=2 * rows * width * owners * columns,
-            bytes_accessed=2 * (rows * width + (width + rows) * owners * columns),
+            flops=2 * rows * total * owners * columns,
+            bytes_accessed=2 * (rows * total + (total + rows) * owners * columns),
             transcendentals=0,
         ),
         name="project",
-    )(places, attended, *pieces)
+    )(places, *heads, *pieces)
 
 
 def join_kernel(*refs):
@@ -234,7 +245,40 @@
     )(*kept, *came)
 
 
+def pick_kernel(asked, pool, *outs):
+    kv_local = len(outs)
+
+    def copy(n, carry):
+        page = asked[n]
+        for head in range(kv_local):
+            outs[head][n] = pool[page, :, :, head * HD : (head + 1) * HD]
+        return carry
+
+    lax.fori_loop(0, outs[0].shape[0], copy, 0, unroll=8)
+
+
+def pick(pool, asked):
+    count = asked.shape[0]
+    kv_local = pool.shape[3] // HD
+    vmem = pl.BlockSpec(memory_space=pltpu.VMEM)
+    return pl.pallas_call(
+        pick_kernel,
+        out_shape=tuple(
+            jax.ShapeDtypeStruct((count,) + pool.shape[1:3] + (HD,), jnp.bfloat16)
+            for _ in range(kv_local)
+        ),
+        in_specs=[pl.BlockSpec(memory_space=pltpu.SMEM), vmem],
+        out_specs=(vmem,) * kv_local,
+        compiler_params=pltpu.CompilerParams(vmem_limit_bytes=VMEM),
+        name="pick",
+    )(asked, pool)
+
+
 SWAP = [(0, 1), (1, 0)]
+
+
+def after(value, *others):
+    return lax.optimization_barrier((value,) + others)[0]
 
 
 def shards(
@@ -247,18 +291,17 @@
     bucket = 2 * slot_count // owner_count
     group, role, tp = lax.axis_index("group"), lax.axis_index("role"), lax.axis_index("tp")
 
+    kv_local = pool.shape[4] // HD
+
+    own = 2 * group + role
     depth = out_weight.shape[0] // 4
     columns = out_weight.shape[1]
     parts = PARTS if columns % (PARTS * LANES) == 0 else 1
     part = columns // parts
-    quarter = lax.dynamic_slice_in_dim(out_weight, (2 * group + role) * depth, depth, 0)
+    quarter = lax.dynamic_slice_in_dim(out_weight, own * depth, depth, 0)
     gathered = [
         lax.all_gather(quarter[:, n * part : (n + 1) * part], "seq", axis=0) for n in range(parts)
     ]
-    weights = []
-    for own in gathered:
-        across = lax.ppermute(own, "group", SWAP)
-        weights.append((own, across, lax.ppermute(own, "role", SWAP), lax.ppermute(across, "role", SWAP)))
 
     slot_owner = page_owner[0]
     position = slot_owner * bucket + bucket_ranks(slot_owner, owner_count)
@@ -269,36 +312,57 @@
         .reshape(owner_count, bucket)
     )
     asked = lax.all_to_all(wanted, "seq", split_axis=0, concat_axis=0, tiled=True)
-    found = pool[0].at[asked].get(mode="promise_in_bounds")
-    fetched = lax.all_to_all(found, "seq", split_axis=0, concat_axis=0, tiled=True)
-    pages = fetched.reshape((owner_count * bucket,) + pool.shape[2:])
-
-    attended = attend(
-        queries[0], pages, new_kv[0].reshape(row_count, -1), position,
-        tok_conv[0], page_conv[0], page_fill[0],
-    )
-
+    found = pick(pool[0], asked.reshape(-1))
+
+    order = [(q ^ own) for q in range(4)]
+    order = [(v % 2) * 2 + v // 2 for v in order]
+    flip = tp if tp_count == 2 else 0
+    places = jnp.stack([jnp.asarray(v, jnp.int32) for v in (flip, 1 - flip, *order)])
+
+    fresh = new_kv[0].reshape(row_count, 2, kv_local, HD)
+    width = queries.shape[2] // kv_local
+    heads = []
+    weights = [None] * parts
+    last = found[0]
+    for head in range(kv_local):
+        leaving = found[head] if head == 0 else after(found[head], last)
+        came = lax.all_to_all(
+            leaving.reshape((owner_count, bucket) + leaving.shape[1:]),
+            "seq", split_axis=0, concat_axis=0, tiled=True,
+        )
+        if head < parts:
+            across = lax.ppermute(after(gathered[head], last), "group", SWAP)
+            weights[head] = (gathered[head], across)
+        heads.append(
+            attend(
+                queries[0, :, head * width : (head + 1) * width],
+                came.reshape((owner_count * bucket,) + leaving.shape[1:]),
+                fresh[:, :, head].reshape(row_count, 2 * HD), position,
+                tok_conv[0], page_conv[0], page_fill[0],
+            )
+        )
+        last = came
+    done = heads[-1]
+    kept, sent, back = [], [], []
+    for n in range(parts):
+        if weights[n] is None:
+            weights[n] = (gathered[n], lax.ppermute(after(gathered[n], done), "group", SWAP))
+        one, two = weights[n]
+        hold = last if n < kv_local else done
+        pieces = (
+            one, two, lax.ppermute(after(one, hold), "role", SWAP),
+            lax.ppermute(after(two, hold), "role", SWAP),
+        )
+        mine, theirs = project(heads, pieces, places)
+        kept.append(mine)
+        sent.append(theirs)
+        if n >= 1:
+            done = mine
     if tp_count != 2:
-        partial = []
-        places = jnp.stack(
-            [0, 1, 2 * group + role, 2 * (1 - group) + role, 2 * group + 1 - role,
-             2 * (1 - group) + 1 - role]
-        ).astype(jnp.int32)
-        for pieces in weights:
-            partial.append(jnp.concatenate(project(attended, pieces, places), axis=1))
+        partial = [jnp.concatenate(both, axis=1) for both in zip(kept, sent)]
         partial = jnp.stack(partial, axis=2).transpose(1, 0, 2, 3).reshape(row_count, -1)
         return lax.psum_scatter(partial, "tp", scatter_dimension=0, tiled=True)[None]
-
-    places = jnp.stack(
-        [tp, 1 - tp, 2 * group + role, 2 * (1 - group) + role, 2 * group + 1 - role,
-         2 * (1 - group) + 1 - role]
-    ).astype(jnp.int32)
-    kept, came = [], []
-    for pieces in weights:
-        mine, theirs = project(attended, pieces, places)
-        kept.append(mine)
-        came.append(lax.ppermute(theirs, "tp", SWAP))
-    return join(kept, came)
+    return join(kept, [lax.ppermute(theirs, "tp", SWAP) for theirs in sent])
 
 
 def solution(mesh):

time: 307 us -> 335 us (1.091)
  Pallas kernels: 48.1 us -> 67.9 us
  starting transfers between devices: 12.8 us -> 23.8 us
  waiting for transfers between devices: 203 us -> 193 us
  local copies, waits for them, and re-layouts: 12.2 us -> 18.6 us
    all_gather x2 -> x4, waiting for transfers between devices: 137 us -> 3.92 us  [shards(): lax.all_gather(quarter[:, n * part:(n + 1) * part], 'seq', axis=0)]
    all_to_all x1 -> x2, waiting for transfers between devices: 0.01 us -> 112 us  [shards(): lax.all_to_all(leaving.reshape((owner_count, bucket) + leaving.shape[1:])...]
    pallas_call x2 -> x5, Pallas kernels: 16.9 us -> 30.3 us  [the longest x4 25.2 us: project(): pl.pallas_call(functools.partial(project_kernel, len(heads)), out_shape=(...]
    ppermute x8 -> x16, waiting for transfers between devices: 65.2 us -> 76.1 us  [the longest x2 38.6 us: shards(): lax.ppermute(after(gathered[n], done), 'group', SWAP)]
    unnamed x17 -> x48, local copies, waits for them, and re-layouts: 1.92 us -> 8.38 us
    pallas_call x1 -> x2, Pallas kernels: 27.1 us -> 33.5 us  [attend(): pl.pallas_call(functools.partial(attend_kernel, spec), out_shape=jax.Shap...]
    all_to_all x1 -> x2, starting transfers between devices: 7.3 us -> 13.6 us  [shards(): lax.all_to_all(leaving.reshape((owner_count, bucket) + leaving.shape[1:])...]
    gather x1 -> x0, local copies, waits for them, and re-layouts: 4.99 us -> none  [shards(): found = pool[0].at[asked].get(mode='promise_in_bounds')]
  transfers between devices with their start and end apart: 11 -> 22, of which waited for: 5 -> 10; matrix products, arithmetic and copies ran while one was open for 4% -> 4% of each run, Pallas kernels for 15% -> 18%
where the time goes in v2:
time: 335 us; the launch traced here: 331 us
  waiting for transfers between devices  193 us (58%)
  Pallas kernels  67.9 us (20%)
  starting transfers between devices  23.8 us (7%)
  local copies, waits for them, and re-layouts  18.6 us (6%)
  between operations  13.3 us (4%)
  blocking collectives  8.19 us (2%)
  other arithmetic  5.89 us (2%)
    all_to_all x2, waiting for transfers between devices, shards(): lax.all_to_all(leaving.reshape((owner_count, bucket) + leaving.shape[1:])...  112 us
    ppermute x2, waiting for transfers between devices, shards(): lax.ppermute(after(gathered[n], done), 'group', SWAP)  38.6 us
    pallas_call x2, Pallas kernels, attend(): pl.pallas_call(functools.partial(attend_kernel, spec), out_shape=jax.Shap...  33.5 us
    pallas_call x4, Pallas kernels, project(): pl.pallas_call(functools.partial(project_kernel, len(heads)), out_shape=(...  25.2 us
    ppermute x4, waiting for transfers between devices, shards(): return join(kept, [lax.ppermute(theirs, 'tp', SWAP) for theirs in sent])  24.7 us
    all_to_all x2, starting transfers between devices, shards(): lax.all_to_all(leaving.reshape((owner_count, bucket) + leaving.shape[1:])...  13.6 us
    ppermute x2, waiting for transfers between devices, shards(): across = lax.ppermute(after(gathered[head], last), 'group', SWAP)  11.8 us
    unnamed x48, local copies, waits for them, and re-layouts  8.38 us
  transfers between devices with their start and end apart: 22, of which 10 were waited for; matrix products, arithmetic and copies ran while one was open for 4% of the time, Pallas kernels for 18%

profile of v2, /device:TPU:16, one launch (start us, length us, event | category | flops | bytes accessed | tf_op | source)
XLA Modules:
  0.0 330.9 jit_solution(4748349951324571661)
XLA Ops:
  6.5 0.7 fusion
  7.4 0.8 select_reduce_fusion
  8.3 0.7 fusion.2
  8.9 1.1 scatter_custom_fusion
  10.1 8.2 %all_to_all.19 = s32[4,1,64]{2,1,0:T(1,128)S(1)} all-to-all(s32[4,1,64]{2,1,0:T(1,128)S(1)} %all_to_all.12), channel_id=1, replica_groups=mesh['group'=2,'seq'=4,'tp'=2,'role'=2] {'seq'}, dimensions={0} | all-to-all | bytes 2048 | tf_op jit(solution)/shard_map/all_to_all | solution.py:314
  18.8 0.7 reduce.8
  19.5 0.6 reshape.71.asked
  20.2 5.2 %pick.1 = (bf16[256,2,16,128]{3,2,1,0:T(8,128)(2,1)}, bf16[256,2,16,128]{3,2,1,0:T(8,128)(2,1)}) custom-call(s32[256]{0:T(256)} %reshape.71.asked, bf16[256,2,16,256]{3,2,1,0:T(8,128)(2,1)} %bitcast.42), custom_call_target="tpu_custom_call" | custom-call | tf_op jit(solution)/shard_map/pick/pallas_call | solution.py:264
  25.3 5.9 %all-to-all-start.1 = ((bf16[4,64,2,16,128]{4,3,2,1,0:T(8,128)(2,1)}), bf16[4,64,2,16,128]{4,3,2,1,0:T(8,128)(2,1)S(1)}, u32[]{:S(2)}, u32[]{:S(2)}) async-start(bf16[4,64,2,16,128]{4,3,2,1,0:T(8,128)(2,1)} %bitcast.45), calls=%async_computation.1 | async-start | bytes 4194304 | tf_op jit(solution)/shard_map/all_to_all | solution.py:329
  31.3 2.2 fusion.9
  33.5 58.4 %all-to-all-done.1 = bf16[4,64,2,16,128]{4,3,2,1,0:T(8,128)(2,1)S(1)} async-done(((bf16[4,64,2,16,128]{4,3,2,1,0:T(8,128)(2,1)}), bf16[4,64,2,16,128]{4,3,2,1,0:T(8,128)(2,1)S(1)}, u32[]{:S(2)}, u32[]{:S(2)}) %all-to-all-start.1) | async-done | bytes 2097184 | tf_op jit(solution)/shard_map/all_to_all | solution.py:329
  91.9 1.3 copy-done
  93.2 7.7 %all-to-all-start.2 = ((bf16[4,64,2,16,128]{4,3,2,1,0:T(8,128)(2,1)}), bf16[4,64,2,16,128]{4,3,2,1,0:T(8,128)(2,1)}, u32[]{:S(2)}, u32[]{:S(2)}) async-start(bf16[4,64,2,16,128]{4,3,2,1,0:T(8,128)(2,1)} %bitcast.44), calls=%async_computation.2 | async-start | bytes 4194304 | tf_op jit(solution)/shard_map/all_to_all | solution.py:329
  100.9 0.7 all-gather.13.cloned.1.call-update
  101.7 1.6 collective-permute-start.3
  104.4 2.5 slice_reduce_fusion
  106.9 1.3 slice_bitcast_fusion
  108.2 53.9 %all-to-all-done.2 = bf16[4,64,2,16,128]{4,3,2,1,0:T(8,128)(2,1)} async-done(((bf16[4,64,2,16,128]{4,3,2,1,0:T(8,128)(2,1)}), bf16[4,64,2,16,128]{4,3,2,1,0:T(8,128)(2,1)}, u32[]{:S(2)}, u32[]{:S(2)}) %all-to-all-start.2) | async-done | bytes 2097184 | tf_op jit(solution)/shard_map/all_to_all | solution.py:329
  162.7 0.6 pad_add_fusion
  163.3 0.7 copy.27
  164.0 0.8 copy.17.tok_conv
  164.8 0.7 copy.26
  165.5 0.6 stack.27.places
  167.8 16.8 %attend.2.refs_0_ = bf16[384,1024]{1,0:T(8,128)(2,1)} custom-call(s32[128]{0:T(128)} %multiply_add_fusion.position, s32[6]{0:T(128)} %get-tuple-element.62.hist_at, s32[6]{0:T(128)} %get-tuple-element.61.hist_steps, s32[6]{0:T(128)} %get-tuple-element.52.fresh_at, s32[6]{0:T(128)} %get-tuple-element.51.fresh_steps, ...), custom_call_target="tpu_custom_call" | custom-call | flops 1258291200 | bytes 8388608 | tf_op jit(solution)/shard_map/attend/pallas_call | solution.py:149
  184.6 16.7 %attend.3.refs_1_ = bf16[384,1024]{1,0:T(8,128)(2,1)} custom-call(s32[128]{0:T(128)} %multiply_add_fusion.position, s32[6]{0:T(128)} %get-tuple-element.62.hist_at, s32[6]{0:T(128)} %get-tuple-element.61.hist_steps, s32[6]{0:T(128)} %get-tuple-element.52.fresh_at, s32[6]{0:T(128)} %get-tuple-element.51.fresh_steps, ...), custom_call_target="tpu_custom_call" | custom-call | flops 1258291200 | bytes 8388608 | tf_op jit(solution)/shard_map/attend/pallas_call | solution.py:149
  201.4 1.0 copy-done.13
  202.3 6.3 %project.5 = (bf16[4,192,256]{2,1,0:T(8,128)(2,1)}, bf16[4,192,256]{2,1,0:T(8,128)(2,1)}) custom-call(s32[6]{0:T(128)} %stack.27.places, bf16[384,1024]{1,0:T(8,128)(2,1)} %attend.2.refs_0_, bf16[384,1024]{1,0:T(8,128)(2,1)} %attend.3.refs_1_, bf16[4,512,256]{2,1,0:T(8,128)(2,1)} %bitcast.65, bf16[4,512,256]{2,1,0:T(8,128)(2,1)} %collective-permute-done.3.refs_3_, ...), custom_call_target="tpu_custom_call" | custom-call | flops 1610612736 | bytes 6553600 | tf_op jit(solution)/shard_map/project/pallas_call | solution.py:204
  208.8 17.1 %collective-permute-done.6.refs_3_ = bf16[4,512,256]{2,1,0:T(8,128)(2,1)S(1)} collective-permute-done((bf16[4,512,256]{2,1,0:T(8,128)(2,1)}, bf16[4,512,256]{2,1,0:T(8,128)(2,1)S(1)}, u32[]{:S(2)}, u32[]{:S(2)}) %collective-permute-start.6) | collective-permute-done | bytes 1048608 | tf_op jit(solution)/shard_map/ppermute | solution.py:349
  225.9 1.8 collective-permute-start
  227.7 1.0 collective-permute-done.8.refs_5_
  228.6 6.3 %project.6 = (bf16[4,192,256]{2,1,0:T(8,128)(2,1)}, bf16[4,192,256]{2,1,0:T(8,128)(2,1)}) custom-call(s32[6]{0:T(128)} %stack.27.places, bf16[384,1024]{1,0:T(8,128)(2,1)} %attend.2.refs_0_, bf16[384,1024]{1,0:T(8,128)(2,1)} %attend.3.refs_1_, bf16[4,512,256]{2,1,0:T(8,128)(2,1)} %bitcast.63, bf16[4,512,256]{2,1,0:T(8,128)(2,1)} %copy-done.18, ...), custom_call_target="tpu_custom_call" | custom-call | flops 1610612736 | bytes 6553600 | tf_op jit(solution)/shard_map/project/pallas_call | solution.py:204
  234.9 3.9 %all-gather.15.cloned.1.call-done = bf16[2048,256]{1,0:T(8,128)(2,1)} async-done(((bf16[512,256]{1,0:T(8,128)(2,1)}), bf16[2048,256]{1,0:T(8,128)(2,1)}) %all-gather.15.cloned.1.call-update) | async-done | bytes 1048592 | tf_op jit(solution)/shard_map/all_gather | solution.py:303
  238.8 1.5 collective-permute-start.9
  240.3 11.8 %collective-permute-done.refs_3_ = bf16[4,512,256]{2,1,0:T(8,128)(2,1)S(1)} collective-permute-done((bf16[4,512,256]{2,1,0:T(8,128)(2,1)}, bf16[4,512,256]{2,1,0:T(8,128)(2,1)S(1)}, u32[]{:S(2)}, u32[]{:S(2)}) %collective-permute-start) | collective-permute-done | bytes 1048608 | tf_op jit(solution)/shard_map/ppermute | solution.py:334
  252.6 21.6 %collective-permute-done.9.refs_3_ = bf16[4,512,256]{2,1,0:T(8,128)(2,1)S(1)} collective-permute-done((bf16[4,512,256]{2,1,0:T(8,128)(2,1)}, bf16[4,512,256]{2,1,0:T(8,128)(2,1)S(1)}, u32[]{:S(2)}, u32[]{:S(2)}) %collective-permute-start.9) | collective-permute-done | bytes 1048608 | tf_op jit(solution)/shard_map/ppermute | solution.py:349
  274.2 1.0 copy-done.19
  275.2 1.0 copy-done.20
  276.2 6.3 %project.4 = (bf16[4,192,256]{2,1,0:T(8,128)(2,1)}, bf16[4,192,256]{2,1,0:T(8,128)(2,1)}) custom-call(s32[6]{0:T(128)} %stack.27.places, bf16[384,1024]{1,0:T(8,128)(2,1)} %attend.2.refs_0_, bf16[384,1024]{1,0:T(8,128)(2,1)} %attend.3.refs_1_, bf16[4,512,256]{2,1,0:T(8,128)(2,1)} %bitcast.59, bf16[4,512,256]{2,1,0:T(8,128)(2,1)} %copy-done.15, ...), custom_call_target="tpu_custom_call" | custom-call | flops 1610612736 | bytes 6553600 | tf_op jit(solution)/shard_map/project/pallas_call | solution.py:204
  282.5 1.5 collective-permute-start.12
  284.6 1.5 collective-permute-start.14
  286.1 1.0 copy-done.16
  287.0 1.0 copy-done.17
  288.0 6.3 %project.7 = (bf16[4,192,256]{2,1,0:T(8,128)(2,1)}, bf16[4,192,256]{2,1,0:T(8,128)(2,1)}) custom-call(s32[6]{0:T(128)} %stack.27.places, bf16[384,1024]{1,0:T(8,128)(2,1)} %attend.2.refs_0_, bf16[384,1024]{1,0:T(8,128)(2,1)} %attend.3.refs_1_, bf16[4,512,256]{2,1,0:T(8,128)(2,1)} %bitcast.69, bf16[4,512,256]{2,1,0:T(8,128)(2,1)} %copy-done.14, ...), custom_call_target="tpu_custom_call" | custom-call | flops 1610612736 | bytes 6553600 | tf_op jit(solution)/shard_map/project/pallas_call | solution.py:204
  294.8 8.3 %collective-permute-done.13.refs_5_ = bf16[4,192,256]{2,1,0:T(8,128)(2,1)S(1)} collective-permute-done((bf16[4,192,256]{2,1,0:T(8,128)(2,1)S(1)}, bf16[4,192,256]{2,1,0:T(8,128)(2,1)S(1)}, u32[]{:S(2)}, u32[]{:S(2)}) %collective-permute-start.13) | collective-permute-done | bytes 393248 | tf_op jit(solution)/shard_map/ppermute | solution.py:365
  303.1 8.4 %collective-permute-done.14.refs_6_ = bf16[4,192,256]{2,1,0:T(8,128)(2,1)S(1)} collective-permute-done((bf16[4,192,256]{2,1,0:T(8,128)(2,1)S(1)}, bf16[4,192,256]{2,1,0:T(8,128)(2,1)S(1)}, u32[]{:S(2)}, u32[]{:S(2)}) %collective-permute-start.14) | collective-permute-done | bytes 393248 | tf_op jit(solution)/shard_map/ppermute | solution.py:365
  311.5 8.0 %collective-permute-done.15.refs_7_ = bf16[4,192,256]{2,1,0:T(8,128)(2,1)S(1)} collective-permute-done((bf16[4,192,256]{2,1,0:T(8,128)(2,1)}, bf16[4,192,256]{2,1,0:T(8,128)(2,1)S(1)}, u32[]{:S(2)}, u32[]{:S(2)}) %collective-permute-start.15) | collective-permute-done | bytes 393248 | tf_op jit(solution)/shard_map/ppermute | solution.py:365
  319.5 0.7 copy-done.5
  320.3 4.0 %join.1 = bf16[1,192,4096]{2,1,0:T(8,128)(2,1)} custom-call(bf16[4,192,256]{2,1,0:T(8,128)(2,1)} %get-tuple-element.32.refs_0_, bf16[4,192,256]{2,1,0:T(8,128)(2,1)} %get-tuple-element.36.refs_1_, bf16[4,192,256]{2,1,0:T(8,128)(2,1)} %get-tuple-element.39.refs_2_, bf16[4,192,256]{2,1,0:T(8,128)(2,1)} %get-tuple-element.42.refs_3_, ...), custom_call_target="tpu_custom_call" | custom-call | tf_op jit(solution)/shard_map/join/pallas_call | solution.py:237
  (85 shorter events, 6.0 us)
Async XLA Ops:
  25.3 66.6 %all-to-all-start.1 = ((bf16[4,64,2,16,128]{4,3,2,1,0:T(8,128)(2,1)}), bf16[4,64,2,16,128]{4,3,2,1,0:T(8,128)(2,1)S(1)}, u32[]{:S(2)}, u32[]{:S(2)}) async-start(bf16[4,64,2,16,128]{4,3,2,1,0:T(8,128)(2,1)} %bitcast.45), calls=%async_computation.1 | async-start | bytes 4194304 | tf_op jit(solution)/shard_map/all_to_all | solution.py:329
  31.3 70.4 %all-gather.11.cloned.1.call-start = ((), (), s32[]{:S(2)}) async-start(), calls=%async_computation.4 | async-start | bytes 1310720 | tf_op jit(solution)/shard_map/all_gather | solution.py:303
  91.9 1.3 copy-start
  91.9 11.5 %copy-start.7 = (s32[1,384]{1,0:T(1,128)S(1)}, s32[1,384]{1,0:T(1,128)}, u32[]{:S(2)}) copy-start(s32[1,384]{1,0:T(1,128)} %param.13) | copy-start | bytes 4612
  91.9 11.7 %copy-start.6 = (bf16[1,384,2,256]{3,2,1,0:T(2,128)(2,1)S(1)}, bf16[1,384,2,256]{3,2,1,0:T(2,128)(2,1)}, u32[]{:S(2)}) copy-start(bf16[1,384,2,256]{3,2,1,0:T(2,128)(2,1)} %param.10) | copy-start | bytes 1179652
  91.9 12.0 %copy-start.9 = (s32[1,128]{1,0:T(1,128)S(1)}, s32[1,128]{1,0:T(1,128)}, u32[]{:S(2)}) copy-start(s32[1,128]{1,0:T(1,128)} %param.14) | copy-start | bytes 1540
  91.9 12.0 %copy-start.10 = (s32[1,128]{1,0:T(1,128)S(1)}, s32[1,128]{1,0:T(1,128)}, u32[]{:S(2)}) copy-start(s32[1,128]{1,0:T(1,128)} %param.15) | copy-start | bytes 1540
  93.2 68.9 %all-to-all-start.2 = ((bf16[4,64,2,16,128]{4,3,2,1,0:T(8,128)(2,1)}), bf16[4,64,2,16,128]{4,3,2,1,0:T(8,128)(2,1)}, u32[]{:S(2)}, u32[]{:S(2)}) async-start(bf16[4,64,2,16,128]{4,3,2,1,0:T(8,128)(2,1)} %bitcast.44), calls=%async_computation.2 | async-start | bytes 4194304 | tf_op jit(solution)/shard_map/all_to_all | solution.py:329
  100.9 6.0 %copy-start.1 = (bf16[1,384,2048]{2,1,0:T(8,128)(2,1)S(1)}, bf16[1,384,2048]{2,1,0:T(8,128)(2,1)}, u32[]{:S(2)}) copy-start(bf16[1,384,2048]{2,1,0:T(8,128)(2,1)} %param.9) | copy-start | bytes 4718596
  100.9 107.7 %all-gather.13.cloned.1.call-start = ((), (), s32[]{:S(2)}) async-start(), calls=%async_computation.5 | async-start | bytes 1310720 | tf_op jit(solution)/shard_map/all_gather | solution.py:303
  101.6 124.2 %all-gather.9.cloned.1.call-start = ((), (), s32[]{:S(2)}) async-start(), calls=%async_computation.3 | async-start | bytes 1310720 | tf_op jit(solution)/shard_map/all_gather | solution.py:303
  101.7 60.5 %collective-permute-start.3 = (bf16[4,512,256]{2,1,0:T(8,128)(2,1)}, bf16[4,512,256]{2,1,0:T(8,128)(2,1)}, u32[]{:S(2)}, u32[]{:S(2)}) collective-permute-start(bf16[4,512,256]{2,1,0:T(8,128)(2,1)} %bitcast.64), channel_id=1, source_target_pairs={{0,16},{16,0},{1,17},{17,1},{2,18},{18,2},{3,19},{19,3},{4,20},{20... | collective-permute-start | bytes 3145736 | tf_op jit(solution)/shard_map/ppermute | solution.py:334
  103.3 135.5 %all-gather.15.cloned.1.call-start = ((), (), s32[]{:S(2)}) async-start(), calls=%async_computation.6 | async-start | bytes 1310720 | tf_op jit(solution)/shard_map/all_gather | solution.py:303
  106.9 55.2 %copy-start.12 = (bf16[2048,256]{1,0:T(8,128)(2,1)S(1)}, bf16[2048,256]{1,0:T(8,128)(2,1)}, u32[]{:S(2)}) copy-start(bf16[2048,256]{1,0:T(8,128)(2,1)} %all-gather.11.cloned.1.call-done) | copy-start | bytes 3145732
  106.9 59.8 %copy-start.8 = (s32[1,128]{1,0:T(1,128)S(1)}, s32[1,128]{1,0:T(1,128)}, u32[]{:S(2)}) copy-start(s32[1,128]{1,0:T(1,128)} %param.16) | copy-start | bytes 1540
  162.2 39.2 %collective-permute-start.4 = (bf16[4,512,256]{2,1,0:T(8,128)(2,1)S(1)}, bf16[4,512,256]{2,1,0:T(8,128)(2,1)S(1)}, u32[]{:S(2)}, u32[]{:S(2)}) collective-permute-start(bf16[4,512,256]{2,1,0:T(8,128)(2,1)S(1)} %bitcast.66), channel_id=1, source_target_pairs={{0,1},{1,0},{2,3},{3,2},{4,5},{5,4},{6,7},{7,6},{8,9},{9,8},{10,11... | collective-permute-start | bytes 3145736 | tf_op jit(solution)/shard_map/ppermute | solution.py:353
  162.2 39.2 %collective-permute-start.5 = (bf16[4,512,256]{2,1,0:T(8,128)(2,1)}, bf16[4,512,256]{2,1,0:T(8,128)(2,1)}, u32[]{:S(2)}, u32[]{:S(2)}) collective-permute-start(bf16[4,512,256]{2,1,0:T(8,128)(2,1)} %collective-permute-done.3.refs_3_), channel_id=1, source_target_pairs={{0,1},{1,0},{2,3},{3,2},{4,5},{5,4},{6,7},{7,6},{8,9},{9,8},{10,11... | collective-permute-start | bytes 3145736 | tf_op jit(solution)/shard_map/ppermute | solution.py:354
  201.3 1.0 copy-start.13
  208.6 17.2 %collective-permute-start.6 = (bf16[4,512,256]{2,1,0:T(8,128)(2,1)}, bf16[4,512,256]{2,1,0:T(8,128)(2,1)S(1)}, u32[]{:S(2)}, u32[]{:S(2)}) collective-permute-start(bf16[4,512,256]{2,1,0:T(8,128)(2,1)} %bitcast.61), channel_id=1, source_target_pairs={{0,16},{16,0},{1,17},{17,1},{2,18},{18,2},{3,19},{19,3},{4,20},{20... | collective-permute-start | bytes 3145736 | tf_op jit(solution)/shard_map/ppermute | solution.py:349
  208.7 19.0 %collective-permute-start.7 = (bf16[4,512,256]{2,1,0:T(8,128)(2,1)}, bf16[4,512,256]{2,1,0:T(8,128)(2,1)}, u32[]{:S(2)}, u32[]{:S(2)}) collective-permute-start(bf16[4,512,256]{2,1,0:T(8,128)(2,1)} %bitcast.62), channel_id=1, source_target_pairs={{0,1},{1,0},{2,3},{3,2},{4,5},{5,4},{6,7},{7,6},{8,9},{9,8},{10,11... | collective-permute-start | bytes 3145736 | tf_op jit(solution)/shard_map/ppermute | solution.py:353
  225.8 2.8 copy-start.18
  225.8 2.8 collective-permute-start.8
  225.8 14.5 %copy-start.11 = (bf16[2048,256]{1,0:T(8,128)(2,1)S(1)}, bf16[2048,256]{1,0:T(8,128)(2,1)}, u32[]{:S(2)}) copy-start(bf16[2048,256]{1,0:T(8,128)(2,1)} %all-gather.9.cloned.1.call-done) | copy-start | bytes 3145732
  225.9 26.2 %collective-permute-start = (bf16[4,512,256]{2,1,0:T(8,128)(2,1)}, bf16[4,512,256]{2,1,0:T(8,128)(2,1)S(1)}, u32[]{:S(2)}, u32[]{:S(2)}) collective-permute-start(bf16[4,512,256]{2,1,0:T(8,128)(2,1)} %bitcast.58), channel_id=1, source_target_pairs={{0,16},{16,0},{1,17},{17,1},{2,18},{18,2},{3,19},{19,3},{4,20},{20... | collective-permute-start | bytes 3145736 | tf_op jit(solution)/shard_map/ppermute | solution.py:334
  238.8 45.2 %copy-start.21 = (bf16[4,192,256]{2,1,0:T(8,128)(2,1)S(1)}, bf16[4,192,256]{2,1,0:T(8,128)(2,1)}, u32[]{:S(2)}) copy-start(bf16[4,192,256]{2,1,0:T(8,128)(2,1)} %get-tuple-element.44) | copy-start | bytes 1179652
  238.8 45.7 %copy-start.22 = (bf16[4,192,256]{2,1,0:T(8,128)(2,1)S(1)}, bf16[4,192,256]{2,1,0:T(8,128)(2,1)}, u32[]{:S(2)}) copy-start(bf16[4,192,256]{2,1,0:T(8,128)(2,1)} %get-tuple-element.45) | copy-start | bytes 1179652
  238.8 35.3 %collective-permute-start.9 = (bf16[4,512,256]{2,1,0:T(8,128)(2,1)}, bf16[4,512,256]{2,1,0:T(8,128)(2,1)S(1)}, u32[]{:S(2)}, u32[]{:S(2)}) collective-permute-start(bf16[4,512,256]{2,1,0:T(8,128)(2,1)} %bitcast.67), channel_id=1, source_target_pairs={{0,16},{16,0},{1,17},{17,1},{2,18},{18,2},{3,19},{19,3},{4,20},{20... | collective-permute-start | bytes 3145736 | tf_op jit(solution)/shard_map/ppermute | solution.py:349
  240.3 33.9 %collective-permute-start.1 = (bf16[4,512,256]{2,1,0:T(8,128)(2,1)S(1)}, bf16[4,512,256]{2,1,0:T(8,128)(2,1)S(1)}, u32[]{:S(2)}, u32[]{:S(2)}) collective-permute-start(bf16[4,512,256]{2,1,0:T(8,128)(2,1)S(1)} %bitcast.60), channel_id=1, source_target_pairs={{0,1},{1,0},{2,3},{3,2},{4,5},{5,4},{6,7},{7,6},{8,9},{9,8},{10,11... | collective-permute-start | bytes 3145736 | tf_op jit(solution)/shard_map/ppermute | solution.py:353
  252.1 22.1 %copy-start.15 = (bf16[4,512,256]{2,1,0:T(8,128)(2,1)}, bf16[4,512,256]{2,1,0:T(8,128)(2,1)S(1)}, u32[]{:S(2)}) copy-start(bf16[4,512,256]{2,1,0:T(8,128)(2,1)S(1)} %collective-permute-done.refs_3_) | copy-start | bytes 3145732
  252.1 22.1 %collective-permute-start.2 = (bf16[4,512,256]{2,1,0:T(8,128)(2,1)S(1)}, bf16[4,512,256]{2,1,0:T(8,128)(2,1)S(1)}, u32[]{:S(2)}, u32[]{:S(2)}) collective-permute-start(bf16[4,512,256]{2,1,0:T(8,128)(2,1)S(1)} %collective-permute-done.refs_3_), channel_id=1, source_target_pairs={{0,1},{1,0},{2,3},{3,2},{4,5},{5,4},{6,7},{7,6},{8,9},{9,8},{10,11... | collective-permute-start | bytes 3145736 | tf_op jit(solution)/shard_map/ppermute | solution.py:354
  252.1 34.0 %collective-permute-start.10 = (bf16[4,512,256]{2,1,0:T(8,128)(2,1)}, bf16[4,512,256]{2,1,0:T(8,128)(2,1)S(1)}, u32[]{:S(2)}, u32[]{:S(2)}) collective-permute-start(bf16[4,512,256]{2,1,0:T(8,128)(2,1)} %bitcast.68), channel_id=1, source_target_pairs={{0,1},{1,0},{2,3},{3,2},{4,5},{5,4},{6,7},{7,6},{8,9},{9,8},{10,11... | collective-permute-start | bytes 3145736 | tf_op jit(solution)/shard_map/ppermute | solution.py:353
  274.2 8.3 %copy-start.14 = (bf16[4,512,256]{2,1,0:T(8,128)(2,1)}, bf16[4,512,256]{2,1,0:T(8,128)(2,1)S(1)}, u32[]{:S(2)}) copy-start(bf16[4,512,256]{2,1,0:T(8,128)(2,1)S(1)} %collective-permute-done.9.refs_3_) | copy-start | bytes 3145732
  274.2 11.9 %collective-permute-start.11 = (bf16[4,512,256]{2,1,0:T(8,128)(2,1)S(1)}, bf16[4,512,256]{2,1,0:T(8,128)(2,1)S(1)}, u32[]{:S(2)}, u32[]{:S(2)}) collective-permute-start(bf16[4,512,256]{2,1,0:T(8,128)(2,1)S(1)} %collective-permute-done.9.refs_3_), channel_id=1, source_target_pairs={{0,1},{1,0},{2,3},{3,2},{4,5},{5,4},{6,7},{7,6},{8,9},{9,8},{10,11... | collective-permute-start | bytes 3145736 | tf_op jit(solution)/shard_map/ppermute | solution.py:354
  274.2 1.0 copy-start.19
  275.2 1.0 copy-start.20
  282.5 12.4 %collective-permute-start.12 = (bf16[4,192,256]{2,1,0:T(8,128)(2,1)}, bf16[4,192,256]{2,1,0:T(8,128)(2,1)S(1)}, u32[]{:S(2)}, u32[]{:S(2)}) collective-permute-start(bf16[4,192,256]{2,1,0:T(8,128)(2,1)} %get-tuple-element.43), channel_id=1, source_target_pairs={{0,2},{2,0},{1,3},{3,1},{4,6},{6,4},{5,7},{7,5},{8,10},{10,8},{9,1... | collective-permute-start | bytes 1179656 | tf_op jit(solution)/shard_map/ppermute | solution.py:365
  284.0 19.1 %collective-permute-start.13 = (bf16[4,192,256]{2,1,0:T(8,128)(2,1)S(1)}, bf16[4,192,256]{2,1,0:T(8,128)(2,1)S(1)}, u32[]{:S(2)}, u32[]{:S(2)}) collective-permute-start(bf16[4,192,256]{2,1,0:T(8,128)(2,1)S(1)} %copy-done.21), channel_id=1, source_target_pairs={{0,2},{2,0},{1,3},{3,1},{4,6},{6,4},{5,7},{7,5},{8,10},{10,8},{9,1... | collective-permute-start | bytes 1179656 | tf_op jit(solution)/shard_map/ppermute | solution.py:365
  284.6 26.9 %collective-permute-start.14 = (bf16[4,192,256]{2,1,0:T(8,128)(2,1)S(1)}, bf16[4,192,256]{2,1,0:T(8,128)(2,1)S(1)}, u32[]{:S(2)}, u32[]{:S(2)}) collective-permute-start(bf16[4,192,256]{2,1,0:T(8,128)(2,1)S(1)} %copy-done.22), channel_id=1, source_target_pairs={{0,2},{2,0},{1,3},{3,1},{4,6},{6,4},{5,7},{7,5},{8,10},{10,8},{9,1... | collective-permute-start | bytes 1179656 | tf_op jit(solution)/shard_map/ppermute | solution.py:365
  286.1 1.0 copy-start.16
  287.0 1.0 copy-start.17
  294.3 25.2 %collective-permute-start.15 = (bf16[4,192,256]{2,1,0:T(8,128)(2,1)}, bf16[4,192,256]{2,1,0:T(8,128)(2,1)S(1)}, u32[]{:S(2)}, u32[]{:S(2)}) collective-permute-start(bf16[4,192,256]{2,1,0:T(8,128)(2,1)} %get-tuple-element.46), channel_id=1, source_target_pairs={{0,2},{2,0},{1,3},{3,1},{4,6},{6,4},{5,7},{7,5},{8,10},{10,8},{9,1... | collective-permute-start | bytes 1179656 | tf_op jit(solution)/shard_map/ppermute | solution.py:365
  294.8 24.7 %copy-start.2 = (bf16[4,192,256]{2,1,0:T(8,128)(2,1)}, bf16[4,192,256]{2,1,0:T(8,128)(2,1)S(1)}, u32[]{:S(2)}) copy-start(bf16[4,192,256]{2,1,0:T(8,128)(2,1)S(1)} %collective-permute-done.12.refs_4_) | copy-start | bytes 1179652
  303.1 16.4 %copy-start.3 = (bf16[4,192,256]{2,1,0:T(8,128)(2,1)}, bf16[4,192,256]{2,1,0:T(8,128)(2,1)S(1)}, u32[]{:S(2)}) copy-start(bf16[4,192,256]{2,1,0:T(8,128)(2,1)S(1)} %collective-permute-done.13.refs_5_) | copy-start | bytes 1179652
  311.5 8.0 %copy-start.4 = (bf16[4,192,256]{2,1,0:T(8,128)(2,1)}, bf16[4,192,256]{2,1,0:T(8,128)(2,1)S(1)}, u32[]{:S(2)}) copy-start(bf16[4,192,256]{2,1,0:T(8,128)(2,1)S(1)} %collective-permute-done.14.refs_6_) | copy-start | bytes 1179652
  319.5 0.8 copy-start.5
Sparse Core Ops, SparseCore 0:
  33.6 54.4 all-gather.10
  103.3 55.0 all-gather.12
  160.0 30.3 all-gather.8
  208.8 29.9 all-gather.14

commit v3 on v1

v3 whole, which is shorter than its diff:
```python
import functools
import math

import jax
import jax.numpy as jnp
from jax import lax
from jax.experimental import pallas as pl
from jax.experimental.pallas import tpu as pltpu
from jax.sharding import PartitionSpec as P

HD = 128
TILE = 32
KEYS = 256
LANES = 128
HIDDEN = -1e30
COLUMNS = 256
VMEM = 56 * 1024 * 1024


def bucket_ranks(slot_owner, owner_count):
    one_hot = (slot_owner[..., None] == jnp.arange(owner_count)).astype(jnp.int32)
    before = jnp.cumsum(one_hot, axis=-2) - one_hot
    return jnp.sum(before * one_hot, axis=-1)


def attend_kernel(
    spec, control, position, hist_at, hist_steps, fresh_at, fresh_steps,
    query, pages, fresh, key_conv, key_row, tok_conv, out, keys, values, scores, sums,
):
    kv_local, group_size, slots, page_len, rows, fresh_base, key_total = spec
    channels = kv_local * HD
    hist = slots * page_len
    half, depth = out.shape[1], out.shape[2]
    tiles = half // TILE
    for head in range(kv_local):
        values[head, :, HD:] = jnp.ones((key_total, HD), jnp.bfloat16)
        for first, last in ((hist, fresh_base), (fresh_base + rows, key_total)):
            keys[head, first:last] = jnp.zeros((last - first, HD), jnp.bfloat16)
            values[head, first:last, :HD] = jnp.zeros((last - first, HD), jnp.bfloat16)
        at = head * HD
        keys[head, fresh_base : fresh_base + rows] = fresh[:, at : at + HD]
        values[head, fresh_base : fresh_base + rows, :HD] = fresh[:, channels + at : channels + at + HD]

    def place(slot, carry):
        page = position[slot]
        row = pl.ds(pl.multiple_of(slot * page_len, page_len), page_len)
        for head in range(kv_local):
            at = head * HD
            keys[head, row] = pages[page, 0, :, at : at + HD]
            values[head, row, :HD] = pages[page, 1, :, at : at + HD]
        return carry

    lax.fori_loop(0, slots, place, 0, unroll=8)
    to_exp2 = math.log2(math.e) / math.sqrt(HD)
    wide = group_size * TILE

    def tile(number_here, carry):
        index = control[0] * tiles + number_here
        first = pl.multiple_of(index * TILE, TILE)
        leaving = pl.ds(pl.multiple_of(number_here * TILE, TILE), TILE)
        tokens = pl.ds(first, TILE)
        conv = tok_conv[tokens]
        number = first + lax.broadcasted_iota(jnp.int32, (TILE, 1), 0)
        steps_h, steps_f = hist_steps[index], fresh_steps[index]
        at_h, at_f = hist_at[index], fresh_at[index]
        heads = [
            jnp.concatenate(
                [
                    query[tokens, (head * group_size + g) * HD : (head * group_size + g + 1) * HD]
                    for g in range(group_size)
                ],
                axis=0,
            )
            for head in range(kv_local)
        ]

        def key_range(step):
            start = jnp.where(
                step < steps_h, at_h + step * KEYS, fresh_base + at_f + (step - steps_h) * KEYS
            )
            return pl.ds(pl.multiple_of(start, LANES), KEYS)

        def score(step, tops):
            where = key_range(step)
            ok = (key_conv[:, where] == conv) & (key_row[:, where] <= number)
            held = pl.ds(pl.multiple_of(step * KEYS, KEYS), KEYS)
            new = []
            for head in range(kv_local):
                s = lax.dot_general(
                    heads[head], keys[head, where], (((1,), (1,)), ((), ())),
                    preferred_element_type=jnp.float32,
                ).reshape(group_size, TILE, KEYS)
                s = jnp.where(ok[None], s, HIDDEN).reshape(wide, KEYS)
                scores[head, :, held] = s
                top = tops[head]
                for k in range(0, KEYS, LANES):
                    top = jnp.maximum(top, s[:, k : k + LANES])
                new.append(top)
            return tuple(new)

        low = jnp.full((wide, LANES), HIDDEN, jnp.float32)
        tops = lax.fori_loop(0, steps_h + steps_f, score, (low,) * kv_local)
        tops = [jnp.max(top, axis=1, keepdims=True) * to_exp2 for top in tops]
        sums[...] = jnp.zeros_like(sums)

        def gather(step, carry):
            where = key_range(step)
            held = pl.ds(pl.multiple_of(step * KEYS, KEYS), KEYS)
            for head in range(kv_local):
                w = jnp.exp2(scores[head, :, held] * to_exp2 - tops[head]).astype(jnp.bfloat16)
                sums[head] += jnp.dot(w, values[head, where], preferred_element_type=jnp.float32)
            return carry

        lax.fori_loop(0, steps_h + steps_f, gather, 0)
        for head in range(kv_local):
            done = (sums[head, :, :HD] / sums[head, :, HD:]).astype(jnp.bfloat16)
            for g in range(group_size):
                at = (head * group_size + g) * HD
                out[control[1 + at // depth], leaving, at % depth : at % depth + HD] = done[
                    g * TILE : (g + 1) * TILE
                ]
        return carry

    lax.fori_loop(0, tiles, tile, 0)


def attend_tables(rows, slots, page_len, tok_conv, page_conv, page_fill):
    hist = slots * page_len
    fresh_base = hist + KEYS
    key_total = fresh_base + pl.cdiv(rows, KEYS) * KEYS + KEYS
    live = jnp.arange(page_len)[None, :] < page_fill[:, None]
    hist_conv = jnp.where(live, page_conv[:, None], -1).reshape(hist)
    tail = key_total - fresh_base - rows
    key_conv = jnp.concatenate(
        [hist_conv, jnp.full((KEYS,), -1, jnp.int32), tok_conv, jnp.full((tail,), -1, jnp.int32)]
    )[None]
    key_row = jnp.maximum(jnp.arange(key_total, dtype=jnp.int32) - fresh_base, -1)[None]
    lowest, highest = tok_conv[::TILE], tok_conv[TILE - 1 :: TILE]
    hist_at = jnp.sum(page_conv[None] < lowest[:, None], axis=1, dtype=jnp.int32) * page_len
    hist_at = hist_at // LANES * LANES
    hist_end = jnp.sum(page_conv[None] <= highest[:, None], axis=1, dtype=jnp.int32) * page_len
    hist_steps = (hist_end - hist_at + KEYS - 1) // KEYS
    fresh_at = jnp.sum(tok_conv[None] < lowest[:, None], axis=1, dtype=jnp.int32) // LANES * LANES
    fresh_end = (jnp.arange(rows // TILE, dtype=jnp.int32) + 1) * TILE
    fresh_steps = (fresh_end - fresh_at + KEYS - 1) // KEYS
    return key_conv, key_row, tok_conv[:, None], hist_at, hist_steps, fresh_at, fresh_steps


def attend(control, tables, position, queries, pages, new_kv):
    rows, width = queries.shape
    page_len, channels = pages.shape[2], pages.shape[3]
    slots = position.shape[0]
    kv_local = channels // HD
    group_size = width // channels
    hist = slots * page_len
    fresh_base = hist + KEYS
    key_total = fresh_base + pl.cdiv(rows, KEYS) * KEYS + KEYS
    key_conv, key_row, tok_conv, *steps = tables
    depth = width // 4
    most = (hist // KEYS + 1 + pl.cdiv(rows, KEYS) + 1) * KEYS
    spec = (kv_local, group_size, slots, page_len, rows, fresh_base, key_total)
    smem = pl.BlockSpec(memory_space=pltpu.SMEM)
    vmem = pl.BlockSpec(memory_space=pltpu.VMEM)
    return pl.pallas_call(
        functools.partial(attend_kernel, spec),
        out_shape=jax.ShapeDtypeStruct((4, rows // 2, depth), jnp.bfloat16),
        in_specs=[smem] * 6 + [vmem] * 6,
        out_specs=vmem,
        scratch_shapes=[
            pltpu.VMEM((kv_local, key_total, HD), jnp.bfloat16),
            pltpu.VMEM((kv_local, key_total, 2 * HD), jnp.bfloat16),
            pltpu.VMEM((kv_local, group_size * TILE, most), jnp.float32),
            pltpu.VMEM((kv_local, group_size * TILE, 2 * HD), jnp.float32),
        ],
        compiler_params=pltpu.CompilerParams(vmem_limit_bytes=VMEM),
        cost_estimate=pl.CostEstimate(
            flops=rows * width * 800 * 2, bytes_accessed=8 << 20, transcendentals=rows * width // HD * 400
        ),
        name="attend",
    )(
        control, position, *steps, queries, pages, new_kv, key_conv, key_row, tok_conv,
    )


def multiply(left, pieces):
    total = None
    for n, piece in enumerate(pieces):
        term = jnp.dot(left[n], piece[...], preferred_element_type=jnp.float32)
        total = term if total is None else total + term
    return total.astype(jnp.bfloat16)


def project_kernel(rows_at, left, *refs):
    refs[-1][...] = multiply(left, refs[:-1])


def finish_kernel(rows_at, left, came, *refs):
    pieces = refs[:4]
    total = multiply(left, pieces).astype(jnp.float32) + came[...].astype(jnp.float32)
    refs[-1][0] = total.astype(jnp.bfloat16)


def project(left, pieces, rows_at, came=None, base=None, out=None, width=None):
    depth = left.shape[2]
    half = left.shape[1]
    columns = pieces[0].shape[1]
    cut = min(COLUMNS, columns)
    table = rows_at if base is None else jnp.concatenate([rows_at, (base * (columns // cut))[None]])
    in_specs = [pl.BlockSpec(left.shape, lambda j, at: (0, 0, 0))]
    operands = [left]
    aliases = {}
    if came is None:
        kernel = project_kernel
        out_shape = jax.ShapeDtypeStruct((half, columns), jnp.bfloat16)
        out_specs = pl.BlockSpec((half, cut), lambda j, at: (0, j))
    else:
        kernel = finish_kernel
        in_specs.append(pl.BlockSpec((half, cut), lambda j, at: (0, j)))
        operands.append(came)
        out_shape = jax.ShapeDtypeStruct((1, half, width), jnp.bfloat16)
        out_specs = pl.BlockSpec((1, half, cut), lambda j, at: (0, 0, at[4] + j))
    for n in range(4):
        in_specs.append(pl.BlockSpec((depth, cut), functools.partial(lambda n, j, at: (at[n], j), n)))
    operands += pieces
    if out is not None:
        in_specs.append(pl.BlockSpec(memory_space=pl.ANY))
        operands.append(out)
        aliases = {len(operands): 0}
    return pl.pallas_call(
        kernel,
        out_shape=out_shape,
        grid_spec=pltpu.PrefetchScalarGridSpec(
            num_scalar_prefetch=1, grid=(columns // cut,), in_specs=in_specs, out_specs=out_specs
        ),
        input_output_aliases=aliases,
        compiler_params=pltpu.CompilerParams(vmem_limit_bytes=VMEM),
        cost_estimate=pl.CostEstimate(
            flops=8 * half * depth * columns, bytes_accessed=8 * depth * (columns + half), transcendentals=0
        ),
        name="project" if came is None else "finish",
    )(table.astype(jnp.int32), *operands)


def pick_kernel(asked, pool, out):
    def copy(n, carry):
        out[n] = pool[asked[n]]
        return carry

    lax.fori_loop(0, out.shape[0], copy, 0, unroll=8)


def pick(pool, asked):
    vmem = pl.BlockSpec(memory_space=pltpu.VMEM)
    return pl.pallas_call(
        pick_kernel,
        out_shape=jax.ShapeDtypeStruct(asked.shape + pool.shape[1:], jnp.bfloat16),
        in_specs=[pl.BlockSpec(memory_space=pltpu.SMEM), vmem],
        out_specs=vmem,
        compiler_params=pltpu.CompilerParams(vmem_limit_bytes=VMEM),
        name="pick",
    )(asked, pool)


SWAP = [(0, 1), (1, 0)]


def after(value, *others):
    return lax.optimization_barrier((value,) + others)[0]


def shards(
    queries, new_kv, pool, out_weight, tok_conv, page_conv, page_fill, page_owner, page_index
):
    row_count = queries.shape[1]
    slot_count = page_owner.shape[1]
    owner_count = lax.axis_size("seq")
    tp_count = lax.axis_size("tp")
    bucket = 2 * slot_count // owner_count
    group, role, tp = lax.axis_index("group"), lax.axis_index("role"), lax.axis_index("tp")
    seq = lax.axis_index("seq")


    own = 2 * group + role
    depth = out_weight.shape[0] // 4
    columns = out_weight.shape[1]
    quarter = lax.dynamic_slice_in_dim(out_weight, own * depth, depth, 0)
    order = [q ^ own for q in range(4)]
    order = [(v % 2) * 2 + v // 2 for v in order]
    flip = tp if tp_count == 2 else 0

    def control(side):
        return jnp.stack([jnp.asarray(v, jnp.int32) for v in (side, *order)])

    whole = jnp.zeros((4,), jnp.int32)
    swap_group = functools.partial(lax.ppermute, axis_name="group", perm=SWAP)
    swap_role = functools.partial(lax.ppermute, axis_name="role", perm=SWAP)

    if owner_count == 4:
        middle = (seq == 1) | (seq == 2)
        near = lax.ppermute(quarter, "seq", [(0, 1), (1, 0), (2, 3), (3, 2)])
        inner = lax.ppermute(quarter, "seq", [(1, 2), (2, 1)])

    slot_owner = page_owner[0]
    position = slot_owner * bucket + bucket_ranks(slot_owner, owner_count)
    wanted = (
        jnp.zeros((owner_count * bucket,), jnp.int32)
        .at[position]
        .set(page_index[0], mode="promise_in_bounds", unique_indices=True)
        .reshape(owner_count, bucket)
    )
    asked = lax.all_to_all(wanted, "seq", split_axis=0, concat_axis=0, tiled=True)
    found = pick(pool[0], asked.reshape(-1))
    pages = lax.all_to_all(
        found.reshape((owner_count, bucket) + found.shape[1:]),
        "seq", split_axis=0, concat_axis=0, tiled=True,
    ).reshape(found.shape)
    fresh = new_kv[0].reshape(row_count, -1)
    tables = attend_tables(
        row_count, slot_count, pool.shape[3], tok_conv[0], page_conv[0], page_fill[0]
    )

    if owner_count != 4 or tp_count != 2:
        mine = lax.all_gather(quarter, "seq", axis=1, tiled=True)
        across = swap_group(mine)
        pieces = [mine, across, swap_role(mine), swap_role(across)]
        partial = [
            project(attend(control(side), tables, position, queries[0], pages, fresh), pieces, whole)
            for side in (0, 1)
        ]
        return lax.psum_scatter(
            jnp.concatenate(partial, axis=0), "tp", scatter_dimension=0, tiled=True
        )[None]

    swap_tp = functools.partial(lax.ppermute, axis_name="tp", perm=SWAP)
    forward = functools.partial(lax.ppermute, axis_name="seq", perm=[(1, 0), (2, 3)])
    cross = functools.partial(lax.ppermute, axis_name="seq", perm=[(1, 2), (2, 1)])
    cut = columns // 2

    def four(one, two, *hold):
        return [one, two, swap_role(after(one, *hold)), swap_role(after(two, *hold))]

    near, inner = after(near, found), after(inner, found)
    near_across = swap_group(near)
    far_a = cross(near[:, :cut])
    next_shard = jnp.where(middle, inner, forward(inner))
    next_across = swap_group(next_shard)
    far_a = jnp.where(middle, far_a, forward(far_a))
    far_a_across = swap_group(far_a)
    near_all = four(near, near_across)
    next_all = four(next_shard, next_across)

    far_b = cross(after(near[:, cut:], pages))
    pages = after(pages, near_across, next_shard, far_a)
    left = attend(control(1 - flip), tables, position, queries[0], pages, fresh)
    far_b_on = forward(after(far_b, left))
    local = jnp.stack([own, own ^ 2, own ^ 1, own ^ 3]).astype(jnp.int32)
    sent = [project(left, [out_weight] * 4, local)]
    far_a_all = four(far_a, far_a_across)
    for pieces in (near_all, next_all, far_a_all):
        sent.append(project(after(left, sent[-1]), pieces, whole))
    came = [swap_tp(part) for part in sent]
    far_b = jnp.where(middle, far_b, after(far_b_on, sent[2]))
    far_b_across = swap_group(far_b)
    stay = attend(
        control(flip), tables, position, queries[0], after(pages, sent[3], far_b), fresh
    )
    far_b_all = four(far_b, far_b_across, stay)
    total = columns * owner_count
    second = jnp.where(seq < 2, 2, 1)
    third = jnp.where(seq < 2, 3, 0)
    out = project(stay, [out_weight] * 4, local, came[0], seq, None, total)
    out = project(stay, near_all, whole, came[1], seq ^ 1, out, total)
    last = project(after(left, out), far_b_all, whole)
    stay = after(stay, last)
    last = swap_tp(last)
    out = project(stay, next_all, whole, came[2], second, out, total)
    out = project(stay, far_a_all, whole, came[3], 2 * third, out, total)
    return project(stay, far_b_all, whole, last, 2 * third + 1, out, total)


def solution(mesh):
    return jax.shard_map(
        shards,
        mesh=mesh,
        in_specs=(
            P("role", ("group", "seq"), "tp"),
            P("role", ("group", "seq"), None, "tp"),
            P("role", ("group", "seq"), None, None, "tp"),
            P("tp", "seq"),
            P("role", ("group", "seq")),
            P("role", ("group", "seq")),
            P("role", ("group", "seq")),
            P("role", ("group", "seq")),
            P("role", ("group", "seq")),
        ),
        out_specs=P("role", ("group", "seq", "tp"), None),
        check_vma=False,
    )
```

time: 307 us -> 301 us (0.980)
  waiting for transfers between devices: 203 us -> 132 us
  Pallas kernels: 48.1 us -> 85.3 us
  starting transfers between devices: 12.8 us -> 39.7 us
  between operations: 13.5 us -> 0.42 us
  local copies, waits for them, and re-layouts: 12.2 us -> 19.8 us
  other arithmetic: 3.26 us -> 10.1 us
    all_gather x2 -> x0, waiting for transfers between devices: 137 us -> none  [shards(): lax.all_gather(quarter[:, n * part:(n + 1) * part], 'seq', axis=0)]
    ppermute x8 -> x24, waiting for transfers between devices: 65.2 us -> 132 us  [the longest x1 108 us: shards(): inner = lax.ppermute(quarter, 'seq', [(1, 2), (2, 1)])]
    pallas_call x3 -> x11, Pallas kernels: 21 us -> 53.7 us  [the longest x10 49.1 us: project(): pl.pallas_call(kernel, out_shape=out_shape, grid_spec=pltpu.PrefetchScala...]
    ppermute x8 -> x24, starting transfers between devices: 5.46 us -> 32.6 us  [the longest x1 5.74 us: shards(): far_a = jnp.where(middle, far_a, forward(far_a))]
    unnamed x17 -> x49, local copies, waits for them, and re-layouts: 1.92 us -> 9.02 us
    gather x1 -> x0, local copies, waits for them, and re-layouts: 4.99 us -> none  [shards(): found = pool[0].at[asked].get(mode='promise_in_bounds')]
    pallas_call x1 -> x2, Pallas kernels: 27.1 us -> 31.6 us  [attend(): pl.pallas_call(functools.partial(attend_kernel, spec), out_shape=jax.Shap...]
    concatenate x0 -> x5, local copies, waits for them, and re-layouts: none -> 3.13 us  [project(): jnp.concatenate([rows_at, (base * (columns // cut))[None]])]
  transfers between devices with their start and end apart: 11 -> 25, of which waited for: 5 -> 4; matrix products, arithmetic and copies ran while one was open for 4% -> 6% of each run, Pallas kernels for 15% -> 26%
where the time goes in v3:
time: 301 us; the launch traced here: 296 us
  waiting for transfers between devices  132 us (44%)
  Pallas kernels  85.3 us (28%)
  starting transfers between devices  39.7 us (13%)
  local copies, waits for them, and re-layouts  19.8 us (7%)
  other arithmetic  10.1 us (3%)
  blocking collectives  8.19 us (3%)
    ppermute x1, waiting for transfers between devices, shards(): inner = lax.ppermute(quarter, 'seq', [(1, 2), (2, 1)])  108 us
    pallas_call x10, Pallas kernels, project(): pl.pallas_call(kernel, out_shape=out_shape, grid_spec=pltpu.PrefetchScala...  49.1 us
    pallas_call x2, Pallas kernels, attend(): pl.pallas_call(functools.partial(attend_kernel, spec), out_shape=jax.Shap...  31.6 us
    ppermute x1, waiting for transfers between devices, shards(): next_shard = jnp.where(middle, inner, forward(inner))  13.7 us
    unnamed x49, local copies, waits for them, and re-layouts  9.02 us
    all_to_all x1, blocking collectives, shards(): lax.all_to_all(wanted, 'seq', split_axis=0, concat_axis=0, tiled=True)  8.19 us
    ppermute x1, waiting for transfers between devices, shards(): next_across = swap_group(next_shard)  7.84 us
    all_to_all x1, starting transfers between devices, shards(): lax.all_to_all(found.reshape((owner_count, bucket) + found.shape[1:]), 's...  7.17 us
  transfers between devices with their start and end apart: 25, of which 4 were waited for; matrix products, arithmetic and copies ran while one was open for 6% of the time, Pallas kernels for 26%

profile of v3, /device:TPU:16, one launch (start us, length us, event | category | flops | bytes accessed | tf_op | source)
XLA Modules:
  0.0 296.1 jit_solution(11033316329689362157)
XLA Ops:
  0.9 0.8 select_reduce_fusion
  2.4 1.1 scatter_custom_fusion
  3.6 8.2 %all_to_all.14 = s32[4,1,64]{2,1,0:T(1,128)S(1)} all-to-all(s32[4,1,64]{2,1,0:T(1,128)S(1)} %all_to_all.9), channel_id=1, replica_groups=mesh['group'=2,'seq'=4,'tp'=2,'role'=2] {'seq'}, dimensions={0} | all-to-all | bytes 2048 | tf_op jit(solution)/shard_map/all_to_all | solution.py:311
  13.6 4.7 %pick.1 = bf16[256,2,16,256]{3,2,1,0:T(8,128)(2,1)} custom-call(s32[256]{0:T(256)} %reshape.64.asked, bf16[256,2,16,256]{3,2,1,0:T(8,128)(2,1)} %bitcast.40), custom_call_target="tpu_custom_call" | custom-call | tf_op jit(solution)/shard_map/pick/pallas_call | solution.py:254
  18.3 7.2 %all-to-all-start.1 = ((bf16[4,64,2,16,256]{4,3,2,1,0:T(8,128)(2,1)}), bf16[4,64,2,16,256]{4,3,2,1,0:T(8,128)(2,1)}, u32[]{:S(2)}, u32[]{:S(2)}) async-start(bf16[4,64,2,16,256]{4,3,2,1,0:T(8,128)(2,1)} %bitcast.37), calls=%async_computation.1 | async-start | bytes 8388608 | tf_op jit(solution)/shard_map/all_to_all | solution.py:313
  25.5 1.3 constant_dynamic-slice_fusion
  26.7 2.5 collective-permute-start.2
  29.3 108.2 %collective-permute-done.2 = bf16[512,1024]{1,0:T(8,128)(2,1)S(1)} collective-permute-done((bf16[512,1024]{1,0:T(8,128)(2,1)S(1)}, bf16[512,1024]{1,0:T(8,128)(2,1)S(1)}, u32[]{:S(2)}, u32[]{:S(2)}) %collective-permute-start.2) | collective-permute-done | bytes 1048608 | tf_op jit(solution)/shard_map/ppermute | solution.py:301
  137.5 2.3 collective-permute-start.3
  139.9 1.5 collective-permute-start.1
  141.4 1.1 fusion.9
  142.5 3.5 %collective-permute-start.4 = (bf16[512,512]{1,0:T(8,128)(2,1)}, bf16[512,512]{1,0:T(8,128)(2,1)}, u32[]{:S(2)}, u32[]{:S(2)}) collective-permute-start(bf16[512,512]{1,0:T(8,128)(2,1)} %get-tuple-element.40), channel_id=1, source_target_pairs={{4,8},{8,4},{5,9},{9,5},{6,10},{10,6},{7,11},{11,7},{20,24},{24,20... | collective-permute-start | bytes 1572872 | tf_op jit(solution)/shard_map/ppermute | solution.py:344
  146.1 13.7 %collective-permute-done.3 = bf16[512,1024]{1,0:T(8,128)(2,1)} collective-permute-done((bf16[512,1024]{1,0:T(8,128)(2,1)S(1)}, bf16[512,1024]{1,0:T(8,128)(2,1)}, u32[]{:S(2)}, u32[]{:S(2)}) %collective-permute-start.3) | collective-permute-done | bytes 1048608 | tf_op jit(solution)/shard_map/ppermute | solution.py:345
  159.8 1.6 collective-permute-start.8
  161.8 0.8 fusion.1
  162.6 5.7 %collective-permute-start.5 = (bf16[512,512]{1,0:T(8,128)(2,1)}, bf16[512,512]{1,0:T(8,128)(2,1)S(1)}, u32[]{:S(2)}, u32[]{:S(2)}) collective-permute-start(bf16[512,512]{1,0:T(8,128)(2,1)} %collective-permute-done.4), channel_id=1, source_target_pairs={{4,0},{8,12},{5,1},{9,13},{6,2},{10,14},{7,3},{11,15},{20,16},{24,... | collective-permute-start | bytes 1572872 | tf_op jit(solution)/shard_map/ppermute | solution.py:347
  168.4 1.2 multiply_add_fusion.position
  169.6 4.4 %collective-permute-start.14 = (bf16[512,512]{1,0:T(8,128)(2,1)}, bf16[512,512]{1,0:T(8,128)(2,1)}, u32[]{:S(2)}, u32[]{:S(2)}) collective-permute-start(bf16[512,512]{1,0:T(8,128)(2,1)} %get-tuple-element.25), channel_id=1, source_target_pairs={{4,8},{8,4},{5,9},{9,5},{6,10},{10,6},{7,11},{11,7},{20,24},{24,20... | collective-permute-start | bytes 1572872 | tf_op jit(solution)/shard_map/ppermute | solution.py:352
  174.3 0.8 copy.18
  175.2 0.8 copy.16.tok_conv
  177.7 7.8 %collective-permute-done.8.refs_1_ = bf16[512,1024]{1,0:T(8,128)(2,1)} collective-permute-done((bf16[512,1024]{1,0:T(8,128)(2,1)S(1)}, bf16[512,1024]{1,0:T(8,128)(2,1)}, u32[]{:S(2)}, u32[]{:S(2)}) %collective-permute-start.8) | collective-permute-done | bytes 1048608 | tf_op jit(solution)/shard_map/ppermute | solution.py:346
  186.1 1.1 broadcast_select_fusion.2.refs_0_
  187.2 1.6 collective-permute-start.11
  190.0 15.5 %attend.2.left = bf16[4,192,512]{2,1,0:T(8,128)(2,1)} custom-call(s32[5]{0:T(128)} %stack.50.control, s32[128]{0:T(128)} %multiply_add_fusion.position, s32[12]{0:T(128)} %get-tuple-element.42.hist_at, s32[12]{0:T(128)} %get-tuple-element.41.hist_steps, s32[12]{0:T(128)} %get-tuple-element.36.fresh_at, s32[12]{0:T(128)} %get-tuple-element.35.fresh_steps, ...), custom_call_target="tpu_custom_call" | custom-call | flops 1258291200 | bytes 8388608 | tf_op jit(solution)/shard_map/attend/pallas_call | solution.py:164
  205.5 1.3 collective-permute-start.15
  207.4 5.6 %project.5 = bf16[192,1024]{1,0:T(8,128)(2,1)} custom-call(s32[4]{0:T(128)} %pad_add_fusion.1.rows_at, bf16[4,192,512]{2,1,0:T(8,128)(2,1)} %attend.2.left, bf16[2048,1024]{1,0:T(8,128)(2,1)} %refs_3_.3, bf16[2048,1024]{1,0:T(8,128)(2,1)} %refs_3_.3, bf16[2048,1024]{1,0:T(8,128)(2,1)} %refs_3_.3, bf16[2048,1024]{1,0:T(8,128)(2,1)} %refs_3_.3), custom_call_target="tpu_custom_call" | custom-call | flops 805306368 | bytes 4980736 | tf_op jit(solution)/shard_map/project/pallas_call | solution.py:229
  214.4 5.6 %project.6 = bf16[192,1024]{1,0:T(8,128)(2,1)} custom-call(s32[4]{0:T(128)} %broadcast_15_rows_at.2.rows_at, bf16[4,192,512]{2,1,0:T(8,128)(2,1)} %attend.2.left, bf16[512,1024]{1,0:T(8,128)(2,1)} %copy-done.1, bf16[512,1024]{1,0:T(8,128)(2,1)} %collective-permute-done.1.refs_1_, bf16[512,1024]{1,0:T(8,128)(2,1)} %copy-done.6, bf16[512,1024]{1,0:T(8,128)(2,1)} %copy-done.7), custom_call_target="tpu_custom_call" | custom-call | flops 805306368 | bytes 4980736 | tf_op jit(solution)/shard_map/project/pallas_call | solution.py:229
  220.1 1.0 copy-done.4
  221.0 1.0 copy-done.5
  222.0 5.6 %project.7 = bf16[192,1024]{1,0:T(8,128)(2,1)} custom-call(s32[4]{0:T(128)} %broadcast_15_rows_at.2.rows_at, bf16[4,192,512]{2,1,0:T(8,128)(2,1)} %attend.2.left, bf16[512,1024]{1,0:T(8,128)(2,1)} %copy-done, bf16[512,1024]{1,0:T(8,128)(2,1)} %collective-permute-done.8.refs_1_, bf16[512,1024]{1,0:T(8,128)(2,1)} %copy-done.4, bf16[512,1024]{1,0:T(8,128)(2,1)} %copy-done.5), custom_call_target="tpu_custom_call" | custom-call | flops 805306368 | bytes 4980736 | tf_op jit(solution)/shard_map/project/pallas_call | solution.py:229
  227.6 1.1 broadcast_select_fusion.1.refs_0_
  228.7 1.8 collective-permute-start.18
  231.1 1.0 collective-permute-start.17
  232.2 0.8 copy-done.9
  233.0 0.8 copy-done.10
  233.7 3.7 %project.8 = bf16[192,512]{1,0:T(8,128)(2,1)} custom-call(s32[4]{0:T(128)} %broadcast_15_rows_at.2.rows_at, bf16[4,192,512]{2,1,0:T(8,128)(2,1)} %attend.2.left, bf16[512,512]{1,0:T(8,128)(2,1)} %copy-done.2, bf16[512,512]{1,0:T(8,128)(2,1)} %copy-done.8, bf16[512,512]{1,0:T(8,128)(2,1)} %copy-done.9, bf16[512,512]{1,0:T(8,128)(2,1)} %copy-done.10), custom_call_target="tpu_custom_call" | custom-call | flops 402653184 | bytes 2883584 | tf_op jit(solution)/shard_map/project/pallas_call | solution.py:229
  237.5 16.1 %attend.3.left = bf16[4,192,512]{2,1,0:T(8,128)(2,1)} custom-call(s32[5]{0:T(128)} %stack.48.control, s32[128]{0:T(128)} %multiply_add_fusion.position, s32[12]{0:T(128)} %get-tuple-element.42.hist_at, s32[12]{0:T(128)} %get-tuple-element.41.hist_steps, s32[12]{0:T(128)} %get-tuple-element.36.fresh_at, s32[12]{0:T(128)} %get-tuple-element.35.fresh_steps, ...), custom_call_target="tpu_custom_call" | custom-call | flops 1258291200 | bytes 8388608 | tf_op jit(solution)/shard_map/attend/pallas_call | solution.py:164
  254.6 1.5 collective-permute-start.23
  257.9 5.7 %finish.5.refs_4_ = bf16[1,192,4096]{2,1,0:T(8,128)(2,1)} custom-call(s32[5]{0:T(128)} %concatenate.22.rows_at, bf16[4,192,512]{2,1,0:T(8,128)(2,1)} %attend.3.left, bf16[192,1024]{1,0:T(8,128)(2,1)} %collective-permute-done.17.came, bf16[2048,1024]{1,0:T(8,128)(2,1)} %refs_3_.3, bf16[2048,1024]{1,0:T(8,128)(2,1)} %refs_3_.3, bf16[2048,1024]{1,0:T(8,128)(2,1)} %refs_3_.3, ...), custom_call_target="tpu_custom_call" | custom-call | flops 805306368 | bytes 4980736 | tf_op jit(solution)/shard_map/finish/pallas_call | solution.py:229
  263.6 2.7 collective-permute-done.16.came
  267.0 5.7 %finish.6.refs_4_ = bf16[1,192,4096]{2,1,0:T(8,128)(2,1)} custom-call(s32[5]{0:T(128)} %concatenate.21.rows_at, bf16[4,192,512]{2,1,0:T(8,128)(2,1)} %attend.3.left, bf16[192,1024]{1,0:T(8,128)(2,1)} %copy-done.15, bf16[512,1024]{1,0:T(8,128)(2,1)} %copy-done.1, bf16[512,1024]{1,0:T(8,128)(2,1)} %collective-permute-done.1.refs_1_, ...), custom_call_target="tpu_custom_call", output_to_operand_aliasing={{}: (7, {})} | custom-call | flops 805306368 | bytes 4980736 | tf_op jit(solution)/shard_map/finish/pallas_call | solution.py:229
  272.8 0.8 copy-done.12
  273.6 0.8 copy-done.13
  274.4 3.7 %project.9 = bf16[192,512]{1,0:T(8,128)(2,1)} custom-call(s32[4]{0:T(128)} %broadcast_15_rows_at.2.rows_at, bf16[4,192,512]{2,1,0:T(8,128)(2,1)} %attend.2.left, bf16[512,512]{1,0:T(8,128)(2,1)} %copy-done.3, bf16[512,512]{1,0:T(8,128)(2,1)} %copy-done.11, bf16[512,512]{1,0:T(8,128)(2,1)} %copy-done.12, bf16[512,512]{1,0:T(8,128)(2,1)} %copy-done.13), custom_call_target="tpu_custom_call" | custom-call | flops 402653184 | bytes 2883584 | tf_op jit(solution)/shard_map/project/pallas_call | solution.py:229
  280.5 0.8 copy-done.14
  281.3 5.7 %finish.7.refs_4_ = bf16[1,192,4096]{2,1,0:T(8,128)(2,1)} custom-call(s32[5]{0:T(128)} %concatenate.24.rows_at, bf16[4,192,512]{2,1,0:T(8,128)(2,1)} %attend.3.left, bf16[192,1024]{1,0:T(8,128)(2,1)} %copy-done.14, bf16[512,1024]{1,0:T(8,128)(2,1)} %copy-done, bf16[512,1024]{1,0:T(8,128)(2,1)} %collective-permute-done.8.refs_1_, ...), custom_call_target="tpu_custom_call", output_to_operand_aliasing={{}: (7, {})} | custom-call | flops 805306368 | bytes 4980736 | tf_op jit(solution)/shard_map/finish/pallas_call | solution.py:229
  287.7 3.8 %finish.8.refs_4_ = bf16[1,192,4096]{2,1,0:T(8,128)(2,1)} custom-call(s32[5]{0:T(128)} %concatenate.23.rows_at, bf16[4,192,512]{2,1,0:T(8,128)(2,1)} %attend.3.left, bf16[192,512]{1,0:T(8,128)(2,1)} %copy-done.18, bf16[512,512]{1,0:T(8,128)(2,1)} %copy-done.2, bf16[512,512]{1,0:T(8,128)(2,1)} %copy-done.8, ...), custom_call_target="tpu_custom_call", output_to_operand_aliasing={{}: (7, {})} | custom-call | flops 402653184 | bytes 2883584 | tf_op jit(solution)/shard_map/finish/pallas_call | solution.py:229
  292.2 3.8 %finish.9 = bf16[1,192,4096]{2,1,0:T(8,128)(2,1)} custom-call(s32[5]{0:T(128)} %concatenate.19.rows_at, bf16[4,192,512]{2,1,0:T(8,128)(2,1)} %attend.3.left, bf16[192,512]{1,0:T(8,128)(2,1)} %copy-done.19, bf16[512,512]{1,0:T(8,128)(2,1)} %copy-done.3, bf16[512,512]{1,0:T(8,128)(2,1)} %copy-done.11, ...), custom_call_target="tpu_custom_call", output_to_operand_aliasing={{}: (7, {})} | custom-call | flops 402653184 | bytes 2883584 | tf_op jit(solution)/shard_map/finish/pallas_call | solution.py:229
  (102 shorter events, 17.7 us)
Async XLA Ops:
  1.7 0.7 copy-start.23
  18.3 151.3 %all-to-all-start.1 = ((bf16[4,64,2,16,256]{4,3,2,1,0:T(8,128)(2,1)}), bf16[4,64,2,16,256]{4,3,2,1,0:T(8,128)(2,1)}, u32[]{:S(2)}, u32[]{:S(2)}) async-start(bf16[4,64,2,16,256]{4,3,2,1,0:T(8,128)(2,1)} %bitcast.37), calls=%async_computation.1 | async-start | bytes 8388608 | tf_op jit(solution)/shard_map/all_to_all | solution.py:313
  26.7 110.8 %collective-permute-start.2 = (bf16[512,1024]{1,0:T(8,128)(2,1)S(1)}, bf16[512,1024]{1,0:T(8,128)(2,1)S(1)}, u32[]{:S(2)}, u32[]{:S(2)}) collective-permute-start(bf16[512,1024]{1,0:T(8,128)(2,1)S(1)} %constant_dynamic-slice_fusion), channel_id=1, source_target_pairs={{4,8},{8,4},{5,9},{9,5},{6,10},{10,6},{7,11},{11,7},{20,24},{24,20... | collective-permute-start | bytes 3145736 | tf_op jit(solution)/shard_map/ppermute | solution.py:301
  29.2 110.7 %collective-permute-start = (bf16[512,1024]{1,0:T(8,128)(2,1)S(1)}, bf16[512,1024]{1,0:T(8,128)(2,1)S(1)}, u32[]{:S(2)}, u32[]{:S(2)}) collective-permute-start(bf16[512,1024]{1,0:T(8,128)(2,1)S(1)} %constant_dynamic-slice_fusion), channel_id=1, source_target_pairs={{0,4},{4,0},{8,12},{12,8},{1,5},{5,1},{9,13},{13,9},{2,6},{6,2},{1... | collective-permute-start | bytes 3145736 | tf_op jit(solution)/shard_map/ppermute | solution.py:300
  137.5 22.2 %collective-permute-start.3 = (bf16[512,1024]{1,0:T(8,128)(2,1)S(1)}, bf16[512,1024]{1,0:T(8,128)(2,1)}, u32[]{:S(2)}, u32[]{:S(2)}) collective-permute-start(bf16[512,1024]{1,0:T(8,128)(2,1)S(1)} %collective-permute-done.2), channel_id=1, source_target_pairs={{4,0},{8,12},{5,1},{9,13},{6,2},{10,14},{7,3},{11,15},{20,16},{24,... | collective-permute-start | bytes 3145736 | tf_op jit(solution)/shard_map/ppermute | solution.py:345
  139.9 37.3 %copy-start.1 = (bf16[512,1024]{1,0:T(8,128)(2,1)}, bf16[512,1024]{1,0:T(8,128)(2,1)S(1)}, u32[]{:S(2)}) copy-start(bf16[512,1024]{1,0:T(8,128)(2,1)S(1)} %collective-permute-done.refs_0_) | copy-start | bytes 3145732
  139.9 37.3 %collective-permute-start.1 = (bf16[512,1024]{1,0:T(8,128)(2,1)S(1)}, bf16[512,1024]{1,0:T(8,128)(2,1)}, u32[]{:S(2)}, u32[]{:S(2)}) collective-permute-start(bf16[512,1024]{1,0:T(8,128)(2,1)S(1)} %collective-permute-done.refs_0_), channel_id=1, source_target_pairs={{0,16},{16,0},{1,17},{17,1},{2,18},{18,2},{3,19},{19,3},{4,20},{20... | collective-permute-start | bytes 3145736 | tf_op jit(solution)/shard_map/ppermute | solution.py:343
  142.5 18.9 %copy-start.20 = (s32[1,384]{1,0:T(1,128)S(1)}, s32[1,384]{1,0:T(1,128)}, u32[]{:S(2)}) copy-start(s32[1,384]{1,0:T(1,128)} %param.13) | copy-start | bytes 4612
  142.5 19.1 %copy-start.22 = (s32[1,128]{1,0:T(1,128)S(1)}, s32[1,128]{1,0:T(1,128)}, u32[]{:S(2)}) copy-start(s32[1,128]{1,0:T(1,128)} %param.14) | copy-start | bytes 1540
  142.5 25.8 %copy-start.21 = (s32[1,128]{1,0:T(1,128)S(1)}, s32[1,128]{1,0:T(1,128)}, u32[]{:S(2)}) copy-start(s32[1,128]{1,0:T(1,128)} %param.16) | copy-start | bytes 1540
  142.5 31.8 %copy-start.16 = (bf16[1,384,2,256]{3,2,1,0:T(2,128)(2,1)S(1)}, bf16[1,384,2,256]{3,2,1,0:T(2,128)(2,1)}, u32[]{:S(2)}) copy-start(bf16[1,384,2,256]{3,2,1,0:T(2,128)(2,1)} %param.10) | copy-start | bytes 1179652
  142.5 20.1 %collective-permute-start.4 = (bf16[512,512]{1,0:T(8,128)(2,1)}, bf16[512,512]{1,0:T(8,128)(2,1)}, u32[]{:S(2)}, u32[]{:S(2)}) collective-permute-start(bf16[512,512]{1,0:T(8,128)(2,1)} %get-tuple-element.40), channel_id=1, source_target_pairs={{4,8},{8,4},{5,9},{9,5},{6,10},{10,6},{7,11},{11,7},{20,24},{24,20... | collective-permute-start | bytes 1572872 | tf_op jit(solution)/shard_map/ppermute | solution.py:344
  159.8 45.7 %copy-start = (bf16[512,1024]{1,0:T(8,128)(2,1)}, bf16[512,1024]{1,0:T(8,128)(2,1)S(1)}, u32[]{:S(2)}) copy-start(bf16[512,1024]{1,0:T(8,128)(2,1)S(1)} %broadcast_select_fusion.refs_0_) | copy-start | bytes 3145732
  159.8 25.7 %collective-permute-start.8 = (bf16[512,1024]{1,0:T(8,128)(2,1)S(1)}, bf16[512,1024]{1,0:T(8,128)(2,1)}, u32[]{:S(2)}, u32[]{:S(2)}) collective-permute-start(bf16[512,1024]{1,0:T(8,128)(2,1)S(1)} %broadcast_select_fusion.refs_0_), channel_id=1, source_target_pairs={{0,16},{16,0},{1,17},{17,1},{2,18},{18,2},{3,19},{19,3},{4,20},{20... | collective-permute-start | bytes 3145736 | tf_op jit(solution)/shard_map/ppermute | solution.py:346
  162.6 23.0 %collective-permute-start.5 = (bf16[512,512]{1,0:T(8,128)(2,1)}, bf16[512,512]{1,0:T(8,128)(2,1)S(1)}, u32[]{:S(2)}, u32[]{:S(2)}) collective-permute-start(bf16[512,512]{1,0:T(8,128)(2,1)} %collective-permute-done.4), channel_id=1, source_target_pairs={{4,0},{8,12},{5,1},{9,13},{6,2},{10,14},{7,3},{11,15},{20,16},{24,... | collective-permute-start | bytes 1572872 | tf_op jit(solution)/shard_map/ppermute | solution.py:347
  169.6 17.6 %collective-permute-start.14 = (bf16[512,512]{1,0:T(8,128)(2,1)}, bf16[512,512]{1,0:T(8,128)(2,1)}, u32[]{:S(2)}, u32[]{:S(2)}) collective-permute-start(bf16[512,512]{1,0:T(8,128)(2,1)} %get-tuple-element.25), channel_id=1, source_target_pairs={{4,8},{8,4},{5,9},{9,5},{6,10},{10,6},{7,11},{11,7},{20,24},{24,20... | collective-permute-start | bytes 1572872 | tf_op jit(solution)/shard_map/ppermute | solution.py:352
  177.2 35.8 %collective-permute-start.6 = (bf16[512,1024]{1,0:T(8,128)(2,1)S(1)}, bf16[512,1024]{1,0:T(8,128)(2,1)S(1)}, u32[]{:S(2)}, u32[]{:S(2)}) collective-permute-start(bf16[512,1024]{1,0:T(8,128)(2,1)S(1)} %collective-permute-done.refs_0_), channel_id=1, source_target_pairs={{0,1},{1,0},{2,3},{3,2},{4,5},{5,4},{6,7},{7,6},{8,9},{9,8},{10,11... | collective-permute-start | bytes 3145736 | tf_op jit(solution)/shard_map/ppermute | solution.py:340
  177.2 35.9 %collective-permute-start.7 = (bf16[512,1024]{1,0:T(8,128)(2,1)}, bf16[512,1024]{1,0:T(8,128)(2,1)S(1)}, u32[]{:S(2)}, u32[]{:S(2)}) collective-permute-start(bf16[512,1024]{1,0:T(8,128)(2,1)} %collective-permute-done.1.refs_1_), channel_id=1, source_target_pairs={{0,1},{1,0},{2,3},{3,2},{4,5},{5,4},{6,7},{7,6},{8,9},{9,8},{10,11... | collective-permute-start | bytes 3145736 | tf_op jit(solution)/shard_map/ppermute | solution.py:340
  185.6 34.5 %collective-permute-start.9 = (bf16[512,1024]{1,0:T(8,128)(2,1)S(1)}, bf16[512,1024]{1,0:T(8,128)(2,1)S(1)}, u32[]{:S(2)}, u32[]{:S(2)}) collective-permute-start(bf16[512,1024]{1,0:T(8,128)(2,1)S(1)} %broadcast_select_fusion.refs_0_), channel_id=1, source_target_pairs={{0,1},{1,0},{2,3},{3,2},{4,5},{5,4},{6,7},{7,6},{8,9},{9,8},{10,11... | collective-permute-start | bytes 3145736 | tf_op jit(solution)/shard_map/ppermute | solution.py:340
  185.6 34.5 %collective-permute-start.10 = (bf16[512,1024]{1,0:T(8,128)(2,1)}, bf16[512,1024]{1,0:T(8,128)(2,1)S(1)}, u32[]{:S(2)}, u32[]{:S(2)}) collective-permute-start(bf16[512,1024]{1,0:T(8,128)(2,1)} %collective-permute-done.8.refs_1_), channel_id=1, source_target_pairs={{0,1},{1,0},{2,3},{3,2},{4,5},{5,4},{6,7},{7,6},{8,9},{9,8},{10,11... | collective-permute-start | bytes 3145736 | tf_op jit(solution)/shard_map/ppermute | solution.py:340
  187.2 25.9 %copy-start.2 = (bf16[512,512]{1,0:T(8,128)(2,1)}, bf16[512,512]{1,0:T(8,128)(2,1)S(1)}, u32[]{:S(2)}) copy-start(bf16[512,512]{1,0:T(8,128)(2,1)S(1)} %broadcast_select_fusion.2.refs_0_) | copy-start | bytes 1572868
  187.2 18.3 %collective-permute-start.11 = (bf16[512,512]{1,0:T(8,128)(2,1)S(1)}, bf16[512,512]{1,0:T(8,128)(2,1)S(1)}, u32[]{:S(2)}, u32[]{:S(2)}) collective-permute-start(bf16[512,512]{1,0:T(8,128)(2,1)S(1)} %broadcast_select_fusion.2.refs_0_), channel_id=1, source_target_pairs={{0,16},{16,0},{1,17},{17,1},{2,18},{18,2},{3,19},{19,3},{4,20},{20... | collective-permute-start | bytes 1572872 | tf_op jit(solution)/shard_map/ppermute | solution.py:348
  205.5 7.6 %copy-start.8 = (bf16[512,512]{1,0:T(8,128)(2,1)}, bf16[512,512]{1,0:T(8,128)(2,1)S(1)}, u32[]{:S(2)}) copy-start(bf16[512,512]{1,0:T(8,128)(2,1)S(1)} %collective-permute-done.11.refs_1_) | copy-start | bytes 1572868
  205.5 22.1 %collective-permute-start.15 = (bf16[512,512]{1,0:T(8,128)(2,1)}, bf16[512,512]{1,0:T(8,128)(2,1)S(1)}, u32[]{:S(2)}, u32[]{:S(2)}) collective-permute-start(bf16[512,512]{1,0:T(8,128)(2,1)} %collective-permute-done.14), channel_id=1, source_target_pairs={{4,0},{8,12},{5,1},{9,13},{6,2},{10,14},{7,3},{11,15},{20,16},{24,... | collective-permute-start | bytes 1572872 | tf_op jit(solution)/shard_map/ppermute | solution.py:355
  213.1 1.3 copy-start.6
  213.1 19.1 %collective-permute-start.12 = (bf16[512,512]{1,0:T(8,128)(2,1)S(1)}, bf16[512,512]{1,0:T(8,128)(2,1)S(1)}, u32[]{:S(2)}, u32[]{:S(2)}) collective-permute-start(bf16[512,512]{1,0:T(8,128)(2,1)S(1)} %broadcast_select_fusion.2.refs_0_), channel_id=1, source_target_pairs={{0,1},{1,0},{2,3},{3,2},{4,5},{5,4},{6,7},{7,6},{8,9},{9,8},{10,11... | collective-permute-start | bytes 1572872 | tf_op jit(solution)/shard_map/ppermute | solution.py:340
  213.2 1.3 copy-start.7
  213.2 19.0 %collective-permute-start.13 = (bf16[512,512]{1,0:T(8,128)(2,1)S(1)}, bf16[512,512]{1,0:T(8,128)(2,1)S(1)}, u32[]{:S(2)}, u32[]{:S(2)}) collective-permute-start(bf16[512,512]{1,0:T(8,128)(2,1)S(1)} %collective-permute-done.11.refs_1_), channel_id=1, source_target_pairs={{0,1},{1,0},{2,3},{3,2},{4,5},{5,4},{6,7},{7,6},{8,9},{9,8},{10,11... | collective-permute-start | bytes 1572872 | tf_op jit(solution)/shard_map/ppermute | solution.py:340
  220.0 1.0 copy-start.4
  221.0 1.0 copy-start.5
  228.7 24.9 %copy-start.3 = (bf16[512,512]{1,0:T(8,128)(2,1)}, bf16[512,512]{1,0:T(8,128)(2,1)S(1)}, u32[]{:S(2)}) copy-start(bf16[512,512]{1,0:T(8,128)(2,1)S(1)} %broadcast_select_fusion.1.refs_0_) | copy-start | bytes 1572868
  228.7 24.9 %collective-permute-start.18 = (bf16[512,512]{1,0:T(8,128)(2,1)S(1)}, bf16[512,512]{1,0:T(8,128)(2,1)S(1)}, u32[]{:S(2)}, u32[]{:S(2)}) collective-permute-start(bf16[512,512]{1,0:T(8,128)(2,1)S(1)} %broadcast_select_fusion.1.refs_0_), channel_id=1, source_target_pairs={{0,16},{16,0},{1,17},{17,1},{2,18},{18,2},{3,19},{19,3},{4,20},{20... | collective-permute-start | bytes 1572872 | tf_op jit(solution)/shard_map/ppermute | solution.py:363
  231.1 26.2 %collective-permute-start.17 = (bf16[192,1024]{1,0:T(8,128)(2,1)}, bf16[192,1024]{1,0:T(8,128)(2,1)}, u32[]{:S(2)}, u32[]{:S(2)}) collective-permute-start(bf16[192,1024]{1,0:T(8,128)(2,1)} %project.5), channel_id=1, source_target_pairs={{0,2},{2,0},{1,3},{3,1},{4,6},{6,4},{5,7},{7,5},{8,10},{10,8},{9,1... | collective-permute-start | bytes 1179656 | tf_op jit(solution)/shard_map/ppermute | solution.py:361
  232.1 0.8 copy-start.9
  233.0 0.8 copy-start.10
  237.5 17.2 %copy-start.17 = (bf16[192,1024]{1,0:T(8,128)(2,1)S(1)}, bf16[192,1024]{1,0:T(8,128)(2,1)}, u32[]{:S(2)}) copy-start(bf16[192,1024]{1,0:T(8,128)(2,1)} %project.7) | copy-start | bytes 1179652
  253.6 19.2 %collective-permute-start.19 = (bf16[512,512]{1,0:T(8,128)(2,1)S(1)}, bf16[512,512]{1,0:T(8,128)(2,1)S(1)}, u32[]{:S(2)}, u32[]{:S(2)}) collective-permute-start(bf16[512,512]{1,0:T(8,128)(2,1)S(1)} %broadcast_select_fusion.1.refs_0_), channel_id=1, source_target_pairs={{0,1},{1,0},{2,3},{3,2},{4,5},{5,4},{6,7},{7,6},{8,9},{9,8},{10,11... | collective-permute-start | bytes 1572872 | tf_op jit(solution)/shard_map/ppermute | solution.py:340
  253.6 10.0 %copy-start.11 = (bf16[512,512]{1,0:T(8,128)(2,1)}, bf16[512,512]{1,0:T(8,128)(2,1)S(1)}, u32[]{:S(2)}) copy-start(bf16[512,512]{1,0:T(8,128)(2,1)S(1)} %collective-permute-done.18.refs_1_) | copy-start | bytes 1572868
  253.6 19.2 %collective-permute-start.20 = (bf16[512,512]{1,0:T(8,128)(2,1)S(1)}, bf16[512,512]{1,0:T(8,128)(2,1)S(1)}, u32[]{:S(2)}, u32[]{:S(2)}) collective-permute-start(bf16[512,512]{1,0:T(8,128)(2,1)S(1)} %collective-permute-done.18.refs_1_), channel_id=1, source_target_pairs={{0,1},{1,0},{2,3},{3,2},{4,5},{5,4},{6,7},{7,6},{8,9},{9,8},{10,11... | collective-permute-start | bytes 1572872 | tf_op jit(solution)/shard_map/ppermute | solution.py:340
  254.1 12.2 %collective-permute-start.16 = (bf16[192,1024]{1,0:T(8,128)(2,1)}, bf16[192,1024]{1,0:T(8,128)(2,1)S(1)}, u32[]{:S(2)}, u32[]{:S(2)}) collective-permute-start(bf16[192,1024]{1,0:T(8,128)(2,1)} %project.6), channel_id=1, source_target_pairs={{0,2},{2,0},{1,3},{3,1},{4,6},{6,4},{5,7},{7,5},{8,10},{10,8},{9,1... | collective-permute-start | bytes 1179656 | tf_op jit(solution)/shard_map/ppermute | solution.py:361
  254.6 25.9 %collective-permute-start.23 = (bf16[192,1024]{1,0:T(8,128)(2,1)S(1)}, bf16[192,1024]{1,0:T(8,128)(2,1)S(1)}, u32[]{:S(2)}, u32[]{:S(2)}) collective-permute-start(bf16[192,1024]{1,0:T(8,128)(2,1)S(1)} %copy-done.17), channel_id=1, source_target_pairs={{0,2},{2,0},{1,3},{3,1},{4,6},{6,4},{5,7},{7,5},{8,10},{10,8},{9,1... | collective-permute-start | bytes 1179656 | tf_op jit(solution)/shard_map/ppermute | solution.py:361
  257.4 29.7 %collective-permute-start.22 = (bf16[192,512]{1,0:T(8,128)(2,1)}, bf16[192,512]{1,0:T(8,128)(2,1)S(1)}, u32[]{:S(2)}, u32[]{:S(2)}) collective-permute-start(bf16[192,512]{1,0:T(8,128)(2,1)} %project.8), channel_id=1, source_target_pairs={{0,2},{2,0},{1,3},{3,1},{4,6},{6,4},{5,7},{7,5},{8,10},{10,8},{9,1... | collective-permute-start | bytes 589832 | tf_op jit(solution)/shard_map/ppermute | solution.py:361
  266.3 0.8 copy-start.15
  272.8 0.8 copy-start.12
  273.6 0.8 copy-start.13
  278.1 13.5 %collective-permute-start.21 = (bf16[192,512]{1,0:T(8,128)(2,1)}, bf16[192,512]{1,0:T(8,128)(2,1)S(1)}, u32[]{:S(2)}, u32[]{:S(2)}) collective-permute-start(bf16[192,512]{1,0:T(8,128)(2,1)} %project.9), channel_id=1, source_target_pairs={{0,2},{2,0},{1,3},{3,1},{4,6},{6,4},{5,7},{7,5},{8,10},{10,8},{9,1... | collective-permute-start | bytes 589832 | tf_op jit(solution)/shard_map/ppermute | solution.py:375
  280.5 0.8 copy-start.14
  287.0 0.7 copy-start.18
  (1 other events, 0.7 us)

commit v4 on v3

--- a/solution.py
+++ b/solution.py
@@ -9,29 +9,63 @@
 from jax.sharding import PartitionSpec as P
 
 HD = 128
-TILE = 32
+TILE = 64
 KEYS = 256
 LANES = 128
 HIDDEN = -1e30
 COLUMNS = 256
-VMEM = 56 * 1024 * 1024
-
-
-def bucket_ranks(slot_owner, owner_count):
-    one_hot = (slot_owner[..., None] == jnp.arange(owner_count)).astype(jnp.int32)
-    before = jnp.cumsum(one_hot, axis=-2) - one_hot
-    return jnp.sum(before * one_hot, axis=-1)
-
-
-def attend_kernel(
-    spec, control, position, hist_at, hist_steps, fresh_at, fresh_steps,
-    query, pages, fresh, key_conv, key_row, tok_conv, out, keys, values, scores, sums,
-):
-    kv_local, group_size, slots, page_len, rows, fresh_base, key_total = spec
+MIB = 1024 * 1024
+
+
+def cost(flops=3 * 10**9):
+    return pl.CostEstimate(flops=flops, bytes_accessed=1000, transcendentals=0)
+
+
+def rank_kernel(owner, page, position, wanted, count):
+    owners, bucket = wanted.shape
+    for n in range(owners):
+        count[n] = 0
+
+    def clear(k, carry):
+        for n in range(owners):
+            wanted[n, k] = 0
+        return carry
+
+    lax.fori_loop(0, bucket, clear, 0)
+
+    def put(slot, carry):
+        to = owner[0, slot]
+        rank = count[to]
+        count[to] = rank + 1
+        wanted[to, rank] = page[0, slot]
+        position[slot] = to * bucket + rank
+        return carry
+
+    lax.fori_loop(0, owner.shape[1], put, 0, unroll=4)
+
+
+def rank(page_owner, page_index, owners, bucket):
+    smem = pl.BlockSpec(memory_space=pltpu.SMEM)
+    return pl.pallas_call(
+        rank_kernel,
+        out_shape=(
+            jax.ShapeDtypeStruct((page_owner.shape[1],), jnp.int32),
+            jax.ShapeDtypeStruct((owners, bucket), jnp.int32),
+        ),
+        in_specs=[smem, smem],
+        out_specs=(smem, smem),
+        scratch_shapes=[pltpu.SMEM((owners,), jnp.int32)],
+        cost_estimate=cost(),
+        name="rank",
+    )(page_owner, page_index)
+
+
+def place_kernel(position, pages, fresh, keys, values):
+    kv_local, key_total = keys.shape[:2]
+    slots, page_len, rows = position.shape[0], pages.shape[2], fresh.shape[0]
     channels = kv_local * HD
     hist = slots * page_len
-    half, depth = out.shape[1], out.shape[2]
-    tiles = half // TILE
+    fresh_base = hist + KEYS
     for head in range(kv_local):
         values[head, :, HD:] = jnp.ones((key_total, HD), jnp.bfloat16)
         for first, last in ((hist, fresh_base), (fresh_base + rows, key_total)):
@@ -51,11 +85,40 @@
         return carry
 
     lax.fori_loop(0, slots, place, 0, unroll=8)
+
+
+def place(position, pages, fresh):
+    kv_local = pages.shape[3] // HD
+    rows = fresh.shape[0]
+    key_total = position.shape[0] * pages.shape[2] + KEYS + pl.cdiv(rows, KEYS) * KEYS + KEYS
+    vmem = pl.BlockSpec(memory_space=pltpu.VMEM)
+    return pl.pallas_call(
+        place_kernel,
+        out_shape=(
+            jax.ShapeDtypeStruct((kv_local, key_total, HD), jnp.bfloat16),
+            jax.ShapeDtypeStruct((kv_local, key_total, 2 * HD), jnp.bfloat16),
+        ),
+        in_specs=[pl.BlockSpec(memory_space=pltpu.SMEM), vmem, vmem],
+        out_specs=(vmem, vmem),
+        compiler_params=pltpu.CompilerParams(vmem_limit_bytes=20 * MIB),
+        cost_estimate=cost(),
+        name="place",
+    )(position, pages, fresh)
+
+
+def attend_kernel(
+    fresh_base, side, control, hist_at, hist_steps, fresh_at, fresh_steps,
+    query, keys, values, key_conv, key_row, tok_conv, out, scores, sums,
+):
+    kv_local = keys.shape[0]
+    group_size = query.shape[1] // (kv_local * HD)
+    half, depth = out.shape[1], out.shape[2]
+    tiles = half // TILE
     to_exp2 = math.log2(math.e) / math.sqrt(HD)
     wide = group_size * TILE
 
     def tile(number_here, carry):
-        index = control[0] * tiles + number_here
+        index = control[side] * tiles + number_here
         first = pl.multiple_of(index * TILE, TILE)
         leaving = pl.ds(pl.multiple_of(number_here * TILE, TILE), TILE)
         tokens = pl.ds(first, TILE)
@@ -116,7 +179,7 @@
             done = (sums[head, :, :HD] / sums[head, :, HD:]).astype(jnp.bfloat16)
             for g in range(group_size):
                 at = (head * group_size + g) * HD
-                out[control[1 + at // depth], leaving, at % depth : at % depth + HD] = done[
+                out[control[2 + at // depth], leaving, at % depth : at % depth + HD] = done[
                     g * TILE : (g + 1) * TILE
                 ]
         return carry
@@ -146,81 +209,81 @@
     return key_conv, key_row, tok_conv[:, None], hist_at, hist_steps, fresh_at, fresh_steps
 
 
-def attend(control, tables, position, queries, pages, new_kv):
+def attend(side, control, tables, queries, keys, values, slots):
     rows, width = queries.shape
-    page_len, channels = pages.shape[2], pages.shape[3]
-    slots = position.shape[0]
-    kv_local = channels // HD
-    group_size = width // channels
-    hist = slots * page_len
-    fresh_base = hist + KEYS
-    key_total = fresh_base + pl.cdiv(rows, KEYS) * KEYS + KEYS
+    kv_local, key_total = keys.shape[:2]
+    group_size = width // (kv_local * HD)
     key_conv, key_row, tok_conv, *steps = tables
-    depth = width // 4
-    most = (hist // KEYS + 1 + pl.cdiv(rows, KEYS) + 1) * KEYS
-    spec = (kv_local, group_size, slots, page_len, rows, fresh_base, key_total)
+    fresh_base = slots + KEYS
+    most = slots // KEYS + pl.cdiv(rows, KEYS) + 2
     smem = pl.BlockSpec(memory_space=pltpu.SMEM)
     vmem = pl.BlockSpec(memory_space=pltpu.VMEM)
     return pl.pallas_call(
-        functools.partial(attend_kernel, spec),
-        out_shape=jax.ShapeDtypeStruct((4, rows // 2, depth), jnp.bfloat16),
-        in_specs=[smem] * 6 + [vmem] * 6,
+        functools.partial(attend_kernel, fresh_base, side),
+        out_shape=jax.ShapeDtypeStruct((4, rows // 2, width // 4), jnp.bfloat16),
+        in_specs=[smem] * 5 + [vmem] * 6,
         out_specs=vmem,
         scratch_shapes=[
-            pltpu.VMEM((kv_local, key_total, HD), jnp.bfloat16),
-            pltpu.VMEM((kv_local, key_total, 2 * HD), jnp.bfloat16),
-            pltpu.VMEM((kv_local, group_size * TILE, most), jnp.float32),
+            pltpu.VMEM((kv_local, group_size * TILE, most * KEYS), jnp.float32),
             pltpu.VMEM((kv_local, group_size * TILE, 2 * HD), jnp.float32),
         ],
-        compiler_params=pltpu.CompilerParams(vmem_limit_bytes=VMEM),
-        cost_estimate=pl.CostEstimate(
-            flops=rows * width * 800 * 2, bytes_accessed=8 << 20, transcendentals=rows * width // HD * 400
-        ),
+        compiler_params=pltpu.CompilerParams(vmem_limit_bytes=28 * MIB),
+        cost_estimate=cost(16 * 10**9),
         name="attend",
-    )(
-        control, position, *steps, queries, pages, new_kv, key_conv, key_row, tok_conv,
-    )
-
-
-def multiply(left, pieces):
+    )(control, *steps, queries, keys, values, key_conv, key_row, tok_conv)
+
+
+def multiply(left, pieces, at):
     total = None
     for n, piece in enumerate(pieces):
-        term = jnp.dot(left[n], piece[...], preferred_element_type=jnp.float32)
+        term = jnp.dot(left[n], piece[:, at], preferred_element_type=jnp.float32)
         total = term if total is None else total + term
     return total.astype(jnp.bfloat16)
 
 
-def project_kernel(rows_at, left, *refs):
-    refs[-1][...] = multiply(left, refs[:-1])
-
-
-def finish_kernel(rows_at, left, came, *refs):
-    pieces = refs[:4]
-    total = multiply(left, pieces).astype(jnp.float32) + came[...].astype(jnp.float32)
-    refs[-1][0] = total.astype(jnp.bfloat16)
-
-
-def project(left, pieces, rows_at, came=None, base=None, out=None, width=None):
-    depth = left.shape[2]
+def blocks(columns):
+    cut = min(COLUMNS, columns)
+    return [slice(k, k + cut) for k in range(0, columns, cut)]
+
+
+def quarters(control, refs):
+    if len(refs) == 4:
+        return refs
+    depth = refs[0].shape[0] // 4
+    return [refs[0].at[pl.ds(pl.multiple_of(control[6 + n] * depth, depth), depth)] for n in range(4)]
+
+
+def project_kernel(control, left, *refs):
+    pieces = quarters(control, refs[:-1])
+    for at in blocks(pieces[0].shape[1]):
+        refs[-1][:, at] = multiply(left, pieces, at)
+
+
+def finish_kernel(has_out, control, left, came, *refs):
+    pieces = quarters(control, refs[: len(refs) - 1 - has_out])
+    for at in blocks(pieces[0].shape[1]):
+        total = multiply(left, pieces, at).astype(jnp.float32) + came[:, at].astype(jnp.float32)
+        refs[-1][0, :, at] = total.astype(jnp.bfloat16)
+
+
+def project(control, left, pieces, came=None, base=None, out=None, width=None):
     half = left.shape[1]
     columns = pieces[0].shape[1]
-    cut = min(COLUMNS, columns)
-    table = rows_at if base is None else jnp.concatenate([rows_at, (base * (columns // cut))[None]])
-    in_specs = [pl.BlockSpec(left.shape, lambda j, at: (0, 0, 0))]
+    vmem = pl.BlockSpec(memory_space=pltpu.VMEM)
+    in_specs = [vmem]
     operands = [left]
     aliases = {}
     if came is None:
         kernel = project_kernel
         out_shape = jax.ShapeDtypeStruct((half, columns), jnp.bfloat16)
-        out_specs = pl.BlockSpec((half, cut), lambda j, at: (0, j))
+        out_specs = vmem
     else:
-        kernel = finish_kernel
-        in_specs.append(pl.BlockSpec((half, cut), lambda j, at: (0, j)))
+        kernel = functools.partial(finish_kernel, int(out is not None))
+        in_specs.append(vmem)
         operands.append(came)
         out_shape = jax.ShapeDtypeStruct((1, half, width), jnp.bfloat16)
-        out_specs = pl.BlockSpec((1, half, cut), lambda j, at: (0, 0, at[4] + j))
-    for n in range(4):
-        in_specs.append(pl.BlockSpec((depth, cut), functools.partial(lambda n, j, at: (at[n], j), n)))
+        out_specs = pl.BlockSpec((1, half, columns), lambda j, control: (0, 0, control[base]))
+    in_specs += [vmem] * len(pieces)
     operands += pieces
     if out is not None:
         in_specs.append(pl.BlockSpec(memory_space=pl.ANY))
@@ -230,23 +293,23 @@
         kernel,
         out_shape=out_shape,
         grid_spec=pltpu.PrefetchScalarGridSpec(
-            num_scalar_prefetch=1, grid=(columns // cut,), in_specs=in_specs, out_specs=out_specs
+            num_scalar_prefetch=1, grid=(1,), in_specs=in_specs, out_specs=out_specs
         ),
         input_output_aliases=aliases,
-        compiler_params=pltpu.CompilerParams(vmem_limit_bytes=VMEM),
-        cost_estimate=pl.CostEstimate(
-            flops=8 * half * depth * columns, bytes_accessed=8 * depth * (columns + half), transcendentals=0
-        ),
+        compiler_params=pltpu.CompilerParams(vmem_limit_bytes=16 * MIB),
+        cost_estimate=cost(),
         name="project" if came is None else "finish",
-    )(table.astype(jnp.int32), *operands)
+    )(control, *operands)
 
 
 def pick_kernel(asked, pool, out):
-    def copy(n, carry):
-        out[n] = pool[asked[n]]
-        return carry
-
-    lax.fori_loop(0, out.shape[0], copy, 0, unroll=8)
+    for owner in range(asked.shape[0]):
+
+        def copy(n, carry):
+            out[owner, n] = pool[asked[owner, n]]
+            return carry
+
+        lax.fori_loop(0, asked.shape[1], copy, 0, unroll=8)
 
 
 def pick(pool, asked):
@@ -256,7 +319,8 @@
         out_shape=jax.ShapeDtypeStruct(asked.shape + pool.shape[1:], jnp.bfloat16),
         in_specs=[pl.BlockSpec(memory_space=pltpu.SMEM), vmem],
         out_specs=vmem,
-        compiler_params=pltpu.CompilerParams(vmem_limit_bytes=VMEM),
+        compiler_params=pltpu.CompilerParams(vmem_limit_bytes=16 * MIB),
+        cost_estimate=cost(),
         name="pick",
     )(asked, pool)
 
@@ -287,11 +351,15 @@
     order = [q ^ own for q in range(4)]
     order = [(v % 2) * 2 + v // 2 for v in order]
     flip = tp if tp_count == 2 else 0
-
-    def control(side):
-        return jnp.stack([jnp.asarray(v, jnp.int32) for v in (side, *order)])
-
-    whole = jnp.zeros((4,), jnp.int32)
+    second = jnp.where(seq < 2, 2, 1)
+    third = 2 * jnp.where(seq < 2, 3, 0)
+    local = [own, own ^ 2, own ^ 1, own ^ 3]
+    control = jnp.stack(
+        [
+            jnp.asarray(v, jnp.int32)
+            for v in (flip, 1 - flip, *order, *local, seq, seq ^ 1, second, third, third + 1)
+        ]
+    )
     swap_group = functools.partial(lax.ppermute, axis_name="group", perm=SWAP)
     swap_role = functools.partial(lax.ppermute, axis_name="role", perm=SWAP)
 
@@ -300,20 +368,15 @@
         near = lax.ppermute(quarter, "seq", [(0, 1), (1, 0), (2, 3), (3, 2)])
         inner = lax.ppermute(quarter, "seq", [(1, 2), (2, 1)])
 
-    slot_owner = page_owner[0]
-    position = slot_owner * bucket + bucket_ranks(slot_owner, owner_count)
-    wanted = (
-        jnp.zeros((owner_count * bucket,), jnp.int32)
-        .at[position]
-        .set(page_index[0], mode="promise_in_bounds", unique_indices=True)
-        .reshape(owner_count, bucket)
-    )
+    position, wanted = rank(page_owner, page_index, owner_count, bucket)
     asked = lax.all_to_all(wanted, "seq", split_axis=0, concat_axis=0, tiled=True)
-    found = pick(pool[0], asked.reshape(-1))
-    pages = lax.all_to_all(
-        found.reshape((owner_count, bucket) + found.shape[1:]),
-        "seq", split_axis=0, concat_axis=0, tiled=True,
-    ).reshape(found.shape)
+    if owner_count == 4:
+        near, inner = after(near, asked), after(inner, asked)
+        asked = after(asked, near, inner)
+    found = pick(pool[0], asked)
+    pages = lax.all_to_all(found, "seq", split_axis=0, concat_axis=0, tiled=True)
+    pages = pages.reshape((owner_count * bucket,) + found.shape[2:])
+    slots = slot_count * pool.shape[3]
     fresh = new_kv[0].reshape(row_count, -1)
     tables = attend_tables(
         row_count, slot_count, pool.shape[3], tok_conv[0], page_conv[0], page_fill[0]
@@ -323,8 +386,9 @@
         mine = lax.all_gather(quarter, "seq", axis=1, tiled=True)
         across = swap_group(mine)
         pieces = [mine, across, swap_role(mine), swap_role(across)]
+        keys, values = place(position, pages, fresh)
         partial = [
-            project(attend(control(side), tables, position, queries[0], pages, fresh), pieces, whole)
+            project(control, attend(side, control, tables, queries[0], keys, values, slots), pieces)
             for side in (0, 1)
         ]
         return lax.psum_scatter(
@@ -339,7 +403,6 @@
     def four(one, two, *hold):
         return [one, two, swap_role(after(one, *hold)), swap_role(after(two, *hold))]
 
-    near, inner = after(near, found), after(inner, found)
     near_across = swap_group(near)
     far_a = cross(near[:, :cut])
     next_shard = jnp.where(middle, inner, forward(inner))
@@ -348,34 +411,29 @@
     far_a_across = swap_group(far_a)
     near_all = four(near, near_across)
     next_all = four(next_shard, next_across)
+    far_a_all = four(far_a, far_a_across)
 
     far_b = cross(after(near[:, cut:], pages))
-    pages = after(pages, near_across, next_shard, far_a)
-    left = attend(control(1 - flip), tables, position, queries[0], pages, fresh)
+    keys, values = place(position, after(pages, near_across, next_shard, far_a), fresh)
+    left = attend(1, control, tables, queries[0], keys, values, slots)
     far_b_on = forward(after(far_b, left))
-    local = jnp.stack([own, own ^ 2, own ^ 1, own ^ 3]).astype(jnp.int32)
-    sent = [project(left, [out_weight] * 4, local)]
-    far_a_all = four(far_a, far_a_across)
+    sent = [project(control, left, [out_weight])]
     for pieces in (near_all, next_all, far_a_all):
-        sent.append(project(after(left, sent[-1]), pieces, whole))
+        sent.append(project(control, after(left, sent[-1]), pieces))
     came = [swap_tp(part) for part in sent]
     far_b = jnp.where(middle, far_b, after(far_b_on, sent[2]))
     far_b_across = swap_group(far_b)
-    stay = attend(
-        control(flip), tables, position, queries[0], after(pages, sent[3], far_b), fresh
-    )
+    stay = attend(0, control, tables, after(queries[0], sent[3], far_b), keys, values, slots)
     far_b_all = four(far_b, far_b_across, stay)
     total = columns * owner_count
-    second = jnp.where(seq < 2, 2, 1)
-    third = jnp.where(seq < 2, 3, 0)
-    out = project(stay, [out_weight] * 4, local, came[0], seq, None, total)
-    out = project(stay, near_all, whole, came[1], seq ^ 1, out, total)
-    last = project(after(left, out), far_b_all, whole)
+    out = project(control, stay, [out_weight], came[0], 10, None, total)
+    out = project(control, stay, near_all, came[1], 11, out, total)
+    last = project(control, after(left, out), far_b_all)
     stay = after(stay, last)
     last = swap_tp(last)
-    out = project(stay, next_all, whole, came[2], second, out, total)
-    out = project(stay, far_a_all, whole, came[3], 2 * third, out, total)
-    return project(stay, far_b_all, whole, last, 2 * third + 1, out, total)
+    out = project(control, stay, next_all, came[2], 12, out, total)
+    out = project(control, stay, far_a_all, came[3], 13, out, total)
+    return project(control, stay, far_b_all, last, 14, out, total)
 
 
 def solution(mesh):

time: 301 us -> 252 us (0.84)
  Pallas kernels: 85.3 us -> 51.7 us
  blocking collectives: 8.19 us -> 22.1 us
  local copies, waits for them, and re-layouts: 19.8 us -> 7.77 us
  other arithmetic: 10.1 us -> 3.05 us
  waiting for transfers between devices: 132 us -> 127 us
  starting transfers between devices: 39.7 us -> 36.3 us
    ppermute x1, waiting for transfers between devices: 108 us -> 0.01 us  [shards(): inner = lax.ppermute(quarter, 'seq', [(1, 2), (2, 1)])]
    ppermute x1, waiting for transfers between devices: 0.01 us -> 91 us  [shards(): far_a = cross(near[:, :cut])]
    pallas_call x10, Pallas kernels: 49.1 us -> 24.7 us  [project(): pl.pallas_call(kernel, out_shape=out_shape, grid_spec=pltpu.PrefetchScala...]
    ppermute x1, waiting for transfers between devices: 0.01 us -> 22.8 us  [shards(): far_a_across = swap_group(far_a)]
    all_to_all x1, blocking collectives: 8.19 us -> 22.1 us  [shards(): lax.all_to_all(wanted, 'seq', split_axis=0, concat_axis=0, tiled=True)]
    ppermute x1, waiting for transfers between devices: 13.7 us -> 0.01 us  [shards(): next_shard = jnp.where(middle, inner, forward(inner))]
    ppermute x1, waiting for transfers between devices: 7.84 us -> 0.01 us  [shards(): next_across = swap_group(next_shard)]
    ppermute x1, waiting for transfers between devices: 0.01 us -> 6.42 us  [shards(): far_a = jnp.where(middle, far_a, forward(far_a))]
  transfers between devices with their start and end apart: 25 -> 25, of which waited for: 4 -> 5; matrix products, arithmetic and copies ran while one was open for 6% -> 2% of each run, Pallas kernels for 26% -> 20%
where the time goes in v4:
time: 252 us; the launch traced here: 248 us
  waiting for transfers between devices  127 us (50%)
  Pallas kernels  51.7 us (21%)
  starting transfers between devices  36.3 us (14%)
  blocking collectives  22.1 us (9%)
  local copies, waits for them, and re-layouts  7.77 us (3%)
  other arithmetic  3.05 us (1%)
    ppermute x1, waiting for transfers between devices, shards(): far_a = cross(near[:, :cut])  91 us
    pallas_call x10, Pallas kernels, project(): pl.pallas_call(kernel, out_shape=out_shape, grid_spec=pltpu.PrefetchScala...  24.7 us
    ppermute x1, waiting for transfers between devices, shards(): far_a_across = swap_group(far_a)  22.8 us
    all_to_all x1, blocking collectives, shards(): lax.all_to_all(wanted, 'seq', split_axis=0, concat_axis=0, tiled=True)  22.1 us
    pallas_call x2, Pallas kernels, attend(): pl.pallas_call(functools.partial(attend_kernel, fresh_base, side), out_sh...  19.8 us
    ppermute x1, waiting for transfers between devices, shards(): far_a = jnp.where(middle, far_a, forward(far_a))  6.42 us
    all_to_all x1, starting transfers between devices, shards(): lax.all_to_all(found, 'seq', split_axis=0, concat_axis=0, tiled=True)  5.88 us
    unnamed x25, local copies, waits for them, and re-layouts  5.1 us
  transfers between devices with their start and end apart: 25, of which 5 were waited for; matrix products, arithmetic and copies ran while one was open for 2% of the time, Pallas kernels for 20%

profile of v4, /device:TPU:16, one launch (start us, length us, event | category | flops | bytes accessed | tf_op | source)
XLA Modules:
  0.0 248.1 jit_solution(4919093539585413420)
XLA Ops:
  0.0 1.3 constant_dynamic-slice_fusion
  1.3 1.6 collective-permute-start
  2.9 1.9 collective-permute-start.1
  4.9 2.6 %rank.1 = (s32[128]{0:T(128)}, s32[4,64]{1,0:T(4,128)}) custom-call(s32[1,128]{1,0:T(1,128)} %owner.1, s32[1,128]{1,0:T(1,128)} %page.1), custom_call_target="tpu_custom_call" | custom-call | flops 3000000000 | bytes 1000 | tf_op jit(solution)/shard_map/rank/pallas_call | solution.py:49
  7.5 22.1 %all_to_all.17 = s32[4,1,64]{2,1,0:T(1,128)S(1)} all-to-all(s32[4,1,64]{2,1,0:T(1,128)} %bitcast.40), channel_id=1, replica_groups=mesh['group'=2,'seq'=4,'tp'=2,'role'=2] {'seq'}, dimensions={0} | all-to-all | bytes 2048 | tf_op jit(solution)/shard_map/all_to_all | solution.py:372
  29.6 2.2 copy-done.2
  31.8 1.3 pick.1
  33.1 2.0 copy-done
  35.1 5.9 %all-to-all-start.1 = ((bf16[4,64,2,16,256]{4,3,2,1,0:T(8,128)(2,1)}), bf16[4,64,2,16,256]{4,3,2,1,0:T(8,128)(2,1)}, u32[]{:S(2)}, u32[]{:S(2)}) async-start(bf16[4,64,2,16,256]{4,3,2,1,0:T(8,128)(2,1)} %copy-done), calls=%async_computation.1 | async-start | bytes 8388608 | tf_op jit(solution)/shard_map/all_to_all | solution.py:377
  41.0 4.5 %collective-permute-start.3 = (bf16[512,1024]{1,0:T(8,128)(2,1)}, bf16[512,1024]{1,0:T(8,128)(2,1)}, u32[]{:S(2)}, u32[]{:S(2)}) collective-permute-start(bf16[512,1024]{1,0:T(8,128)(2,1)} %collective-permute-done.1), channel_id=1, source_target_pairs={{4,0},{8,12},{5,1},{9,13},{6,2},{10,14},{7,3},{11,15},{20,16},{24,... | collective-permute-start | bytes 3145736 | tf_op jit(solution)/shard_map/ppermute | solution.py:408
  45.5 0.9 fusion.5
  46.3 1.9 collective-permute-start.4
  49.4 1.6 collective-permute-start.2
  51.0 91.0 %collective-permute-done.4 = bf16[512,512]{1,0:T(8,128)(2,1)S(1)} collective-permute-done((bf16[512,512]{1,0:T(8,128)(2,1)S(1)}, bf16[512,512]{1,0:T(8,128)(2,1)S(1)}, u32[]{:S(2)}, u32[]{:S(2)}) %collective-permute-start.4) | collective-permute-done | bytes 524320 | tf_op jit(solution)/shard_map/ppermute | solution.py:407
  142.1 1.3 collective-permute-start.5
  143.4 1.3 broadcast_select_fusion.refs_0_
  144.8 1.6 collective-permute-start.8
  146.6 6.4 %collective-permute-done.5 = bf16[512,512]{1,0:T(8,128)(2,1)S(1)} collective-permute-done((bf16[512,512]{1,0:T(8,128)(2,1)S(1)}, bf16[512,512]{1,0:T(8,128)(2,1)S(1)}, u32[]{:S(2)}, u32[]{:S(2)}) %collective-permute-start.5) | collective-permute-done | bytes 524320 | tf_op jit(solution)/shard_map/ppermute | solution.py:410
  153.0 1.1 broadcast_select_fusion.2.refs_0_
  154.1 1.6 collective-permute-start.11
  155.8 0.5 collective-permute-start.7
  156.4 22.8 %collective-permute-done.11.refs_1_ = bf16[512,512]{1,0:T(8,128)(2,1)S(1)} collective-permute-done((bf16[512,512]{1,0:T(8,128)(2,1)S(1)}, bf16[512,512]{1,0:T(8,128)(2,1)S(1)}, u32[]{:S(2)}, u32[]{:S(2)}) %collective-permute-start.11) | collective-permute-done | bytes 524320 | tf_op jit(solution)/shard_map/ppermute | solution.py:411
  179.2 0.8 copy-done.4
  180.0 4.4 %collective-permute-start.14 = (bf16[512,512]{1,0:T(8,128)(2,1)}, bf16[512,512]{1,0:T(8,128)(2,1)S(1)}, u32[]{:S(2)}, u32[]{:S(2)}) collective-permute-start(bf16[512,512]{1,0:T(8,128)(2,1)} %get-tuple-element.35), channel_id=1, source_target_pairs={{4,8},{8,4},{5,9},{9,5},{6,10},{10,6},{7,11},{11,7},{20,24},{24,20... | collective-permute-start | bytes 1572872 | tf_op jit(solution)/shard_map/ppermute | solution.py:416
  184.4 3.3 %place.1 = (bf16[2,3072,128]{2,1,0:T(8,128)(2,1)S(1)}, bf16[2,3072,256]{2,1,0:T(8,128)(2,1)S(1)}) custom-call(s32[128]{0:T(128)S(1)} %copy-done.6, bf16[256,2,16,256]{3,2,1,0:T(8,128)(2,1)} %bitcast.21.pages, bf16[384,512]{1,0:T(8,128)(2,1)S(1)} %bitcast.29), custom_call_target="tpu_custom_call" | custom-call | flops 3000000000 | bytes 1000 | tf_op jit(solution)/shard_map/place/pallas_call | solution.py:95
  187.7 10.2 %attend.2.left = bf16[4,192,512]{2,1,0:T(8,128)(2,1)S(1)} custom-call(s32[15]{0:T(128)S(1)} %stack.63.control, s32[6]{0:T(128)S(1)} %get-tuple-element.52.hist_at, s32[6]{0:T(128)S(1)} %get-tuple-element.51.hist_steps, s32[6]{0:T(128)S(1)} %get-tuple-element.46.fresh_at, s32[6]{0:T(128)S(1)} %get-tuple-element.45.fresh_steps, ...), custom_call_target="tpu_custom_call" | custom-call | flops 16000000000 | bytes 1000 | tf_op jit(solution)/shard_map/attend/pallas_call | solution.py:221
  197.9 1.5 project.5
  199.6 0.5 collective-permute-start.13
  200.1 3.4 %project.6 = bf16[192,1024]{1,0:T(8,128)(2,1)S(1)} custom-call(s32[15]{0:T(128)S(1)} %stack.63.control, bf16[4,192,512]{2,1,0:T(8,128)(2,1)S(1)} %attend.2.left, bf16[512,1024]{1,0:T(8,128)(2,1)S(1)} %collective-permute-done.refs_0_, bf16[512,1024]{1,0:T(8,128)(2,1)} %collective-permute-done.2.refs_1_, bf16[512,1024]{1,0:T(8,128)(2,1)} %collective-permute-done.6.refs_2_, ...), custom_call_target="tpu_custom_call" | custom-call | flops 3000000000 | bytes 1000 | tf_op jit(solution)/shard_map/project/pallas_call | solution.py:292
  203.5 0.9 collective-permute-start.17
  204.4 1.2 collective-permute-start.16
  205.6 1.3 collective-permute-start.15
  206.9 3.4 %project.7 = bf16[192,1024]{1,0:T(8,128)(2,1)S(1)} custom-call(s32[15]{0:T(128)S(1)} %stack.63.control, bf16[4,192,512]{2,1,0:T(8,128)(2,1)S(1)} %attend.2.left, bf16[512,1024]{1,0:T(8,128)(2,1)S(1)} %broadcast_select_fusion.refs_0_, bf16[512,1024]{1,0:T(8,128)(2,1)} %collective-permute-done.8.refs_1_, bf16[512,1024]{1,0:T(8,128)(2,1)} %collective-permute-done.9.refs_2_, ...), custom_call_target="tpu_custom_call" | custom-call | flops 3000000000 | bytes 1000 | tf_op jit(solution)/shard_map/project/pallas_call | solution.py:292
  210.3 0.9 collective-permute-start.23
  211.2 1.1 project.8
  212.3 1.3 collective-permute-start.22
  213.6 4.4 %collective-permute-done.15 = bf16[512,512]{1,0:T(8,128)(2,1)S(1)} collective-permute-done((bf16[512,512]{1,0:T(8,128)(2,1)S(1)}, bf16[512,512]{1,0:T(8,128)(2,1)S(1)}, u32[]{:S(2)}, u32[]{:S(2)}) %collective-permute-start.15) | collective-permute-done | bytes 524320 | tf_op jit(solution)/shard_map/ppermute | solution.py:419
  218.1 1.4 collective-permute-start.18
  219.5 9.5 %attend.3.left = bf16[4,192,512]{2,1,0:T(8,128)(2,1)S(1)} custom-call(s32[15]{0:T(128)S(1)} %stack.63.control, s32[6]{0:T(128)S(1)} %get-tuple-element.52.hist_at, s32[6]{0:T(128)S(1)} %get-tuple-element.51.hist_steps, s32[6]{0:T(128)S(1)} %get-tuple-element.46.fresh_at, s32[6]{0:T(128)S(1)} %get-tuple-element.45.fresh_steps, ...), custom_call_target="tpu_custom_call" | custom-call | flops 16000000000 | bytes 1000 | tf_op jit(solution)/shard_map/attend/pallas_call | solution.py:221
  229.0 1.9 collective-permute-done.18.refs_1_
  230.9 0.5 collective-permute-start.20
  231.4 2.3 finish.5.refs_4_
  233.7 4.1 %finish.6.refs_4_ = bf16[1,192,4096]{2,1,0:T(8,128)(2,1)} custom-call(s32[15]{0:T(128)S(1)} %stack.63.control, bf16[4,192,512]{2,1,0:T(8,128)(2,1)S(1)} %attend.3.left, bf16[192,1024]{1,0:T(8,128)(2,1)S(1)} %collective-permute-done.16.came, bf16[512,1024]{1,0:T(8,128)(2,1)S(1)} %collective-permute-done.refs_0_, ...), custom_call_target="tpu_custom_call", output_to_operand_aliasing={{}: (7, {})} | custom-call | flops 3000000000 | bytes 1000 | tf_op jit(solution)/shard_map/finish/pallas_call | solution.py:292
  237.9 1.1 project.9
  239.0 1.3 collective-permute-start.21
  240.3 4.2 %finish.7.refs_4_ = bf16[1,192,4096]{2,1,0:T(8,128)(2,1)} custom-call(s32[15]{0:T(128)S(1)} %stack.63.control, bf16[4,192,512]{2,1,0:T(8,128)(2,1)S(1)} %attend.3.left, bf16[192,1024]{1,0:T(8,128)(2,1)S(1)} %collective-permute-done.23.came, bf16[512,1024]{1,0:T(8,128)(2,1)S(1)} %broadcast_select_fusion.refs_0_, ...), custom_call_target="tpu_custom_call", output_to_operand_aliasing={{}: (7, {})} | custom-call | flops 3000000000 | bytes 1000 | tf_op jit(solution)/shard_map/finish/pallas_call | solution.py:292
  244.5 1.8 finish.8.refs_4_
  246.3 1.8 finish.9
  (62 shorter events, 1.5 us)
Async XLA Ops:
  1.3 28.3 %collective-permute-start = (bf16[512,1024]{1,0:T(8,128)(2,1)S(1)}, bf16[512,1024]{1,0:T(8,128)(2,1)S(1)}, u32[]{:S(2)}, u32[]{:S(2)}) collective-permute-start(bf16[512,1024]{1,0:T(8,128)(2,1)S(1)} %constant_dynamic-slice_fusion), channel_id=1, source_target_pairs={{0,4},{4,0},{8,12},{12,8},{1,5},{5,1},{9,13},{13,9},{2,6},{6,2},{1... | collective-permute-start | bytes 3145736 | tf_op jit(solution)/shard_map/ppermute | solution.py:368
  2.9 26.6 %collective-permute-start.1 = (bf16[512,1024]{1,0:T(8,128)(2,1)S(1)}, bf16[512,1024]{1,0:T(8,128)(2,1)}, u32[]{:S(2)}, u32[]{:S(2)}) collective-permute-start(bf16[512,1024]{1,0:T(8,128)(2,1)S(1)} %constant_dynamic-slice_fusion), channel_id=1, source_target_pairs={{4,8},{8,4},{5,9},{9,5},{6,10},{10,6},{7,11},{11,7},{20,24},{24,20... | collective-permute-start | bytes 3145736 | tf_op jit(solution)/shard_map/ppermute | solution.py:369
  29.6 2.2 copy-start.2
  33.0 2.0 copy-start
  35.1 144.9 %all-to-all-start.1 = ((bf16[4,64,2,16,256]{4,3,2,1,0:T(8,128)(2,1)}), bf16[4,64,2,16,256]{4,3,2,1,0:T(8,128)(2,1)}, u32[]{:S(2)}, u32[]{:S(2)}) async-start(bf16[4,64,2,16,256]{4,3,2,1,0:T(8,128)(2,1)} %copy-done), calls=%async_computation.1 | async-start | bytes 8388608 | tf_op jit(solution)/shard_map/all_to_all | solution.py:377
  40.9 7.4 %copy-start.9 = (s32[1,384]{1,0:T(1,128)S(1)}, s32[1,384]{1,0:T(1,128)}, u32[]{:S(2)}) copy-start(s32[1,384]{1,0:T(1,128)} %param.13) | copy-start | bytes 4612
  40.9 7.6 %copy-start.8 = (bf16[1,384,2,256]{3,2,1,0:T(2,128)(2,1)S(1)}, bf16[1,384,2,256]{3,2,1,0:T(2,128)(2,1)}, u32[]{:S(2)}) copy-start(bf16[1,384,2,256]{3,2,1,0:T(2,128)(2,1)} %param.10) | copy-start | bytes 1179652
  40.9 7.8 %copy-start.10 = (s32[1,128]{1,0:T(1,128)S(1)}, s32[1,128]{1,0:T(1,128)}, u32[]{:S(2)}) copy-start(s32[1,128]{1,0:T(1,128)} %param.14) | copy-start | bytes 1540
  41.0 7.8 %copy-start.11 = (s32[1,128]{1,0:T(1,128)S(1)}, s32[1,128]{1,0:T(1,128)}, u32[]{:S(2)}) copy-start(s32[1,128]{1,0:T(1,128)} %param.15) | copy-start | bytes 1540
  41.0 102.4 %collective-permute-start.3 = (bf16[512,1024]{1,0:T(8,128)(2,1)}, bf16[512,1024]{1,0:T(8,128)(2,1)}, u32[]{:S(2)}, u32[]{:S(2)}) collective-permute-start(bf16[512,1024]{1,0:T(8,128)(2,1)} %collective-permute-done.1), channel_id=1, source_target_pairs={{4,0},{8,12},{5,1},{9,13},{6,2},{10,14},{7,3},{11,15},{20,16},{24,... | collective-permute-start | bytes 3145736 | tf_op jit(solution)/shard_map/ppermute | solution.py:408
  46.3 95.7 %collective-permute-start.4 = (bf16[512,512]{1,0:T(8,128)(2,1)S(1)}, bf16[512,512]{1,0:T(8,128)(2,1)S(1)}, u32[]{:S(2)}, u32[]{:S(2)}) collective-permute-start(bf16[512,512]{1,0:T(8,128)(2,1)S(1)} %get-tuple-element.50), channel_id=1, source_target_pairs={{4,8},{8,4},{5,9},{9,5},{6,10},{10,6},{7,11},{11,7},{20,24},{24,20... | collective-permute-start | bytes 1572872 | tf_op jit(solution)/shard_map/ppermute | solution.py:407
  49.4 106.4 %collective-permute-start.2 = (bf16[512,1024]{1,0:T(8,128)(2,1)S(1)}, bf16[512,1024]{1,0:T(8,128)(2,1)}, u32[]{:S(2)}, u32[]{:S(2)}) collective-permute-start(bf16[512,1024]{1,0:T(8,128)(2,1)S(1)} %collective-permute-done.refs_0_), channel_id=1, source_target_pairs={{0,16},{16,0},{1,17},{17,1},{2,18},{18,2},{3,19},{19,3},{4,20},{20... | collective-permute-start | bytes 3145736 | tf_op jit(solution)/shard_map/ppermute | solution.py:406
  142.1 2.7 %copy-start.7 = (bf16[512,512]{1,0:T(8,128)(2,1)}, bf16[512,512]{1,0:T(8,128)(2,1)S(1)}, u32[]{:S(2)}) copy-start(bf16[512,512]{1,0:T(8,128)(2,1)S(1)} %collective-permute-done.4) | copy-start | bytes 1572868
  142.1 10.9 %collective-permute-start.5 = (bf16[512,512]{1,0:T(8,128)(2,1)S(1)}, bf16[512,512]{1,0:T(8,128)(2,1)S(1)}, u32[]{:S(2)}, u32[]{:S(2)}) collective-permute-start(bf16[512,512]{1,0:T(8,128)(2,1)S(1)} %collective-permute-done.4), channel_id=1, source_target_pairs={{4,0},{8,12},{5,1},{9,13},{6,2},{10,14},{7,3},{11,15},{20,16},{24,... | collective-permute-start | bytes 1572872 | tf_op jit(solution)/shard_map/ppermute | solution.py:410
  144.8 39.6 %copy-start.6 = (s32[128]{0:T(128)S(1)}, s32[128]{0:T(128)}, u32[]{:S(2)}) copy-start(s32[128]{0:T(128)} %get-tuple-element.24.position) | copy-start | bytes 1540
  144.8 34.4 %collective-permute-start.8 = (bf16[512,1024]{1,0:T(8,128)(2,1)S(1)}, bf16[512,1024]{1,0:T(8,128)(2,1)}, u32[]{:S(2)}, u32[]{:S(2)}) collective-permute-start(bf16[512,1024]{1,0:T(8,128)(2,1)S(1)} %broadcast_select_fusion.refs_0_), channel_id=1, source_target_pairs={{0,16},{16,0},{1,17},{17,1},{2,18},{18,2},{3,19},{19,3},{4,20},{20... | collective-permute-start | bytes 3145736 | tf_op jit(solution)/shard_map/ppermute | solution.py:409
  154.1 25.1 %collective-permute-start.11 = (bf16[512,512]{1,0:T(8,128)(2,1)S(1)}, bf16[512,512]{1,0:T(8,128)(2,1)S(1)}, u32[]{:S(2)}, u32[]{:S(2)}) collective-permute-start(bf16[512,512]{1,0:T(8,128)(2,1)S(1)} %broadcast_select_fusion.2.refs_0_), channel_id=1, source_target_pairs={{0,16},{16,0},{1,17},{17,1},{2,18},{18,2},{3,19},{19,3},{4,20},{20... | collective-permute-start | bytes 1572872 | tf_op jit(solution)/shard_map/ppermute | solution.py:411
  155.7 43.8 %collective-permute-start.6 = (bf16[512,1024]{1,0:T(8,128)(2,1)S(1)}, bf16[512,1024]{1,0:T(8,128)(2,1)}, u32[]{:S(2)}, u32[]{:S(2)}) collective-permute-start(bf16[512,1024]{1,0:T(8,128)(2,1)S(1)} %collective-permute-done.refs_0_), channel_id=1, source_target_pairs={{0,1},{1,0},{2,3},{3,2},{4,5},{5,4},{6,7},{7,6},{8,9},{9,8},{10,11... | collective-permute-start | bytes 3145736 | tf_op jit(solution)/shard_map/ppermute | solution.py:404
  155.8 43.8 %collective-permute-start.7 = (bf16[512,1024]{1,0:T(8,128)(2,1)}, bf16[512,1024]{1,0:T(8,128)(2,1)}, u32[]{:S(2)}, u32[]{:S(2)}) collective-permute-start(bf16[512,1024]{1,0:T(8,128)(2,1)} %collective-permute-done.2.refs_1_), channel_id=1, source_target_pairs={{0,1},{1,0},{2,3},{3,2},{4,5},{5,4},{6,7},{7,6},{8,9},{9,8},{10,11... | collective-permute-start | bytes 3145736 | tf_op jit(solution)/shard_map/ppermute | solution.py:404
  156.3 48.0 %collective-permute-start.9 = (bf16[512,1024]{1,0:T(8,128)(2,1)S(1)}, bf16[512,1024]{1,0:T(8,128)(2,1)}, u32[]{:S(2)}, u32[]{:S(2)}) collective-permute-start(bf16[512,1024]{1,0:T(8,128)(2,1)S(1)} %broadcast_select_fusion.refs_0_), channel_id=1, source_target_pairs={{0,1},{1,0},{2,3},{3,2},{4,5},{5,4},{6,7},{7,6},{8,9},{9,8},{10,11... | collective-permute-start | bytes 3145736 | tf_op jit(solution)/shard_map/ppermute | solution.py:404
  179.2 0.8 copy-start.4
  180.0 25.6 %collective-permute-start.10 = (bf16[512,1024]{1,0:T(8,128)(2,1)}, bf16[512,1024]{1,0:T(8,128)(2,1)}, u32[]{:S(2)}, u32[]{:S(2)}) collective-permute-start(bf16[512,1024]{1,0:T(8,128)(2,1)} %collective-permute-done.8.refs_1_), channel_id=1, source_target_pairs={{0,1},{1,0},{2,3},{3,2},{4,5},{5,4},{6,7},{7,6},{8,9},{9,8},{10,11... | collective-permute-start | bytes 3145736 | tf_op jit(solution)/shard_map/ppermute | solution.py:404
  180.0 23.5 %collective-permute-start.14 = (bf16[512,512]{1,0:T(8,128)(2,1)}, bf16[512,512]{1,0:T(8,128)(2,1)S(1)}, u32[]{:S(2)}, u32[]{:S(2)}) collective-permute-start(bf16[512,512]{1,0:T(8,128)(2,1)} %get-tuple-element.35), channel_id=1, source_target_pairs={{4,8},{8,4},{5,9},{9,5},{6,10},{10,6},{7,11},{11,7},{20,24},{24,20... | collective-permute-start | bytes 1572872 | tf_op jit(solution)/shard_map/ppermute | solution.py:416
  184.4 3.3 %copy-start.3 = (bf16[1,384,2048]{2,1,0:T(8,128)(2,1)S(1)}, bf16[1,384,2048]{2,1,0:T(8,128)(2,1)}, u32[]{:S(2)}) copy-start(bf16[1,384,2048]{2,1,0:T(8,128)(2,1)} %param.9) | copy-start | bytes 4718596
  187.7 10.2 %copy-start.1 = (bf16[2048,1024]{1,0:T(8,128)(2,1)S(1)}, bf16[2048,1024]{1,0:T(8,128)(2,1)}, u32[]{:S(2)}) copy-start(bf16[2048,1024]{1,0:T(8,128)(2,1)} %refs_0_.3) | copy-start | bytes 12582916
  197.9 1.7 copy-start.5
  199.5 10.8 %collective-permute-start.12 = (bf16[512,512]{1,0:T(8,128)(2,1)S(1)}, bf16[512,512]{1,0:T(8,128)(2,1)S(1)}, u32[]{:S(2)}, u32[]{:S(2)}) collective-permute-start(bf16[512,512]{1,0:T(8,128)(2,1)S(1)} %broadcast_select_fusion.2.refs_0_), channel_id=1, source_target_pairs={{0,1},{1,0},{2,3},{3,2},{4,5},{5,4},{6,7},{7,6},{8,9},{9,8},{10,11... | collective-permute-start | bytes 1572872 | tf_op jit(solution)/shard_map/ppermute | solution.py:404
  199.6 11.6 %collective-permute-start.13 = (bf16[512,512]{1,0:T(8,128)(2,1)S(1)}, bf16[512,512]{1,0:T(8,128)(2,1)S(1)}, u32[]{:S(2)}, u32[]{:S(2)}) collective-permute-start(bf16[512,512]{1,0:T(8,128)(2,1)S(1)} %copy-done.5), channel_id=1, source_target_pairs={{0,1},{1,0},{2,3},{3,2},{4,5},{5,4},{6,7},{7,6},{8,9},{9,8},{10,11... | collective-permute-start | bytes 1572872 | tf_op jit(solution)/shard_map/ppermute | solution.py:404
  203.5 27.4 %collective-permute-start.17 = (bf16[192,1024]{1,0:T(8,128)(2,1)S(1)}, bf16[192,1024]{1,0:T(8,128)(2,1)S(1)}, u32[]{:S(2)}, u32[]{:S(2)}) collective-permute-start(bf16[192,1024]{1,0:T(8,128)(2,1)S(1)} %project.5), channel_id=1, source_target_pairs={{0,2},{2,0},{1,3},{3,1},{4,6},{6,4},{5,7},{7,5},{8,10},{10,8},{9,1... | collective-permute-start | bytes 1179656 | tf_op jit(solution)/shard_map/ppermute | solution.py:423
  204.4 29.4 %collective-permute-start.16 = (bf16[192,1024]{1,0:T(8,128)(2,1)S(1)}, bf16[192,1024]{1,0:T(8,128)(2,1)S(1)}, u32[]{:S(2)}, u32[]{:S(2)}) collective-permute-start(bf16[192,1024]{1,0:T(8,128)(2,1)S(1)} %project.6), channel_id=1, source_target_pairs={{0,2},{2,0},{1,3},{3,1},{4,6},{6,4},{5,7},{7,5},{8,10},{10,8},{9,1... | collective-permute-start | bytes 1179656 | tf_op jit(solution)/shard_map/ppermute | solution.py:423
  205.6 12.4 %collective-permute-start.15 = (bf16[512,512]{1,0:T(8,128)(2,1)S(1)}, bf16[512,512]{1,0:T(8,128)(2,1)S(1)}, u32[]{:S(2)}, u32[]{:S(2)}) collective-permute-start(bf16[512,512]{1,0:T(8,128)(2,1)S(1)} %collective-permute-done.14), channel_id=1, source_target_pairs={{4,0},{8,12},{5,1},{9,13},{6,2},{10,14},{7,3},{11,15},{20,16},{24,... | collective-permute-start | bytes 1572872 | tf_op jit(solution)/shard_map/ppermute | solution.py:419
  210.3 30.0 %collective-permute-start.23 = (bf16[192,1024]{1,0:T(8,128)(2,1)S(1)}, bf16[192,1024]{1,0:T(8,128)(2,1)S(1)}, u32[]{:S(2)}, u32[]{:S(2)}) collective-permute-start(bf16[192,1024]{1,0:T(8,128)(2,1)S(1)} %project.7), channel_id=1, source_target_pairs={{0,2},{2,0},{1,3},{3,1},{4,6},{6,4},{5,7},{7,5},{8,10},{10,8},{9,1... | collective-permute-start | bytes 1179656 | tf_op jit(solution)/shard_map/ppermute | solution.py:423
  212.3 32.2 %collective-permute-start.22 = (bf16[192,512]{1,0:T(8,128)(2,1)S(1)}, bf16[192,512]{1,0:T(8,128)(2,1)S(1)}, u32[]{:S(2)}, u32[]{:S(2)}) collective-permute-start(bf16[192,512]{1,0:T(8,128)(2,1)S(1)} %project.8), channel_id=1, source_target_pairs={{0,2},{2,0},{1,3},{3,1},{4,6},{6,4},{5,7},{7,5},{8,10},{10,8},{9,1... | collective-permute-start | bytes 589832 | tf_op jit(solution)/shard_map/ppermute | solution.py:423
  218.1 12.8 %collective-permute-start.18 = (bf16[512,512]{1,0:T(8,128)(2,1)S(1)}, bf16[512,512]{1,0:T(8,128)(2,1)S(1)}, u32[]{:S(2)}, u32[]{:S(2)}) collective-permute-start(bf16[512,512]{1,0:T(8,128)(2,1)S(1)} %broadcast_select_fusion.1.refs_0_), channel_id=1, source_target_pairs={{0,16},{16,0},{1,17},{17,1},{2,18},{18,2},{3,19},{19,3},{4,20},{20... | collective-permute-start | bytes 1572872 | tf_op jit(solution)/shard_map/ppermute | solution.py:425
  230.9 7.0 %collective-permute-start.19 = (bf16[512,512]{1,0:T(8,128)(2,1)S(1)}, bf16[512,512]{1,0:T(8,128)(2,1)S(1)}, u32[]{:S(2)}, u32[]{:S(2)}) collective-permute-start(bf16[512,512]{1,0:T(8,128)(2,1)S(1)} %broadcast_select_fusion.1.refs_0_), channel_id=1, source_target_pairs={{0,1},{1,0},{2,3},{3,2},{4,5},{5,4},{6,7},{7,6},{8,9},{9,8},{10,11... | collective-permute-start | bytes 1572872 | tf_op jit(solution)/shard_map/ppermute | solution.py:404
  230.9 7.0 %collective-permute-start.20 = (bf16[512,512]{1,0:T(8,128)(2,1)S(1)}, bf16[512,512]{1,0:T(8,128)(2,1)S(1)}, u32[]{:S(2)}, u32[]{:S(2)}) collective-permute-start(bf16[512,512]{1,0:T(8,128)(2,1)S(1)} %collective-permute-done.18.refs_1_), channel_id=1, source_target_pairs={{0,1},{1,0},{2,3},{3,2},{4,5},{5,4},{6,7},{7,6},{8,9},{9,8},{10,11... | collective-permute-start | bytes 1572872 | tf_op jit(solution)/shard_map/ppermute | solution.py:404
  239.0 7.3 %collective-permute-start.21 = (bf16[192,512]{1,0:T(8,128)(2,1)S(1)}, bf16[192,512]{1,0:T(8,128)(2,1)S(1)}, u32[]{:S(2)}, u32[]{:S(2)}) collective-permute-start(bf16[192,512]{1,0:T(8,128)(2,1)S(1)} %project.9), channel_id=1, source_target_pairs={{0,2},{2,0},{1,3},{3,1},{4,6},{6,4},{5,7},{7,5},{8,10},{10,8},{9,1... | collective-permute-start | bytes 589832 | tf_op jit(solution)/shard_map/ppermute | solution.py:433

commit v5 on v4

--- a/solution.py
+++ b/solution.py
@@ -352,27 +352,29 @@
     order = [(v % 2) * 2 + v // 2 for v in order]
     flip = tp if tp_count == 2 else 0
     second = jnp.where(seq < 2, 2, 1)
-    third = 2 * jnp.where(seq < 2, 3, 0)
+    third = jnp.where(seq < 2, 3, 0)
     local = [own, own ^ 2, own ^ 1, own ^ 3]
+    halves = [2 * shard + h for shard in (seq ^ 1, second, third) for h in (0, 1)]
     control = jnp.stack(
-        [
-            jnp.asarray(v, jnp.int32)
-            for v in (flip, 1 - flip, *order, *local, seq, seq ^ 1, second, third, third + 1)
-        ]
+        [jnp.asarray(v, jnp.int32) for v in (flip, 1 - flip, *order, *local, seq, *halves)]
     )
     swap_group = functools.partial(lax.ppermute, axis_name="group", perm=SWAP)
     swap_role = functools.partial(lax.ppermute, axis_name="role", perm=SWAP)
 
     if owner_count == 4:
         middle = (seq == 1) | (seq == 2)
-        near = lax.ppermute(quarter, "seq", [(0, 1), (1, 0), (2, 3), (3, 2)])
-        inner = lax.ppermute(quarter, "seq", [(1, 2), (2, 1)])
+        cut = columns // 2
+        parts = [quarter[:, :cut], quarter[:, cut:]]
+        pair = functools.partial(lax.ppermute, axis_name="seq", perm=[(0, 1), (1, 0), (2, 3), (3, 2)])
+        cross = functools.partial(lax.ppermute, axis_name="seq", perm=[(1, 2), (2, 1)])
+        forward = functools.partial(lax.ppermute, axis_name="seq", perm=[(1, 0), (2, 3)])
+        near, inner = [pair(parts[0])], [cross(parts[0])]
 
     position, wanted = rank(page_owner, page_index, owner_count, bucket)
     asked = lax.all_to_all(wanted, "seq", split_axis=0, concat_axis=0, tiled=True)
     if owner_count == 4:
-        near, inner = after(near, asked), after(inner, asked)
-        asked = after(asked, near, inner)
+        near, inner = [after(near[0], asked)], [after(inner[0], asked)]
+        asked = after(asked, near[0], inner[0])
     found = pick(pool[0], asked)
     pages = lax.all_to_all(found, "seq", split_axis=0, concat_axis=0, tiled=True)
     pages = pages.reshape((owner_count * bucket,) + found.shape[2:])
@@ -396,44 +398,51 @@
         )[None]
 
     swap_tp = functools.partial(lax.ppermute, axis_name="tp", perm=SWAP)
-    forward = functools.partial(lax.ppermute, axis_name="seq", perm=[(1, 0), (2, 3)])
-    cross = functools.partial(lax.ppermute, axis_name="seq", perm=[(1, 2), (2, 1)])
-    cut = columns // 2
 
     def four(one, two, *hold):
         return [one, two, swap_role(after(one, *hold)), swap_role(after(two, *hold))]
 
-    near_across = swap_group(near)
-    far_a = cross(near[:, :cut])
-    next_shard = jnp.where(middle, inner, forward(inner))
-    next_across = swap_group(next_shard)
-    far_a = jnp.where(middle, far_a, forward(far_a))
-    far_a_across = swap_group(far_a)
-    near_all = four(near, near_across)
-    next_all = four(next_shard, next_across)
-    far_a_all = four(far_a, far_a_across)
-
-    far_b = cross(after(near[:, cut:], pages))
-    keys, values = place(position, after(pages, near_across, next_shard, far_a), fresh)
+    part = after(parts[1], found)
+    near.append(pair(part))
+    inner.append(cross(part))
+    near_across = [swap_group(near[0])]
+    far = [cross(near[0])]
+    next_shard = [jnp.where(middle, inner[0], forward(inner[0]))]
+    next_across = [swap_group(next_shard[0])]
+    far_on = forward(far[0])
+    near_across.append(swap_group(near[1]))
+    next_shard.append(jnp.where(middle, inner[1], forward(inner[1])))
+    next_across.append(swap_group(next_shard[1]))
+    far.append(cross(near[1]))
+
+    keys, values = place(position, after(pages, next_shard[0], next_shard[1], far[0]), fresh)
     left = attend(1, control, tables, queries[0], keys, values, slots)
-    far_b_on = forward(after(far_b, left))
+    far[0] = jnp.where(middle, far[0], far_on)
+    far_across = [swap_group(far[0])]
     sent = [project(control, left, [out_weight])]
-    for pieces in (near_all, next_all, far_a_all):
-        sent.append(project(control, after(left, sent[-1]), pieces))
-    came = [swap_tp(part) for part in sent]
-    far_b = jnp.where(middle, far_b, after(far_b_on, sent[2]))
-    far_b_across = swap_group(far_b)
-    stay = attend(0, control, tables, after(queries[0], sent[3], far_b), keys, values, slots)
-    far_b_all = four(far_b, far_b_across, stay)
+    far_on = forward(after(far[1], left))
+    weights = []
+    for n in range(4):
+        one, two = ((near, near_across), (next_shard, next_across))[n // 2]
+        weights.append(four(one[n % 2], two[n % 2], *[keys] * (n % 2)))
+        sent.append(project(control, after(left, sent[-1]), weights[-1]))
+    weights.append(four(far[0], far_across[0], sent[2]))
+    sent.append(project(control, after(left, sent[-1]), weights[-1]))
+    came = [swap_tp(each) for each in sent]
+    far[1] = jnp.where(middle, far[1], after(far_on, sent[4]))
+    far_across.append(swap_group(far[1]))
+    stay = attend(0, control, tables, after(queries[0], sent[5], far[1]), keys, values, slots)
+    weights.append(four(far[1], far_across[1], stay))
     total = columns * owner_count
     out = project(control, stay, [out_weight], came[0], 10, None, total)
-    out = project(control, stay, near_all, came[1], 11, out, total)
-    last = project(control, after(left, out), far_b_all)
+    for n in range(2):
+        out = project(control, stay, weights[n], came[n + 1], 11 + n, out, total)
+    last = project(control, after(left, out), weights[5])
     stay = after(stay, last)
-    last = swap_tp(last)
-    out = project(control, stay, next_all, came[2], 12, out, total)
-    out = project(control, stay, far_a_all, came[3], 13, out, total)
-    return project(control, stay, far_b_all, last, 14, out, total)
+    came.append(swap_tp(last))
+    for n in range(2, 6):
+        out = project(control, stay, weights[n], came[n + 1], 11 + n, out, total)
+    return out
 
 
 def solution(mesh):

time: 252 us -> 240 us (0.952)
  waiting for transfers between devices: 127 us -> 110 us
  blocking collectives: 22.1 us -> 10.8 us
  starting transfers between devices: 36.3 us -> 46.8 us
  Pallas kernels: 51.7 us -> 56.2 us
    ppermute x16 -> x23, waiting for transfers between devices: 127 us -> 110 us  [the longest x1 47.3 us: shards(): next_shard = [jnp.where(middle, inner[0], forward(inner[0]))]]
    all_to_all x1, blocking collectives: 22.1 us -> 10.8 us  [shards(): lax.all_to_all(wanted, 'seq', split_axis=0, concat_axis=0, tiled=True)]
    ppermute x16 -> x23, starting transfers between devices: 28.7 us -> 38 us  [the longest x6 7.24 us: shards(): came = [swap_tp(each) for each in sent]]
    pallas_call x10 -> x14, Pallas kernels: 24.7 us -> 28.5 us  [project(): pl.pallas_call(kernel, out_shape=out_shape, grid_spec=pltpu.PrefetchScala...]
    unnamed x25 -> x21, local copies, waits for them, and re-layouts: 5.1 us -> 5.3 us
  transfers between devices with their start and end apart: 25 -> 36, of which waited for: 5 -> 7; matrix products, arithmetic and copies ran while one was open for 2% -> 2% of each run, Pallas kernels for 20% -> 22%
where the time goes in v5:
time: 240 us; the launch traced here: 236 us
  waiting for transfers between devices  110 us (46%)
  Pallas kernels  56.2 us (23%)
  starting transfers between devices  46.8 us (20%)
  blocking collectives  10.8 us (4%)
  local copies, waits for them, and re-layouts  7.87 us (3%)
  other arithmetic  3.93 us (2%)
    ppermute x1, waiting for transfers between devices, shards(): next_shard = [jnp.where(middle, inner[0], forward(inner[0]))]  47.3 us
    ppermute x1, waiting for transfers between devices, shards(): inner.append(cross(part))  43.2 us
    pallas_call x14, Pallas kernels, project(): pl.pallas_call(kernel, out_shape=out_shape, grid_spec=pltpu.PrefetchScala...  28.5 us
    pallas_call x2, Pallas kernels, attend(): pl.pallas_call(functools.partial(attend_kernel, fresh_base, side), out_sh...  20.5 us
    all_to_all x1, blocking collectives, shards(): lax.all_to_all(wanted, 'seq', split_axis=0, concat_axis=0, tiled=True)  10.8 us
    ppermute x6, starting transfers between devices, shards(): came = [swap_tp(each) for each in sent]  7.24 us
    ppermute x1, waiting for transfers between devices, shards(): far = [cross(near[0])]  6.38 us
    ppermute x1, waiting for transfers between devices, shards(): next_across.append(swap_group(next_shard[1]))  6.31 us
  transfers between devices with their start and end apart: 36, of which 7 were waited for; matrix products, arithmetic and copies ran while one was open for 2% of the time, Pallas kernels for 22%

profile of v5, /device:TPU:16, one launch (start us, length us, event | category | flops | bytes accessed | tf_op | source)
XLA Modules:
  0.0 236.5 jit_solution(18343679052276786439)
XLA Ops:
  0.0 2.1 fusion.5
  2.1 1.6 collective-permute-start
  3.6 1.9 collective-permute-start.1
  5.6 2.6 %rank.1 = (s32[128]{0:T(128)}, s32[4,64]{1,0:T(4,128)}) custom-call(s32[1,128]{1,0:T(1,128)} %owner.1, s32[1,128]{1,0:T(1,128)} %page.1), custom_call_target="tpu_custom_call" | custom-call | flops 3000000000 | bytes 1000 | tf_op jit(solution)/shard_map/rank/pallas_call | solution.py:49
  8.2 10.8 %all_to_all.17 = s32[4,1,64]{2,1,0:T(1,128)S(1)} all-to-all(s32[4,1,64]{2,1,0:T(1,128)} %bitcast.42), channel_id=1, replica_groups=mesh['group'=2,'seq'=4,'tp'=2,'role'=2] {'seq'}, dimensions={0} | all-to-all | bytes 2048 | tf_op jit(solution)/shard_map/all_to_all | solution.py:374
  19.0 2.2 copy-done.2
  21.2 1.3 pick.1
  22.5 2.0 copy-done
  24.5 6.0 %all-to-all-start.1 = ((bf16[4,64,2,16,256]{4,3,2,1,0:T(8,128)(2,1)}), bf16[4,64,2,16,256]{4,3,2,1,0:T(8,128)(2,1)}, u32[]{:S(2)}, u32[]{:S(2)}) async-start(bf16[4,64,2,16,256]{4,3,2,1,0:T(8,128)(2,1)} %copy-done), calls=%async_computation.1 | async-start | bytes 8388608 | tf_op jit(solution)/shard_map/all_to_all | solution.py:379
  30.5 3.4 %collective-permute-start.2 = (bf16[512,512]{1,0:T(8,128)(2,1)S(1)}, bf16[512,512]{1,0:T(8,128)(2,1)S(1)}, u32[]{:S(2)}, u32[]{:S(2)}) collective-permute-start(bf16[512,512]{1,0:T(8,128)(2,1)S(1)} %collective-permute-done.1), channel_id=1, source_target_pairs={{4,0},{8,12},{5,1},{9,13},{6,2},{10,14},{7,3},{11,15},{20,16},{24,... | collective-permute-start | bytes 1572872 | tf_op jit(solution)/shard_map/ppermute | solution.py:410
  33.9 1.9 collective-permute-start.3
  35.9 3.9 %collective-permute-start.5 = (bf16[512,512]{1,0:T(8,128)(2,1)S(1)}, bf16[512,512]{1,0:T(8,128)(2,1)S(1)}, u32[]{:S(2)}, u32[]{:S(2)}) collective-permute-start(bf16[512,512]{1,0:T(8,128)(2,1)S(1)} %collective-permute-done.refs_0_), channel_id=1, source_target_pairs={{4,8},{8,4},{5,9},{9,5},{6,10},{10,6},{7,11},{11,7},{20,24},{24,20... | collective-permute-start | bytes 1572872 | tf_op jit(solution)/shard_map/ppermute | solution.py:409
  40.3 1.6 collective-permute-start.6
  41.9 47.3 %collective-permute-done.2 = bf16[512,512]{1,0:T(8,128)(2,1)S(1)} collective-permute-done((bf16[512,512]{1,0:T(8,128)(2,1)S(1)}, bf16[512,512]{1,0:T(8,128)(2,1)S(1)}, u32[]{:S(2)}, u32[]{:S(2)}) %collective-permute-start.2) | collective-permute-done | bytes 524320 | tf_op jit(solution)/shard_map/ppermute | solution.py:410
  89.2 1.6 collective-permute-start.13
  90.8 43.2 %collective-permute-done.3 = bf16[512,512]{1,0:T(8,128)(2,1)S(1)} collective-permute-done((bf16[512,512]{1,0:T(8,128)(2,1)}, bf16[512,512]{1,0:T(8,128)(2,1)S(1)}, u32[]{:S(2)}, u32[]{:S(2)}) %collective-permute-start.3) | collective-permute-done | bytes 524320 | tf_op jit(solution)/shard_map/ppermute | solution.py:407
  134.0 2.1 collective-permute-start.4
  136.5 6.4 %collective-permute-done.5 = bf16[512,512]{1,0:T(8,128)(2,1)S(1)} collective-permute-done((bf16[512,512]{1,0:T(8,128)(2,1)S(1)}, bf16[512,512]{1,0:T(8,128)(2,1)S(1)}, u32[]{:S(2)}, u32[]{:S(2)}) %collective-permute-start.5) | collective-permute-done | bytes 524320 | tf_op jit(solution)/shard_map/ppermute | solution.py:409
  142.9 2.1 collective-permute-start.19
  147.2 3.4 %collective-permute-start.23 = (bf16[512,512]{1,0:T(8,128)(2,1)}, bf16[512,512]{1,0:T(8,128)(2,1)}, u32[]{:S(2)}, u32[]{:S(2)}) collective-permute-start(bf16[512,512]{1,0:T(8,128)(2,1)} %collective-permute-done.9.refs_0_), channel_id=1, source_target_pairs={{4,8},{8,4},{5,9},{9,5},{6,10},{10,6},{7,11},{11,7},{20,24},{24,20... | collective-permute-start | bytes 1572872 | tf_op jit(solution)/shard_map/ppermute | solution.py:416
  150.6 1.6 collective-permute-start.10
  153.9 1.5 collective-permute-start.16
  156.6 3.3 %place.1 = (bf16[2,3072,128]{2,1,0:T(8,128)(2,1)S(1)}, bf16[2,3072,256]{2,1,0:T(8,128)(2,1)S(1)}) custom-call(s32[128]{0:T(128)S(1)} %copy-done.4, bf16[256,2,16,256]{3,2,1,0:T(8,128)(2,1)} %bitcast.23.pages, bf16[384,512]{1,0:T(8,128)(2,1)S(1)} %bitcast.31), custom_call_target="tpu_custom_call" | custom-call | flops 3000000000 | bytes 1000 | tf_op jit(solution)/shard_map/place/pallas_call | solution.py:95
  159.9 9.6 %attend.2.left = bf16[4,192,512]{2,1,0:T(8,128)(2,1)S(1)} custom-call(s32[17]{0:T(128)S(1)} %stack.71.control, s32[6]{0:T(128)S(1)} %get-tuple-element.68.hist_at, s32[6]{0:T(128)S(1)} %get-tuple-element.67.hist_steps, s32[6]{0:T(128)S(1)} %get-tuple-element.62.fresh_at, s32[6]{0:T(128)S(1)} %get-tuple-element.61.fresh_steps, ...), custom_call_target="tpu_custom_call" | custom-call | flops 16000000000 | bytes 1000 | tf_op jit(solution)/shard_map/attend/pallas_call | solution.py:221
  169.6 6.3 %collective-permute-done.16.refs_1_ = bf16[512,512]{1,0:T(8,128)(2,1)} collective-permute-done((bf16[512,512]{1,0:T(8,128)(2,1)S(1)}, bf16[512,512]{1,0:T(8,128)(2,1)}, u32[]{:S(2)}, u32[]{:S(2)}) %collective-permute-start.16) | collective-permute-done | bytes 524320 | tf_op jit(solution)/shard_map/ppermute | solution.py:415
  176.4 1.5 project.7
  178.0 1.6 collective-permute-start.20
  179.6 2.5 %project.8 = bf16[192,512]{1,0:T(8,128)(2,1)S(1)} custom-call(s32[17]{0:T(128)S(1)} %stack.71.control, bf16[4,192,512]{2,1,0:T(8,128)(2,1)S(1)} %attend.2.left, bf16[512,512]{1,0:T(8,128)(2,1)S(1)} %collective-permute-done.refs_0_, bf16[512,512]{1,0:T(8,128)(2,1)} %collective-permute-done.6.refs_1_, bf16[512,512]{1,0:T(8,128)(2,1)} %collective-permute-done.7.refs_2_, ...), custom_call_target="tpu_custom_call" | custom-call | flops 3000000000 | bytes 1000 | tf_op jit(solution)/shard_map/project/pallas_call | solution.py:292
  182.7 2.3 project.9
  185.0 1.6 collective-permute-start.27
  186.6 1.5 collective-permute-start.24
  188.1 1.1 project.10
  189.2 3.2 %collective-permute-done.20.refs_1_ = bf16[512,512]{1,0:T(8,128)(2,1)S(1)} collective-permute-done((bf16[512,512]{1,0:T(8,128)(2,1)S(1)}, bf16[512,512]{1,0:T(8,128)(2,1)S(1)}, u32[]{:S(2)}, u32[]{:S(2)}) %collective-permute-start.20) | collective-permute-done | bytes 524320 | tf_op jit(solution)/shard_map/ppermute | solution.py:421
  192.4 1.5 collective-permute-start.26
  194.4 2.1 project.11
  196.5 3.1 %collective-permute-done.24 = bf16[512,512]{1,0:T(8,128)(2,1)S(1)} collective-permute-done((bf16[512,512]{1,0:T(8,128)(2,1)}, bf16[512,512]{1,0:T(8,128)(2,1)S(1)}, u32[]{:S(2)}, u32[]{:S(2)}) %collective-permute-start.24) | collective-permute-done | bytes 524320 | tf_op jit(solution)/shard_map/ppermute | solution.py:423
  200.2 1.1 broadcast_select_fusion.refs_0_
  201.3 1.5 collective-permute-start.34
  203.4 1.1 project.12
  204.5 11.0 %attend.3.left = bf16[4,192,512]{2,1,0:T(8,128)(2,1)S(1)} custom-call(s32[17]{0:T(128)S(1)} %stack.71.control, s32[6]{0:T(128)S(1)} %get-tuple-element.68.hist_at, s32[6]{0:T(128)S(1)} %get-tuple-element.67.hist_steps, s32[6]{0:T(128)S(1)} %get-tuple-element.62.fresh_at, s32[6]{0:T(128)S(1)} %get-tuple-element.61.fresh_steps, ...), custom_call_target="tpu_custom_call" | custom-call | flops 16000000000 | bytes 1000 | tf_op jit(solution)/shard_map/attend/pallas_call | solution.py:221
  216.0 2.3 finish.7.refs_4_
  218.8 3.2 %finish.8.refs_4_ = bf16[1,192,4096]{2,1,0:T(8,128)(2,1)} custom-call(s32[17]{0:T(128)S(1)} %stack.71.control, bf16[4,192,512]{2,1,0:T(8,128)(2,1)S(1)} %attend.3.left, bf16[192,512]{1,0:T(8,128)(2,1)S(1)} %collective-permute-done.26.came, bf16[512,512]{1,0:T(8,128)(2,1)S(1)} %collective-permute-done.refs_0_, ...), custom_call_target="tpu_custom_call", output_to_operand_aliasing={{}: (7, {})} | custom-call | flops 3000000000 | bytes 1000 | tf_op jit(solution)/shard_map/finish/pallas_call | solution.py:292
  222.0 1.6 collective-permute-start.32
  223.6 3.0 %finish.9.refs_4_ = bf16[1,192,4096]{2,1,0:T(8,128)(2,1)} custom-call(s32[17]{0:T(128)S(1)} %stack.71.control, bf16[4,192,512]{2,1,0:T(8,128)(2,1)S(1)} %attend.3.left, bf16[192,512]{1,0:T(8,128)(2,1)S(1)} %collective-permute-done.25.came, bf16[512,512]{1,0:T(8,128)(2,1)} %collective-permute-done.9.refs_0_, ...), custom_call_target="tpu_custom_call", output_to_operand_aliasing={{}: (7, {})} | custom-call | flops 3000000000 | bytes 1000 | tf_op jit(solution)/shard_map/finish/pallas_call | solution.py:292
  228.2 1.8 finish.10.refs_4_
  230.0 2.8 %finish.11.refs_4_ = bf16[1,192,4096]{2,1,0:T(8,128)(2,1)} custom-call(s32[17]{0:T(128)S(1)} %stack.71.control, bf16[4,192,512]{2,1,0:T(8,128)(2,1)S(1)} %attend.3.left, bf16[192,512]{1,0:T(8,128)(2,1)S(1)} %collective-permute-done.33.came, bf16[512,512]{1,0:T(8,128)(2,1)S(1)} %broadcast_select_fusion.2.refs_0_, ...), custom_call_target="tpu_custom_call", output_to_operand_aliasing={{}: (7, {})} | custom-call | flops 3000000000 | bytes 1000 | tf_op jit(solution)/shard_map/finish/pallas_call | solution.py:292
  232.9 1.8 finish.12.refs_4_
  234.7 1.8 finish.13
  (84 shorter events, 11.2 us)
Async XLA Ops:
  2.1 16.9 %collective-permute-start = (bf16[512,512]{1,0:T(8,128)(2,1)S(1)}, bf16[512,512]{1,0:T(8,128)(2,1)S(1)}, u32[]{:S(2)}, u32[]{:S(2)}) collective-permute-start(bf16[512,512]{1,0:T(8,128)(2,1)S(1)} %get-tuple-element.66), channel_id=1, source_target_pairs={{0,4},{4,0},{8,12},{12,8},{1,5},{5,1},{9,13},{13,9},{2,6},{6,2},{1... | collective-permute-start | bytes 1572872 | tf_op jit(solution)/shard_map/ppermute | solution.py:371
  3.6 15.4 %collective-permute-start.1 = (bf16[512,512]{1,0:T(8,128)(2,1)S(1)}, bf16[512,512]{1,0:T(8,128)(2,1)S(1)}, u32[]{:S(2)}, u32[]{:S(2)}) collective-permute-start(bf16[512,512]{1,0:T(8,128)(2,1)S(1)} %get-tuple-element.66), channel_id=1, source_target_pairs={{4,8},{8,4},{5,9},{9,5},{6,10},{10,6},{7,11},{11,7},{20,24},{24,20... | collective-permute-start | bytes 1572872 | tf_op jit(solution)/shard_map/ppermute | solution.py:371
  19.0 2.2 copy-start.2
  22.5 2.0 copy-start
  24.5 15.3 %copy-start.8 = (s32[1,128]{1,0:T(1,128)S(1)}, s32[1,128]{1,0:T(1,128)}, u32[]{:S(2)}) copy-start(s32[1,128]{1,0:T(1,128)} %param.14) | copy-start | bytes 1540
  24.5 15.3 %copy-start.9 = (s32[1,128]{1,0:T(1,128)S(1)}, s32[1,128]{1,0:T(1,128)}, u32[]{:S(2)}) copy-start(s32[1,128]{1,0:T(1,128)} %param.15) | copy-start | bytes 1540
  24.5 15.4 %copy-start.7 = (s32[1,384]{1,0:T(1,128)S(1)}, s32[1,384]{1,0:T(1,128)}, u32[]{:S(2)}) copy-start(s32[1,384]{1,0:T(1,128)} %param.13) | copy-start | bytes 4612
  24.5 132.1 %all-to-all-start.1 = ((bf16[4,64,2,16,256]{4,3,2,1,0:T(8,128)(2,1)}), bf16[4,64,2,16,256]{4,3,2,1,0:T(8,128)(2,1)}, u32[]{:S(2)}, u32[]{:S(2)}) async-start(bf16[4,64,2,16,256]{4,3,2,1,0:T(8,128)(2,1)} %copy-done), calls=%async_computation.1 | async-start | bytes 8388608 | tf_op jit(solution)/shard_map/all_to_all | solution.py:379
  30.5 58.6 %collective-permute-start.2 = (bf16[512,512]{1,0:T(8,128)(2,1)S(1)}, bf16[512,512]{1,0:T(8,128)(2,1)S(1)}, u32[]{:S(2)}, u32[]{:S(2)}) collective-permute-start(bf16[512,512]{1,0:T(8,128)(2,1)S(1)} %collective-permute-done.1), channel_id=1, source_target_pairs={{4,0},{8,12},{5,1},{9,13},{6,2},{10,14},{7,3},{11,15},{20,16},{24,... | collective-permute-start | bytes 1572872 | tf_op jit(solution)/shard_map/ppermute | solution.py:410
  33.9 100.1 %collective-permute-start.3 = (bf16[512,512]{1,0:T(8,128)(2,1)}, bf16[512,512]{1,0:T(8,128)(2,1)S(1)}, u32[]{:S(2)}, u32[]{:S(2)}) collective-permute-start(bf16[512,512]{1,0:T(8,128)(2,1)} %get-tuple-element.37), channel_id=1, source_target_pairs={{4,8},{8,4},{5,9},{9,5},{6,10},{10,6},{7,11},{11,7},{20,24},{24,20... | collective-permute-start | bytes 1572872 | tf_op jit(solution)/shard_map/ppermute | solution.py:407
  35.9 107.0 %collective-permute-start.5 = (bf16[512,512]{1,0:T(8,128)(2,1)S(1)}, bf16[512,512]{1,0:T(8,128)(2,1)S(1)}, u32[]{:S(2)}, u32[]{:S(2)}) collective-permute-start(bf16[512,512]{1,0:T(8,128)(2,1)S(1)} %collective-permute-done.refs_0_), channel_id=1, source_target_pairs={{4,8},{8,4},{5,9},{9,5},{6,10},{10,6},{7,11},{11,7},{20,24},{24,20... | collective-permute-start | bytes 1572872 | tf_op jit(solution)/shard_map/ppermute | solution.py:409
  40.2 106.5 %collective-permute-start.9 = (bf16[512,512]{1,0:T(8,128)(2,1)}, bf16[512,512]{1,0:T(8,128)(2,1)}, u32[]{:S(2)}, u32[]{:S(2)}) collective-permute-start(bf16[512,512]{1,0:T(8,128)(2,1)} %get-tuple-element.37), channel_id=1, source_target_pairs={{0,4},{4,0},{8,12},{12,8},{1,5},{5,1},{9,13},{13,9},{2,6},{6,2},{1... | collective-permute-start | bytes 1572872 | tf_op jit(solution)/shard_map/ppermute | solution.py:406
  40.3 106.3 %collective-permute-start.6 = (bf16[512,512]{1,0:T(8,128)(2,1)S(1)}, bf16[512,512]{1,0:T(8,128)(2,1)}, u32[]{:S(2)}, u32[]{:S(2)}) collective-permute-start(bf16[512,512]{1,0:T(8,128)(2,1)S(1)} %collective-permute-done.refs_0_), channel_id=1, source_target_pairs={{0,16},{16,0},{1,17},{17,1},{2,18},{18,2},{3,19},{19,3},{4,20},{20... | collective-permute-start | bytes 1572872 | tf_op jit(solution)/shard_map/ppermute | solution.py:408
  89.2 58.0 %collective-permute-start.13 = (bf16[512,512]{1,0:T(8,128)(2,1)S(1)}, bf16[512,512]{1,0:T(8,128)(2,1)S(1)}, u32[]{:S(2)}, u32[]{:S(2)}) collective-permute-start(bf16[512,512]{1,0:T(8,128)(2,1)S(1)} %broadcast_select_fusion.3.refs_0_), channel_id=1, source_target_pairs={{0,16},{16,0},{1,17},{17,1},{2,18},{18,2},{3,19},{19,3},{4,20},{20... | collective-permute-start | bytes 1572872 | tf_op jit(solution)/shard_map/ppermute | solution.py:411
  134.0 16.6 %copy-start.6 = (bf16[512,512]{1,0:T(8,128)(2,1)}, bf16[512,512]{1,0:T(8,128)(2,1)S(1)}, u32[]{:S(2)}) copy-start(bf16[512,512]{1,0:T(8,128)(2,1)S(1)} %collective-permute-done.3) | copy-start | bytes 1572868
  134.0 16.6 %collective-permute-start.4 = (bf16[512,512]{1,0:T(8,128)(2,1)S(1)}, bf16[512,512]{1,0:T(8,128)(2,1)}, u32[]{:S(2)}, u32[]{:S(2)}) collective-permute-start(bf16[512,512]{1,0:T(8,128)(2,1)S(1)} %collective-permute-done.3), channel_id=1, source_target_pairs={{4,0},{8,12},{5,1},{9,13},{6,2},{10,14},{7,3},{11,15},{20,16},{24,... | collective-permute-start | bytes 1572872 | tf_op jit(solution)/shard_map/ppermute | solution.py:414
  142.9 11.0 %copy-start.5 = (bf16[512,512]{1,0:T(8,128)(2,1)}, bf16[512,512]{1,0:T(8,128)(2,1)S(1)}, u32[]{:S(2)}) copy-start(bf16[512,512]{1,0:T(8,128)(2,1)S(1)} %collective-permute-done.5) | copy-start | bytes 1572868
  142.9 11.0 %collective-permute-start.19 = (bf16[512,512]{1,0:T(8,128)(2,1)S(1)}, bf16[512,512]{1,0:T(8,128)(2,1)}, u32[]{:S(2)}, u32[]{:S(2)}) collective-permute-start(bf16[512,512]{1,0:T(8,128)(2,1)S(1)} %collective-permute-done.5), channel_id=1, source_target_pairs={{4,0},{8,12},{5,1},{9,13},{6,2},{10,14},{7,3},{11,15},{20,16},{24,... | collective-permute-start | bytes 1572872 | tf_op jit(solution)/shard_map/ppermute | solution.py:412
  146.6 10.0 %copy-start.4 = (s32[128]{0:T(128)S(1)}, s32[128]{0:T(128)}, u32[]{:S(2)}) copy-start(s32[128]{0:T(128)} %get-tuple-element.32.position) | copy-start | bytes 1540
  146.6 31.3 %collective-permute-start.7 = (bf16[512,512]{1,0:T(8,128)(2,1)S(1)}, bf16[512,512]{1,0:T(8,128)(2,1)}, u32[]{:S(2)}, u32[]{:S(2)}) collective-permute-start(bf16[512,512]{1,0:T(8,128)(2,1)S(1)} %collective-permute-done.refs_0_), channel_id=1, source_target_pairs={{0,1},{1,0},{2,3},{3,2},{4,5},{5,4},{6,7},{7,6},{8,9},{9,8},{10,11... | collective-permute-start | bytes 1572872 | tf_op jit(solution)/shard_map/ppermute | solution.py:403
  146.7 31.3 %collective-permute-start.8 = (bf16[512,512]{1,0:T(8,128)(2,1)}, bf16[512,512]{1,0:T(8,128)(2,1)}, u32[]{:S(2)}, u32[]{:S(2)}) collective-permute-start(bf16[512,512]{1,0:T(8,128)(2,1)} %collective-permute-done.6.refs_1_), channel_id=1, source_target_pairs={{0,1},{1,0},{2,3},{3,2},{4,5},{5,4},{6,7},{7,6},{8,9},{9,8},{10,11... | collective-permute-start | bytes 1572872 | tf_op jit(solution)/shard_map/ppermute | solution.py:403
  147.2 22.2 %collective-permute-start.23 = (bf16[512,512]{1,0:T(8,128)(2,1)}, bf16[512,512]{1,0:T(8,128)(2,1)}, u32[]{:S(2)}, u32[]{:S(2)}) collective-permute-start(bf16[512,512]{1,0:T(8,128)(2,1)} %collective-permute-done.9.refs_0_), channel_id=1, source_target_pairs={{4,8},{8,4},{5,9},{9,5},{6,10},{10,6},{7,11},{11,7},{20,24},{24,20... | collective-permute-start | bytes 1572872 | tf_op jit(solution)/shard_map/ppermute | solution.py:416
  150.6 25.3 %collective-permute-start.10 = (bf16[512,512]{1,0:T(8,128)(2,1)}, bf16[512,512]{1,0:T(8,128)(2,1)}, u32[]{:S(2)}, u32[]{:S(2)}) collective-permute-start(bf16[512,512]{1,0:T(8,128)(2,1)} %collective-permute-done.9.refs_0_), channel_id=1, source_target_pairs={{0,16},{16,0},{1,17},{17,1},{2,18},{18,2},{3,19},{19,3},{4,20},{20... | collective-permute-start | bytes 1572872 | tf_op jit(solution)/shard_map/ppermute | solution.py:413
  153.9 21.9 %collective-permute-start.16 = (bf16[512,512]{1,0:T(8,128)(2,1)S(1)}, bf16[512,512]{1,0:T(8,128)(2,1)}, u32[]{:S(2)}, u32[]{:S(2)}) collective-permute-start(bf16[512,512]{1,0:T(8,128)(2,1)S(1)} %broadcast_select_fusion.2.refs_0_), channel_id=1, source_target_pairs={{0,16},{16,0},{1,17},{17,1},{2,18},{18,2},{3,19},{19,3},{4,20},{20... | collective-permute-start | bytes 1572872 | tf_op jit(solution)/shard_map/ppermute | solution.py:415
  156.6 3.3 %copy-start.3 = (bf16[1,384,2048]{2,1,0:T(8,128)(2,1)S(1)}, bf16[1,384,2048]{2,1,0:T(8,128)(2,1)}, u32[]{:S(2)}) copy-start(bf16[1,384,2048]{2,1,0:T(8,128)(2,1)} %param.9) | copy-start | bytes 4718596
  159.9 16.5 %copy-start.1 = (bf16[2048,1024]{1,0:T(8,128)(2,1)S(1)}, bf16[2048,1024]{1,0:T(8,128)(2,1)}, u32[]{:S(2)}) copy-start(bf16[2048,1024]{1,0:T(8,128)(2,1)} %refs_0_.3) | copy-start | bytes 12582916
  169.5 15.5 %collective-permute-start.14 = (bf16[512,512]{1,0:T(8,128)(2,1)S(1)}, bf16[512,512]{1,0:T(8,128)(2,1)S(1)}, u32[]{:S(2)}, u32[]{:S(2)}) collective-permute-start(bf16[512,512]{1,0:T(8,128)(2,1)S(1)} %broadcast_select_fusion.3.refs_0_), channel_id=1, source_target_pairs={{0,1},{1,0},{2,3},{3,2},{4,5},{5,4},{6,7},{7,6},{8,9},{9,8},{10,11... | collective-permute-start | bytes 1572872 | tf_op jit(solution)/shard_map/ppermute | solution.py:403
  175.9 6.2 %collective-permute-start.12 = (bf16[512,512]{1,0:T(8,128)(2,1)}, bf16[512,512]{1,0:T(8,128)(2,1)S(1)}, u32[]{:S(2)}, u32[]{:S(2)}) collective-permute-start(bf16[512,512]{1,0:T(8,128)(2,1)} %collective-permute-done.10.refs_1_), channel_id=1, source_target_pairs={{0,1},{1,0},{2,3},{3,2},{4,5},{5,4},{6,7},{7,6},{8,9},{9,8},{10,11... | collective-permute-start | bytes 1572872 | tf_op jit(solution)/shard_map/ppermute | solution.py:403
  175.9 6.5 %collective-permute-start.11 = (bf16[512,512]{1,0:T(8,128)(2,1)}, bf16[512,512]{1,0:T(8,128)(2,1)S(1)}, u32[]{:S(2)}, u32[]{:S(2)}) collective-permute-start(bf16[512,512]{1,0:T(8,128)(2,1)} %collective-permute-done.9.refs_0_), channel_id=1, source_target_pairs={{0,1},{1,0},{2,3},{3,2},{4,5},{5,4},{6,7},{7,6},{8,9},{9,8},{10,11... | collective-permute-start | bytes 1572872 | tf_op jit(solution)/shard_map/ppermute | solution.py:403
  177.9 8.6 %collective-permute-start.15 = (bf16[512,512]{1,0:T(8,128)(2,1)S(1)}, bf16[512,512]{1,0:T(8,128)(2,1)S(1)}, u32[]{:S(2)}, u32[]{:S(2)}) collective-permute-start(bf16[512,512]{1,0:T(8,128)(2,1)S(1)} %collective-permute-done.13.refs_1_), channel_id=1, source_target_pairs={{0,1},{1,0},{2,3},{3,2},{4,5},{5,4},{6,7},{7,6},{8,9},{9,8},{10,11... | collective-permute-start | bytes 1572872 | tf_op jit(solution)/shard_map/ppermute | solution.py:403
  178.0 14.3 %collective-permute-start.20 = (bf16[512,512]{1,0:T(8,128)(2,1)S(1)}, bf16[512,512]{1,0:T(8,128)(2,1)S(1)}, u32[]{:S(2)}, u32[]{:S(2)}) collective-permute-start(bf16[512,512]{1,0:T(8,128)(2,1)S(1)} %broadcast_select_fusion.1.refs_0_), channel_id=1, source_target_pairs={{0,16},{16,0},{1,17},{17,1},{2,18},{18,2},{3,19},{19,3},{4,20},{20... | collective-permute-start | bytes 1572872 | tf_op jit(solution)/shard_map/ppermute | solution.py:421
  182.1 11.8 %collective-permute-start.18 = (bf16[512,512]{1,0:T(8,128)(2,1)}, bf16[512,512]{1,0:T(8,128)(2,1)S(1)}, u32[]{:S(2)}, u32[]{:S(2)}) collective-permute-start(bf16[512,512]{1,0:T(8,128)(2,1)} %collective-permute-done.16.refs_1_), channel_id=1, source_target_pairs={{0,1},{1,0},{2,3},{3,2},{4,5},{5,4},{6,7},{7,6},{8,9},{9,8},{10,11... | collective-permute-start | bytes 1572872 | tf_op jit(solution)/shard_map/ppermute | solution.py:403
  182.3 11.5 %collective-permute-start.17 = (bf16[512,512]{1,0:T(8,128)(2,1)S(1)}, bf16[512,512]{1,0:T(8,128)(2,1)S(1)}, u32[]{:S(2)}, u32[]{:S(2)}) collective-permute-start(bf16[512,512]{1,0:T(8,128)(2,1)S(1)} %broadcast_select_fusion.2.refs_0_), channel_id=1, source_target_pairs={{0,1},{1,0},{2,3},{3,2},{4,5},{5,4},{6,7},{7,6},{8,9},{9,8},{10,11... | collective-permute-start | bytes 1572872 | tf_op jit(solution)/shard_map/ppermute | solution.py:403
  185.0 31.0 %collective-permute-start.27 = (bf16[192,1024]{1,0:T(8,128)(2,1)S(1)}, bf16[192,1024]{1,0:T(8,128)(2,1)S(1)}, u32[]{:S(2)}, u32[]{:S(2)}) collective-permute-start(bf16[192,1024]{1,0:T(8,128)(2,1)S(1)} %project.7), channel_id=1, source_target_pairs={{0,2},{2,0},{1,3},{3,1},{4,6},{6,4},{5,7},{7,5},{8,10},{10,8},{9,1... | collective-permute-start | bytes 1179656 | tf_op jit(solution)/shard_map/ppermute | solution.py:431
  186.6 13.1 %collective-permute-start.24 = (bf16[512,512]{1,0:T(8,128)(2,1)}, bf16[512,512]{1,0:T(8,128)(2,1)S(1)}, u32[]{:S(2)}, u32[]{:S(2)}) collective-permute-start(bf16[512,512]{1,0:T(8,128)(2,1)} %collective-permute-done.23), channel_id=1, source_target_pairs={{4,0},{8,12},{5,1},{9,13},{6,2},{10,14},{7,3},{11,15},{20,16},{24,... | collective-permute-start | bytes 1572872 | tf_op jit(solution)/shard_map/ppermute | solution.py:423
  192.4 26.0 %collective-permute-start.26 = (bf16[192,512]{1,0:T(8,128)(2,1)S(1)}, bf16[192,512]{1,0:T(8,128)(2,1)S(1)}, u32[]{:S(2)}, u32[]{:S(2)}) collective-permute-start(bf16[192,512]{1,0:T(8,128)(2,1)S(1)} %project.8), channel_id=1, source_target_pairs={{0,2},{2,0},{1,3},{3,1},{4,6},{6,4},{5,7},{7,5},{8,10},{10,8},{9,1... | collective-permute-start | bytes 589832 | tf_op jit(solution)/shard_map/ppermute | solution.py:431
  193.9 7.5 %collective-permute-start.22 = (bf16[512,512]{1,0:T(8,128)(2,1)S(1)}, bf16[512,512]{1,0:T(8,128)(2,1)S(1)}, u32[]{:S(2)}, u32[]{:S(2)}) collective-permute-start(bf16[512,512]{1,0:T(8,128)(2,1)S(1)} %collective-permute-done.20.refs_1_), channel_id=1, source_target_pairs={{0,1},{1,0},{2,3},{3,2},{4,5},{5,4},{6,7},{7,6},{8,9},{9,8},{10,11... | collective-permute-start | bytes 1572872 | tf_op jit(solution)/shard_map/ppermute | solution.py:403
  193.9 9.0 %collective-permute-start.21 = (bf16[512,512]{1,0:T(8,128)(2,1)S(1)}, bf16[512,512]{1,0:T(8,128)(2,1)S(1)}, u32[]{:S(2)}, u32[]{:S(2)}) collective-permute-start(bf16[512,512]{1,0:T(8,128)(2,1)S(1)} %broadcast_select_fusion.1.refs_0_), channel_id=1, source_target_pairs={{0,1},{1,0},{2,3},{3,2},{4,5},{5,4},{6,7},{7,6},{8,9},{9,8},{10,11... | collective-permute-start | bytes 1572872 | tf_op jit(solution)/shard_map/ppermute | solution.py:403
  199.6 22.4 %collective-permute-start.25 = (bf16[192,512]{1,0:T(8,128)(2,1)S(1)}, bf16[192,512]{1,0:T(8,128)(2,1)S(1)}, u32[]{:S(2)}, u32[]{:S(2)}) collective-permute-start(bf16[192,512]{1,0:T(8,128)(2,1)S(1)} %project.9), channel_id=1, source_target_pairs={{0,2},{2,0},{1,3},{3,1},{4,6},{6,4},{5,7},{7,5},{8,10},{10,8},{9,1... | collective-permute-start | bytes 589832 | tf_op jit(solution)/shard_map/ppermute | solution.py:431
  201.3 26.9 %collective-permute-start.34 = (bf16[192,512]{1,0:T(8,128)(2,1)S(1)}, bf16[192,512]{1,0:T(8,128)(2,1)S(1)}, u32[]{:S(2)}, u32[]{:S(2)}) collective-permute-start(bf16[192,512]{1,0:T(8,128)(2,1)S(1)} %project.10), channel_id=1, source_target_pairs={{0,2},{2,0},{1,3},{3,1},{4,6},{6,4},{5,7},{7,5},{8,10},{10,8},{9,1... | collective-permute-start | bytes 589832 | tf_op jit(solution)/shard_map/ppermute | solution.py:431
  202.9 12.6 %collective-permute-start.28 = (bf16[512,512]{1,0:T(8,128)(2,1)S(1)}, bf16[512,512]{1,0:T(8,128)(2,1)S(1)}, u32[]{:S(2)}, u32[]{:S(2)}) collective-permute-start(bf16[512,512]{1,0:T(8,128)(2,1)S(1)} %broadcast_select_fusion.refs_0_), channel_id=1, source_target_pairs={{0,16},{16,0},{1,17},{17,1},{2,18},{18,2},{3,19},{19,3},{4,20},{20... | collective-permute-start | bytes 1572872 | tf_op jit(solution)/shard_map/ppermute | solution.py:433
  215.5 14.5 %collective-permute-start.33 = (bf16[192,512]{1,0:T(8,128)(2,1)S(1)}, bf16[192,512]{1,0:T(8,128)(2,1)S(1)}, u32[]{:S(2)}, u32[]{:S(2)}) collective-permute-start(bf16[192,512]{1,0:T(8,128)(2,1)S(1)} %project.11), channel_id=1, source_target_pairs={{0,2},{2,0},{1,3},{3,1},{4,6},{6,4},{5,7},{7,5},{8,10},{10,8},{9,1... | collective-permute-start | bytes 589832 | tf_op jit(solution)/shard_map/ppermute | solution.py:431
  216.0 10.5 %collective-permute-start.30 = (bf16[512,512]{1,0:T(8,128)(2,1)S(1)}, bf16[512,512]{1,0:T(8,128)(2,1)S(1)}, u32[]{:S(2)}, u32[]{:S(2)}) collective-permute-start(bf16[512,512]{1,0:T(8,128)(2,1)S(1)} %collective-permute-done.28.refs_1_), channel_id=1, source_target_pairs={{0,1},{1,0},{2,3},{3,2},{4,5},{5,4},{6,7},{7,6},{8,9},{9,8},{10,11... | collective-permute-start | bytes 1572872 | tf_op jit(solution)/shard_map/ppermute | solution.py:403
  218.3 8.2 %collective-permute-start.29 = (bf16[512,512]{1,0:T(8,128)(2,1)S(1)}, bf16[512,512]{1,0:T(8,128)(2,1)S(1)}, u32[]{:S(2)}, u32[]{:S(2)}) collective-permute-start(bf16[512,512]{1,0:T(8,128)(2,1)S(1)} %broadcast_select_fusion.refs_0_), channel_id=1, source_target_pairs={{0,1},{1,0},{2,3},{3,2},{4,5},{5,4},{6,7},{7,6},{8,9},{9,8},{10,11... | collective-permute-start | bytes 1572872 | tf_op jit(solution)/shard_map/ppermute | solution.py:403
  222.0 10.9 %collective-permute-start.32 = (bf16[192,512]{1,0:T(8,128)(2,1)S(1)}, bf16[192,512]{1,0:T(8,128)(2,1)S(1)}, u32[]{:S(2)}, u32[]{:S(2)}) collective-permute-start(bf16[192,512]{1,0:T(8,128)(2,1)S(1)} %project.12), channel_id=1, source_target_pairs={{0,2},{2,0},{1,3},{3,1},{4,6},{6,4},{5,7},{7,5},{8,10},{10,8},{9,1... | collective-permute-start | bytes 589832 | tf_op jit(solution)/shard_map/ppermute | solution.py:431
  227.7 7.0 %collective-permute-start.31 = (bf16[192,512]{1,0:T(8,128)(2,1)S(1)}, bf16[192,512]{1,0:T(8,128)(2,1)S(1)}, u32[]{:S(2)}, u32[]{:S(2)}) collective-permute-start(bf16[192,512]{1,0:T(8,128)(2,1)S(1)} %project.13), channel_id=1, source_target_pairs={{0,2},{2,0},{1,3},{3,1},{4,6},{6,4},{5,7},{7,5},{8,10},{10,8},{9,1... | collective-permute-start | bytes 589832 | tf_op jit(solution)/shard_map/ppermute | solution.py:442

commit v6 on v5

--- a/solution.py
+++ b/solution.py
@@ -246,29 +246,33 @@
     return [slice(k, k + cut) for k in range(0, columns, cut)]
 
 
-def quarters(control, refs):
-    if len(refs) == 4:
-        return refs
-    depth = refs[0].shape[0] // 4
-    return [refs[0].at[pl.ds(pl.multiple_of(control[6 + n] * depth, depth), depth)] for n in range(4)]
+def parts_of(control, refs):
+    if len(refs) == 1:
+        depth = refs[0].shape[0] // 4
+        return [
+            (0, [refs[0].at[pl.ds(pl.multiple_of(control[6 + n] * depth, depth), depth)] for n in range(4)])
+        ]
+    columns = refs[0].shape[1]
+    return [(k // 4 * columns, refs[k : k + 4]) for k in range(0, len(refs), 4)]
 
 
 def project_kernel(control, left, *refs):
-    pieces = quarters(control, refs[:-1])
-    for at in blocks(pieces[0].shape[1]):
-        refs[-1][:, at] = multiply(left, pieces, at)
+    for first, pieces in parts_of(control, refs[:-1]):
+        for at in blocks(pieces[0].shape[1]):
+            refs[-1][:, first + at.start : first + at.stop] = multiply(left, pieces, at)
 
 
 def finish_kernel(has_out, control, left, came, *refs):
-    pieces = quarters(control, refs[: len(refs) - 1 - has_out])
-    for at in blocks(pieces[0].shape[1]):
-        total = multiply(left, pieces, at).astype(jnp.float32) + came[:, at].astype(jnp.float32)
-        refs[-1][0, :, at] = total.astype(jnp.bfloat16)
+    for first, pieces in parts_of(control, refs[: len(refs) - 1 - has_out]):
+        for at in blocks(pieces[0].shape[1]):
+            to = slice(first + at.start, first + at.stop)
+            total = multiply(left, pieces, at).astype(jnp.float32) + came[:, to].astype(jnp.float32)
+            refs[-1][0, :, to] = total.astype(jnp.bfloat16)
 
 
 def project(control, left, pieces, came=None, base=None, out=None, width=None):
     half = left.shape[1]
-    columns = pieces[0].shape[1]
+    columns = pieces[0].shape[1] * max(1, len(pieces) // 4)
     vmem = pl.BlockSpec(memory_space=pltpu.VMEM)
     in_specs = [vmem]
     operands = [left]
@@ -354,9 +358,8 @@
     second = jnp.where(seq < 2, 2, 1)
     third = jnp.where(seq < 2, 3, 0)
     local = [own, own ^ 2, own ^ 1, own ^ 3]
-    halves = [2 * shard + h for shard in (seq ^ 1, second, third) for h in (0, 1)]
     control = jnp.stack(
-        [jnp.asarray(v, jnp.int32) for v in (flip, 1 - flip, *order, *local, seq, *halves)]
+        [jnp.asarray(v, jnp.int32) for v in (flip, 1 - flip, *order, *local, seq, seq ^ 1, second, 2 * third, 2 * third + 1)]
     )
     swap_group = functools.partial(lax.ppermute, axis_name="group", perm=SWAP)
     swap_role = functools.partial(lax.ppermute, axis_name="role", perm=SWAP)
@@ -374,8 +377,14 @@
     asked = lax.all_to_all(wanted, "seq", split_axis=0, concat_axis=0, tiled=True)
     if owner_count == 4:
         near, inner = [after(near[0], asked)], [after(inner[0], asked)]
+        later = after(parts[1], near[0], inner[0])
+        near.append(pair(later))
+        inner.append(cross(later))
         asked = after(asked, near[0], inner[0])
     found = pick(pool[0], asked)
+    if owner_count == 4:
+        near[1], inner[1] = after(near[1], found), after(inner[1], found)
+        found = after(found, near[1], inner[1])
     pages = lax.all_to_all(found, "seq", split_axis=0, concat_axis=0, tiled=True)
     pages = pages.reshape((owner_count * bucket,) + found.shape[2:])
     slots = slot_count * pool.shape[3]
@@ -402,46 +411,35 @@
     def four(one, two, *hold):
         return [one, two, swap_role(after(one, *hold)), swap_role(after(two, *hold))]
 
-    part = after(parts[1], found)
-    near.append(pair(part))
-    inner.append(cross(part))
-    near_across = [swap_group(near[0])]
-    far = [cross(near[0])]
-    next_shard = [jnp.where(middle, inner[0], forward(inner[0]))]
-    next_across = [swap_group(next_shard[0])]
-    far_on = forward(far[0])
-    near_across.append(swap_group(near[1]))
-    next_shard.append(jnp.where(middle, inner[1], forward(inner[1])))
-    next_across.append(swap_group(next_shard[1]))
-    far.append(cross(near[1]))
-
-    keys, values = place(position, after(pages, next_shard[0], next_shard[1], far[0]), fresh)
+    near_across = [swap_group(part) for part in near]
+    next_shard = [jnp.where(middle, part, forward(part)) for part in inner]
+    next_across = [swap_group(part) for part in next_shard]
+    near_all = four(near[0], near_across[0]) + four(near[1], near_across[1])
+    next_all = four(next_shard[0], next_across[0]) + four(next_shard[1], next_across[1])
+    far = [cross(after(near[0], *next_shard)), cross(after(near[1], pages))]
+
+    keys, values = place(position, after(pages, far[0], *near_all, *next_all), fresh)
     left = attend(1, control, tables, queries[0], keys, values, slots)
-    far[0] = jnp.where(middle, far[0], far_on)
-    far_across = [swap_group(far[0])]
+    far_on = [forward(far[0]), forward(after(far[1], left))]
     sent = [project(control, left, [out_weight])]
-    far_on = forward(after(far[1], left))
-    weights = []
-    for n in range(4):
-        one, two = ((near, near_across), (next_shard, next_across))[n // 2]
-        weights.append(four(one[n % 2], two[n % 2], *[keys] * (n % 2)))
-        sent.append(project(control, after(left, sent[-1]), weights[-1]))
-    weights.append(four(far[0], far_across[0], sent[2]))
-    sent.append(project(control, after(left, sent[-1]), weights[-1]))
+    sent.append(project(control, after(left, sent[-1]), near_all))
+    sent.append(project(control, after(left, sent[-1]), next_all))
     came = [swap_tp(each) for each in sent]
-    far[1] = jnp.where(middle, far[1], after(far_on, sent[4]))
-    far_across.append(swap_group(far[1]))
-    stay = attend(0, control, tables, after(queries[0], sent[5], far[1]), keys, values, slots)
-    weights.append(four(far[1], far_across[1], stay))
+    far[0] = jnp.where(middle, far[0], after(far_on[0], sent[0]))
+    far[1] = jnp.where(middle, far[1], after(far_on[1], sent[2]))
+    far_across = [swap_group(part) for part in far]
+    stay = attend(0, control, tables, after(queries[0], sent[2], far[1]), keys, values, slots)
+    far_all = [four(far[n], far_across[n], stay) for n in (0, 1)]
     total = columns * owner_count
     out = project(control, stay, [out_weight], came[0], 10, None, total)
     for n in range(2):
-        out = project(control, stay, weights[n], came[n + 1], 11 + n, out, total)
-    last = project(control, after(left, out), weights[5])
-    stay = after(stay, last)
-    came.append(swap_tp(last))
-    for n in range(2, 6):
-        out = project(control, stay, weights[n], came[n + 1], 11 + n, out, total)
+        sent.append(project(control, after(left, out), far_all[n]))
+        came.append(swap_tp(sent[-1]))
+        out = project(
+            control, after(stay, sent[-1]), (near_all, next_all)[n], came[n + 1], 11 + n, out, total
+        )
+    for n in range(2):
+        out = project(control, stay, far_all[n], came[n + 3], 13 + n, out, total)
     return out
 
 

time: 240 us -> 220 us (0.917)
  waiting for transfers between devices: 110 us -> 97.9 us
  Pallas kernels: 56.2 us -> 50.6 us
  starting transfers between devices: 46.8 us -> 43.6 us
    ppermute x15 -> x16, waiting for transfers between devices: 110 us -> 87 us  [the longest x2 56.2 us: shards(): next_shard = [jnp.where(middle, part, forward(part)) for part in inner]]
    ppermute x6 -> x3, waiting for transfers between devices: 0.02 us -> 8.99 us  [shards(): came = [swap_tp(each) for each in sent]]
    pallas_call x14 -> x10, Pallas kernels: 28.5 us -> 24.3 us  [project(): pl.pallas_call(kernel, out_shape=out_shape, grid_spec=pltpu.PrefetchScala...]
    ppermute x6 -> x3, starting transfers between devices: 7.24 us -> 4.96 us  [shards(): came = [swap_tp(each) for each in sent]]
    ppermute x15 -> x16, starting transfers between devices: 27.2 us -> 25.9 us  [the longest x2 5.59 us: shards(): next_shard = [jnp.where(middle, part, forward(part)) for part in inner]]
    unnamed x21 -> x17, local copies, waits for them, and re-layouts: 5.3 us -> 6.07 us
  transfers between devices with their start and end apart: 36 -> 34, of which waited for: 7 -> 12; matrix products, arithmetic and copies ran while one was open for 2% -> 3% of each run, Pallas kernels for 22% -> 23%
where the time goes in v6:
time: 220 us; the launch traced here: 216 us
  waiting for transfers between devices  97.9 us (44%)
  Pallas kernels  50.6 us (23%)
  starting transfers between devices  43.6 us (20%)
  blocking collectives  10.8 us (5%)
  local copies, waits for them, and re-layouts  8.91 us (4%)
  other arithmetic  3.76 us (2%)
    ppermute x2, waiting for transfers between devices, shards(): next_shard = [jnp.where(middle, part, forward(part)) for part in inner]  56.2 us
    pallas_call x10, Pallas kernels, project(): pl.pallas_call(kernel, out_shape=out_shape, grid_spec=pltpu.PrefetchScala...  24.3 us
    pallas_call x2, Pallas kernels, attend(): pl.pallas_call(functools.partial(attend_kernel, fresh_base, side), out_sh...  19.1 us
    ppermute x2, waiting for transfers between devices, shards(): far = [cross(after(near[0], *next_shard)), cross(after(near[1], pages))]  11.2 us
    all_to_all x1, blocking collectives, shards(): lax.all_to_all(wanted, 'seq', split_axis=0, concat_axis=0, tiled=True)  10.8 us
    ppermute x2, waiting for transfers between devices, shards(): next_across = [swap_group(part) for part in next_shard]  9.7 us
    ppermute x3, waiting for transfers between devices, shards(): came = [swap_tp(each) for each in sent]  8.99 us
    ppermute x1, waiting for transfers between devices, shards(): inner.append(cross(later))  6.51 us
  transfers between devices with their start and end apart: 34, of which 12 were waited for; matrix products, arithmetic and copies ran while one was open for 3% of the time, Pallas kernels for 23%

profile of v6, /device:TPU:16, one launch (start us, length us, event | category | flops | bytes accessed | tf_op | source)
XLA Modules:
  0.0 216.2 jit_solution(806765948375902886)
XLA Ops:
  0.0 1.3 fusion.5
  1.3 1.6 collective-permute-start
  2.9 1.9 collective-permute-start.1
  4.8 2.6 %rank.1 = (s32[128]{0:T(128)}, s32[4,64]{1,0:T(4,128)}) custom-call(s32[1,128]{1,0:T(1,128)} %owner.1, s32[1,128]{1,0:T(1,128)} %page.1), custom_call_target="tpu_custom_call" | custom-call | flops 3000000000 | bytes 1000 | tf_op jit(solution)/shard_map/rank/pallas_call | solution.py:49
  7.5 10.8 %all_to_all.17 = s32[4,1,64]{2,1,0:T(1,128)S(1)} all-to-all(s32[4,1,64]{2,1,0:T(1,128)} %bitcast.40), channel_id=1, replica_groups=mesh['group'=2,'seq'=4,'tp'=2,'role'=2] {'seq'}, dimensions={0} | all-to-all | bytes 2048 | tf_op jit(solution)/shard_map/all_to_all | solution.py:377
  18.3 2.2 %collective-permute-start.3 = (bf16[512,512]{1,0:T(8,128)(2,1)S(1)}, bf16[512,512]{1,0:T(8,128)(2,1)S(1)}, u32[]{:S(2)}, u32[]{:S(2)}) collective-permute-start(bf16[512,512]{1,0:T(8,128)(2,1)S(1)} %get-tuple-element.38), channel_id=1, source_target_pairs={{4,8},{8,4},{5,9},{9,5},{6,10},{10,6},{7,11},{11,7},{20,24},{24,20... | collective-permute-start | bytes 1572872 | tf_op jit(solution)/shard_map/ppermute | solution.py:382
  20.6 2.2 %copy-done.2 = bf16[1,256,2,16,256]{4,3,2,1,0:T(8,128)(2,1)S(1)} copy-done((bf16[1,256,2,16,256]{4,3,2,1,0:T(8,128)(2,1)S(1)}, bf16[1,256,2,16,256]{4,3,2,1,0:T(8,128)(2,1)}, u32[]{:S(2)}) %copy-start.2) | copy-done | bytes 4194328
  22.7 1.3 pick.1
  24.0 2.0 copy-done
  26.1 6.5 %collective-permute-done.3 = bf16[512,512]{1,0:T(8,128)(2,1)S(1)} collective-permute-done((bf16[512,512]{1,0:T(8,128)(2,1)S(1)}, bf16[512,512]{1,0:T(8,128)(2,1)S(1)}, u32[]{:S(2)}, u32[]{:S(2)}) %collective-permute-start.3) | collective-permute-done | bytes 524320 | tf_op jit(solution)/shard_map/ppermute | solution.py:382
  33.0 5.9 %all-to-all-start.1 = ((bf16[4,64,2,16,256]{4,3,2,1,0:T(8,128)(2,1)}), bf16[4,64,2,16,256]{4,3,2,1,0:T(8,128)(2,1)}, u32[]{:S(2)}, u32[]{:S(2)}) async-start(bf16[4,64,2,16,256]{4,3,2,1,0:T(8,128)(2,1)} %copy-done), calls=%async_computation.1 | async-start | bytes 8388608 | tf_op jit(solution)/shard_map/all_to_all | solution.py:388
  38.9 4.3 %collective-permute-start.4 = (bf16[512,512]{1,0:T(8,128)(2,1)S(1)}, bf16[512,512]{1,0:T(8,128)(2,1)}, u32[]{:S(2)}, u32[]{:S(2)}) collective-permute-start(bf16[512,512]{1,0:T(8,128)(2,1)S(1)} %collective-permute-done.1), channel_id=1, source_target_pairs={{4,0},{8,12},{5,1},{9,13},{6,2},{10,14},{7,3},{11,15},{20,16},{24,... | collective-permute-start | bytes 1572872 | tf_op jit(solution)/shard_map/ppermute | solution.py:415
  43.2 1.5 collective-permute-start.7
  44.7 1.3 collective-permute-start.5
  46.6 51.5 %collective-permute-done.4 = bf16[512,512]{1,0:T(8,128)(2,1)} collective-permute-done((bf16[512,512]{1,0:T(8,128)(2,1)S(1)}, bf16[512,512]{1,0:T(8,128)(2,1)}, u32[]{:S(2)}, u32[]{:S(2)}) %collective-permute-start.4) | collective-permute-done | bytes 524320 | tf_op jit(solution)/shard_map/ppermute | solution.py:415
  98.2 1.6 collective-permute-start.13
  101.0 1.0 copy.22
  102.8 4.8 %collective-permute-done.5 = bf16[512,512]{1,0:T(8,128)(2,1)S(1)} collective-permute-done((bf16[512,512]{1,0:T(8,128)(2,1)S(1)}, bf16[512,512]{1,0:T(8,128)(2,1)S(1)}, u32[]{:S(2)}, u32[]{:S(2)}) %collective-permute-start.5) | collective-permute-done | bytes 524320 | tf_op jit(solution)/shard_map/ppermute | solution.py:415
  109.0 1.5 collective-permute-start.16
  113.3 9.7 %collective-permute-done.16.refs_5_ = bf16[512,512]{1,0:T(8,128)(2,1)} collective-permute-done((bf16[512,512]{1,0:T(8,128)(2,1)S(1)}, bf16[512,512]{1,0:T(8,128)(2,1)}, u32[]{:S(2)}, u32[]{:S(2)}) %collective-permute-start.16) | collective-permute-done | bytes 524320 | tf_op jit(solution)/shard_map/ppermute | solution.py:416
  123.0 1.9 collective-permute-start.6
  126.1 1.9 all-to-all-done.1
  128.0 11.2 %collective-permute-done.6 = bf16[512,512]{1,0:T(8,128)(2,1)} collective-permute-done((bf16[512,512]{1,0:T(8,128)(2,1)S(1)}, bf16[512,512]{1,0:T(8,128)(2,1)}, u32[]{:S(2)}, u32[]{:S(2)}) %collective-permute-start.6) | collective-permute-done | bytes 524320 | tf_op jit(solution)/shard_map/ppermute | solution.py:419
  139.1 1.3 collective-permute-start.22
  140.5 3.4 %collective-permute-start.19 = (bf16[512,512]{1,0:T(8,128)(2,1)S(1)}, bf16[512,512]{1,0:T(8,128)(2,1)S(1)}, u32[]{:S(2)}, u32[]{:S(2)}) collective-permute-start(bf16[512,512]{1,0:T(8,128)(2,1)S(1)} %collective-permute-done.2.refs_4_), channel_id=1, source_target_pairs={{4,8},{8,4},{5,9},{9,5},{6,10},{10,6},{7,11},{11,7},{20,24},{24,20... | collective-permute-start | bytes 1572872 | tf_op jit(solution)/shard_map/ppermute | solution.py:419
  143.9 3.3 %place.1 = (bf16[2,3072,128]{2,1,0:T(8,128)(2,1)S(1)}, bf16[2,3072,256]{2,1,0:T(8,128)(2,1)S(1)}) custom-call(s32[128]{0:T(128)S(1)} %copy-done.4, bf16[256,2,16,256]{3,2,1,0:T(8,128)(2,1)} %bitcast.21.pages, bf16[384,512]{1,0:T(8,128)(2,1)S(1)} %bitcast.29), custom_call_target="tpu_custom_call" | custom-call | flops 3000000000 | bytes 1000 | tf_op jit(solution)/shard_map/place/pallas_call | solution.py:95
  147.2 8.9 %attend.2.left = bf16[4,192,512]{2,1,0:T(8,128)(2,1)S(1)} custom-call(s32[15]{0:T(128)S(1)} %stack.63.control, s32[6]{0:T(128)S(1)} %get-tuple-element.70.hist_at, s32[6]{0:T(128)S(1)} %get-tuple-element.69.hist_steps, s32[6]{0:T(128)S(1)} %get-tuple-element.64.fresh_at, s32[6]{0:T(128)S(1)} %get-tuple-element.63.fresh_steps, ...), custom_call_target="tpu_custom_call" | custom-call | flops 16000000000 | bytes 1000 | tf_op jit(solution)/shard_map/attend/pallas_call | solution.py:221
  156.1 1.5 project.5
  157.6 2.9 %collective-permute-start.21 = (bf16[192,1024]{1,0:T(8,128)(2,1)S(1)}, bf16[192,1024]{1,0:T(8,128)(2,1)S(1)}, u32[]{:S(2)}, u32[]{:S(2)}) collective-permute-start(bf16[192,1024]{1,0:T(8,128)(2,1)S(1)} %project.5), channel_id=1, source_target_pairs={{0,2},{2,0},{1,3},{3,1},{4,6},{6,4},{5,7},{7,5},{8,10},{10,8},{9,1... | collective-permute-start | bytes 1179656 | tf_op jit(solution)/shard_map/ppermute | solution.py:427
  160.6 3.4 %project.6 = bf16[192,1024]{1,0:T(8,128)(2,1)S(1)} custom-call(s32[15]{0:T(128)S(1)} %stack.63.control, bf16[4,192,512]{2,1,0:T(8,128)(2,1)S(1)} %attend.2.left, bf16[512,512]{1,0:T(8,128)(2,1)S(1)} %collective-permute-done.refs_0_, bf16[512,512]{1,0:T(8,128)(2,1)} %collective-permute-done.7.refs_1_, bf16[512,512]{1,0:T(8,128)(2,1)} %collective-permute-done.8.refs_2_, ...), custom_call_target="tpu_custom_call" | custom-call | flops 3000000000 | bytes 1000 | tf_op jit(solution)/shard_map/project/pallas_call | solution.py:296
  164.0 1.5 collective-permute-start.20
  165.5 1.1 broadcast_select_fusion.refs_0_
  166.6 2.3 %collective-permute-start.23 = (bf16[512,512]{1,0:T(8,128)(2,1)S(1)}, bf16[512,512]{1,0:T(8,128)(2,1)S(1)}, u32[]{:S(2)}, u32[]{:S(2)}) collective-permute-start(bf16[512,512]{1,0:T(8,128)(2,1)S(1)} %broadcast_select_fusion.refs_0_), channel_id=1, source_target_pairs={{0,16},{16,0},{1,17},{17,1},{2,18},{18,2},{3,19},{19,3},{4,20},{20... | collective-permute-start | bytes 1572872 | tf_op jit(solution)/shard_map/ppermute | solution.py:430
  168.9 3.2 %project.7 = bf16[192,1024]{1,0:T(8,128)(2,1)S(1)} custom-call(s32[15]{0:T(128)S(1)} %stack.63.control, bf16[4,192,512]{2,1,0:T(8,128)(2,1)S(1)} %attend.2.left, bf16[512,512]{1,0:T(8,128)(2,1)S(1)} %broadcast_select_fusion.3.refs_0_, bf16[512,512]{1,0:T(8,128)(2,1)S(1)} %collective-permute-done.13.refs_1_, ...), custom_call_target="tpu_custom_call" | custom-call | flops 3000000000 | bytes 1000 | tf_op jit(solution)/shard_map/project/pallas_call | solution.py:296
  172.1 1.2 collective-permute-done.20
  173.3 2.3 %collective-permute-start.27 = (bf16[512,512]{1,0:T(8,128)(2,1)S(1)}, bf16[512,512]{1,0:T(8,128)(2,1)S(1)}, u32[]{:S(2)}, u32[]{:S(2)}) collective-permute-start(bf16[512,512]{1,0:T(8,128)(2,1)S(1)} %broadcast_select_fusion.1.refs_0_), channel_id=1, source_target_pairs={{0,16},{16,0},{1,17},{17,1},{2,18},{18,2},{3,19},{19,3},{4,20},{20... | collective-permute-start | bytes 1572872 | tf_op jit(solution)/shard_map/ppermute | solution.py:430
  175.6 10.3 %attend.3.left = bf16[4,192,512]{2,1,0:T(8,128)(2,1)S(1)} custom-call(s32[15]{0:T(128)S(1)} %stack.63.control, s32[6]{0:T(128)S(1)} %get-tuple-element.70.hist_at, s32[6]{0:T(128)S(1)} %get-tuple-element.69.hist_steps, s32[6]{0:T(128)S(1)} %get-tuple-element.64.fresh_at, s32[6]{0:T(128)S(1)} %get-tuple-element.63.fresh_steps, ...), custom_call_target="tpu_custom_call" | custom-call | flops 16000000000 | bytes 1000 | tf_op jit(solution)/shard_map/attend/pallas_call | solution.py:221
  186.5 2.0 collective-permute-start.32
  188.5 2.3 %finish.5.refs_8_ = bf16[1,192,4096]{2,1,0:T(8,128)(2,1)} custom-call(s32[15]{0:T(128)S(1)} %stack.63.control, bf16[4,192,512]{2,1,0:T(8,128)(2,1)S(1)} %attend.3.left, bf16[192,1024]{1,0:T(8,128)(2,1)S(1)} %collective-permute-done.21.came, bf16[2048,1024]{1,0:T(8,128)(2,1)S(1)} %copy-done.1), custom_call_target="tpu_custom_call" | custom-call | flops 3000000000 | bytes 1000 | tf_op jit(solution)/shard_map/finish/pallas_call | solution.py:296
  191.3 1.1 project.8
  192.5 5.9 %collective-permute-done.26.came = bf16[192,1024]{1,0:T(8,128)(2,1)S(1)} collective-permute-done((bf16[192,1024]{1,0:T(8,128)(2,1)S(1)}, bf16[192,1024]{1,0:T(8,128)(2,1)S(1)}, u32[]{:S(2)}, u32[]{:S(2)}) %collective-permute-start.26) | collective-permute-done | bytes 393248 | tf_op jit(solution)/shard_map/ppermute | solution.py:427
  198.4 4.1 %finish.6.refs_8_ = bf16[1,192,4096]{2,1,0:T(8,128)(2,1)} custom-call(s32[15]{0:T(128)S(1)} %stack.63.control, bf16[4,192,512]{2,1,0:T(8,128)(2,1)S(1)} %attend.3.left, bf16[192,1024]{1,0:T(8,128)(2,1)S(1)} %collective-permute-done.26.came, bf16[512,512]{1,0:T(8,128)(2,1)S(1)} %collective-permute-done.refs_0_, ...), custom_call_target="tpu_custom_call", output_to_operand_aliasing={{}: (11, {})} | custom-call | flops 3000000000 | bytes 1000 | tf_op jit(solution)/shard_map/finish/pallas_call | solution.py:296
  202.6 1.1 project.9
  203.8 3.1 %collective-permute-done.32.came = bf16[192,1024]{1,0:T(8,128)(2,1)S(1)} collective-permute-done((bf16[192,1024]{1,0:T(8,128)(2,1)S(1)}, bf16[192,1024]{1,0:T(8,128)(2,1)S(1)}, u32[]{:S(2)}, u32[]{:S(2)}) %collective-permute-start.32) | collective-permute-done | bytes 393248 | tf_op jit(solution)/shard_map/ppermute | solution.py:427
  206.9 4.0 %finish.7.refs_4_ = bf16[1,192,4096]{2,1,0:T(8,128)(2,1)} custom-call(s32[15]{0:T(128)S(1)} %stack.63.control, bf16[4,192,512]{2,1,0:T(8,128)(2,1)S(1)} %attend.3.left, bf16[192,1024]{1,0:T(8,128)(2,1)S(1)} %collective-permute-done.32.came, bf16[512,512]{1,0:T(8,128)(2,1)S(1)} %broadcast_select_fusion.3.refs_0_, ...), custom_call_target="tpu_custom_call", output_to_operand_aliasing={{}: (11, {})} | custom-call | flops 3000000000 | bytes 1000 | tf_op jit(solution)/shard_map/finish/pallas_call | solution.py:296
  211.1 1.8 finish.8.refs_4_
  212.9 1.5 collective-permute-done.30.came
  214.4 1.8 finish.9
  (72 shorter events, 9.9 us)
Async XLA Ops:
  1.3 17.0 %collective-permute-start = (bf16[512,512]{1,0:T(8,128)(2,1)S(1)}, bf16[512,512]{1,0:T(8,128)(2,1)S(1)}, u32[]{:S(2)}, u32[]{:S(2)}) collective-permute-start(bf16[512,512]{1,0:T(8,128)(2,1)S(1)} %get-tuple-element.68), channel_id=1, source_target_pairs={{0,4},{4,0},{8,12},{12,8},{1,5},{5,1},{9,13},{13,9},{2,6},{6,2},{1... | collective-permute-start | bytes 1572872 | tf_op jit(solution)/shard_map/ppermute | solution.py:374
  2.9 15.4 %collective-permute-start.1 = (bf16[512,512]{1,0:T(8,128)(2,1)S(1)}, bf16[512,512]{1,0:T(8,128)(2,1)S(1)}, u32[]{:S(2)}, u32[]{:S(2)}) collective-permute-start(bf16[512,512]{1,0:T(8,128)(2,1)S(1)} %get-tuple-element.68), channel_id=1, source_target_pairs={{4,8},{8,4},{5,9},{9,5},{6,10},{10,6},{7,11},{11,7},{20,24},{24,20... | collective-permute-start | bytes 1572872 | tf_op jit(solution)/shard_map/ppermute | solution.py:374
  18.3 14.3 %collective-permute-start.3 = (bf16[512,512]{1,0:T(8,128)(2,1)S(1)}, bf16[512,512]{1,0:T(8,128)(2,1)S(1)}, u32[]{:S(2)}, u32[]{:S(2)}) collective-permute-start(bf16[512,512]{1,0:T(8,128)(2,1)S(1)} %get-tuple-element.38), channel_id=1, source_target_pairs={{4,8},{8,4},{5,9},{9,5},{6,10},{10,6},{7,11},{11,7},{20,24},{24,20... | collective-permute-start | bytes 1572872 | tf_op jit(solution)/shard_map/ppermute | solution.py:382
  20.5 12.5 %collective-permute-start.2 = (bf16[512,512]{1,0:T(8,128)(2,1)S(1)}, bf16[512,512]{1,0:T(8,128)(2,1)S(1)}, u32[]{:S(2)}, u32[]{:S(2)}) collective-permute-start(bf16[512,512]{1,0:T(8,128)(2,1)S(1)} %get-tuple-element.38), channel_id=1, source_target_pairs={{0,4},{4,0},{8,12},{12,8},{1,5},{5,1},{9,13},{13,9},{2,6},{6,2},{1... | collective-permute-start | bytes 1572872 | tf_op jit(solution)/shard_map/ppermute | solution.py:381
  20.6 2.2 %copy-start.2 = (bf16[1,256,2,16,256]{4,3,2,1,0:T(8,128)(2,1)S(1)}, bf16[1,256,2,16,256]{4,3,2,1,0:T(8,128)(2,1)}, u32[]{:S(2)}) copy-start(bf16[1,256,2,16,256]{4,3,2,1,0:T(8,128)(2,1)} %param.11) | copy-start | bytes 12582916
  24.0 2.0 copy-start
  33.0 95.0 %all-to-all-start.1 = ((bf16[4,64,2,16,256]{4,3,2,1,0:T(8,128)(2,1)}), bf16[4,64,2,16,256]{4,3,2,1,0:T(8,128)(2,1)}, u32[]{:S(2)}, u32[]{:S(2)}) async-start(bf16[4,64,2,16,256]{4,3,2,1,0:T(8,128)(2,1)} %copy-done), calls=%async_computation.1 | async-start | bytes 8388608 | tf_op jit(solution)/shard_map/all_to_all | solution.py:388
  38.9 60.8 %copy-start.6 = (s32[1,384]{1,0:T(1,128)S(1)}, s32[1,384]{1,0:T(1,128)}, u32[]{:S(2)}) copy-start(s32[1,384]{1,0:T(1,128)} %param.13) | copy-start | bytes 4612
  38.9 59.1 %collective-permute-start.4 = (bf16[512,512]{1,0:T(8,128)(2,1)S(1)}, bf16[512,512]{1,0:T(8,128)(2,1)}, u32[]{:S(2)}, u32[]{:S(2)}) collective-permute-start(bf16[512,512]{1,0:T(8,128)(2,1)S(1)} %collective-permute-done.1), channel_id=1, source_target_pairs={{4,0},{8,12},{5,1},{9,13},{6,2},{10,14},{7,3},{11,15},{20,16},{24,... | collective-permute-start | bytes 1572872 | tf_op jit(solution)/shard_map/ppermute | solution.py:415
  43.2 59.0 %collective-permute-start.7 = (bf16[512,512]{1,0:T(8,128)(2,1)S(1)}, bf16[512,512]{1,0:T(8,128)(2,1)}, u32[]{:S(2)}, u32[]{:S(2)}) collective-permute-start(bf16[512,512]{1,0:T(8,128)(2,1)S(1)} %collective-permute-done.refs_0_), channel_id=1, source_target_pairs={{0,16},{16,0},{1,17},{17,1},{2,18},{18,2},{3,19},{19,3},{4,20},{20... | collective-permute-start | bytes 1572872 | tf_op jit(solution)/shard_map/ppermute | solution.py:414
  44.7 62.8 %collective-permute-start.5 = (bf16[512,512]{1,0:T(8,128)(2,1)S(1)}, bf16[512,512]{1,0:T(8,128)(2,1)S(1)}, u32[]{:S(2)}, u32[]{:S(2)}) collective-permute-start(bf16[512,512]{1,0:T(8,128)(2,1)S(1)} %collective-permute-done.3), channel_id=1, source_target_pairs={{4,0},{8,12},{5,1},{9,13},{6,2},{10,14},{7,3},{11,15},{20,16},{24,... | collective-permute-start | bytes 1572872 | tf_op jit(solution)/shard_map/ppermute | solution.py:415
  46.0 62.4 %collective-permute-start.10 = (bf16[512,512]{1,0:T(8,128)(2,1)S(1)}, bf16[512,512]{1,0:T(8,128)(2,1)}, u32[]{:S(2)}, u32[]{:S(2)}) collective-permute-start(bf16[512,512]{1,0:T(8,128)(2,1)S(1)} %collective-permute-done.2.refs_4_), channel_id=1, source_target_pairs={{0,16},{16,0},{1,17},{17,1},{2,18},{18,2},{3,19},{19,3},{4,20},{20... | collective-permute-start | bytes 1572872 | tf_op jit(solution)/shard_map/ppermute | solution.py:414
  98.1 12.4 %copy-start.7 = (s32[1,128]{1,0:T(1,128)S(1)}, s32[1,128]{1,0:T(1,128)}, u32[]{:S(2)}) copy-start(s32[1,128]{1,0:T(1,128)} %param.14) | copy-start | bytes 1540
  98.1 45.7 %copy-start.4 = (s32[128]{0:T(128)S(1)}, s32[128]{0:T(128)}, u32[]{:S(2)}) copy-start(s32[128]{0:T(128)} %get-tuple-element.33.position) | copy-start | bytes 1540
  98.2 10.9 %collective-permute-start.13 = (bf16[512,512]{1,0:T(8,128)(2,1)S(1)}, bf16[512,512]{1,0:T(8,128)(2,1)S(1)}, u32[]{:S(2)}, u32[]{:S(2)}) collective-permute-start(bf16[512,512]{1,0:T(8,128)(2,1)S(1)} %broadcast_select_fusion.3.refs_0_), channel_id=1, source_target_pairs={{0,16},{16,0},{1,17},{17,1},{2,18},{18,2},{3,19},{19,3},{4,20},{20... | collective-permute-start | bytes 1572872 | tf_op jit(solution)/shard_map/ppermute | solution.py:416
  102.2 22.8 %collective-permute-start.8 = (bf16[512,512]{1,0:T(8,128)(2,1)S(1)}, bf16[512,512]{1,0:T(8,128)(2,1)}, u32[]{:S(2)}, u32[]{:S(2)}) collective-permute-start(bf16[512,512]{1,0:T(8,128)(2,1)S(1)} %collective-permute-done.refs_0_), channel_id=1, source_target_pairs={{0,1},{1,0},{2,3},{3,2},{4,5},{5,4},{6,7},{7,6},{8,9},{9,8},{10,11... | collective-permute-start | bytes 1572872 | tf_op jit(solution)/shard_map/ppermute | solution.py:412
  102.3 22.8 %collective-permute-start.11 = (bf16[512,512]{1,0:T(8,128)(2,1)S(1)}, bf16[512,512]{1,0:T(8,128)(2,1)}, u32[]{:S(2)}, u32[]{:S(2)}) collective-permute-start(bf16[512,512]{1,0:T(8,128)(2,1)S(1)} %collective-permute-done.2.refs_4_), channel_id=1, source_target_pairs={{0,1},{1,0},{2,3},{3,2},{4,5},{5,4},{6,7},{7,6},{8,9},{9,8},{10,11... | collective-permute-start | bytes 1572872 | tf_op jit(solution)/shard_map/ppermute | solution.py:412
  107.5 0.8 copy-start.5
  108.3 17.2 %collective-permute-start.14 = (bf16[512,512]{1,0:T(8,128)(2,1)S(1)}, bf16[512,512]{1,0:T(8,128)(2,1)}, u32[]{:S(2)}, u32[]{:S(2)}) collective-permute-start(bf16[512,512]{1,0:T(8,128)(2,1)S(1)} %broadcast_select_fusion.3.refs_0_), channel_id=1, source_target_pairs={{0,1},{1,0},{2,3},{3,2},{4,5},{5,4},{6,7},{7,6},{8,9},{9,8},{10,11... | collective-permute-start | bytes 1572872 | tf_op jit(solution)/shard_map/ppermute | solution.py:412
  108.4 17.2 %collective-permute-start.9 = (bf16[512,512]{1,0:T(8,128)(2,1)}, bf16[512,512]{1,0:T(8,128)(2,1)}, u32[]{:S(2)}, u32[]{:S(2)}) collective-permute-start(bf16[512,512]{1,0:T(8,128)(2,1)} %collective-permute-done.7.refs_1_), channel_id=1, source_target_pairs={{0,1},{1,0},{2,3},{3,2},{4,5},{5,4},{6,7},{7,6},{8,9},{9,8},{10,11... | collective-permute-start | bytes 1572872 | tf_op jit(solution)/shard_map/ppermute | solution.py:412
  109.0 14.0 %collective-permute-start.16 = (bf16[512,512]{1,0:T(8,128)(2,1)S(1)}, bf16[512,512]{1,0:T(8,128)(2,1)}, u32[]{:S(2)}, u32[]{:S(2)}) collective-permute-start(bf16[512,512]{1,0:T(8,128)(2,1)S(1)} %broadcast_select_fusion.2.refs_4_), channel_id=1, source_target_pairs={{0,16},{16,0},{1,17},{17,1},{2,18},{18,2},{3,19},{19,3},{4,20},{20... | collective-permute-start | bytes 1572872 | tf_op jit(solution)/shard_map/ppermute | solution.py:416
  123.0 16.1 %collective-permute-start.6 = (bf16[512,512]{1,0:T(8,128)(2,1)S(1)}, bf16[512,512]{1,0:T(8,128)(2,1)}, u32[]{:S(2)}, u32[]{:S(2)}) collective-permute-start(bf16[512,512]{1,0:T(8,128)(2,1)S(1)} %collective-permute-done.refs_0_), channel_id=1, source_target_pairs={{4,8},{8,4},{5,9},{9,5},{6,10},{10,6},{7,11},{11,7},{20,24},{24,20... | collective-permute-start | bytes 1572872 | tf_op jit(solution)/shard_map/ppermute | solution.py:419
  125.0 15.5 %collective-permute-start.17 = (bf16[512,512]{1,0:T(8,128)(2,1)S(1)}, bf16[512,512]{1,0:T(8,128)(2,1)}, u32[]{:S(2)}, u32[]{:S(2)}) collective-permute-start(bf16[512,512]{1,0:T(8,128)(2,1)S(1)} %broadcast_select_fusion.2.refs_4_), channel_id=1, source_target_pairs={{0,1},{1,0},{2,3},{3,2},{4,5},{5,4},{6,7},{7,6},{8,9},{9,8},{10,11... | collective-permute-start | bytes 1572872 | tf_op jit(solution)/shard_map/ppermute | solution.py:412
  125.0 15.4 %collective-permute-start.12 = (bf16[512,512]{1,0:T(8,128)(2,1)}, bf16[512,512]{1,0:T(8,128)(2,1)}, u32[]{:S(2)}, u32[]{:S(2)}) collective-permute-start(bf16[512,512]{1,0:T(8,128)(2,1)} %collective-permute-done.10.refs_5_), channel_id=1, source_target_pairs={{0,1},{1,0},{2,3},{3,2},{4,5},{5,4},{6,7},{7,6},{8,9},{9,8},{10,11... | collective-permute-start | bytes 1572872 | tf_op jit(solution)/shard_map/ppermute | solution.py:412
  125.5 14.9 %collective-permute-start.15 = (bf16[512,512]{1,0:T(8,128)(2,1)S(1)}, bf16[512,512]{1,0:T(8,128)(2,1)}, u32[]{:S(2)}, u32[]{:S(2)}) collective-permute-start(bf16[512,512]{1,0:T(8,128)(2,1)S(1)} %collective-permute-done.13.refs_1_), channel_id=1, source_target_pairs={{0,1},{1,0},{2,3},{3,2},{4,5},{5,4},{6,7},{7,6},{8,9},{9,8},{10,11... | collective-permute-start | bytes 1572872 | tf_op jit(solution)/shard_map/ppermute | solution.py:412
  125.6 14.9 %collective-permute-start.18 = (bf16[512,512]{1,0:T(8,128)(2,1)}, bf16[512,512]{1,0:T(8,128)(2,1)}, u32[]{:S(2)}, u32[]{:S(2)}) collective-permute-start(bf16[512,512]{1,0:T(8,128)(2,1)} %collective-permute-done.16.refs_5_), channel_id=1, source_target_pairs={{0,1},{1,0},{2,3},{3,2},{4,5},{5,4},{6,7},{7,6},{8,9},{9,8},{10,11... | collective-permute-start | bytes 1572872 | tf_op jit(solution)/shard_map/ppermute | solution.py:412
  139.1 24.8 %collective-permute-start.22 = (bf16[512,512]{1,0:T(8,128)(2,1)}, bf16[512,512]{1,0:T(8,128)(2,1)S(1)}, u32[]{:S(2)}, u32[]{:S(2)}) collective-permute-start(bf16[512,512]{1,0:T(8,128)(2,1)} %collective-permute-done.6), channel_id=1, source_target_pairs={{4,0},{8,12},{5,1},{9,13},{6,2},{10,14},{7,3},{11,15},{20,16},{24,... | collective-permute-start | bytes 1572872 | tf_op jit(solution)/shard_map/ppermute | solution.py:423
  140.5 23.5 %collective-permute-start.19 = (bf16[512,512]{1,0:T(8,128)(2,1)S(1)}, bf16[512,512]{1,0:T(8,128)(2,1)S(1)}, u32[]{:S(2)}, u32[]{:S(2)}) collective-permute-start(bf16[512,512]{1,0:T(8,128)(2,1)S(1)} %collective-permute-done.2.refs_4_), channel_id=1, source_target_pairs={{4,8},{8,4},{5,9},{9,5},{6,10},{10,6},{7,11},{11,7},{20,24},{24,20... | collective-permute-start | bytes 1572872 | tf_op jit(solution)/shard_map/ppermute | solution.py:419
  143.9 3.3 %copy-start.3 = (bf16[1,384,2048]{2,1,0:T(8,128)(2,1)S(1)}, bf16[1,384,2048]{2,1,0:T(8,128)(2,1)}, u32[]{:S(2)}) copy-start(bf16[1,384,2048]{2,1,0:T(8,128)(2,1)} %param.9) | copy-start | bytes 4718596
  147.2 8.9 %copy-start.1 = (bf16[2048,1024]{1,0:T(8,128)(2,1)S(1)}, bf16[2048,1024]{1,0:T(8,128)(2,1)}, u32[]{:S(2)}) copy-start(bf16[2048,1024]{1,0:T(8,128)(2,1)} %refs_0_.3) | copy-start | bytes 12582916
  157.6 28.8 %collective-permute-start.21 = (bf16[192,1024]{1,0:T(8,128)(2,1)S(1)}, bf16[192,1024]{1,0:T(8,128)(2,1)S(1)}, u32[]{:S(2)}, u32[]{:S(2)}) collective-permute-start(bf16[192,1024]{1,0:T(8,128)(2,1)S(1)} %project.5), channel_id=1, source_target_pairs={{0,2},{2,0},{1,3},{3,1},{4,6},{6,4},{5,7},{7,5},{8,10},{10,8},{9,1... | collective-permute-start | bytes 1179656 | tf_op jit(solution)/shard_map/ppermute | solution.py:427
  164.0 9.3 %collective-permute-start.20 = (bf16[512,512]{1,0:T(8,128)(2,1)S(1)}, bf16[512,512]{1,0:T(8,128)(2,1)S(1)}, u32[]{:S(2)}, u32[]{:S(2)}) collective-permute-start(bf16[512,512]{1,0:T(8,128)(2,1)S(1)} %collective-permute-done.19), channel_id=1, source_target_pairs={{4,0},{8,12},{5,1},{9,13},{6,2},{10,14},{7,3},{11,15},{20,16},{24,... | collective-permute-start | bytes 1572872 | tf_op jit(solution)/shard_map/ppermute | solution.py:423
  166.6 19.3 %collective-permute-start.23 = (bf16[512,512]{1,0:T(8,128)(2,1)S(1)}, bf16[512,512]{1,0:T(8,128)(2,1)S(1)}, u32[]{:S(2)}, u32[]{:S(2)}) collective-permute-start(bf16[512,512]{1,0:T(8,128)(2,1)S(1)} %broadcast_select_fusion.refs_0_), channel_id=1, source_target_pairs={{0,16},{16,0},{1,17},{17,1},{2,18},{18,2},{3,19},{19,3},{4,20},{20... | collective-permute-start | bytes 1572872 | tf_op jit(solution)/shard_map/ppermute | solution.py:430
  173.3 17.5 %collective-permute-start.27 = (bf16[512,512]{1,0:T(8,128)(2,1)S(1)}, bf16[512,512]{1,0:T(8,128)(2,1)S(1)}, u32[]{:S(2)}, u32[]{:S(2)}) collective-permute-start(bf16[512,512]{1,0:T(8,128)(2,1)S(1)} %broadcast_select_fusion.1.refs_0_), channel_id=1, source_target_pairs={{0,16},{16,0},{1,17},{17,1},{2,18},{18,2},{3,19},{19,3},{4,20},{20... | collective-permute-start | bytes 1572872 | tf_op jit(solution)/shard_map/ppermute | solution.py:430
  185.9 4.9 %collective-permute-start.25 = (bf16[512,512]{1,0:T(8,128)(2,1)S(1)}, bf16[512,512]{1,0:T(8,128)(2,1)S(1)}, u32[]{:S(2)}, u32[]{:S(2)}) collective-permute-start(bf16[512,512]{1,0:T(8,128)(2,1)S(1)} %collective-permute-done.23.refs_1_), channel_id=1, source_target_pairs={{0,1},{1,0},{2,3},{3,2},{4,5},{5,4},{6,7},{7,6},{8,9},{9,8},{10,11... | collective-permute-start | bytes 1572872 | tf_op jit(solution)/shard_map/ppermute | solution.py:412
  186.0 5.3 %collective-permute-start.24 = (bf16[512,512]{1,0:T(8,128)(2,1)S(1)}, bf16[512,512]{1,0:T(8,128)(2,1)S(1)}, u32[]{:S(2)}, u32[]{:S(2)}) collective-permute-start(bf16[512,512]{1,0:T(8,128)(2,1)S(1)} %broadcast_select_fusion.refs_0_), channel_id=1, source_target_pairs={{0,1},{1,0},{2,3},{3,2},{4,5},{5,4},{6,7},{7,6},{8,9},{9,8},{10,11... | collective-permute-start | bytes 1572872 | tf_op jit(solution)/shard_map/ppermute | solution.py:412
  186.5 12.0 %collective-permute-start.26 = (bf16[192,1024]{1,0:T(8,128)(2,1)S(1)}, bf16[192,1024]{1,0:T(8,128)(2,1)S(1)}, u32[]{:S(2)}, u32[]{:S(2)}) collective-permute-start(bf16[192,1024]{1,0:T(8,128)(2,1)S(1)} %project.6), channel_id=1, source_target_pairs={{0,2},{2,0},{1,3},{3,1},{4,6},{6,4},{5,7},{7,5},{8,10},{10,8},{9,1... | collective-permute-start | bytes 1179656 | tf_op jit(solution)/shard_map/ppermute | solution.py:427
  186.5 20.4 %collective-permute-start.32 = (bf16[192,1024]{1,0:T(8,128)(2,1)S(1)}, bf16[192,1024]{1,0:T(8,128)(2,1)S(1)}, u32[]{:S(2)}, u32[]{:S(2)}) collective-permute-start(bf16[192,1024]{1,0:T(8,128)(2,1)S(1)} %project.7), channel_id=1, source_target_pairs={{0,2},{2,0},{1,3},{3,1},{4,6},{6,4},{5,7},{7,5},{8,10},{10,8},{9,1... | collective-permute-start | bytes 1179656 | tf_op jit(solution)/shard_map/ppermute | solution.py:427
  190.8 11.8 %collective-permute-start.28 = (bf16[512,512]{1,0:T(8,128)(2,1)S(1)}, bf16[512,512]{1,0:T(8,128)(2,1)S(1)}, u32[]{:S(2)}, u32[]{:S(2)}) collective-permute-start(bf16[512,512]{1,0:T(8,128)(2,1)S(1)} %broadcast_select_fusion.1.refs_0_), channel_id=1, source_target_pairs={{0,1},{1,0},{2,3},{3,2},{4,5},{5,4},{6,7},{7,6},{8,9},{9,8},{10,11... | collective-permute-start | bytes 1572872 | tf_op jit(solution)/shard_map/ppermute | solution.py:412
  190.8 11.8 %collective-permute-start.29 = (bf16[512,512]{1,0:T(8,128)(2,1)S(1)}, bf16[512,512]{1,0:T(8,128)(2,1)S(1)}, u32[]{:S(2)}, u32[]{:S(2)}) collective-permute-start(bf16[512,512]{1,0:T(8,128)(2,1)S(1)} %collective-permute-done.27.refs_1_), channel_id=1, source_target_pairs={{0,1},{1,0},{2,3},{3,2},{4,5},{5,4},{6,7},{7,6},{8,9},{9,8},{10,11... | collective-permute-start | bytes 1572872 | tf_op jit(solution)/shard_map/ppermute | solution.py:412
  192.4 18.7 %collective-permute-start.31 = (bf16[192,512]{1,0:T(8,128)(2,1)S(1)}, bf16[192,512]{1,0:T(8,128)(2,1)S(1)}, u32[]{:S(2)}, u32[]{:S(2)}) collective-permute-start(bf16[192,512]{1,0:T(8,128)(2,1)S(1)} %project.8), channel_id=1, source_target_pairs={{0,2},{2,0},{1,3},{3,1},{4,6},{6,4},{5,7},{7,5},{8,10},{10,8},{9,1... | collective-permute-start | bytes 589832 | tf_op jit(solution)/shard_map/ppermute | solution.py:437
  203.7 10.7 %collective-permute-start.30 = (bf16[192,512]{1,0:T(8,128)(2,1)S(1)}, bf16[192,512]{1,0:T(8,128)(2,1)S(1)}, u32[]{:S(2)}, u32[]{:S(2)}) collective-permute-start(bf16[192,512]{1,0:T(8,128)(2,1)S(1)} %project.9), channel_id=1, source_target_pairs={{0,2},{2,0},{1,3},{3,1},{4,6},{6,4},{5,7},{7,5},{8,10},{10,8},{9,1... | collective-permute-start | bytes 589832 | tf_op jit(solution)/shard_map/ppermute | solution.py:437

commit v7 on v6

--- a/solution.py
+++ b/solution.py
@@ -100,7 +100,7 @@
         ),
         in_specs=[pl.BlockSpec(memory_space=pltpu.SMEM), vmem, vmem],
         out_specs=(vmem, vmem),
-        compiler_params=pltpu.CompilerParams(vmem_limit_bytes=20 * MIB),
+        compiler_params=pltpu.CompilerParams(vmem_limit_bytes=12 * MIB),
         cost_estimate=cost(),
         name="place",
     )(position, pages, fresh)
@@ -215,7 +215,7 @@
     group_size = width // (kv_local * HD)
     key_conv, key_row, tok_conv, *steps = tables
     fresh_base = slots + KEYS
-    most = slots // KEYS + pl.cdiv(rows, KEYS) + 2
+    most = slots // KEYS + pl.cdiv(rows, KEYS)
     smem = pl.BlockSpec(memory_space=pltpu.SMEM)
     vmem = pl.BlockSpec(memory_space=pltpu.VMEM)
     return pl.pallas_call(
@@ -227,7 +227,7 @@
             pltpu.VMEM((kv_local, group_size * TILE, most * KEYS), jnp.float32),
             pltpu.VMEM((kv_local, group_size * TILE, 2 * HD), jnp.float32),
         ],
-        compiler_params=pltpu.CompilerParams(vmem_limit_bytes=28 * MIB),
+        compiler_params=pltpu.CompilerParams(vmem_limit_bytes=20 * MIB),
         cost_estimate=cost(16 * 10**9),
         name="attend",
     )(control, *steps, queries, keys, values, key_conv, key_row, tok_conv)
@@ -300,30 +300,34 @@
             num_scalar_prefetch=1, grid=(1,), in_specs=in_specs, out_specs=out_specs
         ),
         input_output_aliases=aliases,
-        compiler_params=pltpu.CompilerParams(vmem_limit_bytes=16 * MIB),
+        compiler_params=pltpu.CompilerParams(vmem_limit_bytes=10 * MIB),
         cost_estimate=cost(),
         name="project" if came is None else "finish",
     )(control, *operands)
 
 
 def pick_kernel(asked, pool, out):
-    for owner in range(asked.shape[0]):
-
-        def copy(n, carry):
-            out[owner, n] = pool[asked[owner, n]]
-            return carry
-
-        lax.fori_loop(0, asked.shape[1], copy, 0, unroll=8)
+    owner = pl.program_id(0)
+
+    def copy(n, carry):
+        out[0, n] = pool[asked[owner, n]]
+        return carry
+
+    lax.fori_loop(0, asked.shape[1], copy, 0, unroll=8)
 
 
 def pick(pool, asked):
-    vmem = pl.BlockSpec(memory_space=pltpu.VMEM)
+    block = (1, asked.shape[1]) + pool.shape[1:]
     return pl.pallas_call(
         pick_kernel,
         out_shape=jax.ShapeDtypeStruct(asked.shape + pool.shape[1:], jnp.bfloat16),
-        in_specs=[pl.BlockSpec(memory_space=pltpu.SMEM), vmem],
-        out_specs=vmem,
-        compiler_params=pltpu.CompilerParams(vmem_limit_bytes=16 * MIB),
+        grid=(asked.shape[0],),
+        in_specs=[
+            pl.BlockSpec(memory_space=pltpu.SMEM),
+            pl.BlockSpec(memory_space=pltpu.VMEM),
+        ],
+        out_specs=pl.BlockSpec(block, lambda owner: (owner, 0, 0, 0, 0)),
+        compiler_params=pltpu.CompilerParams(vmem_limit_bytes=12 * MIB),
         cost_estimate=cost(),
         name="pick",
     )(asked, pool)
@@ -415,29 +419,33 @@
     next_shard = [jnp.where(middle, part, forward(part)) for part in inner]
     next_across = [swap_group(part) for part in next_shard]
     near_all = four(near[0], near_across[0]) + four(near[1], near_across[1])
-    next_all = four(next_shard[0], next_across[0]) + four(next_shard[1], next_across[1])
-    far = [cross(after(near[0], *next_shard)), cross(after(near[1], pages))]
-
-    keys, values = place(position, after(pages, far[0], *near_all, *next_all), fresh)
+    far = [cross(after(near[0], *next_shard))]
+    far.append(cross(after(near[1], far[0])))
+    next_all = four(next_shard[0], next_across[0], far[0]) + four(next_shard[1], next_across[1], far[0])
+    far_on = [forward(far[0])]
+
+    keys, values = place(position, after(pages, *near_all, *next_all), fresh)
     left = attend(1, control, tables, queries[0], keys, values, slots)
-    far_on = [forward(far[0]), forward(after(far[1], left))]
+    far[0] = jnp.where(middle, far[0], after(far_on[0], left))
+    far_across = [swap_group(far[0])]
     sent = [project(control, left, [out_weight])]
+    far_on.append(forward(after(far[1], sent[0])))
     sent.append(project(control, after(left, sent[-1]), near_all))
     sent.append(project(control, after(left, sent[-1]), next_all))
     came = [swap_tp(each) for each in sent]
-    far[0] = jnp.where(middle, far[0], after(far_on[0], sent[0]))
+    far_all = [four(far[0], far_across[0], sent[2])]
     far[1] = jnp.where(middle, far[1], after(far_on[1], sent[2]))
-    far_across = [swap_group(part) for part in far]
+    far_across.append(swap_group(far[1]))
     stay = attend(0, control, tables, after(queries[0], sent[2], far[1]), keys, values, slots)
-    far_all = [four(far[n], far_across[n], stay) for n in (0, 1)]
+    sent.append(project(control, after(left, stay, *came), far_all[0]))
+    far_all.append(four(far[1], far_across[1], sent[3]))
+    came.append(swap_tp(sent[3]))
     total = columns * owner_count
-    out = project(control, stay, [out_weight], came[0], 10, None, total)
-    for n in range(2):
-        sent.append(project(control, after(left, out), far_all[n]))
-        came.append(swap_tp(sent[-1]))
-        out = project(
-            control, after(stay, sent[-1]), (near_all, next_all)[n], came[n + 1], 11 + n, out, total
-        )
+    out = project(control, after(stay, sent[3]), [out_weight], came[0], 10, None, total)
+    out = project(control, stay, near_all, came[1], 11, out, total)
+    sent.append(project(control, after(left, out), far_all[1]))
+    came.append(swap_tp(sent[4]))
+    out = project(control, after(stay, sent[4]), next_all, came[2], 12, out, total)
     for n in range(2):
         out = project(control, stay, far_all[n], came[n + 3], 13 + n, out, total)
     return out

time: 220 us -> 228 us (1.036); the launches traced: 216 us -> 227 us
  waiting for transfers between devices: 97.9 us -> 108 us
    ppermute x8, waiting for transfers between devices: 14.2 us -> 32.2 us  [the longest x1 26.8 us: shards(): far = [cross(after(near[0], *next_shard))]]
    ppermute x3, waiting for transfers between devices: 8.99 us -> 0.01 us  [shards(): came = [swap_tp(each) for each in sent]]
    ppermute x2, waiting for transfers between devices: 56.2 us -> 60.2 us  [shards(): next_shard = [jnp.where(middle, part, forward(part)) for part in inner]]
    ppermute x1, waiting for transfers between devices: 6.51 us -> 2.76 us  [shards(): inner.append(cross(later))]
    unnamed x17 -> x37, local copies, waits for them, and re-layouts: 6.07 us -> 9.31 us
    ppermute x1, waiting for transfers between devices: 0.42 us -> 3.18 us  [shards(): near.append(pair(later))]
  transfers between devices with their start and end apart: 34 -> 34, of which waited for: 12 -> 9; matrix products, arithmetic and copies ran while one was open for 3% -> 2% of each run, Pallas kernels for 23% -> 21%
where the time goes in v7:
time: 228 us; the launch traced here: 227 us
  waiting for transfers between devices  108 us (47%)
  Pallas kernels  50.6 us (22%)
  starting transfers between devices  43.5 us (19%)
  local copies, waits for them, and re-layouts  11.1 us (5%)
  blocking collectives  10.8 us (5%)
  other arithmetic  2.91 us (1%)
    ppermute x2, waiting for transfers between devices, shards(): next_shard = [jnp.where(middle, part, forward(part)) for part in inner]  60.2 us
    ppermute x1, waiting for transfers between devices, shards(): far = [cross(after(near[0], *next_shard))]  26.8 us
    pallas_call x10, Pallas kernels, project(): pl.pallas_call(kernel, out_shape=out_shape, grid_spec=pltpu.PrefetchScala...  22.7 us
    pallas_call x2, Pallas kernels, attend(): pl.pallas_call(functools.partial(attend_kernel, fresh_base, side), out_sh...  20.5 us
    all_to_all x1, blocking collectives, shards(): lax.all_to_all(wanted, 'seq', split_axis=0, concat_axis=0, tiled=True)  10.8 us
    ppermute x2, waiting for transfers between devices, shards(): next_across = [swap_group(part) for part in next_shard]  9.67 us
    unnamed x37, local copies, waits for them, and re-layouts  9.31 us
    ppermute x2, starting transfers between devices, shards(): next_shard = [jnp.where(middle, part, forward(part)) for part in inner]  5.6 us
  transfers between devices with their start and end apart: 34, of which 9 were waited for; matrix products, arithmetic and copies ran while one was open for 2% of the time, Pallas kernels for 21%

profile of v7, /device:TPU:16, one launch (start us, length us, event | category | flops | bytes accessed | tf_op | source)
XLA Modules:
  0.0 227.4 jit_solution(14520242894869597193)
XLA Ops:
  0.0 1.3 fusion.5
  1.3 1.6 collective-permute-start
  2.9 1.9 collective-permute-start.1
  4.8 2.6 %rank.1 = (s32[128]{0:T(128)}, s32[4,64]{1,0:T(4,128)}) custom-call(s32[1,128]{1,0:T(1,128)} %owner.1, s32[1,128]{1,0:T(1,128)} %page.1), custom_call_target="tpu_custom_call" | custom-call | flops 3000000000 | bytes 1000 | tf_op jit(solution)/shard_map/rank/pallas_call | solution.py:49
  7.5 10.8 %all_to_all.17 = s32[4,1,64]{2,1,0:T(1,128)S(1)} all-to-all(s32[4,1,64]{2,1,0:T(1,128)} %bitcast.40), channel_id=1, replica_groups=mesh['group'=2,'seq'=4,'tp'=2,'role'=2] {'seq'}, dimensions={0} | all-to-all | bytes 2048 | tf_op jit(solution)/shard_map/all_to_all | solution.py:381
  18.3 1.4 collective-permute-start.2
  19.7 2.2 collective-permute-start.3
  21.9 2.2 copy-done.2
  24.1 1.4 pick.1
  25.5 2.0 copy-done
  27.5 3.2 %collective-permute-done.2.refs_4_ = bf16[512,512]{1,0:T(8,128)(2,1)S(1)} collective-permute-done((bf16[512,512]{1,0:T(8,128)(2,1)S(1)}, bf16[512,512]{1,0:T(8,128)(2,1)S(1)}, u32[]{:S(2)}, u32[]{:S(2)}) %collective-permute-start.2) | collective-permute-done | bytes 524320 | tf_op jit(solution)/shard_map/ppermute | solution.py:385
  30.7 2.8 %collective-permute-done.3 = bf16[512,512]{1,0:T(8,128)(2,1)S(1)} collective-permute-done((bf16[512,512]{1,0:T(8,128)(2,1)S(1)}, bf16[512,512]{1,0:T(8,128)(2,1)S(1)}, u32[]{:S(2)}, u32[]{:S(2)}) %collective-permute-start.3) | collective-permute-done | bytes 524320 | tf_op jit(solution)/shard_map/ppermute | solution.py:386
  33.4 4.8 %all-to-all-start.1 = ((bf16[4,64,2,16,256]{4,3,2,1,0:T(8,128)(2,1)}), bf16[4,64,2,16,256]{4,3,2,1,0:T(8,128)(2,1)}, u32[]{:S(2)}, u32[]{:S(2)}) async-start(bf16[4,64,2,16,256]{4,3,2,1,0:T(8,128)(2,1)} %copy-done), calls=%async_computation.1 | async-start | bytes 8388608 | tf_op jit(solution)/shard_map/all_to_all | solution.py:392
  38.3 3.5 %collective-permute-start.10 = (bf16[512,512]{1,0:T(8,128)(2,1)S(1)}, bf16[512,512]{1,0:T(8,128)(2,1)}, u32[]{:S(2)}, u32[]{:S(2)}) collective-permute-start(bf16[512,512]{1,0:T(8,128)(2,1)S(1)} %collective-permute-done.1), channel_id=1, source_target_pairs={{4,0},{8,12},{5,1},{9,13},{6,2},{10,14},{7,3},{11,15},{20,16},{24,... | collective-permute-start | bytes 1572872 | tf_op jit(solution)/shard_map/ppermute | solution.py:419
  41.8 2.1 collective-permute-start.12
  43.9 1.5 collective-permute-start.4
  45.9 50.6 %collective-permute-done.10 = bf16[512,512]{1,0:T(8,128)(2,1)} collective-permute-done((bf16[512,512]{1,0:T(8,128)(2,1)S(1)}, bf16[512,512]{1,0:T(8,128)(2,1)}, u32[]{:S(2)}, u32[]{:S(2)}) %collective-permute-start.10) | collective-permute-done | bytes 524320 | tf_op jit(solution)/shard_map/ppermute | solution.py:419
  96.7 9.5 %collective-permute-done.12 = bf16[512,512]{1,0:T(8,128)(2,1)} collective-permute-done((bf16[512,512]{1,0:T(8,128)(2,1)S(1)}, bf16[512,512]{1,0:T(8,128)(2,1)}, u32[]{:S(2)}, u32[]{:S(2)}) %collective-permute-start.12) | collective-permute-done | bytes 524320 | tf_op jit(solution)/shard_map/ppermute | solution.py:419
  106.3 1.9 collective-permute-start.13
  108.5 1.1 copy.22
  109.7 1.6 collective-permute-start.11
  111.8 26.8 %collective-permute-done.13 = bf16[512,512]{1,0:T(8,128)(2,1)} collective-permute-done((bf16[512,512]{1,0:T(8,128)(2,1)S(1)}, bf16[512,512]{1,0:T(8,128)(2,1)}, u32[]{:S(2)}, u32[]{:S(2)}) %collective-permute-start.13) | collective-permute-done | bytes 524320 | tf_op jit(solution)/shard_map/ppermute | solution.py:422
  138.6 1.5 collective-permute-start.16
  141.1 9.7 %collective-permute-done.16.refs_5_ = bf16[512,512]{1,0:T(8,128)(2,1)} collective-permute-done((bf16[512,512]{1,0:T(8,128)(2,1)S(1)}, bf16[512,512]{1,0:T(8,128)(2,1)}, u32[]{:S(2)}, u32[]{:S(2)}) %collective-permute-start.16) | collective-permute-done | bytes 524320 | tf_op jit(solution)/shard_map/ppermute | solution.py:420
  152.7 4.5 %collective-permute-start.19 = (bf16[512,512]{1,0:T(8,128)(2,1)S(1)}, bf16[512,512]{1,0:T(8,128)(2,1)}, u32[]{:S(2)}, u32[]{:S(2)}) collective-permute-start(bf16[512,512]{1,0:T(8,128)(2,1)S(1)} %collective-permute-done.2.refs_4_), channel_id=1, source_target_pairs={{4,8},{8,4},{5,9},{9,5},{6,10},{10,6},{7,11},{11,7},{20,24},{24,20... | collective-permute-start | bytes 1572872 | tf_op jit(solution)/shard_map/ppermute | solution.py:423
  158.0 2.1 collective-permute-start.24
  162.5 3.3 %place.1 = (bf16[2,3072,128]{2,1,0:T(8,128)(2,1)S(1)}, bf16[2,3072,256]{2,1,0:T(8,128)(2,1)S(1)}) custom-call(s32[128]{0:T(128)S(1)} %copy-done.14, bf16[256,2,16,256]{3,2,1,0:T(8,128)(2,1)} %bitcast.21.pages, bf16[384,512]{1,0:T(8,128)(2,1)S(1)} %bitcast.29), custom_call_target="tpu_custom_call" | custom-call | flops 3000000000 | bytes 1000 | tf_op jit(solution)/shard_map/place/pallas_call | solution.py:95
  165.8 10.9 %attend.2.left = bf16[4,192,512]{2,1,0:T(8,128)(2,1)S(1)} custom-call(s32[15]{0:T(128)S(1)} %stack.63.control, s32[6]{0:T(128)S(1)} %get-tuple-element.78.hist_at, s32[6]{0:T(128)S(1)} %get-tuple-element.77.hist_steps, s32[6]{0:T(128)S(1)} %get-tuple-element.72.fresh_at, s32[6]{0:T(128)S(1)} %get-tuple-element.71.fresh_steps, ...), custom_call_target="tpu_custom_call" | custom-call | flops 16000000000 | bytes 1000 | tf_op jit(solution)/shard_map/attend/pallas_call | solution.py:221
  176.8 1.5 project.5
  178.4 3.0 %project.6 = bf16[192,1024]{1,0:T(8,128)(2,1)S(1)} custom-call(s32[15]{0:T(128)S(1)} %stack.63.control, bf16[4,192,512]{2,1,0:T(8,128)(2,1)S(1)} %attend.2.left, bf16[512,512]{1,0:T(8,128)(2,1)S(1)} %collective-permute-done.refs_0_, bf16[512,512]{1,0:T(8,128)(2,1)S(1)} %collective-permute-done.4.refs_1_, bf16[512,512]{1,0:T(8,128)(2,1)} %collective-permute-done.5.refs_2_, ...), custom_call_target="tpu_custom_call" | custom-call | flops 3000000000 | bytes 1000 | tf_op jit(solution)/shard_map/project/pallas_call | solution.py:296
  181.6 1.9 collective-permute-start.22
  183.5 1.5 collective-permute-start.20
  185.0 1.1 broadcast_select_fusion.refs_0_
  187.1 2.7 %project.7 = bf16[192,1024]{1,0:T(8,128)(2,1)S(1)} custom-call(s32[15]{0:T(128)S(1)} %stack.63.control, bf16[4,192,512]{2,1,0:T(8,128)(2,1)S(1)} %attend.2.left, bf16[512,512]{1,0:T(8,128)(2,1)S(1)} %broadcast_select_fusion.3.refs_0_, bf16[512,512]{1,0:T(8,128)(2,1)} %collective-permute-done.11.refs_1_, bf16[512,512]{1,0:T(8,128)(2,1)S(1)} %copy-done.5, ...), custom_call_target="tpu_custom_call" | custom-call | flops 3000000000 | bytes 1000 | tf_op jit(solution)/shard_map/project/pallas_call | solution.py:296
  189.8 1.5 collective-permute-start.23
  191.3 1.7 collective-permute-done.20
  193.0 1.1 broadcast_select_fusion.1.refs_0_
  194.2 2.2 collective-permute-done.25.refs_1_
  197.2 9.6 %attend.3.left = bf16[4,192,512]{2,1,0:T(8,128)(2,1)S(1)} custom-call(s32[15]{0:T(128)S(1)} %stack.63.control, s32[6]{0:T(128)S(1)} %get-tuple-element.78.hist_at, s32[6]{0:T(128)S(1)} %get-tuple-element.77.hist_steps, s32[6]{0:T(128)S(1)} %get-tuple-element.72.fresh_at, s32[6]{0:T(128)S(1)} %get-tuple-element.71.fresh_steps, ...), custom_call_target="tpu_custom_call" | custom-call | flops 16000000000 | bytes 1000 | tf_op jit(solution)/shard_map/attend/pallas_call | solution.py:221
  206.8 1.1 project.8
  207.9 3.1 %collective-permute-start.32 = (bf16[192,512]{1,0:T(8,128)(2,1)S(1)}, bf16[192,512]{1,0:T(8,128)(2,1)S(1)}, u32[]{:S(2)}, u32[]{:S(2)}) collective-permute-start(bf16[192,512]{1,0:T(8,128)(2,1)S(1)} %project.8), channel_id=1, source_target_pairs={{0,2},{2,0},{1,3},{3,1},{4,6},{6,4},{5,7},{7,5},{8,10},{10,8},{9,1... | collective-permute-start | bytes 589832 | tf_op jit(solution)/shard_map/ppermute | solution.py:442
  211.5 2.3 %finish.5.refs_8_ = bf16[1,192,4096]{2,1,0:T(8,128)(2,1)} custom-call(s32[15]{0:T(128)S(1)} %stack.63.control, bf16[4,192,512]{2,1,0:T(8,128)(2,1)S(1)} %attend.3.left, bf16[192,1024]{1,0:T(8,128)(2,1)S(1)} %collective-permute-done.22.came, bf16[2048,1024]{1,0:T(8,128)(2,1)S(1)} %copy-done.1), custom_call_target="tpu_custom_call" | custom-call | flops 3000000000 | bytes 1000 | tf_op jit(solution)/shard_map/finish/pallas_call | solution.py:296
  213.8 3.8 %finish.6.refs_8_ = bf16[1,192,4096]{2,1,0:T(8,128)(2,1)} custom-call(s32[15]{0:T(128)S(1)} %stack.63.control, bf16[4,192,512]{2,1,0:T(8,128)(2,1)S(1)} %attend.3.left, bf16[192,1024]{1,0:T(8,128)(2,1)S(1)} %collective-permute-done.21.came, bf16[512,512]{1,0:T(8,128)(2,1)S(1)} %collective-permute-done.refs_0_, ...), custom_call_target="tpu_custom_call", output_to_operand_aliasing={{}: (11, {})} | custom-call | flops 3000000000 | bytes 1000 | tf_op jit(solution)/shard_map/finish/pallas_call | solution.py:296
  217.6 1.1 project.9
  218.9 3.5 %finish.7.refs_4_ = bf16[1,192,4096]{2,1,0:T(8,128)(2,1)} custom-call(s32[15]{0:T(128)S(1)} %stack.63.control, bf16[4,192,512]{2,1,0:T(8,128)(2,1)S(1)} %attend.3.left, bf16[192,1024]{1,0:T(8,128)(2,1)S(1)} %collective-permute-done.23.came, bf16[512,512]{1,0:T(8,128)(2,1)S(1)} %broadcast_select_fusion.3.refs_0_, ...), custom_call_target="tpu_custom_call", output_to_operand_aliasing={{}: (11, {})} | custom-call | flops 3000000000 | bytes 1000 | tf_op jit(solution)/shard_map/finish/pallas_call | solution.py:296
  222.4 1.8 finish.8.refs_4_
  224.2 1.4 collective-permute-done.31.came
  225.6 1.8 finish.9
  (92 shorter events, 10.1 us)
Async XLA Ops:
  1.3 17.0 %collective-permute-start = (bf16[512,512]{1,0:T(8,128)(2,1)S(1)}, bf16[512,512]{1,0:T(8,128)(2,1)S(1)}, u32[]{:S(2)}, u32[]{:S(2)}) collective-permute-start(bf16[512,512]{1,0:T(8,128)(2,1)S(1)} %get-tuple-element.76), channel_id=1, source_target_pairs={{0,4},{4,0},{8,12},{12,8},{1,5},{5,1},{9,13},{13,9},{2,6},{6,2},{1... | collective-permute-start | bytes 1572872 | tf_op jit(solution)/shard_map/ppermute | solution.py:378
  2.9 15.4 %collective-permute-start.1 = (bf16[512,512]{1,0:T(8,128)(2,1)S(1)}, bf16[512,512]{1,0:T(8,128)(2,1)S(1)}, u32[]{:S(2)}, u32[]{:S(2)}) collective-permute-start(bf16[512,512]{1,0:T(8,128)(2,1)S(1)} %get-tuple-element.76), channel_id=1, source_target_pairs={{4,8},{8,4},{5,9},{9,5},{6,10},{10,6},{7,11},{11,7},{20,24},{24,20... | collective-permute-start | bytes 1572872 | tf_op jit(solution)/shard_map/ppermute | solution.py:378
  18.3 12.4 %collective-permute-start.2 = (bf16[512,512]{1,0:T(8,128)(2,1)S(1)}, bf16[512,512]{1,0:T(8,128)(2,1)S(1)}, u32[]{:S(2)}, u32[]{:S(2)}) collective-permute-start(bf16[512,512]{1,0:T(8,128)(2,1)S(1)} %get-tuple-element.42), channel_id=1, source_target_pairs={{0,4},{4,0},{8,12},{12,8},{1,5},{5,1},{9,13},{13,9},{2,6},{6,2},{1... | collective-permute-start | bytes 1572872 | tf_op jit(solution)/shard_map/ppermute | solution.py:385
  19.7 13.8 %collective-permute-start.3 = (bf16[512,512]{1,0:T(8,128)(2,1)S(1)}, bf16[512,512]{1,0:T(8,128)(2,1)S(1)}, u32[]{:S(2)}, u32[]{:S(2)}) collective-permute-start(bf16[512,512]{1,0:T(8,128)(2,1)S(1)} %get-tuple-element.42), channel_id=1, source_target_pairs={{4,8},{8,4},{5,9},{9,5},{6,10},{10,6},{7,11},{11,7},{20,24},{24,20... | collective-permute-start | bytes 1572872 | tf_op jit(solution)/shard_map/ppermute | solution.py:386
  21.9 2.2 copy-start.2
  25.5 2.0 copy-start
  33.4 129.1 %all-to-all-start.1 = ((bf16[4,64,2,16,256]{4,3,2,1,0:T(8,128)(2,1)}), bf16[4,64,2,16,256]{4,3,2,1,0:T(8,128)(2,1)}, u32[]{:S(2)}, u32[]{:S(2)}) async-start(bf16[4,64,2,16,256]{4,3,2,1,0:T(8,128)(2,1)} %copy-done), calls=%async_computation.1 | async-start | bytes 8388608 | tf_op jit(solution)/shard_map/all_to_all | solution.py:392
  38.3 58.3 %collective-permute-start.10 = (bf16[512,512]{1,0:T(8,128)(2,1)S(1)}, bf16[512,512]{1,0:T(8,128)(2,1)}, u32[]{:S(2)}, u32[]{:S(2)}) collective-permute-start(bf16[512,512]{1,0:T(8,128)(2,1)S(1)} %collective-permute-done.1), channel_id=1, source_target_pairs={{4,0},{8,12},{5,1},{9,13},{6,2},{10,14},{7,3},{11,15},{20,16},{24,... | collective-permute-start | bytes 1572872 | tf_op jit(solution)/shard_map/ppermute | solution.py:419
  41.8 64.4 %collective-permute-start.12 = (bf16[512,512]{1,0:T(8,128)(2,1)S(1)}, bf16[512,512]{1,0:T(8,128)(2,1)}, u32[]{:S(2)}, u32[]{:S(2)}) collective-permute-start(bf16[512,512]{1,0:T(8,128)(2,1)S(1)} %collective-permute-done.3), channel_id=1, source_target_pairs={{4,0},{8,12},{5,1},{9,13},{6,2},{10,14},{7,3},{11,15},{20,16},{24,... | collective-permute-start | bytes 1572872 | tf_op jit(solution)/shard_map/ppermute | solution.py:419
  43.9 64.4 %copy-start.15 = (s32[1,384]{1,0:T(1,128)S(1)}, s32[1,384]{1,0:T(1,128)}, u32[]{:S(2)}) copy-start(s32[1,384]{1,0:T(1,128)} %param.13) | copy-start | bytes 4612
  43.9 67.4 %collective-permute-start.4 = (bf16[512,512]{1,0:T(8,128)(2,1)S(1)}, bf16[512,512]{1,0:T(8,128)(2,1)S(1)}, u32[]{:S(2)}, u32[]{:S(2)}) collective-permute-start(bf16[512,512]{1,0:T(8,128)(2,1)S(1)} %collective-permute-done.refs_0_), channel_id=1, source_target_pairs={{0,16},{16,0},{1,17},{17,1},{2,18},{18,2},{3,19},{19,3},{4,20},{20... | collective-permute-start | bytes 1572872 | tf_op jit(solution)/shard_map/ppermute | solution.py:418
  45.4 66.0 %collective-permute-start.7 = (bf16[512,512]{1,0:T(8,128)(2,1)S(1)}, bf16[512,512]{1,0:T(8,128)(2,1)}, u32[]{:S(2)}, u32[]{:S(2)}) collective-permute-start(bf16[512,512]{1,0:T(8,128)(2,1)S(1)} %collective-permute-done.2.refs_4_), channel_id=1, source_target_pairs={{0,16},{16,0},{1,17},{17,1},{2,18},{18,2},{3,19},{19,3},{4,20},{20... | collective-permute-start | bytes 1572872 | tf_op jit(solution)/shard_map/ppermute | solution.py:418
  96.6 43.5 %copy-start.16 = (s32[1,128]{1,0:T(1,128)S(1)}, s32[1,128]{1,0:T(1,128)}, u32[]{:S(2)}) copy-start(s32[1,128]{1,0:T(1,128)} %param.14) | copy-start | bytes 1540
  96.6 43.5 %copy-start.17 = (s32[1,128]{1,0:T(1,128)S(1)}, s32[1,128]{1,0:T(1,128)}, u32[]{:S(2)}) copy-start(s32[1,128]{1,0:T(1,128)} %param.15) | copy-start | bytes 1540
  96.7 65.9 %copy-start.14 = (s32[128]{0:T(128)S(1)}, s32[128]{0:T(128)}, u32[]{:S(2)}) copy-start(s32[128]{0:T(128)} %get-tuple-element.37.position) | copy-start | bytes 1540
  106.3 32.4 %collective-permute-start.13 = (bf16[512,512]{1,0:T(8,128)(2,1)S(1)}, bf16[512,512]{1,0:T(8,128)(2,1)}, u32[]{:S(2)}, u32[]{:S(2)}) collective-permute-start(bf16[512,512]{1,0:T(8,128)(2,1)S(1)} %collective-permute-done.refs_0_), channel_id=1, source_target_pairs={{4,8},{8,4},{5,9},{9,5},{6,10},{10,6},{7,11},{11,7},{20,24},{24,20... | collective-permute-start | bytes 1572872 | tf_op jit(solution)/shard_map/ppermute | solution.py:422
  109.6 41.2 %collective-permute-start.5 = (bf16[512,512]{1,0:T(8,128)(2,1)S(1)}, bf16[512,512]{1,0:T(8,128)(2,1)}, u32[]{:S(2)}, u32[]{:S(2)}) collective-permute-start(bf16[512,512]{1,0:T(8,128)(2,1)S(1)} %collective-permute-done.refs_0_), channel_id=1, source_target_pairs={{0,1},{1,0},{2,3},{3,2},{4,5},{5,4},{6,7},{7,6},{8,9},{9,8},{10,11... | collective-permute-start | bytes 1572872 | tf_op jit(solution)/shard_map/ppermute | solution.py:416
  109.7 31.4 %collective-permute-start.11 = (bf16[512,512]{1,0:T(8,128)(2,1)S(1)}, bf16[512,512]{1,0:T(8,128)(2,1)}, u32[]{:S(2)}, u32[]{:S(2)}) collective-permute-start(bf16[512,512]{1,0:T(8,128)(2,1)S(1)} %broadcast_select_fusion.3.refs_0_), channel_id=1, source_target_pairs={{0,16},{16,0},{1,17},{17,1},{2,18},{18,2},{3,19},{19,3},{4,20},{20... | collective-permute-start | bytes 1572872 | tf_op jit(solution)/shard_map/ppermute | solution.py:420
  111.3 40.1 %collective-permute-start.6 = (bf16[512,512]{1,0:T(8,128)(2,1)S(1)}, bf16[512,512]{1,0:T(8,128)(2,1)}, u32[]{:S(2)}, u32[]{:S(2)}) collective-permute-start(bf16[512,512]{1,0:T(8,128)(2,1)S(1)} %collective-permute-done.4.refs_1_), channel_id=1, source_target_pairs={{0,1},{1,0},{2,3},{3,2},{4,5},{5,4},{6,7},{7,6},{8,9},{9,8},{10,11... | collective-permute-start | bytes 1572872 | tf_op jit(solution)/shard_map/ppermute | solution.py:416
  111.4 40.0 %collective-permute-start.8 = (bf16[512,512]{1,0:T(8,128)(2,1)S(1)}, bf16[512,512]{1,0:T(8,128)(2,1)}, u32[]{:S(2)}, u32[]{:S(2)}) collective-permute-start(bf16[512,512]{1,0:T(8,128)(2,1)S(1)} %collective-permute-done.2.refs_4_), channel_id=1, source_target_pairs={{0,1},{1,0},{2,3},{3,2},{4,5},{5,4},{6,7},{7,6},{8,9},{9,8},{10,11... | collective-permute-start | bytes 1572872 | tf_op jit(solution)/shard_map/ppermute | solution.py:416
  138.6 12.2 %collective-permute-start.16 = (bf16[512,512]{1,0:T(8,128)(2,1)S(1)}, bf16[512,512]{1,0:T(8,128)(2,1)}, u32[]{:S(2)}, u32[]{:S(2)}) collective-permute-start(bf16[512,512]{1,0:T(8,128)(2,1)S(1)} %broadcast_select_fusion.2.refs_4_), channel_id=1, source_target_pairs={{0,16},{16,0},{1,17},{17,1},{2,18},{18,2},{3,19},{19,3},{4,20},{20... | collective-permute-start | bytes 1572872 | tf_op jit(solution)/shard_map/ppermute | solution.py:420
  141.1 10.8 %collective-permute-start.9 = (bf16[512,512]{1,0:T(8,128)(2,1)}, bf16[512,512]{1,0:T(8,128)(2,1)S(1)}, u32[]{:S(2)}, u32[]{:S(2)}) collective-permute-start(bf16[512,512]{1,0:T(8,128)(2,1)} %collective-permute-done.7.refs_5_), channel_id=1, source_target_pairs={{0,1},{1,0},{2,3},{3,2},{4,5},{5,4},{6,7},{7,6},{8,9},{9,8},{10,11... | collective-permute-start | bytes 1572872 | tf_op jit(solution)/shard_map/ppermute | solution.py:416
  150.8 6.4 %collective-permute-start.14 = (bf16[512,512]{1,0:T(8,128)(2,1)S(1)}, bf16[512,512]{1,0:T(8,128)(2,1)S(1)}, u32[]{:S(2)}, u32[]{:S(2)}) collective-permute-start(bf16[512,512]{1,0:T(8,128)(2,1)S(1)} %broadcast_select_fusion.3.refs_0_), channel_id=1, source_target_pairs={{0,1},{1,0},{2,3},{3,2},{4,5},{5,4},{6,7},{7,6},{8,9},{9,8},{10,11... | collective-permute-start | bytes 1572872 | tf_op jit(solution)/shard_map/ppermute | solution.py:416
  150.8 9.3 %collective-permute-start.15 = (bf16[512,512]{1,0:T(8,128)(2,1)}, bf16[512,512]{1,0:T(8,128)(2,1)S(1)}, u32[]{:S(2)}, u32[]{:S(2)}) collective-permute-start(bf16[512,512]{1,0:T(8,128)(2,1)} %collective-permute-done.11.refs_1_), channel_id=1, source_target_pairs={{0,1},{1,0},{2,3},{3,2},{4,5},{5,4},{6,7},{7,6},{8,9},{9,8},{10,11... | collective-permute-start | bytes 1572872 | tf_op jit(solution)/shard_map/ppermute | solution.py:416
  151.3 9.6 %collective-permute-start.17 = (bf16[512,512]{1,0:T(8,128)(2,1)S(1)}, bf16[512,512]{1,0:T(8,128)(2,1)S(1)}, u32[]{:S(2)}, u32[]{:S(2)}) collective-permute-start(bf16[512,512]{1,0:T(8,128)(2,1)S(1)} %broadcast_select_fusion.2.refs_4_), channel_id=1, source_target_pairs={{0,1},{1,0},{2,3},{3,2},{4,5},{5,4},{6,7},{7,6},{8,9},{9,8},{10,11... | collective-permute-start | bytes 1572872 | tf_op jit(solution)/shard_map/ppermute | solution.py:416
  151.4 10.3 %collective-permute-start.18 = (bf16[512,512]{1,0:T(8,128)(2,1)}, bf16[512,512]{1,0:T(8,128)(2,1)S(1)}, u32[]{:S(2)}, u32[]{:S(2)}) collective-permute-start(bf16[512,512]{1,0:T(8,128)(2,1)} %collective-permute-done.16.refs_5_), channel_id=1, source_target_pairs={{0,1},{1,0},{2,3},{3,2},{4,5},{5,4},{6,7},{7,6},{8,9},{9,8},{10,11... | collective-permute-start | bytes 1572872 | tf_op jit(solution)/shard_map/ppermute | solution.py:416
  152.7 30.8 %collective-permute-start.19 = (bf16[512,512]{1,0:T(8,128)(2,1)S(1)}, bf16[512,512]{1,0:T(8,128)(2,1)}, u32[]{:S(2)}, u32[]{:S(2)}) collective-permute-start(bf16[512,512]{1,0:T(8,128)(2,1)S(1)} %collective-permute-done.2.refs_4_), channel_id=1, source_target_pairs={{4,8},{8,4},{5,9},{9,5},{6,10},{10,6},{7,11},{11,7},{20,24},{24,20... | collective-permute-start | bytes 1572872 | tf_op jit(solution)/shard_map/ppermute | solution.py:423
  158.0 27.1 %collective-permute-start.24 = (bf16[512,512]{1,0:T(8,128)(2,1)}, bf16[512,512]{1,0:T(8,128)(2,1)}, u32[]{:S(2)}, u32[]{:S(2)}) collective-permute-start(bf16[512,512]{1,0:T(8,128)(2,1)} %collective-permute-done.13), channel_id=1, source_target_pairs={{4,0},{8,12},{5,1},{9,13},{6,2},{10,14},{7,3},{11,15},{20,16},{24,... | collective-permute-start | bytes 1572872 | tf_op jit(solution)/shard_map/ppermute | solution.py:425
  160.9 0.8 copy-start.8
  162.5 3.3 %copy-start.3 = (bf16[1,384,2048]{2,1,0:T(8,128)(2,1)S(1)}, bf16[1,384,2048]{2,1,0:T(8,128)(2,1)}, u32[]{:S(2)}) copy-start(bf16[1,384,2048]{2,1,0:T(8,128)(2,1)} %param.9) | copy-start | bytes 4718596
  165.8 11.0 %copy-start.1 = (bf16[2048,1024]{1,0:T(8,128)(2,1)S(1)}, bf16[2048,1024]{1,0:T(8,128)(2,1)}, u32[]{:S(2)}) copy-start(bf16[2048,1024]{1,0:T(8,128)(2,1)} %refs_0_.3) | copy-start | bytes 12582916
  176.8 1.6 copy-start.11
  178.3 8.7 %copy-start.13 = (bf16[512,512]{1,0:T(8,128)(2,1)S(1)}, bf16[512,512]{1,0:T(8,128)(2,1)}, u32[]{:S(2)}) copy-start(bf16[512,512]{1,0:T(8,128)(2,1)} %copy-done.12) | copy-start | bytes 1572868
  181.4 5.7 %copy-start.5 = (bf16[512,512]{1,0:T(8,128)(2,1)S(1)}, bf16[512,512]{1,0:T(8,128)(2,1)}, u32[]{:S(2)}) copy-start(bf16[512,512]{1,0:T(8,128)(2,1)} %copy-done.4) | copy-start | bytes 1572868
  181.4 5.7 %copy-start.7 = (bf16[512,512]{1,0:T(8,128)(2,1)S(1)}, bf16[512,512]{1,0:T(8,128)(2,1)}, u32[]{:S(2)}) copy-start(bf16[512,512]{1,0:T(8,128)(2,1)} %copy-done.6) | copy-start | bytes 1572868
  181.4 5.6 %copy-start.9 = (bf16[512,512]{1,0:T(8,128)(2,1)S(1)}, bf16[512,512]{1,0:T(8,128)(2,1)}, u32[]{:S(2)}) copy-start(bf16[512,512]{1,0:T(8,128)(2,1)} %copy-done.8) | copy-start | bytes 1572868
  181.4 15.7 %collective-permute-start.21 = (bf16[192,1024]{1,0:T(8,128)(2,1)S(1)}, bf16[192,1024]{1,0:T(8,128)(2,1)S(1)}, u32[]{:S(2)}, u32[]{:S(2)}) collective-permute-start(bf16[192,1024]{1,0:T(8,128)(2,1)S(1)} %project.6), channel_id=1, source_target_pairs={{0,2},{2,0},{1,3},{3,1},{4,6},{6,4},{5,7},{7,5},{8,10},{10,8},{9,1... | collective-permute-start | bytes 1179656 | tf_op jit(solution)/shard_map/ppermute | solution.py:435
  181.6 25.1 %collective-permute-start.22 = (bf16[192,1024]{1,0:T(8,128)(2,1)S(1)}, bf16[192,1024]{1,0:T(8,128)(2,1)S(1)}, u32[]{:S(2)}, u32[]{:S(2)}) collective-permute-start(bf16[192,1024]{1,0:T(8,128)(2,1)S(1)} %project.5), channel_id=1, source_target_pairs={{0,2},{2,0},{1,3},{3,1},{4,6},{6,4},{5,7},{7,5},{8,10},{10,8},{9,1... | collective-permute-start | bytes 1179656 | tf_op jit(solution)/shard_map/ppermute | solution.py:435
  183.5 9.5 %collective-permute-start.20 = (bf16[512,512]{1,0:T(8,128)(2,1)}, bf16[512,512]{1,0:T(8,128)(2,1)S(1)}, u32[]{:S(2)}, u32[]{:S(2)}) collective-permute-start(bf16[512,512]{1,0:T(8,128)(2,1)} %collective-permute-done.19), channel_id=1, source_target_pairs={{4,0},{8,12},{5,1},{9,13},{6,2},{10,14},{7,3},{11,15},{20,16},{24,... | collective-permute-start | bytes 1572872 | tf_op jit(solution)/shard_map/ppermute | solution.py:432
  186.2 10.2 %collective-permute-start.25 = (bf16[512,512]{1,0:T(8,128)(2,1)S(1)}, bf16[512,512]{1,0:T(8,128)(2,1)S(1)}, u32[]{:S(2)}, u32[]{:S(2)}) collective-permute-start(bf16[512,512]{1,0:T(8,128)(2,1)S(1)} %broadcast_select_fusion.refs_0_), channel_id=1, source_target_pairs={{0,16},{16,0},{1,17},{17,1},{2,18},{18,2},{3,19},{19,3},{4,20},{20... | collective-permute-start | bytes 1572872 | tf_op jit(solution)/shard_map/ppermute | solution.py:430
  189.8 16.9 %collective-permute-start.23 = (bf16[192,1024]{1,0:T(8,128)(2,1)S(1)}, bf16[192,1024]{1,0:T(8,128)(2,1)S(1)}, u32[]{:S(2)}, u32[]{:S(2)}) collective-permute-start(bf16[192,1024]{1,0:T(8,128)(2,1)S(1)} %project.7), channel_id=1, source_target_pairs={{0,2},{2,0},{1,3},{3,1},{4,6},{6,4},{5,7},{7,5},{8,10},{10,8},{9,1... | collective-permute-start | bytes 1179656 | tf_op jit(solution)/shard_map/ppermute | solution.py:435
  193.0 13.7 %collective-permute-start.26 = (bf16[512,512]{1,0:T(8,128)(2,1)S(1)}, bf16[512,512]{1,0:T(8,128)(2,1)S(1)}, u32[]{:S(2)}, u32[]{:S(2)}) collective-permute-start(bf16[512,512]{1,0:T(8,128)(2,1)S(1)} %broadcast_select_fusion.refs_0_), channel_id=1, source_target_pairs={{0,1},{1,0},{2,3},{3,2},{4,5},{5,4},{6,7},{7,6},{8,9},{9,8},{10,11... | collective-permute-start | bytes 1572872 | tf_op jit(solution)/shard_map/ppermute | solution.py:416
  196.3 14.7 %collective-permute-start.28 = (bf16[512,512]{1,0:T(8,128)(2,1)S(1)}, bf16[512,512]{1,0:T(8,128)(2,1)S(1)}, u32[]{:S(2)}, u32[]{:S(2)}) collective-permute-start(bf16[512,512]{1,0:T(8,128)(2,1)S(1)} %broadcast_select_fusion.1.refs_0_), channel_id=1, source_target_pairs={{0,16},{16,0},{1,17},{17,1},{2,18},{18,2},{3,19},{19,3},{4,20},{20... | collective-permute-start | bytes 1572872 | tf_op jit(solution)/shard_map/ppermute | solution.py:438
  197.2 9.6 %collective-permute-start.27 = (bf16[512,512]{1,0:T(8,128)(2,1)S(1)}, bf16[512,512]{1,0:T(8,128)(2,1)S(1)}, u32[]{:S(2)}, u32[]{:S(2)}) collective-permute-start(bf16[512,512]{1,0:T(8,128)(2,1)S(1)} %collective-permute-done.25.refs_1_), channel_id=1, source_target_pairs={{0,1},{1,0},{2,3},{3,2},{4,5},{5,4},{6,7},{7,6},{8,9},{9,8},{10,11... | collective-permute-start | bytes 1572872 | tf_op jit(solution)/shard_map/ppermute | solution.py:416
  207.9 14.5 %collective-permute-start.32 = (bf16[192,512]{1,0:T(8,128)(2,1)S(1)}, bf16[192,512]{1,0:T(8,128)(2,1)S(1)}, u32[]{:S(2)}, u32[]{:S(2)}) collective-permute-start(bf16[192,512]{1,0:T(8,128)(2,1)S(1)} %project.8), channel_id=1, source_target_pairs={{0,2},{2,0},{1,3},{3,1},{4,6},{6,4},{5,7},{7,5},{8,10},{10,8},{9,1... | collective-permute-start | bytes 589832 | tf_op jit(solution)/shard_map/ppermute | solution.py:442
  211.0 6.6 %collective-permute-start.29 = (bf16[512,512]{1,0:T(8,128)(2,1)S(1)}, bf16[512,512]{1,0:T(8,128)(2,1)S(1)}, u32[]{:S(2)}, u32[]{:S(2)}) collective-permute-start(bf16[512,512]{1,0:T(8,128)(2,1)S(1)} %broadcast_select_fusion.1.refs_0_), channel_id=1, source_target_pairs={{0,1},{1,0},{2,3},{3,2},{4,5},{5,4},{6,7},{7,6},{8,9},{9,8},{10,11... | collective-permute-start | bytes 1572872 | tf_op jit(solution)/shard_map/ppermute | solution.py:416
  211.0 6.6 %collective-permute-start.30 = (bf16[512,512]{1,0:T(8,128)(2,1)S(1)}, bf16[512,512]{1,0:T(8,128)(2,1)S(1)}, u32[]{:S(2)}, u32[]{:S(2)}) collective-permute-start(bf16[512,512]{1,0:T(8,128)(2,1)S(1)} %collective-permute-done.28.refs_1_), channel_id=1, source_target_pairs={{0,1},{1,0},{2,3},{3,2},{4,5},{5,4},{6,7},{7,6},{8,9},{9,8},{10,11... | collective-permute-start | bytes 1572872 | tf_op jit(solution)/shard_map/ppermute | solution.py:416
  218.8 6.9 %collective-permute-start.31 = (bf16[192,512]{1,0:T(8,128)(2,1)S(1)}, bf16[192,512]{1,0:T(8,128)(2,1)S(1)}, u32[]{:S(2)}, u32[]{:S(2)}) collective-permute-start(bf16[192,512]{1,0:T(8,128)(2,1)S(1)} %project.9), channel_id=1, source_target_pairs={{0,2},{2,0},{1,3},{3,1},{4,6},{6,4},{5,7},{7,5},{8,10},{10,8},{9,1... | collective-permute-start | bytes 589832 | tf_op jit(solution)/shard_map/ppermute | solution.py:447
  (4 other events, 3.2 us)

commit v8 on v7

--- a/solution.py
+++ b/solution.py
@@ -100,8 +100,8 @@
         ),
         in_specs=[pl.BlockSpec(memory_space=pltpu.SMEM), vmem, vmem],
         out_specs=(vmem, vmem),
-        compiler_params=pltpu.CompilerParams(vmem_limit_bytes=12 * MIB),
-        cost_estimate=cost(),
+        compiler_params=pltpu.CompilerParams(vmem_limit_bytes=20 * MIB),
+        cost_estimate=cost(10**9),
         name="place",
     )(position, pages, fresh)
 
@@ -227,8 +227,8 @@
             pltpu.VMEM((kv_local, group_size * TILE, most * KEYS), jnp.float32),
             pltpu.VMEM((kv_local, group_size * TILE, 2 * HD), jnp.float32),
         ],
-        compiler_params=pltpu.CompilerParams(vmem_limit_bytes=20 * MIB),
-        cost_estimate=cost(16 * 10**9),
+        compiler_params=pltpu.CompilerParams(vmem_limit_bytes=28 * MIB),
+        cost_estimate=cost((16 - 15 * side) * 10**9),
         name="attend",
     )(control, *steps, queries, keys, values, key_conv, key_row, tok_conv)
 
@@ -300,7 +300,7 @@
             num_scalar_prefetch=1, grid=(1,), in_specs=in_specs, out_specs=out_specs
         ),
         input_output_aliases=aliases,
-        compiler_params=pltpu.CompilerParams(vmem_limit_bytes=10 * MIB),
+        compiler_params=pltpu.CompilerParams(vmem_limit_bytes=16 * MIB),
         cost_estimate=cost(),
         name="project" if came is None else "finish",
     )(control, *operands)
@@ -419,35 +419,33 @@
     next_shard = [jnp.where(middle, part, forward(part)) for part in inner]
     next_across = [swap_group(part) for part in next_shard]
     near_all = four(near[0], near_across[0]) + four(near[1], near_across[1])
-    far = [cross(after(near[0], *next_shard))]
-    far.append(cross(after(near[1], far[0])))
-    next_all = four(next_shard[0], next_across[0], far[0]) + four(next_shard[1], next_across[1], far[0])
-    far_on = [forward(far[0])]
+    next_all = four(next_shard[0], next_across[0]) + four(next_shard[1], next_across[1])
+    far = [cross(after(part, *next_across)) for part in near]
 
     keys, values = place(position, after(pages, *near_all, *next_all), fresh)
     left = attend(1, control, tables, queries[0], keys, values, slots)
-    far[0] = jnp.where(middle, far[0], after(far_on[0], left))
-    far_across = [swap_group(far[0])]
+    far_on = [forward(after(far[0], left))]
     sent = [project(control, left, [out_weight])]
     far_on.append(forward(after(far[1], sent[0])))
     sent.append(project(control, after(left, sent[-1]), near_all))
+    far[0] = jnp.where(middle, far[0], after(far_on[0], sent[1]))
+    far_across = [swap_group(far[0])]
     sent.append(project(control, after(left, sent[-1]), next_all))
     came = [swap_tp(each) for each in sent]
-    far_all = [four(far[0], far_across[0], sent[2])]
-    far[1] = jnp.where(middle, far[1], after(far_on[1], sent[2]))
+    stay = attend(0, control, tables, after(queries[0], sent[2], far[0]), keys, values, slots)
+    far[1] = jnp.where(middle, far[1], after(far_on[1], stay))
     far_across.append(swap_group(far[1]))
-    stay = attend(0, control, tables, after(queries[0], sent[2], far[1]), keys, values, slots)
-    sent.append(project(control, after(left, stay, *came), far_all[0]))
-    far_all.append(four(far[1], far_across[1], sent[3]))
+    far_all = [four(far[n], far_across[n], stay) for n in (0, 1)]
+    total = columns * owner_count
+    out = project(control, after(stay, *came[:2]), [out_weight], came[0], 10, None, total)
+    out = project(control, stay, near_all, came[1], 11, out, total)
+    sent.append(project(control, after(left, out), far_all[0]))
     came.append(swap_tp(sent[3]))
-    total = columns * owner_count
-    out = project(control, after(stay, sent[3]), [out_weight], came[0], 10, None, total)
-    out = project(control, stay, near_all, came[1], 11, out, total)
+    out = project(control, after(stay, sent[3]), next_all, came[2], 12, out, total)
     sent.append(project(control, after(left, out), far_all[1]))
     came.append(swap_tp(sent[4]))
-    out = project(control, after(stay, sent[4]), next_all, came[2], 12, out, total)
     for n in range(2):
-        out = project(control, stay, far_all[n], came[n + 3], 13 + n, out, total)
+        out = project(control, after(stay, sent[4]), far_all[n], came[n + 3], 13 + n, out, total)
     return out
 
 

time: 228 us -> 207 us (0.908)
  waiting for transfers between devices: 108 us -> 84.3 us
  starting transfers between devices: 43.5 us -> 46.9 us
  local copies, waits for them, and re-layouts: 11.1 us -> 8.69 us
    ppermute x3, waiting for transfers between devices: 26.8 us -> 1.78 us  [the longest x1 0.89 us: shards(): far_on = [forward(after(far[0], left))]]
    ppermute x1, waiting for transfers between devices: 0.01 us -> 7.6 us  [shards(): far_across.append(swap_group(far[1]))]
    ppermute x3, starting transfers between devices: 8.49 us -> 13.2 us  [the longest x1 7.32 us: shards(): far_on = [forward(after(far[0], left))]]
    ppermute x2, waiting for transfers between devices: 9.67 us -> 5.89 us  [shards(): next_across = [swap_group(part) for part in next_shard]]
    ppermute x1, waiting for transfers between devices: 1.45 us -> 4.38 us  [shards(): came.append(swap_tp(sent[4]))]
    unnamed x37 -> x29, local copies, waits for them, and re-layouts: 9.31 us -> 6.91 us
  transfers between devices with their start and end apart: 34 -> 34, of which waited for: 9 -> 10; matrix products, arithmetic and copies ran while one was open for 2% -> 2% of each run, Pallas kernels for 21% -> 24%
where the time goes in v8:
time: 207 us; the launch traced here: 206 us
  waiting for transfers between devices  84.3 us (41%)
  Pallas kernels  51.5 us (25%)
  starting transfers between devices  46.9 us (23%)
  blocking collectives  10.8 us (5%)
  local copies, waits for them, and re-layouts  8.69 us (4%)
  other arithmetic  2.91 us (1%)
    ppermute x2, waiting for transfers between devices, shards(): next_shard = [jnp.where(middle, part, forward(part)) for part in inner]  58.5 us
    pallas_call x10, Pallas kernels, project(): pl.pallas_call(kernel, out_shape=out_shape, grid_spec=pltpu.PrefetchScala...  23.7 us
    pallas_call x2, Pallas kernels, attend(): pl.pallas_call(functools.partial(attend_kernel, fresh_base, side), out_sh...  20.5 us
    all_to_all x1, blocking collectives, shards(): lax.all_to_all(wanted, 'seq', split_axis=0, concat_axis=0, tiled=True)  10.8 us
    ppermute x1, waiting for transfers between devices, shards(): far_across.append(swap_group(far[1]))  7.6 us
    ppermute x1, starting transfers between devices, shards(): far_on = [forward(after(far[0], left))]  7.32 us
    unnamed x29, local copies, waits for them, and re-layouts  6.91 us
    ppermute x2, waiting for transfers between devices, shards(): next_across = [swap_group(part) for part in next_shard]  5.89 us
  transfers between devices with their start and end apart: 34, of which 10 were waited for; matrix products, arithmetic and copies ran while one was open for 2% of the time, Pallas kernels for 24%

profile of v8, /device:TPU:16, one launch (start us, length us, event | category | flops | bytes accessed | tf_op | source)
XLA Modules:
  0.0 205.8 jit_solution(1785995299680293792)
XLA Ops:
  0.0 1.3 fusion.5
  1.3 1.6 collective-permute-start
  2.9 1.9 collective-permute-start.1
  4.8 2.6 %rank.1 = (s32[128]{0:T(128)}, s32[4,64]{1,0:T(4,128)}) custom-call(s32[1,128]{1,0:T(1,128)} %owner.1, s32[1,128]{1,0:T(1,128)} %page.1), custom_call_target="tpu_custom_call" | custom-call | flops 3000000000 | bytes 1000 | tf_op jit(solution)/shard_map/rank/pallas_call | solution.py:49
  7.5 10.8 %all_to_all.17 = s32[4,1,64]{2,1,0:T(1,128)S(1)} all-to-all(s32[4,1,64]{2,1,0:T(1,128)} %bitcast.40), channel_id=1, replica_groups=mesh['group'=2,'seq'=4,'tp'=2,'role'=2] {'seq'}, dimensions={0} | all-to-all | bytes 2048 | tf_op jit(solution)/shard_map/all_to_all | solution.py:381
  18.3 1.4 collective-permute-start.2
  19.7 2.2 %collective-permute-start.3 = (bf16[512,512]{1,0:T(8,128)(2,1)S(1)}, bf16[512,512]{1,0:T(8,128)(2,1)S(1)}, u32[]{:S(2)}, u32[]{:S(2)}) collective-permute-start(bf16[512,512]{1,0:T(8,128)(2,1)S(1)} %get-tuple-element.40), channel_id=1, source_target_pairs={{4,8},{8,4},{5,9},{9,5},{6,10},{10,6},{7,11},{11,7},{20,24},{24,20... | collective-permute-start | bytes 1572872 | tf_op jit(solution)/shard_map/ppermute | solution.py:386
  21.9 2.2 %copy-done.4 = bf16[1,256,2,16,256]{4,3,2,1,0:T(8,128)(2,1)S(1)} copy-done((bf16[1,256,2,16,256]{4,3,2,1,0:T(8,128)(2,1)S(1)}, bf16[1,256,2,16,256]{4,3,2,1,0:T(8,128)(2,1)}, u32[]{:S(2)}) %copy-start.4) | copy-done | bytes 4194328
  24.1 1.4 pick.1
  25.5 2.0 copy-done
  27.5 3.2 %collective-permute-done.2.refs_4_ = bf16[512,512]{1,0:T(8,128)(2,1)S(1)} collective-permute-done((bf16[512,512]{1,0:T(8,128)(2,1)S(1)}, bf16[512,512]{1,0:T(8,128)(2,1)S(1)}, u32[]{:S(2)}, u32[]{:S(2)}) %collective-permute-start.2) | collective-permute-done | bytes 524320 | tf_op jit(solution)/shard_map/ppermute | solution.py:385
  30.7 2.8 %collective-permute-done.3 = bf16[512,512]{1,0:T(8,128)(2,1)S(1)} collective-permute-done((bf16[512,512]{1,0:T(8,128)(2,1)S(1)}, bf16[512,512]{1,0:T(8,128)(2,1)S(1)}, u32[]{:S(2)}, u32[]{:S(2)}) %collective-permute-start.3) | collective-permute-done | bytes 524320 | tf_op jit(solution)/shard_map/ppermute | solution.py:386
  33.4 4.9 %all-to-all-start.1 = ((bf16[4,64,2,16,256]{4,3,2,1,0:T(8,128)(2,1)}), bf16[4,64,2,16,256]{4,3,2,1,0:T(8,128)(2,1)}, u32[]{:S(2)}, u32[]{:S(2)}) async-start(bf16[4,64,2,16,256]{4,3,2,1,0:T(8,128)(2,1)} %copy-done), calls=%async_computation.1 | async-start | bytes 8388608 | tf_op jit(solution)/shard_map/all_to_all | solution.py:392
  38.3 3.5 %collective-permute-start.10 = (bf16[512,512]{1,0:T(8,128)(2,1)S(1)}, bf16[512,512]{1,0:T(8,128)(2,1)}, u32[]{:S(2)}, u32[]{:S(2)}) collective-permute-start(bf16[512,512]{1,0:T(8,128)(2,1)S(1)} %collective-permute-done.1), channel_id=1, source_target_pairs={{4,0},{8,12},{5,1},{9,13},{6,2},{10,14},{7,3},{11,15},{20,16},{24,... | collective-permute-start | bytes 1572872 | tf_op jit(solution)/shard_map/ppermute | solution.py:419
  41.9 2.1 %collective-permute-start.14 = (bf16[512,512]{1,0:T(8,128)(2,1)S(1)}, bf16[512,512]{1,0:T(8,128)(2,1)}, u32[]{:S(2)}, u32[]{:S(2)}) collective-permute-start(bf16[512,512]{1,0:T(8,128)(2,1)S(1)} %collective-permute-done.3), channel_id=1, source_target_pairs={{4,0},{8,12},{5,1},{9,13},{6,2},{10,14},{7,3},{11,15},{20,16},{24,... | collective-permute-start | bytes 1572872 | tf_op jit(solution)/shard_map/ppermute | solution.py:419
  44.0 1.6 collective-permute-start.4
  46.0 50.6 %collective-permute-done.10 = bf16[512,512]{1,0:T(8,128)(2,1)} collective-permute-done((bf16[512,512]{1,0:T(8,128)(2,1)S(1)}, bf16[512,512]{1,0:T(8,128)(2,1)}, u32[]{:S(2)}, u32[]{:S(2)}) %collective-permute-start.10) | collective-permute-done | bytes 524320 | tf_op jit(solution)/shard_map/ppermute | solution.py:419
  96.7 1.6 collective-permute-start.11
  98.3 8.0 %collective-permute-done.14 = bf16[512,512]{1,0:T(8,128)(2,1)} collective-permute-done((bf16[512,512]{1,0:T(8,128)(2,1)S(1)}, bf16[512,512]{1,0:T(8,128)(2,1)}, u32[]{:S(2)}, u32[]{:S(2)}) %collective-permute-start.14) | collective-permute-done | bytes 524320 | tf_op jit(solution)/shard_map/ppermute | solution.py:419
  106.3 1.6 collective-permute-start.15
  111.4 5.9 %collective-permute-done.15.refs_5_ = bf16[512,512]{1,0:T(8,128)(2,1)} collective-permute-done((bf16[512,512]{1,0:T(8,128)(2,1)S(1)}, bf16[512,512]{1,0:T(8,128)(2,1)}, u32[]{:S(2)}, u32[]{:S(2)}) %collective-permute-start.15) | collective-permute-done | bytes 524320 | tf_op jit(solution)/shard_map/ppermute | solution.py:420
  118.4 2.9 %collective-permute-start.18 = (bf16[512,512]{1,0:T(8,128)(2,1)S(1)}, bf16[512,512]{1,0:T(8,128)(2,1)}, u32[]{:S(2)}, u32[]{:S(2)}) collective-permute-start(bf16[512,512]{1,0:T(8,128)(2,1)S(1)} %collective-permute-done.refs_0_), channel_id=1, source_target_pairs={{4,8},{8,4},{5,9},{9,5},{6,10},{10,6},{7,11},{11,7},{20,24},{24,20... | collective-permute-start | bytes 1572872 | tf_op jit(solution)/shard_map/ppermute | solution.py:423
  121.5 1.1 copy.22
  122.8 2.9 %collective-permute-start.26 = (bf16[512,512]{1,0:T(8,128)(2,1)S(1)}, bf16[512,512]{1,0:T(8,128)(2,1)}, u32[]{:S(2)}, u32[]{:S(2)}) collective-permute-start(bf16[512,512]{1,0:T(8,128)(2,1)S(1)} %collective-permute-done.2.refs_4_), channel_id=1, source_target_pairs={{4,8},{8,4},{5,9},{9,5},{6,10},{10,6},{7,11},{11,7},{20,24},{24,20... | collective-permute-start | bytes 1572872 | tf_op jit(solution)/shard_map/ppermute | solution.py:423
  125.9 3.3 %place.1 = (bf16[2,3072,128]{2,1,0:T(8,128)(2,1)S(1)}, bf16[2,3072,256]{2,1,0:T(8,128)(2,1)S(1)}) custom-call(s32[128]{0:T(128)S(1)} %copy-done.3, bf16[256,2,16,256]{3,2,1,0:T(8,128)(2,1)} %bitcast.21.pages, bf16[384,512]{1,0:T(8,128)(2,1)S(1)} %bitcast.31), custom_call_target="tpu_custom_call" | custom-call | flops 1000000000 | bytes 1000 | tf_op jit(solution)/shard_map/place/pallas_call | solution.py:95
  129.1 10.3 %attend.2.left = bf16[4,192,512]{2,1,0:T(8,128)(2,1)S(1)} custom-call(s32[15]{0:T(128)S(1)} %stack.63.control, s32[6]{0:T(128)S(1)} %get-tuple-element.74.hist_at, s32[6]{0:T(128)S(1)} %get-tuple-element.73.hist_steps, s32[6]{0:T(128)S(1)} %get-tuple-element.68.fresh_at, s32[6]{0:T(128)S(1)} %get-tuple-element.67.fresh_steps, ...), custom_call_target="tpu_custom_call" | custom-call | flops 1000000000 | bytes 1000 | tf_op jit(solution)/shard_map/attend/pallas_call | solution.py:221
  139.5 1.6 project.5
  141.9 7.3 %collective-permute-start.19 = (bf16[512,512]{1,0:T(8,128)(2,1)}, bf16[512,512]{1,0:T(8,128)(2,1)S(1)}, u32[]{:S(2)}, u32[]{:S(2)}) collective-permute-start(bf16[512,512]{1,0:T(8,128)(2,1)} %collective-permute-done.18), channel_id=1, source_target_pairs={{4,0},{8,12},{5,1},{9,13},{6,2},{10,14},{7,3},{11,15},{20,16},{24,... | collective-permute-start | bytes 1572872 | tf_op jit(solution)/shard_map/ppermute | solution.py:427
  149.3 3.0 %project.6 = bf16[192,1024]{1,0:T(8,128)(2,1)S(1)} custom-call(s32[15]{0:T(128)S(1)} %stack.63.control, bf16[4,192,512]{2,1,0:T(8,128)(2,1)S(1)} %attend.2.left, bf16[512,512]{1,0:T(8,128)(2,1)S(1)} %collective-permute-done.refs_0_, bf16[512,512]{1,0:T(8,128)(2,1)S(1)} %copy-done.6, bf16[512,512]{1,0:T(8,128)(2,1)} %collective-permute-done.5.refs_2_, ...), custom_call_target="tpu_custom_call" | custom-call | flops 3000000000 | bytes 1000 | tf_op jit(solution)/shard_map/project/pallas_call | solution.py:296
  153.2 1.2 collective-permute-start.21
  154.4 3.2 %project.7 = bf16[192,1024]{1,0:T(8,128)(2,1)S(1)} custom-call(s32[15]{0:T(128)S(1)} %stack.63.control, bf16[4,192,512]{2,1,0:T(8,128)(2,1)S(1)} %attend.2.left, bf16[512,512]{1,0:T(8,128)(2,1)S(1)} %broadcast_select_fusion.3.refs_0_, bf16[512,512]{1,0:T(8,128)(2,1)S(1)} %collective-permute-done.11.refs_1_, ...), custom_call_target="tpu_custom_call" | custom-call | flops 3000000000 | bytes 1000 | tf_op jit(solution)/shard_map/project/pallas_call | solution.py:296
  157.6 0.9 collective-permute-start.25
  158.5 1.3 collective-permute-start.27
  159.8 0.9 collective-permute-done.19
  160.7 1.1 broadcast_select_fusion.1.refs_0_
  161.8 1.6 collective-permute-start.22
  163.4 10.3 %attend.3.left = bf16[4,192,512]{2,1,0:T(8,128)(2,1)S(1)} custom-call(s32[15]{0:T(128)S(1)} %stack.63.control, s32[6]{0:T(128)S(1)} %get-tuple-element.74.hist_at, s32[6]{0:T(128)S(1)} %get-tuple-element.73.hist_steps, s32[6]{0:T(128)S(1)} %get-tuple-element.68.fresh_at, s32[6]{0:T(128)S(1)} %get-tuple-element.67.fresh_steps, ...), custom_call_target="tpu_custom_call" | custom-call | flops 16000000000 | bytes 1000 | tf_op jit(solution)/shard_map/attend/pallas_call | solution.py:221
  173.8 1.1 broadcast_select_fusion.refs_0_
  175.6 2.3 %finish.5.refs_8_ = bf16[1,192,4096]{2,1,0:T(8,128)(2,1)} custom-call(s32[15]{0:T(128)S(1)} %stack.63.control, bf16[4,192,512]{2,1,0:T(8,128)(2,1)S(1)} %attend.3.left, bf16[192,1024]{1,0:T(8,128)(2,1)S(1)} %collective-permute-done.21.came, bf16[2048,1024]{1,0:T(8,128)(2,1)S(1)} %copy-done.2), custom_call_target="tpu_custom_call" | custom-call | flops 3000000000 | bytes 1000 | tf_op jit(solution)/shard_map/finish/pallas_call | solution.py:296
  177.9 3.8 %finish.6.refs_8_ = bf16[1,192,4096]{2,1,0:T(8,128)(2,1)} custom-call(s32[15]{0:T(128)S(1)} %stack.63.control, bf16[4,192,512]{2,1,0:T(8,128)(2,1)S(1)} %attend.3.left, bf16[192,1024]{1,0:T(8,128)(2,1)S(1)} %collective-permute-done.20.came, bf16[512,512]{1,0:T(8,128)(2,1)S(1)} %collective-permute-done.refs_0_, ...), custom_call_target="tpu_custom_call", output_to_operand_aliasing={{}: (11, {})} | custom-call | flops 3000000000 | bytes 1000 | tf_op jit(solution)/shard_map/finish/pallas_call | solution.py:296
  181.7 7.6 %collective-permute-done.28.refs_1_ = bf16[512,512]{1,0:T(8,128)(2,1)S(1)} collective-permute-done((bf16[512,512]{1,0:T(8,128)(2,1)S(1)}, bf16[512,512]{1,0:T(8,128)(2,1)S(1)}, u32[]{:S(2)}, u32[]{:S(2)}) %collective-permute-start.28) | collective-permute-done | bytes 524320 | tf_op jit(solution)/shard_map/ppermute | solution.py:437
  189.3 1.1 project.8
  190.4 1.4 collective-permute-start.32
  191.8 4.0 %finish.7.refs_4_ = bf16[1,192,4096]{2,1,0:T(8,128)(2,1)} custom-call(s32[15]{0:T(128)S(1)} %stack.63.control, bf16[4,192,512]{2,1,0:T(8,128)(2,1)S(1)} %attend.3.left, bf16[192,1024]{1,0:T(8,128)(2,1)S(1)} %collective-permute-done.25.came, bf16[512,512]{1,0:T(8,128)(2,1)S(1)} %broadcast_select_fusion.3.refs_0_, ...), custom_call_target="tpu_custom_call", output_to_operand_aliasing={{}: (11, {})} | custom-call | flops 3000000000 | bytes 1000 | tf_op jit(solution)/shard_map/finish/pallas_call | solution.py:296
  195.8 1.1 project.9
  197.8 1.8 finish.8.refs_4_
  199.6 4.4 %collective-permute-done.31.came = bf16[192,512]{1,0:T(8,128)(2,1)S(1)} collective-permute-done((bf16[192,512]{1,0:T(8,128)(2,1)S(1)}, bf16[192,512]{1,0:T(8,128)(2,1)S(1)}, u32[]{:S(2)}, u32[]{:S(2)}) %collective-permute-start.31) | collective-permute-done | bytes 196640 | tf_op jit(solution)/shard_map/ppermute | solution.py:446
  204.0 1.8 finish.9
  (84 shorter events, 8.9 us)
Async XLA Ops:
  1.3 17.0 %collective-permute-start = (bf16[512,512]{1,0:T(8,128)(2,1)S(1)}, bf16[512,512]{1,0:T(8,128)(2,1)S(1)}, u32[]{:S(2)}, u32[]{:S(2)}) collective-permute-start(bf16[512,512]{1,0:T(8,128)(2,1)S(1)} %get-tuple-element.72), channel_id=1, source_target_pairs={{0,4},{4,0},{8,12},{12,8},{1,5},{5,1},{9,13},{13,9},{2,6},{6,2},{1... | collective-permute-start | bytes 1572872 | tf_op jit(solution)/shard_map/ppermute | solution.py:378
  2.9 15.4 %collective-permute-start.1 = (bf16[512,512]{1,0:T(8,128)(2,1)S(1)}, bf16[512,512]{1,0:T(8,128)(2,1)S(1)}, u32[]{:S(2)}, u32[]{:S(2)}) collective-permute-start(bf16[512,512]{1,0:T(8,128)(2,1)S(1)} %get-tuple-element.72), channel_id=1, source_target_pairs={{4,8},{8,4},{5,9},{9,5},{6,10},{10,6},{7,11},{11,7},{20,24},{24,20... | collective-permute-start | bytes 1572872 | tf_op jit(solution)/shard_map/ppermute | solution.py:378
  18.3 12.4 %collective-permute-start.2 = (bf16[512,512]{1,0:T(8,128)(2,1)S(1)}, bf16[512,512]{1,0:T(8,128)(2,1)S(1)}, u32[]{:S(2)}, u32[]{:S(2)}) collective-permute-start(bf16[512,512]{1,0:T(8,128)(2,1)S(1)} %get-tuple-element.40), channel_id=1, source_target_pairs={{0,4},{4,0},{8,12},{12,8},{1,5},{5,1},{9,13},{13,9},{2,6},{6,2},{1... | collective-permute-start | bytes 1572872 | tf_op jit(solution)/shard_map/ppermute | solution.py:385
  19.7 13.8 %collective-permute-start.3 = (bf16[512,512]{1,0:T(8,128)(2,1)S(1)}, bf16[512,512]{1,0:T(8,128)(2,1)S(1)}, u32[]{:S(2)}, u32[]{:S(2)}) collective-permute-start(bf16[512,512]{1,0:T(8,128)(2,1)S(1)} %get-tuple-element.40), channel_id=1, source_target_pairs={{4,8},{8,4},{5,9},{9,5},{6,10},{10,6},{7,11},{11,7},{20,24},{24,20... | collective-permute-start | bytes 1572872 | tf_op jit(solution)/shard_map/ppermute | solution.py:386
  21.9 2.2 %copy-start.4 = (bf16[1,256,2,16,256]{4,3,2,1,0:T(8,128)(2,1)S(1)}, bf16[1,256,2,16,256]{4,3,2,1,0:T(8,128)(2,1)}, u32[]{:S(2)}) copy-start(bf16[1,256,2,16,256]{4,3,2,1,0:T(8,128)(2,1)} %param.11) | copy-start | bytes 12582916
  25.5 2.0 copy-start
  33.4 8.4 %copy-start.9 = (bf16[512,512]{1,0:T(8,128)(2,1)}, bf16[512,512]{1,0:T(8,128)(2,1)S(1)}, u32[]{:S(2)}) copy-start(bf16[512,512]{1,0:T(8,128)(2,1)S(1)} %collective-permute-done.3) | copy-start | bytes 1572868
  33.4 92.4 %all-to-all-start.1 = ((bf16[4,64,2,16,256]{4,3,2,1,0:T(8,128)(2,1)}), bf16[4,64,2,16,256]{4,3,2,1,0:T(8,128)(2,1)}, u32[]{:S(2)}, u32[]{:S(2)}) async-start(bf16[4,64,2,16,256]{4,3,2,1,0:T(8,128)(2,1)} %copy-done), calls=%async_computation.1 | async-start | bytes 8388608 | tf_op jit(solution)/shard_map/all_to_all | solution.py:392
  38.3 58.3 %collective-permute-start.10 = (bf16[512,512]{1,0:T(8,128)(2,1)S(1)}, bf16[512,512]{1,0:T(8,128)(2,1)}, u32[]{:S(2)}, u32[]{:S(2)}) collective-permute-start(bf16[512,512]{1,0:T(8,128)(2,1)S(1)} %collective-permute-done.1), channel_id=1, source_target_pairs={{4,0},{8,12},{5,1},{9,13},{6,2},{10,14},{7,3},{11,15},{20,16},{24,... | collective-permute-start | bytes 1572872 | tf_op jit(solution)/shard_map/ppermute | solution.py:419
  41.9 64.4 %collective-permute-start.14 = (bf16[512,512]{1,0:T(8,128)(2,1)S(1)}, bf16[512,512]{1,0:T(8,128)(2,1)}, u32[]{:S(2)}, u32[]{:S(2)}) collective-permute-start(bf16[512,512]{1,0:T(8,128)(2,1)S(1)} %collective-permute-done.3), channel_id=1, source_target_pairs={{4,0},{8,12},{5,1},{9,13},{6,2},{10,14},{7,3},{11,15},{20,16},{24,... | collective-permute-start | bytes 1572872 | tf_op jit(solution)/shard_map/ppermute | solution.py:419
  43.9 62.3 %copy-start.10 = (bf16[512,512]{1,0:T(8,128)(2,1)S(1)}, bf16[512,512]{1,0:T(8,128)(2,1)}, u32[]{:S(2)}) copy-start(bf16[512,512]{1,0:T(8,128)(2,1)} %copy-done.9) | copy-start | bytes 1572868
  44.0 66.1 %copy-start.11 = (s32[1,384]{1,0:T(1,128)S(1)}, s32[1,384]{1,0:T(1,128)}, u32[]{:S(2)}) copy-start(s32[1,384]{1,0:T(1,128)} %param.13) | copy-start | bytes 4612
  44.0 66.5 %copy-start.12 = (s32[1,128]{1,0:T(1,128)S(1)}, s32[1,128]{1,0:T(1,128)}, u32[]{:S(2)}) copy-start(s32[1,128]{1,0:T(1,128)} %param.14) | copy-start | bytes 1540
  44.0 66.7 %copy-start.13 = (s32[1,128]{1,0:T(1,128)S(1)}, s32[1,128]{1,0:T(1,128)}, u32[]{:S(2)}) copy-start(s32[1,128]{1,0:T(1,128)} %param.15) | copy-start | bytes 1540
  44.0 64.0 %collective-permute-start.4 = (bf16[512,512]{1,0:T(8,128)(2,1)S(1)}, bf16[512,512]{1,0:T(8,128)(2,1)S(1)}, u32[]{:S(2)}, u32[]{:S(2)}) collective-permute-start(bf16[512,512]{1,0:T(8,128)(2,1)S(1)} %collective-permute-done.refs_0_), channel_id=1, source_target_pairs={{0,16},{16,0},{1,17},{17,1},{2,18},{18,2},{3,19},{19,3},{4,20},{20... | collective-permute-start | bytes 1572872 | tf_op jit(solution)/shard_map/ppermute | solution.py:418
  45.5 63.7 %collective-permute-start.7 = (bf16[512,512]{1,0:T(8,128)(2,1)S(1)}, bf16[512,512]{1,0:T(8,128)(2,1)S(1)}, u32[]{:S(2)}, u32[]{:S(2)}) collective-permute-start(bf16[512,512]{1,0:T(8,128)(2,1)S(1)} %collective-permute-done.2.refs_4_), channel_id=1, source_target_pairs={{0,16},{16,0},{1,17},{17,1},{2,18},{18,2},{3,19},{19,3},{4,20},{20... | collective-permute-start | bytes 1572872 | tf_op jit(solution)/shard_map/ppermute | solution.py:418
  96.7 29.2 %copy-start.3 = (s32[128]{0:T(128)S(1)}, s32[128]{0:T(128)}, u32[]{:S(2)}) copy-start(s32[128]{0:T(128)} %get-tuple-element.35.position) | copy-start | bytes 1540
  96.7 14.1 %collective-permute-start.11 = (bf16[512,512]{1,0:T(8,128)(2,1)S(1)}, bf16[512,512]{1,0:T(8,128)(2,1)S(1)}, u32[]{:S(2)}, u32[]{:S(2)}) collective-permute-start(bf16[512,512]{1,0:T(8,128)(2,1)S(1)} %broadcast_select_fusion.3.refs_0_), channel_id=1, source_target_pairs={{0,16},{16,0},{1,17},{17,1},{2,18},{18,2},{3,19},{19,3},{4,20},{20... | collective-permute-start | bytes 1572872 | tf_op jit(solution)/shard_map/ppermute | solution.py:420
  106.3 10.9 %collective-permute-start.15 = (bf16[512,512]{1,0:T(8,128)(2,1)S(1)}, bf16[512,512]{1,0:T(8,128)(2,1)}, u32[]{:S(2)}, u32[]{:S(2)}) collective-permute-start(bf16[512,512]{1,0:T(8,128)(2,1)S(1)} %broadcast_select_fusion.2.refs_4_), channel_id=1, source_target_pairs={{0,16},{16,0},{1,17},{17,1},{2,18},{18,2},{3,19},{19,3},{4,20},{20... | collective-permute-start | bytes 1572872 | tf_op jit(solution)/shard_map/ppermute | solution.py:420
  107.9 9.3 %collective-permute-start.5 = (bf16[512,512]{1,0:T(8,128)(2,1)S(1)}, bf16[512,512]{1,0:T(8,128)(2,1)}, u32[]{:S(2)}, u32[]{:S(2)}) collective-permute-start(bf16[512,512]{1,0:T(8,128)(2,1)S(1)} %collective-permute-done.refs_0_), channel_id=1, source_target_pairs={{0,1},{1,0},{2,3},{3,2},{4,5},{5,4},{6,7},{7,6},{8,9},{9,8},{10,11... | collective-permute-start | bytes 1572872 | tf_op jit(solution)/shard_map/ppermute | solution.py:416
  107.9 9.8 %collective-permute-start.6 = (bf16[512,512]{1,0:T(8,128)(2,1)S(1)}, bf16[512,512]{1,0:T(8,128)(2,1)}, u32[]{:S(2)}, u32[]{:S(2)}) collective-permute-start(bf16[512,512]{1,0:T(8,128)(2,1)S(1)} %collective-permute-done.4.refs_1_), channel_id=1, source_target_pairs={{0,1},{1,0},{2,3},{3,2},{4,5},{5,4},{6,7},{7,6},{8,9},{9,8},{10,11... | collective-permute-start | bytes 1572872 | tf_op jit(solution)/shard_map/ppermute | solution.py:416
  108.4 0.8 copy-start.5
  109.2 0.8 copy-start.7
  110.0 7.8 %collective-permute-start.8 = (bf16[512,512]{1,0:T(8,128)(2,1)S(1)}, bf16[512,512]{1,0:T(8,128)(2,1)}, u32[]{:S(2)}, u32[]{:S(2)}) collective-permute-start(bf16[512,512]{1,0:T(8,128)(2,1)S(1)} %collective-permute-done.2.refs_4_), channel_id=1, source_target_pairs={{0,1},{1,0},{2,3},{3,2},{4,5},{5,4},{6,7},{7,6},{8,9},{9,8},{10,11... | collective-permute-start | bytes 1572872 | tf_op jit(solution)/shard_map/ppermute | solution.py:416
  110.8 7.6 %collective-permute-start.12 = (bf16[512,512]{1,0:T(8,128)(2,1)S(1)}, bf16[512,512]{1,0:T(8,128)(2,1)}, u32[]{:S(2)}, u32[]{:S(2)}) collective-permute-start(bf16[512,512]{1,0:T(8,128)(2,1)S(1)} %broadcast_select_fusion.3.refs_0_), channel_id=1, source_target_pairs={{0,1},{1,0},{2,3},{3,2},{4,5},{5,4},{6,7},{7,6},{8,9},{9,8},{10,11... | collective-permute-start | bytes 1572872 | tf_op jit(solution)/shard_map/ppermute | solution.py:416
  117.3 5.6 %collective-permute-start.9 = (bf16[512,512]{1,0:T(8,128)(2,1)}, bf16[512,512]{1,0:T(8,128)(2,1)}, u32[]{:S(2)}, u32[]{:S(2)}) collective-permute-start(bf16[512,512]{1,0:T(8,128)(2,1)} %copy-done.7), channel_id=1, source_target_pairs={{0,1},{1,0},{2,3},{3,2},{4,5},{5,4},{6,7},{7,6},{8,9},{9,8},{10,11... | collective-permute-start | bytes 1572872 | tf_op jit(solution)/shard_map/ppermute | solution.py:416
  117.3 8.5 %collective-permute-start.13 = (bf16[512,512]{1,0:T(8,128)(2,1)S(1)}, bf16[512,512]{1,0:T(8,128)(2,1)}, u32[]{:S(2)}, u32[]{:S(2)}) collective-permute-start(bf16[512,512]{1,0:T(8,128)(2,1)S(1)} %collective-permute-done.11.refs_1_), channel_id=1, source_target_pairs={{0,1},{1,0},{2,3},{3,2},{4,5},{5,4},{6,7},{7,6},{8,9},{9,8},{10,11... | collective-permute-start | bytes 1572872 | tf_op jit(solution)/shard_map/ppermute | solution.py:416
  117.8 8.0 %collective-permute-start.16 = (bf16[512,512]{1,0:T(8,128)(2,1)S(1)}, bf16[512,512]{1,0:T(8,128)(2,1)}, u32[]{:S(2)}, u32[]{:S(2)}) collective-permute-start(bf16[512,512]{1,0:T(8,128)(2,1)S(1)} %broadcast_select_fusion.2.refs_4_), channel_id=1, source_target_pairs={{0,1},{1,0},{2,3},{3,2},{4,5},{5,4},{6,7},{7,6},{8,9},{9,8},{10,11... | collective-permute-start | bytes 1572872 | tf_op jit(solution)/shard_map/ppermute | solution.py:416
  117.8 8.0 %collective-permute-start.17 = (bf16[512,512]{1,0:T(8,128)(2,1)}, bf16[512,512]{1,0:T(8,128)(2,1)}, u32[]{:S(2)}, u32[]{:S(2)}) collective-permute-start(bf16[512,512]{1,0:T(8,128)(2,1)} %collective-permute-done.15.refs_5_), channel_id=1, source_target_pairs={{0,1},{1,0},{2,3},{3,2},{4,5},{5,4},{6,7},{7,6},{8,9},{9,8},{10,11... | collective-permute-start | bytes 1572872 | tf_op jit(solution)/shard_map/ppermute | solution.py:416
  118.4 23.5 %collective-permute-start.18 = (bf16[512,512]{1,0:T(8,128)(2,1)S(1)}, bf16[512,512]{1,0:T(8,128)(2,1)}, u32[]{:S(2)}, u32[]{:S(2)}) collective-permute-start(bf16[512,512]{1,0:T(8,128)(2,1)S(1)} %collective-permute-done.refs_0_), channel_id=1, source_target_pairs={{4,8},{8,4},{5,9},{9,5},{6,10},{10,6},{7,11},{11,7},{20,24},{24,20... | collective-permute-start | bytes 1572872 | tf_op jit(solution)/shard_map/ppermute | solution.py:423
  122.8 35.6 %collective-permute-start.26 = (bf16[512,512]{1,0:T(8,128)(2,1)S(1)}, bf16[512,512]{1,0:T(8,128)(2,1)}, u32[]{:S(2)}, u32[]{:S(2)}) collective-permute-start(bf16[512,512]{1,0:T(8,128)(2,1)S(1)} %collective-permute-done.2.refs_4_), channel_id=1, source_target_pairs={{4,8},{8,4},{5,9},{9,5},{6,10},{10,6},{7,11},{11,7},{20,24},{24,20... | collective-permute-start | bytes 1572872 | tf_op jit(solution)/shard_map/ppermute | solution.py:423
  125.8 3.3 %copy-start.1 = (bf16[1,384,2048]{2,1,0:T(8,128)(2,1)S(1)}, bf16[1,384,2048]{2,1,0:T(8,128)(2,1)}, u32[]{:S(2)}) copy-start(bf16[1,384,2048]{2,1,0:T(8,128)(2,1)} %param.9) | copy-start | bytes 4718596
  129.1 10.3 %copy-start.2 = (bf16[2048,1024]{1,0:T(8,128)(2,1)S(1)}, bf16[2048,1024]{1,0:T(8,128)(2,1)}, u32[]{:S(2)}) copy-start(bf16[2048,1024]{1,0:T(8,128)(2,1)} %refs_0_.3) | copy-start | bytes 12582916
  139.4 9.8 %copy-start.6 = (bf16[512,512]{1,0:T(8,128)(2,1)S(1)}, bf16[512,512]{1,0:T(8,128)(2,1)}, u32[]{:S(2)}) copy-start(bf16[512,512]{1,0:T(8,128)(2,1)} %copy-done.5) | copy-start | bytes 1572868
  139.4 9.8 %copy-start.8 = (bf16[512,512]{1,0:T(8,128)(2,1)S(1)}, bf16[512,512]{1,0:T(8,128)(2,1)}, u32[]{:S(2)}) copy-start(bf16[512,512]{1,0:T(8,128)(2,1)} %copy-done.7) | copy-start | bytes 1572868
  141.9 18.8 %collective-permute-start.19 = (bf16[512,512]{1,0:T(8,128)(2,1)}, bf16[512,512]{1,0:T(8,128)(2,1)S(1)}, u32[]{:S(2)}, u32[]{:S(2)}) collective-permute-start(bf16[512,512]{1,0:T(8,128)(2,1)} %collective-permute-done.18), channel_id=1, source_target_pairs={{4,0},{8,12},{5,1},{9,13},{6,2},{10,14},{7,3},{11,15},{20,16},{24,... | collective-permute-start | bytes 1572872 | tf_op jit(solution)/shard_map/ppermute | solution.py:427
  152.3 21.4 %collective-permute-start.20 = (bf16[192,1024]{1,0:T(8,128)(2,1)S(1)}, bf16[192,1024]{1,0:T(8,128)(2,1)S(1)}, u32[]{:S(2)}, u32[]{:S(2)}) collective-permute-start(bf16[192,1024]{1,0:T(8,128)(2,1)S(1)} %project.6), channel_id=1, source_target_pairs={{0,2},{2,0},{1,3},{3,1},{4,6},{6,4},{5,7},{7,5},{8,10},{10,8},{9,1... | collective-permute-start | bytes 1179656 | tf_op jit(solution)/shard_map/ppermute | solution.py:434
  153.2 20.5 %collective-permute-start.21 = (bf16[192,1024]{1,0:T(8,128)(2,1)S(1)}, bf16[192,1024]{1,0:T(8,128)(2,1)S(1)}, u32[]{:S(2)}, u32[]{:S(2)}) collective-permute-start(bf16[192,1024]{1,0:T(8,128)(2,1)S(1)} %project.5), channel_id=1, source_target_pairs={{0,2},{2,0},{1,3},{3,1},{4,6},{6,4},{5,7},{7,5},{8,10},{10,8},{9,1... | collective-permute-start | bytes 1179656 | tf_op jit(solution)/shard_map/ppermute | solution.py:434
  157.6 34.2 %collective-permute-start.25 = (bf16[192,1024]{1,0:T(8,128)(2,1)S(1)}, bf16[192,1024]{1,0:T(8,128)(2,1)S(1)}, u32[]{:S(2)}, u32[]{:S(2)}) collective-permute-start(bf16[192,1024]{1,0:T(8,128)(2,1)S(1)} %project.7), channel_id=1, source_target_pairs={{0,2},{2,0},{1,3},{3,1},{4,6},{6,4},{5,7},{7,5},{8,10},{10,8},{9,1... | collective-permute-start | bytes 1179656 | tf_op jit(solution)/shard_map/ppermute | solution.py:434
  158.5 15.3 %collective-permute-start.27 = (bf16[512,512]{1,0:T(8,128)(2,1)}, bf16[512,512]{1,0:T(8,128)(2,1)S(1)}, u32[]{:S(2)}, u32[]{:S(2)}) collective-permute-start(bf16[512,512]{1,0:T(8,128)(2,1)} %collective-permute-done.26), channel_id=1, source_target_pairs={{4,0},{8,12},{5,1},{9,13},{6,2},{10,14},{7,3},{11,15},{20,16},{24,... | collective-permute-start | bytes 1572872 | tf_op jit(solution)/shard_map/ppermute | solution.py:429
  161.8 13.2 %collective-permute-start.22 = (bf16[512,512]{1,0:T(8,128)(2,1)S(1)}, bf16[512,512]{1,0:T(8,128)(2,1)S(1)}, u32[]{:S(2)}, u32[]{:S(2)}) collective-permute-start(bf16[512,512]{1,0:T(8,128)(2,1)S(1)} %broadcast_select_fusion.1.refs_0_), channel_id=1, source_target_pairs={{0,16},{16,0},{1,17},{17,1},{2,18},{18,2},{3,19},{19,3},{4,20},{20... | collective-permute-start | bytes 1572872 | tf_op jit(solution)/shard_map/ppermute | solution.py:432
  173.7 15.6 %collective-permute-start.23 = (bf16[512,512]{1,0:T(8,128)(2,1)S(1)}, bf16[512,512]{1,0:T(8,128)(2,1)S(1)}, u32[]{:S(2)}, u32[]{:S(2)}) collective-permute-start(bf16[512,512]{1,0:T(8,128)(2,1)S(1)} %broadcast_select_fusion.1.refs_0_), channel_id=1, source_target_pairs={{0,1},{1,0},{2,3},{3,2},{4,5},{5,4},{6,7},{7,6},{8,9},{9,8},{10,11... | collective-permute-start | bytes 1572872 | tf_op jit(solution)/shard_map/ppermute | solution.py:416
  174.9 14.4 %collective-permute-start.28 = (bf16[512,512]{1,0:T(8,128)(2,1)S(1)}, bf16[512,512]{1,0:T(8,128)(2,1)S(1)}, u32[]{:S(2)}, u32[]{:S(2)}) collective-permute-start(bf16[512,512]{1,0:T(8,128)(2,1)S(1)} %broadcast_select_fusion.refs_0_), channel_id=1, source_target_pairs={{0,16},{16,0},{1,17},{17,1},{2,18},{18,2},{3,19},{19,3},{4,20},{20... | collective-permute-start | bytes 1572872 | tf_op jit(solution)/shard_map/ppermute | solution.py:437
  175.0 14.3 %collective-permute-start.24 = (bf16[512,512]{1,0:T(8,128)(2,1)S(1)}, bf16[512,512]{1,0:T(8,128)(2,1)S(1)}, u32[]{:S(2)}, u32[]{:S(2)}) collective-permute-start(bf16[512,512]{1,0:T(8,128)(2,1)S(1)} %collective-permute-done.22.refs_1_), channel_id=1, source_target_pairs={{0,1},{1,0},{2,3},{3,2},{4,5},{5,4},{6,7},{7,6},{8,9},{9,8},{10,11... | collective-permute-start | bytes 1572872 | tf_op jit(solution)/shard_map/ppermute | solution.py:416
  181.7 14.1 %collective-permute-start.29 = (bf16[512,512]{1,0:T(8,128)(2,1)S(1)}, bf16[512,512]{1,0:T(8,128)(2,1)S(1)}, u32[]{:S(2)}, u32[]{:S(2)}) collective-permute-start(bf16[512,512]{1,0:T(8,128)(2,1)S(1)} %broadcast_select_fusion.refs_0_), channel_id=1, source_target_pairs={{0,1},{1,0},{2,3},{3,2},{4,5},{5,4},{6,7},{7,6},{8,9},{9,8},{10,11... | collective-permute-start | bytes 1572872 | tf_op jit(solution)/shard_map/ppermute | solution.py:416
  189.3 6.5 %collective-permute-start.30 = (bf16[512,512]{1,0:T(8,128)(2,1)S(1)}, bf16[512,512]{1,0:T(8,128)(2,1)S(1)}, u32[]{:S(2)}, u32[]{:S(2)}) collective-permute-start(bf16[512,512]{1,0:T(8,128)(2,1)S(1)} %collective-permute-done.28.refs_1_), channel_id=1, source_target_pairs={{0,1},{1,0},{2,3},{3,2},{4,5},{5,4},{6,7},{7,6},{8,9},{9,8},{10,11... | collective-permute-start | bytes 1572872 | tf_op jit(solution)/shard_map/ppermute | solution.py:416
  190.4 7.4 %collective-permute-start.32 = (bf16[192,512]{1,0:T(8,128)(2,1)S(1)}, bf16[192,512]{1,0:T(8,128)(2,1)S(1)}, u32[]{:S(2)}, u32[]{:S(2)}) collective-permute-start(bf16[192,512]{1,0:T(8,128)(2,1)S(1)} %project.8), channel_id=1, source_target_pairs={{0,2},{2,0},{1,3},{3,1},{4,6},{6,4},{5,7},{7,5},{8,10},{10,8},{9,1... | collective-permute-start | bytes 589832 | tf_op jit(solution)/shard_map/ppermute | solution.py:443
  196.9 7.1 %collective-permute-start.31 = (bf16[192,512]{1,0:T(8,128)(2,1)S(1)}, bf16[192,512]{1,0:T(8,128)(2,1)S(1)}, u32[]{:S(2)}, u32[]{:S(2)}) collective-permute-start(bf16[192,512]{1,0:T(8,128)(2,1)S(1)} %project.9), channel_id=1, source_target_pairs={{0,2},{2,0},{1,3},{3,1},{4,6},{6,4},{5,7},{7,5},{8,10},{10,8},{9,1... | collective-permute-start | bytes 589832 | tf_op jit(solution)/shard_map/ppermute | solution.py:446

commit v9 on v8

--- a/solution.py
+++ b/solution.py
@@ -243,7 +243,7 @@
 
 def blocks(columns):
     cut = min(COLUMNS, columns)
-    return [slice(k, k + cut) for k in range(0, columns, cut)]
+    return [slice(k, min(k + cut, columns)) for k in range(0, columns, cut)]
 
 
 def parts_of(control, refs):
@@ -252,8 +252,11 @@
         return [
             (0, [refs[0].at[pl.ds(pl.multiple_of(control[6 + n] * depth, depth), depth)] for n in range(4)])
         ]
-    columns = refs[0].shape[1]
-    return [(k // 4 * columns, refs[k : k + 4]) for k in range(0, len(refs), 4)]
+    parts, first = [], 0
+    for k in range(0, len(refs), 4):
+        parts.append((first, refs[k : k + 4]))
+        first += refs[k].shape[1]
+    return parts
 
 
 def project_kernel(control, left, *refs):
@@ -272,7 +275,7 @@
 
 def project(control, left, pieces, came=None, base=None, out=None, width=None):
     half = left.shape[1]
-    columns = pieces[0].shape[1] * max(1, len(pieces) // 4)
+    columns = sum(piece.shape[1] for piece in pieces[::4])
     vmem = pl.BlockSpec(memory_space=pltpu.VMEM)
     in_specs = [vmem]
     operands = [left]
@@ -306,28 +309,26 @@
     )(control, *operands)
 
 
-def pick_kernel(asked, pool, out):
-    owner = pl.program_id(0)
-
-    def copy(n, carry):
-        out[0, n] = pool[asked[owner, n]]
-        return carry
-
-    lax.fori_loop(0, asked.shape[1], copy, 0, unroll=8)
+def pick_kernel(asked, pool, out, sem):
+    owners, bucket = asked.shape
+    for owner in range(owners):
+
+        def start(n, carry):
+            pltpu.make_async_copy(pool.at[asked[owner, n]], out.at[owner, n], sem).start()
+            return carry
+
+        lax.fori_loop(0, bucket, start, 0, unroll=8)
+    pltpu.make_async_copy(out, out, sem).wait()
 
 
 def pick(pool, asked):
-    block = (1, asked.shape[1]) + pool.shape[1:]
+    hbm = pl.BlockSpec(memory_space=pltpu.HBM)
     return pl.pallas_call(
         pick_kernel,
         out_shape=jax.ShapeDtypeStruct(asked.shape + pool.shape[1:], jnp.bfloat16),
-        grid=(asked.shape[0],),
-        in_specs=[
-            pl.BlockSpec(memory_space=pltpu.SMEM),
-            pl.BlockSpec(memory_space=pltpu.VMEM),
-        ],
-        out_specs=pl.BlockSpec(block, lambda owner: (owner, 0, 0, 0, 0)),
-        compiler_params=pltpu.CompilerParams(vmem_limit_bytes=12 * MIB),
+        in_specs=[pl.BlockSpec(memory_space=pltpu.SMEM), hbm],
+        out_specs=hbm,
+        scratch_shapes=[pltpu.SemaphoreType.DMA],
         cost_estimate=cost(),
         name="pick",
     )(asked, pool)
@@ -370,8 +371,8 @@
 
     if owner_count == 4:
         middle = (seq == 1) | (seq == 2)
-        cut = columns // 2
-        parts = [quarter[:, :cut], quarter[:, cut:]]
+        cut, early = columns // 2, columns // LANES * 5 // 8 * LANES
+        parts = [quarter[:, :early], quarter[:, early:]]
         pair = functools.partial(lax.ppermute, axis_name="seq", perm=[(0, 1), (1, 0), (2, 3), (3, 2)])
         cross = functools.partial(lax.ppermute, axis_name="seq", perm=[(1, 2), (2, 1)])
         forward = functools.partial(lax.ppermute, axis_name="seq", perm=[(1, 0), (2, 3)])
@@ -420,7 +421,8 @@
     next_across = [swap_group(part) for part in next_shard]
     near_all = four(near[0], near_across[0]) + four(near[1], near_across[1])
     next_all = four(next_shard[0], next_across[0]) + four(next_shard[1], next_across[1])
-    far = [cross(after(part, *next_across)) for part in near]
+    far = [near[0][:, :cut], jnp.concatenate([near[0][:, cut:], near[1]], axis=1)]
+    far = [cross(after(part, *next_across)) for part in far]
 
     keys, values = place(position, after(pages, *near_all, *next_all), fresh)
     left = attend(1, control, tables, queries[0], keys, values, slots)
@@ -435,18 +437,18 @@
     stay = attend(0, control, tables, after(queries[0], sent[2], far[0]), keys, values, slots)
     far[1] = jnp.where(middle, far[1], after(far_on[1], stay))
     far_across.append(swap_group(far[1]))
-    far_all = [four(far[n], far_across[n], stay) for n in (0, 1)]
+    far_all = [four(far[0], far_across[0], stay)]
     total = columns * owner_count
     out = project(control, after(stay, *came[:2]), [out_weight], came[0], 10, None, total)
     out = project(control, stay, near_all, came[1], 11, out, total)
+    out = project(control, stay, next_all, came[2], 12, out, total)
     sent.append(project(control, after(left, out), far_all[0]))
     came.append(swap_tp(sent[3]))
-    out = project(control, after(stay, sent[3]), next_all, came[2], 12, out, total)
-    sent.append(project(control, after(left, out), far_all[1]))
+    far_all.append(four(far[1], far_across[1], sent[3]))
+    sent.append(project(control, left, far_all[1]))
     came.append(swap_tp(sent[4]))
-    for n in range(2):
-        out = project(control, after(stay, sent[4]), far_all[n], came[n + 3], 13 + n, out, total)
-    return out
+    out = project(control, after(stay, sent[4]), far_all[0], came[3], 13, out, total)
+    return project(control, stay, far_all[1], came[4], 14, out, total)
 
 
 def solution(mesh):

time: 207 us -> 332 us (1.60)
  Pallas kernels: 51.5 us -> 179 us
  blocking collectives: 10.8 us -> 0 us
  waiting for transfers between devices: 84.3 us -> 88 us
    pallas_call x1, Pallas kernels: 1.42 us -> 129 us  [pick(): pl.pallas_call(pick_kernel, out_shape=jax.ShapeDtypeStruct(asked.shape +...]
    ppermute x2, waiting for transfers between devices: 5.89 us -> 17.1 us  [shards(): next_across = [swap_group(part) for part in next_shard]]
    all_to_all x1 -> x0, blocking collectives: 10.8 us -> none  [shards(): lax.all_to_all(wanted, 'seq', split_axis=0, concat_axis=0, tiled=True)]
    all_to_all x0 -> x1, waiting for transfers between devices: none -> 7.8 us  [shards(): lax.all_to_all(wanted, 'seq', split_axis=0, concat_axis=0, tiled=True)]
    ppermute x1, waiting for transfers between devices: 7.6 us -> 0.01 us  [shards(): far_across.append(swap_group(far[1]))]
    ppermute x1, starting transfers between devices: 7.32 us -> 1.32 us  [shards(): far_on = [forward(after(far[0], left))]]
    unnamed x29 -> x25, local copies, waits for them, and re-layouts: 6.91 us -> 1.84 us
    all_to_all x0 -> x1, starting transfers between devices: none -> 4.76 us  [shards(): lax.all_to_all(wanted, 'seq', split_axis=0, concat_axis=0, tiled=True)]
  transfers between devices with their start and end apart: 34 -> 35, of which waited for: 10 -> 7; matrix products, arithmetic and copies ran while one was open for 2% -> 3% of each run, Pallas kernels for 24% -> 54%
where the time goes in v9:
time: 332 us; the launch traced here: 328 us
  Pallas kernels  179 us (54%)
  waiting for transfers between devices  88 us (27%)
  starting transfers between devices  49.4 us (15%)
  local copies, waits for them, and re-layouts  5.37 us (2%)
  other arithmetic  4.9 us (1%)
    pallas_call x1, Pallas kernels, pick(): pl.pallas_call(pick_kernel, out_shape=jax.ShapeDtypeStruct(asked.shape +...  129 us
    ppermute x2, waiting for transfers between devices, shards(): next_shard = [jnp.where(middle, part, forward(part)) for part in inner]  58.9 us
    pallas_call x10, Pallas kernels, project(): pl.pallas_call(kernel, out_shape=out_shape, grid_spec=pltpu.PrefetchScala...  24.8 us
    pallas_call x2, Pallas kernels, attend(): pl.pallas_call(functools.partial(attend_kernel, fresh_base, side), out_sh...  19.8 us
    ppermute x2, waiting for transfers between devices, shards(): next_across = [swap_group(part) for part in next_shard]  17.1 us
    all_to_all x1, waiting for transfers between devices, shards(): lax.all_to_all(wanted, 'seq', split_axis=0, concat_axis=0, tiled=True)  7.8 us
    ppermute x2, starting transfers between devices, shards(): far = [cross(after(part, *next_across)) for part in far]  7.38 us
  transfers between devices with their start and end apart: 35, of which 7 were waited for; matrix products, arithmetic and copies ran while one was open for 3% of the time, Pallas kernels for 54%

profile of v9, /device:TPU:16, one launch (start us, length us, event | category | flops | bytes accessed | tf_op | source)
XLA Modules:
  0.0 327.7 jit_solution(15917437609927404625)
XLA Ops:
  0.0 1.1 constant_dynamic-slice_fusion
  1.1 1.6 collective-permute-start
  2.8 1.9 collective-permute-start.1
  4.7 2.6 rank.1
  7.4 4.8 %all-to-all-start = ((s32[4,1,64]{2,1,0:T(1,128)}), s32[4,1,64]{2,1,0:T(1,128)S(1)}, u32[]{:S(2)}, u32[]{:S(2)}) async-start(s32[4,1,64]{2,1,0:T(1,128)} %bitcast.39), calls=%async_computation | async-start | bytes 4096 | tf_op jit(solution)/shard_map/all_to_all | solution.py:382
  12.1 1.0 dynamic-slice.1
  13.2 7.8 %all-to-all-done = s32[4,1,64]{2,1,0:T(1,128)S(1)} async-done(((s32[4,1,64]{2,1,0:T(1,128)}), s32[4,1,64]{2,1,0:T(1,128)S(1)}, u32[]{:S(2)}, u32[]{:S(2)}) %all-to-all-start) | async-done | bytes 1056 | tf_op jit(solution)/shard_map/all_to_all | solution.py:382
  21.0 1.4 collective-permute-start.2
  22.4 2.2 collective-permute-start.3
  24.6 128.9 %pick.1 = bf16[4,64,2,16,256]{4,3,2,1,0:T(8,128)(2,1)} custom-call(s32[4,64]{1,0:T(4,128)} %bitcast.38, bf16[256,2,16,256]{3,2,1,0:T(8,128)(2,1)} %bitcast.41), custom_call_target="tpu_custom_call" | custom-call | flops 3000000000 | bytes 1000 | tf_op jit(solution)/shard_map/pick/pallas_call | solution.py:326
  153.5 4.8 %all-to-all-start.1 = ((bf16[4,64,2,16,256]{4,3,2,1,0:T(8,128)(2,1)}), bf16[4,64,2,16,256]{4,3,2,1,0:T(8,128)(2,1)}, u32[]{:S(2)}, u32[]{:S(2)}) async-start(bf16[4,64,2,16,256]{4,3,2,1,0:T(8,128)(2,1)} %pick.1), calls=%async_computation.1 | async-start | bytes 8388608 | tf_op jit(solution)/shard_map/all_to_all | solution.py:393
  158.4 3.9 %collective-permute-start.10 = (bf16[512,640]{1,0:T(8,128)(2,1)S(1)}, bf16[512,640]{1,0:T(8,128)(2,1)}, u32[]{:S(2)}, u32[]{:S(2)}) collective-permute-start(bf16[512,640]{1,0:T(8,128)(2,1)S(1)} %collective-permute-done.1), channel_id=1, source_target_pairs={{4,0},{8,12},{5,1},{9,13},{6,2},{10,14},{7,3},{11,15},{20,16},{24,... | collective-permute-start | bytes 1966088 | tf_op jit(solution)/shard_map/ppermute | solution.py:420
  162.3 2.0 collective-permute-start.14
  164.3 1.6 collective-permute-start.4
  166.4 52.8 %collective-permute-done.10 = bf16[512,640]{1,0:T(8,128)(2,1)} collective-permute-done((bf16[512,640]{1,0:T(8,128)(2,1)S(1)}, bf16[512,640]{1,0:T(8,128)(2,1)}, u32[]{:S(2)}, u32[]{:S(2)}) %collective-permute-start.10) | collective-permute-done | bytes 655392 | tf_op jit(solution)/shard_map/ppermute | solution.py:420
  219.2 1.2 broadcast_select_fusion.refs_0_
  220.4 6.0 %collective-permute-done.14 = bf16[512,384]{1,0:T(8,128)(2,1)} collective-permute-done((bf16[512,384]{1,0:T(8,128)(2,1)S(1)}, bf16[512,384]{1,0:T(8,128)(2,1)}, u32[]{:S(2)}, u32[]{:S(2)}) %collective-permute-start.14) | collective-permute-done | bytes 393248 | tf_op jit(solution)/shard_map/ppermute | solution.py:420
  226.4 1.5 collective-permute-start.11
  229.8 13.7 %collective-permute-done.11.refs_1_ = bf16[512,640]{1,0:T(8,128)(2,1)} collective-permute-done((bf16[512,640]{1,0:T(8,128)(2,1)S(1)}, bf16[512,640]{1,0:T(8,128)(2,1)}, u32[]{:S(2)}, u32[]{:S(2)}) %collective-permute-start.11) | collective-permute-done | bytes 655392 | tf_op jit(solution)/shard_map/ppermute | solution.py:421
  244.2 3.4 %collective-permute-done.15.refs_5_ = bf16[512,384]{1,0:T(8,128)(2,1)} collective-permute-done((bf16[512,384]{1,0:T(8,128)(2,1)S(1)}, bf16[512,384]{1,0:T(8,128)(2,1)}, u32[]{:S(2)}, u32[]{:S(2)}) %collective-permute-start.15) | collective-permute-done | bytes 393248 | tf_op jit(solution)/shard_map/ppermute | solution.py:421
  248.6 1.1 copy.22
  250.8 5.5 %collective-permute-start.18 = (bf16[512,512]{1,0:T(8,128)(2,1)}, bf16[512,512]{1,0:T(8,128)(2,1)}, u32[]{:S(2)}, u32[]{:S(2)}) collective-permute-start(bf16[512,512]{1,0:T(8,128)(2,1)} %slice.22), channel_id=1, source_target_pairs={{4,8},{8,4},{5,9},{9,5},{6,10},{10,6},{7,11},{11,7},{20,24},{24,20... | collective-permute-start | bytes 1572872 | tf_op jit(solution)/shard_map/ppermute | solution.py:425
  257.2 1.9 collective-permute-start.20
  259.2 3.3 place.1
  262.4 10.2 %attend.2.left = bf16[4,192,512]{2,1,0:T(8,128)(2,1)S(1)} custom-call(s32[15]{0:T(128)S(1)} %stack.63.control, s32[6]{0:T(128)S(1)} %get-tuple-element.68.hist_at, s32[6]{0:T(128)S(1)} %get-tuple-element.67.hist_steps, s32[6]{0:T(128)S(1)} %get-tuple-element.64.fresh_at, s32[6]{0:T(128)S(1)} %get-tuple-element.63.fresh_steps, ...), custom_call_target="tpu_custom_call" | custom-call | flops 1000000000 | bytes 1000 | tf_op jit(solution)/shard_map/attend/pallas_call | solution.py:221
  272.7 1.5 project.5
  274.3 1.3 collective-permute-start.19
  275.6 3.3 project.6
  278.9 0.9 collective-permute-start.24
  279.8 1.2 collective-permute-start.25
  281.0 1.5 collective-permute-start.21
  282.5 3.6 %project.7 = bf16[192,1024]{1,0:T(8,128)(2,1)S(1)} custom-call(s32[15]{0:T(128)S(1)} %stack.63.control, bf16[4,192,512]{2,1,0:T(8,128)(2,1)S(1)} %attend.2.left, bf16[512,640]{1,0:T(8,128)(2,1)S(1)} %broadcast_select_fusion.refs_0_, bf16[512,640]{1,0:T(8,128)(2,1)} %collective-permute-done.11.refs_1_, bf16[512,640]{1,0:T(8,128)(2,1)} %collective-permute-done.12.refs_2_, ...), custom_call_target="tpu_custom_call" | custom-call | flops 3000000000 | bytes 1000 | tf_op jit(solution)/shard_map/project/pallas_call | solution.py:299
  286.0 0.9 collective-permute-start.23
  286.9 1.1 broadcast_select_fusion.2.refs_0_
  288.0 1.6 collective-permute-start.26
  289.6 9.6 %attend.3.left = bf16[4,192,512]{2,1,0:T(8,128)(2,1)S(1)} custom-call(s32[15]{0:T(128)S(1)} %stack.63.control, s32[6]{0:T(128)S(1)} %get-tuple-element.68.hist_at, s32[6]{0:T(128)S(1)} %get-tuple-element.67.hist_steps, s32[6]{0:T(128)S(1)} %get-tuple-element.64.fresh_at, s32[6]{0:T(128)S(1)} %get-tuple-element.63.fresh_steps, ...), custom_call_target="tpu_custom_call" | custom-call | flops 16000000000 | bytes 1000 | tf_op jit(solution)/shard_map/attend/pallas_call | solution.py:221
  299.2 1.1 broadcast_select_fusion.1.refs_0_
  300.9 2.3 finish.5.refs_8_
  303.7 4.0 %finish.6.refs_8_ = bf16[1,192,4096]{2,1,0:T(8,128)(2,1)} custom-call(s32[15]{0:T(128)S(1)} %stack.63.control, bf16[4,192,512]{2,1,0:T(8,128)(2,1)S(1)} %attend.3.left, bf16[192,1024]{1,0:T(8,128)(2,1)S(1)} %collective-permute-done.24.came, bf16[512,640]{1,0:T(8,128)(2,1)S(1)} %collective-permute-done.refs_0_, ...), custom_call_target="tpu_custom_call", output_to_operand_aliasing={{}: (11, {})} | custom-call | flops 3000000000 | bytes 1000 | tf_op jit(solution)/shard_map/finish/pallas_call | solution.py:299
  307.7 4.3 %finish.7.refs_4_ = bf16[1,192,4096]{2,1,0:T(8,128)(2,1)} custom-call(s32[15]{0:T(128)S(1)} %stack.63.control, bf16[4,192,512]{2,1,0:T(8,128)(2,1)S(1)} %attend.3.left, bf16[192,1024]{1,0:T(8,128)(2,1)S(1)} %collective-permute-done.23.came, bf16[512,640]{1,0:T(8,128)(2,1)S(1)} %broadcast_select_fusion.refs_0_, ...), custom_call_target="tpu_custom_call", output_to_operand_aliasing={{}: (11, {})} | custom-call | flops 3000000000 | bytes 1000 | tf_op jit(solution)/shard_map/finish/pallas_call | solution.py:299
  312.1 1.1 project.8
  313.8 2.7 collective-permute-start.32
  316.5 1.1 project.9
  317.7 2.2 collective-permute-start.31
  319.9 2.4 collective-permute-done.32.came
  322.2 1.8 finish.8.refs_4_
  324.0 1.9 collective-permute-done.31.came
  325.9 1.8 finish.9
  (85 shorter events, 7.6 us)
Async XLA Ops:
  1.1 19.8 %collective-permute-start = (bf16[512,640]{1,0:T(8,128)(2,1)S(1)}, bf16[512,640]{1,0:T(8,128)(2,1)S(1)}, u32[]{:S(2)}, u32[]{:S(2)}) collective-permute-start(bf16[512,640]{1,0:T(8,128)(2,1)S(1)} %constant_dynamic-slice_fusion), channel_id=1, source_target_pairs={{0,4},{4,0},{8,12},{12,8},{1,5},{5,1},{9,13},{13,9},{2,6},{6,2},{1... | collective-permute-start | bytes 1966088 | tf_op jit(solution)/shard_map/ppermute | solution.py:379
  2.8 18.2 %collective-permute-start.1 = (bf16[512,640]{1,0:T(8,128)(2,1)S(1)}, bf16[512,640]{1,0:T(8,128)(2,1)S(1)}, u32[]{:S(2)}, u32[]{:S(2)}) collective-permute-start(bf16[512,640]{1,0:T(8,128)(2,1)S(1)} %constant_dynamic-slice_fusion), channel_id=1, source_target_pairs={{4,8},{8,4},{5,9},{9,5},{6,10},{10,6},{7,11},{11,7},{20,24},{24,20... | collective-permute-start | bytes 1966088 | tf_op jit(solution)/shard_map/ppermute | solution.py:379
  7.4 13.6 %all-to-all-start = ((s32[4,1,64]{2,1,0:T(1,128)}), s32[4,1,64]{2,1,0:T(1,128)S(1)}, u32[]{:S(2)}, u32[]{:S(2)}) async-start(s32[4,1,64]{2,1,0:T(1,128)} %bitcast.39), calls=%async_computation | async-start | bytes 4096 | tf_op jit(solution)/shard_map/all_to_all | solution.py:382
  21.0 3.7 %copy-start.10 = (s32[4,1,64]{2,1,0:T(1,128)}, s32[4,1,64]{2,1,0:T(1,128)S(1)}, u32[]{:S(2)}) copy-start(s32[4,1,64]{2,1,0:T(1,128)S(1)} %all-to-all-done) | copy-start | bytes 3076
  21.0 137.4 %copy-start.5 = (bf16[512,640]{1,0:T(8,128)(2,1)}, bf16[512,640]{1,0:T(8,128)(2,1)S(1)}, u32[]{:S(2)}) copy-start(bf16[512,640]{1,0:T(8,128)(2,1)S(1)} %collective-permute-done.1) | copy-start | bytes 1966084
  21.0 132.5 %collective-permute-start.2 = (bf16[512,384]{1,0:T(8,128)(2,1)S(1)}, bf16[512,384]{1,0:T(8,128)(2,1)S(1)}, u32[]{:S(2)}, u32[]{:S(2)}) collective-permute-start(bf16[512,384]{1,0:T(8,128)(2,1)S(1)} %dynamic-slice.1), channel_id=1, source_target_pairs={{0,4},{4,0},{8,12},{12,8},{1,5},{5,1},{9,13},{13,9},{2,6},{6,2},{1... | collective-permute-start | bytes 1179656 | tf_op jit(solution)/shard_map/ppermute | solution.py:386
  22.4 131.1 %collective-permute-start.3 = (bf16[512,384]{1,0:T(8,128)(2,1)S(1)}, bf16[512,384]{1,0:T(8,128)(2,1)S(1)}, u32[]{:S(2)}, u32[]{:S(2)}) collective-permute-start(bf16[512,384]{1,0:T(8,128)(2,1)S(1)} %dynamic-slice.1), channel_id=1, source_target_pairs={{4,8},{8,4},{5,9},{9,5},{6,10},{10,6},{7,11},{11,7},{20,24},{24,20... | collective-permute-start | bytes 1179656 | tf_op jit(solution)/shard_map/ppermute | solution.py:387
  153.5 8.7 %copy-start.6 = (bf16[512,384]{1,0:T(8,128)(2,1)}, bf16[512,384]{1,0:T(8,128)(2,1)S(1)}, u32[]{:S(2)}) copy-start(bf16[512,384]{1,0:T(8,128)(2,1)S(1)} %collective-permute-done.3) | copy-start | bytes 1179652
  153.5 105.6 %all-to-all-start.1 = ((bf16[4,64,2,16,256]{4,3,2,1,0:T(8,128)(2,1)}), bf16[4,64,2,16,256]{4,3,2,1,0:T(8,128)(2,1)}, u32[]{:S(2)}, u32[]{:S(2)}) async-start(bf16[4,64,2,16,256]{4,3,2,1,0:T(8,128)(2,1)} %pick.1), calls=%async_computation.1 | async-start | bytes 8388608 | tf_op jit(solution)/shard_map/all_to_all | solution.py:393
  158.4 60.8 %collective-permute-start.10 = (bf16[512,640]{1,0:T(8,128)(2,1)S(1)}, bf16[512,640]{1,0:T(8,128)(2,1)}, u32[]{:S(2)}, u32[]{:S(2)}) collective-permute-start(bf16[512,640]{1,0:T(8,128)(2,1)S(1)} %collective-permute-done.1), channel_id=1, source_target_pairs={{4,0},{8,12},{5,1},{9,13},{6,2},{10,14},{7,3},{11,15},{20,16},{24,... | collective-permute-start | bytes 1966088 | tf_op jit(solution)/shard_map/ppermute | solution.py:420
  162.3 64.2 %collective-permute-start.14 = (bf16[512,384]{1,0:T(8,128)(2,1)S(1)}, bf16[512,384]{1,0:T(8,128)(2,1)}, u32[]{:S(2)}, u32[]{:S(2)}) collective-permute-start(bf16[512,384]{1,0:T(8,128)(2,1)S(1)} %collective-permute-done.3), channel_id=1, source_target_pairs={{4,0},{8,12},{5,1},{9,13},{6,2},{10,14},{7,3},{11,15},{20,16},{24,... | collective-permute-start | bytes 1179656 | tf_op jit(solution)/shard_map/ppermute | solution.py:420
  164.3 63.6 %copy-start.7 = (bf16[512,384]{1,0:T(8,128)(2,1)S(1)}, bf16[512,384]{1,0:T(8,128)(2,1)}, u32[]{:S(2)}) copy-start(bf16[512,384]{1,0:T(8,128)(2,1)} %copy-done.6) | copy-start | bytes 1179652
  164.3 64.3 %copy-start.8 = (s32[1,384]{1,0:T(1,128)S(1)}, s32[1,384]{1,0:T(1,128)}, u32[]{:S(2)}) copy-start(s32[1,384]{1,0:T(1,128)} %param.13) | copy-start | bytes 4612
  164.3 65.4 %copy-start.9 = (s32[1,128]{1,0:T(1,128)S(1)}, s32[1,128]{1,0:T(1,128)}, u32[]{:S(2)}) copy-start(s32[1,128]{1,0:T(1,128)} %param.14) | copy-start | bytes 1540
  164.3 65.4 %copy-start.11 = (s32[1,128]{1,0:T(1,128)S(1)}, s32[1,128]{1,0:T(1,128)}, u32[]{:S(2)}) copy-start(s32[1,128]{1,0:T(1,128)} %param.15) | copy-start | bytes 1540
  164.3 64.5 %collective-permute-start.4 = (bf16[512,640]{1,0:T(8,128)(2,1)S(1)}, bf16[512,640]{1,0:T(8,128)(2,1)S(1)}, u32[]{:S(2)}, u32[]{:S(2)}) collective-permute-start(bf16[512,640]{1,0:T(8,128)(2,1)S(1)} %collective-permute-done.refs_0_), channel_id=1, source_target_pairs={{0,16},{16,0},{1,17},{17,1},{2,18},{18,2},{3,19},{19,3},{4,20},{20... | collective-permute-start | bytes 1966088 | tf_op jit(solution)/shard_map/ppermute | solution.py:419
  165.9 77.5 %collective-permute-start.5 = (bf16[512,640]{1,0:T(8,128)(2,1)S(1)}, bf16[512,640]{1,0:T(8,128)(2,1)}, u32[]{:S(2)}, u32[]{:S(2)}) collective-permute-start(bf16[512,640]{1,0:T(8,128)(2,1)S(1)} %collective-permute-done.refs_0_), channel_id=1, source_target_pairs={{0,1},{1,0},{2,3},{3,2},{4,5},{5,4},{6,7},{7,6},{8,9},{9,8},{10,11... | collective-permute-start | bytes 1966088 | tf_op jit(solution)/shard_map/ppermute | solution.py:417
  165.9 62.1 %collective-permute-start.7 = (bf16[512,384]{1,0:T(8,128)(2,1)S(1)}, bf16[512,384]{1,0:T(8,128)(2,1)S(1)}, u32[]{:S(2)}, u32[]{:S(2)}) collective-permute-start(bf16[512,384]{1,0:T(8,128)(2,1)S(1)} %collective-permute-done.2.refs_4_), channel_id=1, source_target_pairs={{0,16},{16,0},{1,17},{17,1},{2,18},{18,2},{3,19},{19,3},{4,20},{20... | collective-permute-start | bytes 1179656 | tf_op jit(solution)/shard_map/ppermute | solution.py:419
  219.2 24.7 %collective-permute-start.8 = (bf16[512,384]{1,0:T(8,128)(2,1)S(1)}, bf16[512,384]{1,0:T(8,128)(2,1)}, u32[]{:S(2)}, u32[]{:S(2)}) collective-permute-start(bf16[512,384]{1,0:T(8,128)(2,1)S(1)} %collective-permute-done.2.refs_4_), channel_id=1, source_target_pairs={{0,1},{1,0},{2,3},{3,2},{4,5},{5,4},{6,7},{7,6},{8,9},{9,8},{10,11... | collective-permute-start | bytes 1179656 | tf_op jit(solution)/shard_map/ppermute | solution.py:417
  226.4 17.0 %collective-permute-start.11 = (bf16[512,640]{1,0:T(8,128)(2,1)S(1)}, bf16[512,640]{1,0:T(8,128)(2,1)}, u32[]{:S(2)}, u32[]{:S(2)}) collective-permute-start(bf16[512,640]{1,0:T(8,128)(2,1)S(1)} %broadcast_select_fusion.refs_0_), channel_id=1, source_target_pairs={{0,16},{16,0},{1,17},{17,1},{2,18},{18,2},{3,19},{19,3},{4,20},{20... | collective-permute-start | bytes 1966088 | tf_op jit(solution)/shard_map/ppermute | solution.py:421
  228.0 19.6 %collective-permute-start.15 = (bf16[512,384]{1,0:T(8,128)(2,1)S(1)}, bf16[512,384]{1,0:T(8,128)(2,1)}, u32[]{:S(2)}, u32[]{:S(2)}) collective-permute-start(bf16[512,384]{1,0:T(8,128)(2,1)S(1)} %broadcast_select_fusion.3.refs_4_), channel_id=1, source_target_pairs={{0,16},{16,0},{1,17},{17,1},{2,18},{18,2},{3,19},{19,3},{4,20},{20... | collective-permute-start | bytes 1179656 | tf_op jit(solution)/shard_map/ppermute | solution.py:421
  228.8 19.1 %collective-permute-start.9 = (bf16[512,384]{1,0:T(8,128)(2,1)S(1)}, bf16[512,384]{1,0:T(8,128)(2,1)}, u32[]{:S(2)}, u32[]{:S(2)}) collective-permute-start(bf16[512,384]{1,0:T(8,128)(2,1)S(1)} %collective-permute-done.7.refs_5_), channel_id=1, source_target_pairs={{0,1},{1,0},{2,3},{3,2},{4,5},{5,4},{6,7},{7,6},{8,9},{9,8},{10,11... | collective-permute-start | bytes 1179656 | tf_op jit(solution)/shard_map/ppermute | solution.py:417
  228.9 0.7 copy-start.3
  243.4 13.8 %collective-permute-start.6 = (bf16[512,640]{1,0:T(8,128)(2,1)S(1)}, bf16[512,640]{1,0:T(8,128)(2,1)}, u32[]{:S(2)}, u32[]{:S(2)}) collective-permute-start(bf16[512,640]{1,0:T(8,128)(2,1)S(1)} %collective-permute-done.4.refs_1_), channel_id=1, source_target_pairs={{0,1},{1,0},{2,3},{3,2},{4,5},{5,4},{6,7},{7,6},{8,9},{9,8},{10,11... | collective-permute-start | bytes 1966088 | tf_op jit(solution)/shard_map/ppermute | solution.py:417
  243.4 15.7 %collective-permute-start.12 = (bf16[512,640]{1,0:T(8,128)(2,1)S(1)}, bf16[512,640]{1,0:T(8,128)(2,1)}, u32[]{:S(2)}, u32[]{:S(2)}) collective-permute-start(bf16[512,640]{1,0:T(8,128)(2,1)S(1)} %broadcast_select_fusion.refs_0_), channel_id=1, source_target_pairs={{0,1},{1,0},{2,3},{3,2},{4,5},{5,4},{6,7},{7,6},{8,9},{9,8},{10,11... | collective-permute-start | bytes 1966088 | tf_op jit(solution)/shard_map/ppermute | solution.py:417
  243.9 15.2 %collective-permute-start.13 = (bf16[512,640]{1,0:T(8,128)(2,1)}, bf16[512,640]{1,0:T(8,128)(2,1)}, u32[]{:S(2)}, u32[]{:S(2)}) collective-permute-start(bf16[512,640]{1,0:T(8,128)(2,1)} %collective-permute-done.11.refs_1_), channel_id=1, source_target_pairs={{0,1},{1,0},{2,3},{3,2},{4,5},{5,4},{6,7},{7,6},{8,9},{9,8},{10,11... | collective-permute-start | bytes 1966088 | tf_op jit(solution)/shard_map/ppermute | solution.py:417
  247.6 3.2 collective-permute-start.16
  247.9 11.2 %collective-permute-start.17 = (bf16[512,384]{1,0:T(8,128)(2,1)}, bf16[512,384]{1,0:T(8,128)(2,1)}, u32[]{:S(2)}, u32[]{:S(2)}) collective-permute-start(bf16[512,384]{1,0:T(8,128)(2,1)} %collective-permute-done.15.refs_5_), channel_id=1, source_target_pairs={{0,1},{1,0},{2,3},{3,2},{4,5},{5,4},{6,7},{7,6},{8,9},{9,8},{10,11... | collective-permute-start | bytes 1179656 | tf_op jit(solution)/shard_map/ppermute | solution.py:417
  248.6 10.5 %copy-start.2 = (s32[128]{0:T(128)S(1)}, s32[128]{0:T(128)}, u32[]{:S(2)}) copy-start(s32[128]{0:T(128)} %get-tuple-element.33.position) | copy-start | bytes 1540
  250.8 23.4 %collective-permute-start.18 = (bf16[512,512]{1,0:T(8,128)(2,1)}, bf16[512,512]{1,0:T(8,128)(2,1)}, u32[]{:S(2)}, u32[]{:S(2)}) collective-permute-start(bf16[512,512]{1,0:T(8,128)(2,1)} %slice.22), channel_id=1, source_target_pairs={{4,8},{8,4},{5,9},{9,5},{6,10},{10,6},{7,11},{11,7},{20,24},{24,20... | collective-permute-start | bytes 1572872 | tf_op jit(solution)/shard_map/ppermute | solution.py:425
  257.2 23.8 %collective-permute-start.20 = (bf16[512,512]{1,0:T(8,128)(2,1)}, bf16[512,512]{1,0:T(8,128)(2,1)}, u32[]{:S(2)}, u32[]{:S(2)}) collective-permute-start(bf16[512,512]{1,0:T(8,128)(2,1)} %pad_maximum_fusion), channel_id=1, source_target_pairs={{4,8},{8,4},{5,9},{9,5},{6,10},{10,6},{7,11},{11,7},{20,24},{24,20... | collective-permute-start | bytes 1572872 | tf_op jit(solution)/shard_map/ppermute | solution.py:425
  259.1 3.3 %copy-start = (bf16[1,384,2048]{2,1,0:T(8,128)(2,1)S(1)}, bf16[1,384,2048]{2,1,0:T(8,128)(2,1)}, u32[]{:S(2)}) copy-start(bf16[1,384,2048]{2,1,0:T(8,128)(2,1)} %param.9) | copy-start | bytes 4718596
  262.4 10.3 %copy-start.1 = (bf16[2048,1024]{1,0:T(8,128)(2,1)S(1)}, bf16[2048,1024]{1,0:T(8,128)(2,1)}, u32[]{:S(2)}) copy-start(bf16[2048,1024]{1,0:T(8,128)(2,1)} %refs_0_.3) | copy-start | bytes 12582916
  272.7 2.9 copy-start.4
  274.3 12.6 %collective-permute-start.19 = (bf16[512,512]{1,0:T(8,128)(2,1)}, bf16[512,512]{1,0:T(8,128)(2,1)S(1)}, u32[]{:S(2)}, u32[]{:S(2)}) collective-permute-start(bf16[512,512]{1,0:T(8,128)(2,1)} %collective-permute-done.18), channel_id=1, source_target_pairs={{4,0},{8,12},{5,1},{9,13},{6,2},{10,14},{7,3},{11,15},{20,16},{24,... | collective-permute-start | bytes 1572872 | tf_op jit(solution)/shard_map/ppermute | solution.py:429
  278.9 22.0 %collective-permute-start.24 = (bf16[192,1024]{1,0:T(8,128)(2,1)S(1)}, bf16[192,1024]{1,0:T(8,128)(2,1)S(1)}, u32[]{:S(2)}, u32[]{:S(2)}) collective-permute-start(bf16[192,1024]{1,0:T(8,128)(2,1)S(1)} %project.6), channel_id=1, source_target_pairs={{0,2},{2,0},{1,3},{3,1},{4,6},{6,4},{5,7},{7,5},{8,10},{10,8},{9,1... | collective-permute-start | bytes 1179656 | tf_op jit(solution)/shard_map/ppermute | solution.py:436
  279.8 21.2 %collective-permute-start.25 = (bf16[192,1024]{1,0:T(8,128)(2,1)S(1)}, bf16[192,1024]{1,0:T(8,128)(2,1)S(1)}, u32[]{:S(2)}, u32[]{:S(2)}) collective-permute-start(bf16[192,1024]{1,0:T(8,128)(2,1)S(1)} %project.5), channel_id=1, source_target_pairs={{0,2},{2,0},{1,3},{3,1},{4,6},{6,4},{5,7},{7,5},{8,10},{10,8},{9,1... | collective-permute-start | bytes 1179656 | tf_op jit(solution)/shard_map/ppermute | solution.py:436
  281.0 18.2 %collective-permute-start.21 = (bf16[512,512]{1,0:T(8,128)(2,1)}, bf16[512,512]{1,0:T(8,128)(2,1)S(1)}, u32[]{:S(2)}, u32[]{:S(2)}) collective-permute-start(bf16[512,512]{1,0:T(8,128)(2,1)} %collective-permute-done.20), channel_id=1, source_target_pairs={{4,0},{8,12},{5,1},{9,13},{6,2},{10,14},{7,3},{11,15},{20,16},{24,... | collective-permute-start | bytes 1572872 | tf_op jit(solution)/shard_map/ppermute | solution.py:431
  286.0 21.7 %collective-permute-start.23 = (bf16[192,1024]{1,0:T(8,128)(2,1)S(1)}, bf16[192,1024]{1,0:T(8,128)(2,1)S(1)}, u32[]{:S(2)}, u32[]{:S(2)}) collective-permute-start(bf16[192,1024]{1,0:T(8,128)(2,1)S(1)} %project.7), channel_id=1, source_target_pairs={{0,2},{2,0},{1,3},{3,1},{4,6},{6,4},{5,7},{7,5},{8,10},{10,8},{9,1... | collective-permute-start | bytes 1179656 | tf_op jit(solution)/shard_map/ppermute | solution.py:436
  288.0 15.2 %collective-permute-start.26 = (bf16[512,512]{1,0:T(8,128)(2,1)S(1)}, bf16[512,512]{1,0:T(8,128)(2,1)S(1)}, u32[]{:S(2)}, u32[]{:S(2)}) collective-permute-start(bf16[512,512]{1,0:T(8,128)(2,1)S(1)} %broadcast_select_fusion.2.refs_0_), channel_id=1, source_target_pairs={{0,16},{16,0},{1,17},{17,1},{2,18},{18,2},{3,19},{19,3},{4,20},{20... | collective-permute-start | bytes 1572872 | tf_op jit(solution)/shard_map/ppermute | solution.py:434
  300.3 12.9 %collective-permute-start.22 = (bf16[512,512]{1,0:T(8,128)(2,1)S(1)}, bf16[512,512]{1,0:T(8,128)(2,1)S(1)}, u32[]{:S(2)}, u32[]{:S(2)}) collective-permute-start(bf16[512,512]{1,0:T(8,128)(2,1)S(1)} %broadcast_select_fusion.1.refs_0_), channel_id=1, source_target_pairs={{0,16},{16,0},{1,17},{17,1},{2,18},{18,2},{3,19},{19,3},{4,20},{20... | collective-permute-start | bytes 1572872 | tf_op jit(solution)/shard_map/ppermute | solution.py:439
  300.9 11.2 %collective-permute-start.27 = (bf16[512,512]{1,0:T(8,128)(2,1)S(1)}, bf16[512,512]{1,0:T(8,128)(2,1)S(1)}, u32[]{:S(2)}, u32[]{:S(2)}) collective-permute-start(bf16[512,512]{1,0:T(8,128)(2,1)S(1)} %broadcast_select_fusion.2.refs_0_), channel_id=1, source_target_pairs={{0,1},{1,0},{2,3},{3,2},{4,5},{5,4},{6,7},{7,6},{8,9},{9,8},{10,11... | collective-permute-start | bytes 1572872 | tf_op jit(solution)/shard_map/ppermute | solution.py:417
  303.2 8.9 %collective-permute-start.28 = (bf16[512,512]{1,0:T(8,128)(2,1)S(1)}, bf16[512,512]{1,0:T(8,128)(2,1)S(1)}, u32[]{:S(2)}, u32[]{:S(2)}) collective-permute-start(bf16[512,512]{1,0:T(8,128)(2,1)S(1)} %collective-permute-done.26.refs_1_), channel_id=1, source_target_pairs={{0,1},{1,0},{2,3},{3,2},{4,5},{5,4},{6,7},{7,6},{8,9},{9,8},{10,11... | collective-permute-start | bytes 1572872 | tf_op jit(solution)/shard_map/ppermute | solution.py:417
  313.2 3.3 %collective-permute-start.29 = (bf16[512,512]{1,0:T(8,128)(2,1)S(1)}, bf16[512,512]{1,0:T(8,128)(2,1)S(1)}, u32[]{:S(2)}, u32[]{:S(2)}) collective-permute-start(bf16[512,512]{1,0:T(8,128)(2,1)S(1)} %broadcast_select_fusion.1.refs_0_), channel_id=1, source_target_pairs={{0,1},{1,0},{2,3},{3,2},{4,5},{5,4},{6,7},{7,6},{8,9},{9,8},{10,11... | collective-permute-start | bytes 1572872 | tf_op jit(solution)/shard_map/ppermute | solution.py:417
  313.3 3.2 collective-permute-start.30
  313.8 8.4 %collective-permute-start.32 = (bf16[192,512]{1,0:T(8,128)(2,1)S(1)}, bf16[192,512]{1,0:T(8,128)(2,1)S(1)}, u32[]{:S(2)}, u32[]{:S(2)}) collective-permute-start(bf16[192,512]{1,0:T(8,128)(2,1)S(1)} %project.8), channel_id=1, source_target_pairs={{0,2},{2,0},{1,3},{3,1},{4,6},{6,4},{5,7},{7,5},{8,10},{10,8},{9,1... | collective-permute-start | bytes 589832 | tf_op jit(solution)/shard_map/ppermute | solution.py:446
  317.7 8.2 %collective-permute-start.31 = (bf16[192,512]{1,0:T(8,128)(2,1)S(1)}, bf16[192,512]{1,0:T(8,128)(2,1)S(1)}, u32[]{:S(2)}, u32[]{:S(2)}) collective-permute-start(bf16[192,512]{1,0:T(8,128)(2,1)S(1)} %project.9), channel_id=1, source_target_pairs={{0,2},{2,0},{1,3},{3,1},{4,6},{6,4},{5,7},{7,5},{8,10},{10,8},{9,1... | collective-permute-start | bytes 589832 | tf_op jit(solution)/shard_map/ppermute | solution.py:449

commit v10 on v8

--- a/solution.py
+++ b/solution.py
@@ -262,71 +262,90 @@
             refs[-1][:, first + at.start : first + at.stop] = multiply(left, pieces, at)
 
 
-def finish_kernel(has_out, control, left, came, *refs):
-    for first, pieces in parts_of(control, refs[: len(refs) - 1 - has_out]):
+def project_both_kernel(control, left, stay, *refs):
+    sent, kept = refs[-2:]
+    half = left.shape[1]
+    for first, pieces in parts_of(control, refs[:-2]):
         for at in blocks(pieces[0].shape[1]):
+            total = multiply([jnp.concatenate([left[n], stay[n]], axis=0) for n in range(4)], pieces, at)
             to = slice(first + at.start, first + at.stop)
-            total = multiply(left, pieces, at).astype(jnp.float32) + came[:, to].astype(jnp.float32)
-            refs[-1][0, :, to] = total.astype(jnp.bfloat16)
-
-
-def project(control, left, pieces, came=None, base=None, out=None, width=None):
+            sent[:, to] = total[:half]
+            kept[:, to] = total[half:]
+
+
+def project(control, left, pieces, stay=None):
     half = left.shape[1]
     columns = pieces[0].shape[1] * max(1, len(pieces) // 4)
+    smem = pl.BlockSpec(memory_space=pltpu.SMEM)
     vmem = pl.BlockSpec(memory_space=pltpu.VMEM)
-    in_specs = [vmem]
-    operands = [left]
-    aliases = {}
-    if came is None:
-        kernel = project_kernel
-        out_shape = jax.ShapeDtypeStruct((half, columns), jnp.bfloat16)
-        out_specs = vmem
-    else:
-        kernel = functools.partial(finish_kernel, int(out is not None))
-        in_specs.append(vmem)
-        operands.append(came)
-        out_shape = jax.ShapeDtypeStruct((1, half, width), jnp.bfloat16)
-        out_specs = pl.BlockSpec((1, half, columns), lambda j, control: (0, 0, control[base]))
-    in_specs += [vmem] * len(pieces)
-    operands += pieces
-    if out is not None:
-        in_specs.append(pl.BlockSpec(memory_space=pl.ANY))
-        operands.append(out)
-        aliases = {len(operands): 0}
-    return pl.pallas_call(
-        kernel,
-        out_shape=out_shape,
-        grid_spec=pltpu.PrefetchScalarGridSpec(
-            num_scalar_prefetch=1, grid=(1,), in_specs=in_specs, out_specs=out_specs
-        ),
-        input_output_aliases=aliases,
+    shape = jax.ShapeDtypeStruct((half, columns), jnp.bfloat16)
+    rows = [left] if stay is None else [left, stay]
+    return pl.pallas_call(
+        project_kernel if stay is None else project_both_kernel,
+        out_shape=shape if stay is None else (shape, shape),
+        in_specs=[smem] + [vmem] * (len(rows) + len(pieces)),
+        out_specs=vmem if stay is None else (vmem, vmem),
         compiler_params=pltpu.CompilerParams(vmem_limit_bytes=16 * MIB),
-        cost_estimate=cost(),
-        name="project" if came is None else "finish",
-    )(control, *operands)
-
-
-def pick_kernel(asked, pool, out):
-    owner = pl.program_id(0)
-
-    def copy(n, carry):
-        out[0, n] = pool[asked[owner, n]]
-        return carry
-
-    lax.fori_loop(0, asked.shape[1], copy, 0, unroll=8)
+        cost_estimate=cost((3 if stay is None else 6) * 10**9),
+        name="project",
+    )(control, *rows, *pieces)
+
+
+def join_kernel(count, control, *refs):
+    out = refs[-1]
+    for n in range(count):
+        kept, came = refs[n], refs[count + n]
+        columns = kept.shape[1]
+        to = pl.ds(pl.multiple_of(control[10 + n] * LANES, LANES), columns)
+        total = kept[...].astype(jnp.float32) + came[...].astype(jnp.float32)
+        out[0, :, to] = total.astype(jnp.bfloat16)
+
+
+def join(control, kept, came):
+    smem = pl.BlockSpec(memory_space=pltpu.SMEM)
+    vmem = pl.BlockSpec(memory_space=pltpu.VMEM)
+    total = sum(part.shape[1] for part in kept)
+    return pl.pallas_call(
+        functools.partial(join_kernel, len(kept)),
+        out_shape=jax.ShapeDtypeStruct((1, kept[0].shape[0], total), jnp.bfloat16),
+        in_specs=[smem] + [vmem] * (2 * len(kept)),
+        out_specs=vmem,
+        compiler_params=pltpu.CompilerParams(vmem_limit_bytes=16 * MIB),
+        cost_estimate=cost(3 * 10**8),
+        name="join",
+    )(control, *kept, *came)
+
+
+def pick_kernel(asked, pool, out, held, rows, sem):
+    owners, bucket = asked.shape
+    whole = pltpu.make_async_copy(pool, held, sem.at[owners])
+    whole.start()
+    whole.wait()
+    for owner in range(owners):
+
+        def copy(n, carry):
+            rows[owner, n] = held[asked[owner, n]]
+            return carry
+
+        lax.fori_loop(0, bucket, copy, 0, unroll=8)
+        pltpu.make_async_copy(rows.at[owner], out.at[owner], sem.at[owner]).start()
+    for owner in range(owners):
+        pltpu.make_async_copy(rows.at[owner], out.at[owner], sem.at[owner]).wait()
 
 
 def pick(pool, asked):
-    block = (1, asked.shape[1]) + pool.shape[1:]
+    hbm = pl.BlockSpec(memory_space=pltpu.HBM)
+    out = asked.shape + pool.shape[1:]
     return pl.pallas_call(
         pick_kernel,
-        out_shape=jax.ShapeDtypeStruct(asked.shape + pool.shape[1:], jnp.bfloat16),
-        grid=(asked.shape[0],),
-        in_specs=[
-            pl.BlockSpec(memory_space=pltpu.SMEM),
-            pl.BlockSpec(memory_space=pltpu.VMEM),
+        out_shape=jax.ShapeDtypeStruct(out, jnp.bfloat16),
+        in_specs=[pl.BlockSpec(memory_space=pltpu.SMEM), hbm],
+        out_specs=hbm,
+        scratch_shapes=[
+            pltpu.VMEM(pool.shape, jnp.bfloat16),
+            pltpu.VMEM(out, jnp.bfloat16),
+            pltpu.SemaphoreType.DMA((asked.shape[0] + 1,)),
         ],
-        out_specs=pl.BlockSpec(block, lambda owner: (owner, 0, 0, 0, 0)),
         compiler_params=pltpu.CompilerParams(vmem_limit_bytes=12 * MIB),
         cost_estimate=cost(),
         name="pick",
@@ -362,8 +381,10 @@
     second = jnp.where(seq < 2, 2, 1)
     third = jnp.where(seq < 2, 3, 0)
     local = [own, own ^ 2, own ^ 1, own ^ 3]
+    begins = [v * columns // LANES for v in (seq, seq ^ 1, second, third)]
+    begins.append(begins[-1] + columns // 2 // LANES)
     control = jnp.stack(
-        [jnp.asarray(v, jnp.int32) for v in (flip, 1 - flip, *order, *local, seq, seq ^ 1, second, 2 * third, 2 * third + 1)]
+        [jnp.asarray(v, jnp.int32) for v in (flip, 1 - flip, *order, *local, *begins)]
     )
     swap_group = functools.partial(lax.ppermute, axis_name="group", perm=SWAP)
     swap_role = functools.partial(lax.ppermute, axis_name="role", perm=SWAP)
@@ -425,28 +446,27 @@
     keys, values = place(position, after(pages, *near_all, *next_all), fresh)
     left = attend(1, control, tables, queries[0], keys, values, slots)
     far_on = [forward(after(far[0], left))]
-    sent = [project(control, left, [out_weight])]
-    far_on.append(forward(after(far[1], sent[0])))
-    sent.append(project(control, after(left, sent[-1]), near_all))
-    far[0] = jnp.where(middle, far[0], after(far_on[0], sent[1]))
+    sent, kept = [project(control, left, [out_weight])], []
+    came = [swap_tp(sent[0])]
+    stay = attend(0, control, tables, after(queries[0], sent[0], far[0]), keys, values, slots)
+    far_on.append(forward(after(far[1], stay)))
+    far[0] = jnp.where(middle, far[0], after(far_on[0], stay))
     far_across = [swap_group(far[0])]
-    sent.append(project(control, after(left, sent[-1]), next_all))
-    came = [swap_tp(each) for each in sent]
-    stay = attend(0, control, tables, after(queries[0], sent[2], far[0]), keys, values, slots)
-    far[1] = jnp.where(middle, far[1], after(far_on[1], stay))
+    for pieces in (near_all, next_all):
+        both = project(control, after(left, far[0], came[0], *sent), pieces, stay)
+        sent.append(both[0])
+        kept.append(both[1])
+        came.append(swap_tp(sent[-1]))
+    far[1] = jnp.where(middle, far[1], after(far_on[1], sent[2]))
     far_across.append(swap_group(far[1]))
-    far_all = [four(far[n], far_across[n], stay) for n in (0, 1)]
-    total = columns * owner_count
-    out = project(control, after(stay, *came[:2]), [out_weight], came[0], 10, None, total)
-    out = project(control, stay, near_all, came[1], 11, out, total)
-    sent.append(project(control, after(left, out), far_all[0]))
-    came.append(swap_tp(sent[3]))
-    out = project(control, after(stay, sent[3]), next_all, came[2], 12, out, total)
-    sent.append(project(control, after(left, out), far_all[1]))
-    came.append(swap_tp(sent[4]))
+    kept.insert(0, project(control, after(stay, sent[2], came[1], far_across[0]), [out_weight]))
     for n in range(2):
-        out = project(control, after(stay, sent[4]), far_all[n], came[n + 3], 13 + n, out, total)
-    return out
+        pieces = four(far[n], far_across[n], *sent[3:])
+        both = project(control, after(left, kept[0], *came[2 : 2 + 2 * n]), pieces, stay)
+        sent.append(both[0])
+        kept.append(both[1])
+        came.append(swap_tp(sent[-1]))
+    return join(control, kept, came)
 
 
 def solution(mesh):

time: 207 us -> 216 us (1.043)
  waiting for transfers between devices: 84.3 us -> 99.5 us
  Pallas kernels: 51.5 us -> 43 us
  starting transfers between devices: 46.9 us -> 50 us
    ppermute x6, waiting for transfers between devices: 4.52 us -> 20 us  [the longest x4 19.9 us: shards(): came.append(swap_tp(sent[-1]))]
    pallas_call x11 -> x8, Pallas kernels: 25.1 us -> 17.3 us  [the longest x6 13.3 us: project(): pl.pallas_call(project_kernel if stay is None else project_both_kernel, o...]
    unnamed x29 -> x25, local copies, waits for them, and re-layouts: 6.91 us -> 6.12 us
  transfers between devices with their start and end apart: 34 -> 34, of which waited for: 10 -> 11; matrix products, arithmetic and copies ran while one was open for 2% -> 3% of each run, Pallas kernels for 24% -> 18%
where the time goes in v10:
time: 216 us
  waiting for transfers between devices  99.5 us (46%)
  starting transfers between devices  50 us (23%)
  Pallas kernels  43 us (20%)
  blocking collectives  10.8 us (5%)
  local copies, waits for them, and re-layouts  7.89 us (4%)
  other arithmetic  3.92 us (2%)
    ppermute x2, waiting for transfers between devices, shards(): next_shard = [jnp.where(middle, part, forward(part)) for part in inner]  59.4 us
    ppermute x4, waiting for transfers between devices, shards(): came.append(swap_tp(sent[-1]))  19.9 us
    pallas_call x2, Pallas kernels, attend(): pl.pallas_call(functools.partial(attend_kernel, fresh_base, side), out_sh...  19.9 us
    pallas_call x6, Pallas kernels, project(): pl.pallas_call(project_kernel if stay is None else project_both_kernel, o...  13.3 us
    all_to_all x1, blocking collectives, shards(): lax.all_to_all(wanted, 'seq', split_axis=0, concat_axis=0, tiled=True)  10.8 us
    ppermute x1, waiting for transfers between devices, shards(): far_across.append(swap_group(far[1]))  8.39 us
    ppermute x1, starting transfers between devices, shards(): far_on = [forward(after(far[0], left))]  7.33 us
    unnamed x25, local copies, waits for them, and re-layouts  6.12 us
  transfers between devices with their start and end apart: 34, of which 11 were waited for; matrix products, arithmetic and copies ran while one was open for 3% of the time, Pallas kernels for 18%

profile of v10, /device:TPU:16, one launch (start us, length us, event | category | flops | bytes accessed | tf_op | source)
XLA Modules:
  0.0 215.8 jit_solution(12215236961230491575)
XLA Ops:
  0.0 1.3 fusion.5
  1.3 1.6 collective-permute-start
  2.9 1.9 collective-permute-start.1
  4.8 2.6 %rank.1 = (s32[128]{0:T(128)}, s32[4,64]{1,0:T(4,128)}) custom-call(s32[1,128]{1,0:T(1,128)} %owner.1, s32[1,128]{1,0:T(1,128)} %page.1), custom_call_target="tpu_custom_call" | custom-call | flops 3000000000 | bytes 1000 | tf_op jit(solution)/shard_map/rank/pallas_call | solution.py:49
  7.5 10.8 %all_to_all.17 = s32[4,1,64]{2,1,0:T(1,128)S(1)} all-to-all(s32[4,1,64]{2,1,0:T(1,128)} %bitcast.40), channel_id=1, replica_groups=mesh['group'=2,'seq'=4,'tp'=2,'role'=2] {'seq'}, dimensions={0} | all-to-all | bytes 2048 | tf_op jit(solution)/shard_map/all_to_all | solution.py:402
  18.3 1.4 collective-permute-start.2
  19.7 2.2 %collective-permute-start.3 = (bf16[512,512]{1,0:T(8,128)(2,1)S(1)}, bf16[512,512]{1,0:T(8,128)(2,1)}, u32[]{:S(2)}, u32[]{:S(2)}) collective-permute-start(bf16[512,512]{1,0:T(8,128)(2,1)S(1)} %get-tuple-element.44), channel_id=1, source_target_pairs={{4,8},{8,4},{5,9},{9,5},{6,10},{10,6},{7,11},{11,7},{20,24},{24,20... | collective-permute-start | bytes 1572872 | tf_op jit(solution)/shard_map/ppermute | solution.py:407
  21.9 2.2 %copy-done.4 = bf16[1,256,2,16,256]{4,3,2,1,0:T(8,128)(2,1)S(1)} copy-done((bf16[1,256,2,16,256]{4,3,2,1,0:T(8,128)(2,1)S(1)}, bf16[1,256,2,16,256]{4,3,2,1,0:T(8,128)(2,1)}, u32[]{:S(2)}) %copy-start.4) | copy-done | bytes 4194328
  24.1 1.9 pick.1
  26.0 2.0 copy-done
  28.0 2.7 %collective-permute-done.2.refs_4_ = bf16[512,512]{1,0:T(8,128)(2,1)S(1)} collective-permute-done((bf16[512,512]{1,0:T(8,128)(2,1)S(1)}, bf16[512,512]{1,0:T(8,128)(2,1)S(1)}, u32[]{:S(2)}, u32[]{:S(2)}) %collective-permute-start.2) | collective-permute-done | bytes 524320 | tf_op jit(solution)/shard_map/ppermute | solution.py:406
  30.7 2.9 %collective-permute-done.3 = bf16[512,512]{1,0:T(8,128)(2,1)} collective-permute-done((bf16[512,512]{1,0:T(8,128)(2,1)S(1)}, bf16[512,512]{1,0:T(8,128)(2,1)}, u32[]{:S(2)}, u32[]{:S(2)}) %collective-permute-start.3) | collective-permute-done | bytes 524320 | tf_op jit(solution)/shard_map/ppermute | solution.py:407
  33.6 4.8 %all-to-all-start.1 = ((bf16[4,64,2,16,256]{4,3,2,1,0:T(8,128)(2,1)}), bf16[4,64,2,16,256]{4,3,2,1,0:T(8,128)(2,1)}, u32[]{:S(2)}, u32[]{:S(2)}) async-start(bf16[4,64,2,16,256]{4,3,2,1,0:T(8,128)(2,1)} %copy-done), calls=%async_computation.1 | async-start | bytes 8388608 | tf_op jit(solution)/shard_map/all_to_all | solution.py:413
  38.4 2.9 %collective-permute-start.10 = (bf16[512,512]{1,0:T(8,128)(2,1)S(1)}, bf16[512,512]{1,0:T(8,128)(2,1)S(1)}, u32[]{:S(2)}, u32[]{:S(2)}) collective-permute-start(bf16[512,512]{1,0:T(8,128)(2,1)S(1)} %collective-permute-done.1), channel_id=1, source_target_pairs={{4,0},{8,12},{5,1},{9,13},{6,2},{10,14},{7,3},{11,15},{20,16},{24,... | collective-permute-start | bytes 1572872 | tf_op jit(solution)/shard_map/ppermute | solution.py:440
  41.3 2.1 collective-permute-start.14
  43.4 1.5 collective-permute-start.4
  45.4 51.3 %collective-permute-done.10 = bf16[512,512]{1,0:T(8,128)(2,1)S(1)} collective-permute-done((bf16[512,512]{1,0:T(8,128)(2,1)S(1)}, bf16[512,512]{1,0:T(8,128)(2,1)S(1)}, u32[]{:S(2)}, u32[]{:S(2)}) %collective-permute-start.10) | collective-permute-done | bytes 524320 | tf_op jit(solution)/shard_map/ppermute | solution.py:440
  96.8 1.6 collective-permute-start.11
  98.3 8.1 %collective-permute-done.14 = bf16[512,512]{1,0:T(8,128)(2,1)} collective-permute-done((bf16[512,512]{1,0:T(8,128)(2,1)}, bf16[512,512]{1,0:T(8,128)(2,1)}, u32[]{:S(2)}, u32[]{:S(2)}) %collective-permute-start.14) | collective-permute-done | bytes 524320 | tf_op jit(solution)/shard_map/ppermute | solution.py:440
  106.4 1.1 broadcast_select_fusion.2.refs_4_
  107.5 1.6 collective-permute-start.15
  111.8 5.6 %collective-permute-done.15.refs_5_ = bf16[512,512]{1,0:T(8,128)(2,1)} collective-permute-done((bf16[512,512]{1,0:T(8,128)(2,1)S(1)}, bf16[512,512]{1,0:T(8,128)(2,1)}, u32[]{:S(2)}, u32[]{:S(2)}) %collective-permute-start.15) | collective-permute-done | bytes 524320 | tf_op jit(solution)/shard_map/ppermute | solution.py:441
  118.5 4.1 %collective-permute-start.18 = (bf16[512,512]{1,0:T(8,128)(2,1)}, bf16[512,512]{1,0:T(8,128)(2,1)}, u32[]{:S(2)}, u32[]{:S(2)}) collective-permute-start(bf16[512,512]{1,0:T(8,128)(2,1)} %collective-permute-done.refs_0_), channel_id=1, source_target_pairs={{4,8},{8,4},{5,9},{9,5},{6,10},{10,6},{7,11},{11,7},{20,24},{24,20... | collective-permute-start | bytes 1572872 | tf_op jit(solution)/shard_map/ppermute | solution.py:444
  124.2 1.9 collective-permute-start.27
  126.1 3.1 %place.1 = (bf16[2,3072,128]{2,1,0:T(8,128)(2,1)S(1)}, bf16[2,3072,256]{2,1,0:T(8,128)(2,1)S(1)}) custom-call(s32[128]{0:T(128)S(1)} %copy-done.3, bf16[256,2,16,256]{3,2,1,0:T(8,128)(2,1)} %bitcast.21.pages, bf16[384,512]{1,0:T(8,128)(2,1)S(1)} %bitcast.31), custom_call_target="tpu_custom_call" | custom-call | flops 1000000000 | bytes 1000 | tf_op jit(solution)/shard_map/place/pallas_call | solution.py:95
  129.3 9.6 %attend.2.left = bf16[4,192,512]{2,1,0:T(8,128)(2,1)S(1)} custom-call(s32[15]{0:T(128)S(1)} %stack.63.control, s32[6]{0:T(128)S(1)} %get-tuple-element.82.hist_at, s32[6]{0:T(128)S(1)} %get-tuple-element.81.hist_steps, s32[6]{0:T(128)S(1)} %get-tuple-element.76.fresh_at, s32[6]{0:T(128)S(1)} %get-tuple-element.75.fresh_steps, ...), custom_call_target="tpu_custom_call" | custom-call | flops 1000000000 | bytes 1000 | tf_op jit(solution)/shard_map/attend/pallas_call | solution.py:221
  138.9 1.5 project.6
  140.5 2.2 %collective-permute-start.20 = (bf16[192,1024]{1,0:T(8,128)(2,1)S(1)}, bf16[192,1024]{1,0:T(8,128)(2,1)S(1)}, u32[]{:S(2)}, u32[]{:S(2)}) collective-permute-start(bf16[192,1024]{1,0:T(8,128)(2,1)S(1)} %project.6), channel_id=1, source_target_pairs={{0,2},{2,0},{1,3},{3,1},{4,6},{6,4},{5,7},{7,5},{8,10},{10,8},{9,1... | collective-permute-start | bytes 1179656 | tf_op jit(solution)/shard_map/ppermute | solution.py:450
  142.7 7.3 %collective-permute-start.19 = (bf16[512,512]{1,0:T(8,128)(2,1)}, bf16[512,512]{1,0:T(8,128)(2,1)S(1)}, u32[]{:S(2)}, u32[]{:S(2)}) collective-permute-start(bf16[512,512]{1,0:T(8,128)(2,1)} %collective-permute-done.18), channel_id=1, source_target_pairs={{4,0},{8,12},{5,1},{9,13},{6,2},{10,14},{7,3},{11,15},{20,16},{24,... | collective-permute-start | bytes 1572872 | tf_op jit(solution)/shard_map/ppermute | solution.py:448
  150.1 10.3 %attend.3.stay.left = bf16[4,192,512]{2,1,0:T(8,128)(2,1)S(1)} custom-call(s32[15]{0:T(128)S(1)} %stack.63.control, s32[6]{0:T(128)S(1)} %get-tuple-element.82.hist_at, s32[6]{0:T(128)S(1)} %get-tuple-element.81.hist_steps, s32[6]{0:T(128)S(1)} %get-tuple-element.76.fresh_at, s32[6]{0:T(128)S(1)} %get-tuple-element.75.fresh_steps, ...), custom_call_target="tpu_custom_call" | custom-call | flops 16000000000 | bytes 1000 | tf_op jit(solution)/shard_map/attend/pallas_call | solution.py:221
  160.4 1.3 collective-permute-start.28
  162.3 1.1 broadcast_select_fusion.1.refs_0_
  163.4 3.1 %collective-permute-start.22 = (bf16[512,512]{1,0:T(8,128)(2,1)S(1)}, bf16[512,512]{1,0:T(8,128)(2,1)S(1)}, u32[]{:S(2)}, u32[]{:S(2)}) collective-permute-start(bf16[512,512]{1,0:T(8,128)(2,1)S(1)} %broadcast_select_fusion.1.refs_0_), channel_id=1, source_target_pairs={{0,16},{16,0},{1,17},{17,1},{2,18},{18,2},{3,19},{19,3},{4,20},{20... | collective-permute-start | bytes 1572872 | tf_op jit(solution)/shard_map/ppermute | solution.py:454
  166.5 3.6 %project.7 = (bf16[192,1024]{1,0:T(8,128)(2,1)S(1)}, bf16[192,1024]{1,0:T(8,128)(2,1)S(1)}) custom-call(s32[15]{0:T(128)S(1)} %stack.63.control, bf16[4,192,512]{2,1,0:T(8,128)(2,1)S(1)} %attend.2.left, bf16[4,192,512]{2,1,0:T(8,128)(2,1)S(1)} %attend.3.stay.left, bf16[512,512]{1,0:T(8,128)(2,1)} %collective-permute-done.refs_0_, ...), custom_call_target="tpu_custom_call" | custom-call | flops 6000000000 | bytes 1000 | tf_op jit(solution)/shard_map/project/pallas_call | solution.py:283
  170.3 3.6 %project.8 = (bf16[192,1024]{1,0:T(8,128)(2,1)S(1)}, bf16[192,1024]{1,0:T(8,128)(2,1)S(1)}) custom-call(s32[15]{0:T(128)S(1)} %stack.63.control, bf16[4,192,512]{2,1,0:T(8,128)(2,1)S(1)} %attend.2.left, bf16[4,192,512]{2,1,0:T(8,128)(2,1)S(1)} %attend.3.stay.left, bf16[512,512]{1,0:T(8,128)(2,1)S(1)} %broadcast_select_fusion.3.refs_0_, ...), custom_call_target="tpu_custom_call" | custom-call | flops 6000000000 | bytes 1000 | tf_op jit(solution)/shard_map/project/pallas_call | solution.py:283
  174.5 1.1 broadcast_select_fusion.refs_0_
  175.6 1.2 collective-permute-start.29
  176.9 1.1 collective-permute-done.21.refs_6_
  178.0 1.5 project.9.refs_0_
  179.5 1.5 project.10
  181.1 8.4 %collective-permute-done.29.refs_1_ = bf16[512,512]{1,0:T(8,128)(2,1)S(1)} collective-permute-done((bf16[512,512]{1,0:T(8,128)(2,1)S(1)}, bf16[512,512]{1,0:T(8,128)(2,1)S(1)}, u32[]{:S(2)}, u32[]{:S(2)}) %collective-permute-start.29) | collective-permute-done | bytes 524320 | tf_op jit(solution)/shard_map/ppermute | solution.py:461
  189.5 1.9 collective-permute-start.25
  191.6 10.0 %collective-permute-done.25.refs_7_ = bf16[192,1024]{1,0:T(8,128)(2,1)S(1)} collective-permute-done((bf16[192,1024]{1,0:T(8,128)(2,1)S(1)}, bf16[192,1024]{1,0:T(8,128)(2,1)S(1)}, u32[]{:S(2)}, u32[]{:S(2)}) %collective-permute-start.25) | collective-permute-done | bytes 393248 | tf_op jit(solution)/shard_map/ppermute | solution.py:459
  201.5 4.0 %collective-permute-done.26.refs_8_ = bf16[192,512]{1,0:T(8,128)(2,1)S(1)} collective-permute-done((bf16[192,512]{1,0:T(8,128)(2,1)S(1)}, bf16[192,512]{1,0:T(8,128)(2,1)S(1)}, u32[]{:S(2)}, u32[]{:S(2)}) %collective-permute-start.26) | collective-permute-done | bytes 196640 | tf_op jit(solution)/shard_map/ppermute | solution.py:468
  205.5 1.5 project.11
  207.0 1.8 collective-permute-start.32
  208.8 4.9 %collective-permute-done.32.refs_9_ = bf16[192,512]{1,0:T(8,128)(2,1)S(1)} collective-permute-done((bf16[192,512]{1,0:T(8,128)(2,1)S(1)}, bf16[192,512]{1,0:T(8,128)(2,1)S(1)}, u32[]{:S(2)}, u32[]{:S(2)}) %collective-permute-start.32) | collective-permute-done | bytes 196640 | tf_op jit(solution)/shard_map/ppermute | solution.py:468
  213.7 2.0 join.1
  (77 shorter events, 7.2 us)
Async XLA Ops:
  1.3 17.0 %collective-permute-start = (bf16[512,512]{1,0:T(8,128)(2,1)S(1)}, bf16[512,512]{1,0:T(8,128)(2,1)}, u32[]{:S(2)}, u32[]{:S(2)}) collective-permute-start(bf16[512,512]{1,0:T(8,128)(2,1)S(1)} %get-tuple-element.80), channel_id=1, source_target_pairs={{0,4},{4,0},{8,12},{12,8},{1,5},{5,1},{9,13},{13,9},{2,6},{6,2},{1... | collective-permute-start | bytes 1572872 | tf_op jit(solution)/shard_map/ppermute | solution.py:399
  2.9 15.4 %collective-permute-start.1 = (bf16[512,512]{1,0:T(8,128)(2,1)S(1)}, bf16[512,512]{1,0:T(8,128)(2,1)S(1)}, u32[]{:S(2)}, u32[]{:S(2)}) collective-permute-start(bf16[512,512]{1,0:T(8,128)(2,1)S(1)} %get-tuple-element.80), channel_id=1, source_target_pairs={{4,8},{8,4},{5,9},{9,5},{6,10},{10,6},{7,11},{11,7},{20,24},{24,20... | collective-permute-start | bytes 1572872 | tf_op jit(solution)/shard_map/ppermute | solution.py:399
  18.3 12.4 %collective-permute-start.2 = (bf16[512,512]{1,0:T(8,128)(2,1)S(1)}, bf16[512,512]{1,0:T(8,128)(2,1)S(1)}, u32[]{:S(2)}, u32[]{:S(2)}) collective-permute-start(bf16[512,512]{1,0:T(8,128)(2,1)S(1)} %get-tuple-element.44), channel_id=1, source_target_pairs={{0,4},{4,0},{8,12},{12,8},{1,5},{5,1},{9,13},{13,9},{2,6},{6,2},{1... | collective-permute-start | bytes 1572872 | tf_op jit(solution)/shard_map/ppermute | solution.py:406
  19.7 13.9 %collective-permute-start.3 = (bf16[512,512]{1,0:T(8,128)(2,1)S(1)}, bf16[512,512]{1,0:T(8,128)(2,1)}, u32[]{:S(2)}, u32[]{:S(2)}) collective-permute-start(bf16[512,512]{1,0:T(8,128)(2,1)S(1)} %get-tuple-element.44), channel_id=1, source_target_pairs={{4,8},{8,4},{5,9},{9,5},{6,10},{10,6},{7,11},{11,7},{20,24},{24,20... | collective-permute-start | bytes 1572872 | tf_op jit(solution)/shard_map/ppermute | solution.py:407
  21.9 2.2 %copy-start.4 = (bf16[1,256,2,16,256]{4,3,2,1,0:T(8,128)(2,1)S(1)}, bf16[1,256,2,16,256]{4,3,2,1,0:T(8,128)(2,1)}, u32[]{:S(2)}) copy-start(bf16[1,256,2,16,256]{4,3,2,1,0:T(8,128)(2,1)} %param.11) | copy-start | bytes 12582916
  26.0 2.0 copy-start
  28.0 82.4 %copy-start.9 = (s32[1,384]{1,0:T(1,128)S(1)}, s32[1,384]{1,0:T(1,128)}, u32[]{:S(2)}) copy-start(s32[1,384]{1,0:T(1,128)} %param.13) | copy-start | bytes 4612
  28.0 82.8 %copy-start.10 = (s32[1,128]{1,0:T(1,128)S(1)}, s32[1,128]{1,0:T(1,128)}, u32[]{:S(2)}) copy-start(s32[1,128]{1,0:T(1,128)} %param.14) | copy-start | bytes 1540
  28.0 83.1 %copy-start.11 = (s32[1,128]{1,0:T(1,128)S(1)}, s32[1,128]{1,0:T(1,128)}, u32[]{:S(2)}) copy-start(s32[1,128]{1,0:T(1,128)} %param.15) | copy-start | bytes 1540
  30.7 78.9 %copy-start.5 = (bf16[512,512]{1,0:T(8,128)(2,1)}, bf16[512,512]{1,0:T(8,128)(2,1)S(1)}, u32[]{:S(2)}) copy-start(bf16[512,512]{1,0:T(8,128)(2,1)S(1)} %collective-permute-done.2.refs_4_) | copy-start | bytes 1572868
  33.6 92.6 %all-to-all-start.1 = ((bf16[4,64,2,16,256]{4,3,2,1,0:T(8,128)(2,1)}), bf16[4,64,2,16,256]{4,3,2,1,0:T(8,128)(2,1)}, u32[]{:S(2)}, u32[]{:S(2)}) async-start(bf16[4,64,2,16,256]{4,3,2,1,0:T(8,128)(2,1)} %copy-done), calls=%async_computation.1 | async-start | bytes 8388608 | tf_op jit(solution)/shard_map/all_to_all | solution.py:413
  38.4 87.7 %copy-start.3 = (s32[128]{0:T(128)S(1)}, s32[128]{0:T(128)}, u32[]{:S(2)}) copy-start(s32[128]{0:T(128)} %get-tuple-element.39.position) | copy-start | bytes 1540
  38.4 58.3 %collective-permute-start.10 = (bf16[512,512]{1,0:T(8,128)(2,1)S(1)}, bf16[512,512]{1,0:T(8,128)(2,1)S(1)}, u32[]{:S(2)}, u32[]{:S(2)}) collective-permute-start(bf16[512,512]{1,0:T(8,128)(2,1)S(1)} %collective-permute-done.1), channel_id=1, source_target_pairs={{4,0},{8,12},{5,1},{9,13},{6,2},{10,14},{7,3},{11,15},{20,16},{24,... | collective-permute-start | bytes 1572872 | tf_op jit(solution)/shard_map/ppermute | solution.py:440
  41.3 65.1 %collective-permute-start.14 = (bf16[512,512]{1,0:T(8,128)(2,1)}, bf16[512,512]{1,0:T(8,128)(2,1)}, u32[]{:S(2)}, u32[]{:S(2)}) collective-permute-start(bf16[512,512]{1,0:T(8,128)(2,1)} %collective-permute-done.3), channel_id=1, source_target_pairs={{4,0},{8,12},{5,1},{9,13},{6,2},{10,14},{7,3},{11,15},{20,16},{24,... | collective-permute-start | bytes 1572872 | tf_op jit(solution)/shard_map/ppermute | solution.py:440
  43.4 65.7 %collective-permute-start.4 = (bf16[512,512]{1,0:T(8,128)(2,1)}, bf16[512,512]{1,0:T(8,128)(2,1)}, u32[]{:S(2)}, u32[]{:S(2)}) collective-permute-start(bf16[512,512]{1,0:T(8,128)(2,1)} %collective-permute-done.refs_0_), channel_id=1, source_target_pairs={{0,16},{16,0},{1,17},{17,1},{2,18},{18,2},{3,19},{19,3},{4,20},{20... | collective-permute-start | bytes 1572872 | tf_op jit(solution)/shard_map/ppermute | solution.py:439
  44.9 64.7 %collective-permute-start.7 = (bf16[512,512]{1,0:T(8,128)(2,1)S(1)}, bf16[512,512]{1,0:T(8,128)(2,1)S(1)}, u32[]{:S(2)}, u32[]{:S(2)}) collective-permute-start(bf16[512,512]{1,0:T(8,128)(2,1)S(1)} %collective-permute-done.2.refs_4_), channel_id=1, source_target_pairs={{0,16},{16,0},{1,17},{17,1},{2,18},{18,2},{3,19},{19,3},{4,20},{20... | collective-permute-start | bytes 1572872 | tf_op jit(solution)/shard_map/ppermute | solution.py:439
  96.7 32.6 %copy-start.1 = (bf16[1,384,2048]{2,1,0:T(8,128)(2,1)S(1)}, bf16[1,384,2048]{2,1,0:T(8,128)(2,1)}, u32[]{:S(2)}) copy-start(bf16[1,384,2048]{2,1,0:T(8,128)(2,1)} %param.9) | copy-start | bytes 4718596
  96.8 14.4 %collective-permute-start.11 = (bf16[512,512]{1,0:T(8,128)(2,1)S(1)}, bf16[512,512]{1,0:T(8,128)(2,1)}, u32[]{:S(2)}, u32[]{:S(2)}) collective-permute-start(bf16[512,512]{1,0:T(8,128)(2,1)S(1)} %broadcast_select_fusion.3.refs_0_), channel_id=1, source_target_pairs={{0,16},{16,0},{1,17},{17,1},{2,18},{18,2},{3,19},{19,3},{4,20},{20... | collective-permute-start | bytes 1572872 | tf_op jit(solution)/shard_map/ppermute | solution.py:441
  107.5 9.8 %collective-permute-start.15 = (bf16[512,512]{1,0:T(8,128)(2,1)S(1)}, bf16[512,512]{1,0:T(8,128)(2,1)}, u32[]{:S(2)}, u32[]{:S(2)}) collective-permute-start(bf16[512,512]{1,0:T(8,128)(2,1)S(1)} %broadcast_select_fusion.2.refs_4_), channel_id=1, source_target_pairs={{0,16},{16,0},{1,17},{17,1},{2,18},{18,2},{3,19},{19,3},{4,20},{20... | collective-permute-start | bytes 1572872 | tf_op jit(solution)/shard_map/ppermute | solution.py:441
  109.1 8.2 %collective-permute-start.5 = (bf16[512,512]{1,0:T(8,128)(2,1)}, bf16[512,512]{1,0:T(8,128)(2,1)}, u32[]{:S(2)}, u32[]{:S(2)}) collective-permute-start(bf16[512,512]{1,0:T(8,128)(2,1)} %collective-permute-done.refs_0_), channel_id=1, source_target_pairs={{0,1},{1,0},{2,3},{3,2},{4,5},{5,4},{6,7},{7,6},{8,9},{9,8},{10,11... | collective-permute-start | bytes 1572872 | tf_op jit(solution)/shard_map/ppermute | solution.py:437
  109.1 8.7 %collective-permute-start.6 = (bf16[512,512]{1,0:T(8,128)(2,1)}, bf16[512,512]{1,0:T(8,128)(2,1)}, u32[]{:S(2)}, u32[]{:S(2)}) collective-permute-start(bf16[512,512]{1,0:T(8,128)(2,1)} %collective-permute-done.4.refs_1_), channel_id=1, source_target_pairs={{0,1},{1,0},{2,3},{3,2},{4,5},{5,4},{6,7},{7,6},{8,9},{9,8},{10,11... | collective-permute-start | bytes 1572872 | tf_op jit(solution)/shard_map/ppermute | solution.py:437
  109.6 0.8 copy-start.7
  110.4 7.5 %collective-permute-start.8 = (bf16[512,512]{1,0:T(8,128)(2,1)S(1)}, bf16[512,512]{1,0:T(8,128)(2,1)}, u32[]{:S(2)}, u32[]{:S(2)}) collective-permute-start(bf16[512,512]{1,0:T(8,128)(2,1)S(1)} %collective-permute-done.2.refs_4_), channel_id=1, source_target_pairs={{0,1},{1,0},{2,3},{3,2},{4,5},{5,4},{6,7},{7,6},{8,9},{9,8},{10,11... | collective-permute-start | bytes 1572872 | tf_op jit(solution)/shard_map/ppermute | solution.py:437
  111.2 7.3 %collective-permute-start.12 = (bf16[512,512]{1,0:T(8,128)(2,1)S(1)}, bf16[512,512]{1,0:T(8,128)(2,1)}, u32[]{:S(2)}, u32[]{:S(2)}) collective-permute-start(bf16[512,512]{1,0:T(8,128)(2,1)S(1)} %broadcast_select_fusion.3.refs_0_), channel_id=1, source_target_pairs={{0,1},{1,0},{2,3},{3,2},{4,5},{5,4},{6,7},{7,6},{8,9},{9,8},{10,11... | collective-permute-start | bytes 1572872 | tf_op jit(solution)/shard_map/ppermute | solution.py:437
  117.3 6.8 %collective-permute-start.9 = (bf16[512,512]{1,0:T(8,128)(2,1)}, bf16[512,512]{1,0:T(8,128)(2,1)}, u32[]{:S(2)}, u32[]{:S(2)}) collective-permute-start(bf16[512,512]{1,0:T(8,128)(2,1)} %copy-done.7), channel_id=1, source_target_pairs={{0,1},{1,0},{2,3},{3,2},{4,5},{5,4},{6,7},{7,6},{8,9},{9,8},{10,11... | collective-permute-start | bytes 1572872 | tf_op jit(solution)/shard_map/ppermute | solution.py:437
  117.3 8.8 %collective-permute-start.13 = (bf16[512,512]{1,0:T(8,128)(2,1)}, bf16[512,512]{1,0:T(8,128)(2,1)}, u32[]{:S(2)}, u32[]{:S(2)}) collective-permute-start(bf16[512,512]{1,0:T(8,128)(2,1)} %collective-permute-done.11.refs_1_), channel_id=1, source_target_pairs={{0,1},{1,0},{2,3},{3,2},{4,5},{5,4},{6,7},{7,6},{8,9},{9,8},{10,11... | collective-permute-start | bytes 1572872 | tf_op jit(solution)/shard_map/ppermute | solution.py:437
  117.9 8.3 %collective-permute-start.16 = (bf16[512,512]{1,0:T(8,128)(2,1)S(1)}, bf16[512,512]{1,0:T(8,128)(2,1)}, u32[]{:S(2)}, u32[]{:S(2)}) collective-permute-start(bf16[512,512]{1,0:T(8,128)(2,1)S(1)} %broadcast_select_fusion.2.refs_4_), channel_id=1, source_target_pairs={{0,1},{1,0},{2,3},{3,2},{4,5},{5,4},{6,7},{7,6},{8,9},{9,8},{10,11... | collective-permute-start | bytes 1572872 | tf_op jit(solution)/shard_map/ppermute | solution.py:437
  117.9 8.2 %collective-permute-start.17 = (bf16[512,512]{1,0:T(8,128)(2,1)}, bf16[512,512]{1,0:T(8,128)(2,1)}, u32[]{:S(2)}, u32[]{:S(2)}) collective-permute-start(bf16[512,512]{1,0:T(8,128)(2,1)} %collective-permute-done.15.refs_5_), channel_id=1, source_target_pairs={{0,1},{1,0},{2,3},{3,2},{4,5},{5,4},{6,7},{7,6},{8,9},{9,8},{10,11... | collective-permute-start | bytes 1572872 | tf_op jit(solution)/shard_map/ppermute | solution.py:437
  118.5 24.2 %collective-permute-start.18 = (bf16[512,512]{1,0:T(8,128)(2,1)}, bf16[512,512]{1,0:T(8,128)(2,1)}, u32[]{:S(2)}, u32[]{:S(2)}) collective-permute-start(bf16[512,512]{1,0:T(8,128)(2,1)} %collective-permute-done.refs_0_), channel_id=1, source_target_pairs={{4,8},{8,4},{5,9},{9,5},{6,10},{10,6},{7,11},{11,7},{20,24},{24,20... | collective-permute-start | bytes 1572872 | tf_op jit(solution)/shard_map/ppermute | solution.py:444
  124.2 36.2 %collective-permute-start.27 = (bf16[512,512]{1,0:T(8,128)(2,1)}, bf16[512,512]{1,0:T(8,128)(2,1)}, u32[]{:S(2)}, u32[]{:S(2)}) collective-permute-start(bf16[512,512]{1,0:T(8,128)(2,1)} %copy-done.5), channel_id=1, source_target_pairs={{4,8},{8,4},{5,9},{9,5},{6,10},{10,6},{7,11},{11,7},{20,24},{24,20... | collective-permute-start | bytes 1572872 | tf_op jit(solution)/shard_map/ppermute | solution.py:444
  129.3 9.6 %copy-start.2 = (bf16[2048,1024]{1,0:T(8,128)(2,1)S(1)}, bf16[2048,1024]{1,0:T(8,128)(2,1)}, u32[]{:S(2)}) copy-start(bf16[2048,1024]{1,0:T(8,128)(2,1)} %refs_0_.3) | copy-start | bytes 12582916
  140.5 26.0 %copy-start.6 = (bf16[512,512]{1,0:T(8,128)(2,1)S(1)}, bf16[512,512]{1,0:T(8,128)(2,1)}, u32[]{:S(2)}) copy-start(bf16[512,512]{1,0:T(8,128)(2,1)} %copy-done.5) | copy-start | bytes 1572868
  140.5 26.0 %copy-start.8 = (bf16[512,512]{1,0:T(8,128)(2,1)S(1)}, bf16[512,512]{1,0:T(8,128)(2,1)}, u32[]{:S(2)}) copy-start(bf16[512,512]{1,0:T(8,128)(2,1)} %copy-done.7) | copy-start | bytes 1572868
  140.5 26.0 %collective-permute-start.20 = (bf16[192,1024]{1,0:T(8,128)(2,1)S(1)}, bf16[192,1024]{1,0:T(8,128)(2,1)S(1)}, u32[]{:S(2)}, u32[]{:S(2)}) collective-permute-start(bf16[192,1024]{1,0:T(8,128)(2,1)S(1)} %project.6), channel_id=1, source_target_pairs={{0,2},{2,0},{1,3},{3,1},{4,6},{6,4},{5,7},{7,5},{8,10},{10,8},{9,1... | collective-permute-start | bytes 1179656 | tf_op jit(solution)/shard_map/ppermute | solution.py:450
  142.7 19.6 %collective-permute-start.19 = (bf16[512,512]{1,0:T(8,128)(2,1)}, bf16[512,512]{1,0:T(8,128)(2,1)S(1)}, u32[]{:S(2)}, u32[]{:S(2)}) collective-permute-start(bf16[512,512]{1,0:T(8,128)(2,1)} %collective-permute-done.18), channel_id=1, source_target_pairs={{4,0},{8,12},{5,1},{9,13},{6,2},{10,14},{7,3},{11,15},{20,16},{24,... | collective-permute-start | bytes 1572872 | tf_op jit(solution)/shard_map/ppermute | solution.py:448
  160.4 13.6 %collective-permute-start.28 = (bf16[512,512]{1,0:T(8,128)(2,1)}, bf16[512,512]{1,0:T(8,128)(2,1)S(1)}, u32[]{:S(2)}, u32[]{:S(2)}) collective-permute-start(bf16[512,512]{1,0:T(8,128)(2,1)} %collective-permute-done.27), channel_id=1, source_target_pairs={{4,0},{8,12},{5,1},{9,13},{6,2},{10,14},{7,3},{11,15},{20,16},{24,... | collective-permute-start | bytes 1572872 | tf_op jit(solution)/shard_map/ppermute | solution.py:452
  163.4 10.5 %collective-permute-start.22 = (bf16[512,512]{1,0:T(8,128)(2,1)S(1)}, bf16[512,512]{1,0:T(8,128)(2,1)S(1)}, u32[]{:S(2)}, u32[]{:S(2)}) collective-permute-start(bf16[512,512]{1,0:T(8,128)(2,1)S(1)} %broadcast_select_fusion.1.refs_0_), channel_id=1, source_target_pairs={{0,16},{16,0},{1,17},{17,1},{2,18},{18,2},{3,19},{19,3},{4,20},{20... | collective-permute-start | bytes 1572872 | tf_op jit(solution)/shard_map/ppermute | solution.py:454
  170.1 7.8 %collective-permute-start.21 = (bf16[192,1024]{1,0:T(8,128)(2,1)S(1)}, bf16[192,1024]{1,0:T(8,128)(2,1)S(1)}, u32[]{:S(2)}, u32[]{:S(2)}) collective-permute-start(bf16[192,1024]{1,0:T(8,128)(2,1)S(1)} %get-tuple-element.56), channel_id=1, source_target_pairs={{0,2},{2,0},{1,3},{3,1},{4,6},{6,4},{5,7},{7,5},{8,10},{10,8},{9,1... | collective-permute-start | bytes 1179656 | tf_op jit(solution)/shard_map/ppermute | solution.py:459
  170.2 9.3 %collective-permute-start.23 = (bf16[512,512]{1,0:T(8,128)(2,1)S(1)}, bf16[512,512]{1,0:T(8,128)(2,1)S(1)}, u32[]{:S(2)}, u32[]{:S(2)}) collective-permute-start(bf16[512,512]{1,0:T(8,128)(2,1)S(1)} %broadcast_select_fusion.1.refs_0_), channel_id=1, source_target_pairs={{0,1},{1,0},{2,3},{3,2},{4,5},{5,4},{6,7},{7,6},{8,9},{9,8},{10,11... | collective-permute-start | bytes 1572872 | tf_op jit(solution)/shard_map/ppermute | solution.py:437
  174.0 5.6 %collective-permute-start.24 = (bf16[512,512]{1,0:T(8,128)(2,1)S(1)}, bf16[512,512]{1,0:T(8,128)(2,1)S(1)}, u32[]{:S(2)}, u32[]{:S(2)}) collective-permute-start(bf16[512,512]{1,0:T(8,128)(2,1)S(1)} %collective-permute-done.22.refs_1_), channel_id=1, source_target_pairs={{0,1},{1,0},{2,3},{3,2},{4,5},{5,4},{6,7},{7,6},{8,9},{9,8},{10,11... | collective-permute-start | bytes 1572872 | tf_op jit(solution)/shard_map/ppermute | solution.py:437
  175.6 13.9 %collective-permute-start.29 = (bf16[512,512]{1,0:T(8,128)(2,1)S(1)}, bf16[512,512]{1,0:T(8,128)(2,1)S(1)}, u32[]{:S(2)}, u32[]{:S(2)}) collective-permute-start(bf16[512,512]{1,0:T(8,128)(2,1)S(1)} %broadcast_select_fusion.refs_0_), channel_id=1, source_target_pairs={{0,16},{16,0},{1,17},{17,1},{2,18},{18,2},{3,19},{19,3},{4,20},{20... | collective-permute-start | bytes 1572872 | tf_op jit(solution)/shard_map/ppermute | solution.py:461
  181.1 24.4 %collective-permute-start.30 = (bf16[512,512]{1,0:T(8,128)(2,1)S(1)}, bf16[512,512]{1,0:T(8,128)(2,1)S(1)}, u32[]{:S(2)}, u32[]{:S(2)}) collective-permute-start(bf16[512,512]{1,0:T(8,128)(2,1)S(1)} %broadcast_select_fusion.refs_0_), channel_id=1, source_target_pairs={{0,1},{1,0},{2,3},{3,2},{4,5},{5,4},{6,7},{7,6},{8,9},{9,8},{10,11... | collective-permute-start | bytes 1572872 | tf_op jit(solution)/shard_map/ppermute | solution.py:437
  189.5 16.0 %collective-permute-start.31 = (bf16[512,512]{1,0:T(8,128)(2,1)S(1)}, bf16[512,512]{1,0:T(8,128)(2,1)S(1)}, u32[]{:S(2)}, u32[]{:S(2)}) collective-permute-start(bf16[512,512]{1,0:T(8,128)(2,1)S(1)} %collective-permute-done.29.refs_1_), channel_id=1, source_target_pairs={{0,1},{1,0},{2,3},{3,2},{4,5},{5,4},{6,7},{7,6},{8,9},{9,8},{10,11... | collective-permute-start | bytes 1572872 | tf_op jit(solution)/shard_map/ppermute | solution.py:437
  189.5 12.0 %collective-permute-start.25 = (bf16[192,1024]{1,0:T(8,128)(2,1)S(1)}, bf16[192,1024]{1,0:T(8,128)(2,1)S(1)}, u32[]{:S(2)}, u32[]{:S(2)}) collective-permute-start(bf16[192,1024]{1,0:T(8,128)(2,1)S(1)} %get-tuple-element.58), channel_id=1, source_target_pairs={{0,2},{2,0},{1,3},{3,1},{4,6},{6,4},{5,7},{7,5},{8,10},{10,8},{9,1... | collective-permute-start | bytes 1179656 | tf_op jit(solution)/shard_map/ppermute | solution.py:459
  191.5 14.0 %collective-permute-start.26 = (bf16[192,512]{1,0:T(8,128)(2,1)S(1)}, bf16[192,512]{1,0:T(8,128)(2,1)S(1)}, u32[]{:S(2)}, u32[]{:S(2)}) collective-permute-start(bf16[192,512]{1,0:T(8,128)(2,1)S(1)} %get-tuple-element.64), channel_id=1, source_target_pairs={{0,2},{2,0},{1,3},{3,1},{4,6},{6,4},{5,7},{7,5},{8,10},{10,8},{9,1... | collective-permute-start | bytes 589832 | tf_op jit(solution)/shard_map/ppermute | solution.py:468
  207.0 6.7 %collective-permute-start.32 = (bf16[192,512]{1,0:T(8,128)(2,1)S(1)}, bf16[192,512]{1,0:T(8,128)(2,1)S(1)}, u32[]{:S(2)}, u32[]{:S(2)}) collective-permute-start(bf16[192,512]{1,0:T(8,128)(2,1)S(1)} %get-tuple-element.72), channel_id=1, source_target_pairs={{0,2},{2,0},{1,3},{3,1},{4,6},{6,4},{5,7},{7,5},{8,10},{10,8},{9,1... | collective-permute-start | bytes 589832 | tf_op jit(solution)/shard_map/ppermute | solution.py:468

commit v11 on v10

--- a/solution.py
+++ b/solution.py
@@ -346,7 +346,7 @@
             pltpu.VMEM(out, jnp.bfloat16),
             pltpu.SemaphoreType.DMA((asked.shape[0] + 1,)),
         ],
-        compiler_params=pltpu.CompilerParams(vmem_limit_bytes=12 * MIB),
+        compiler_params=pltpu.CompilerParams(vmem_limit_bytes=56 * MIB),
         cost_estimate=cost(),
         name="pick",
     )(asked, pool)
@@ -453,16 +453,17 @@
     far[0] = jnp.where(middle, far[0], after(far_on[0], stay))
     far_across = [swap_group(far[0])]
     for pieces in (near_all, next_all):
-        both = project(control, after(left, far[0], came[0], *sent), pieces, stay)
+        both = project(control, after(left, far[0], far[-1], came[0], *sent), pieces, stay)
         sent.append(both[0])
         kept.append(both[1])
         came.append(swap_tp(sent[-1]))
-    far[1] = jnp.where(middle, far[1], after(far_on[1], sent[2]))
-    far_across.append(swap_group(far[1]))
+        if len(far_across) == 1:
+            far[1] = jnp.where(middle, far[1], after(far_on[1], sent[1]))
+            far_across.append(swap_group(far[1]))
     kept.insert(0, project(control, after(stay, sent[2], came[1], far_across[0]), [out_weight]))
     for n in range(2):
-        pieces = four(far[n], far_across[n], *sent[3:])
-        both = project(control, after(left, kept[0], *came[2 : 2 + 2 * n]), pieces, stay)
+        pieces = four(far[n], far_across[n], sent[-1])
+        both = project(control, after(left, kept[0], *came[2 : 3 + n]), pieces, stay)
         sent.append(both[0])
         kept.append(both[1])
         came.append(swap_tp(sent[-1]))

time: 216 us -> 209 us (0.968); the launches traced: 216 us -> 206 us
  waiting for transfers between devices: 99.5 us -> 91.3 us
  local copies, waits for them, and re-layouts: 7.89 us -> 3.68 us
  Pallas kernels: 43 us -> 46.1 us
    ppermute x1, waiting for transfers between devices: 8.39 us -> 1.38 us  [shards(): far_across.append(swap_group(far[1]))]
    unnamed x25 -> x21, local copies, waits for them, and re-layouts: 6.12 us -> 1.9 us
    pallas_call x1, Pallas kernels: 1.93 us -> 5.05 us  [pick(): pl.pallas_call(pick_kernel, out_shape=jax.ShapeDtypeStruct(out, jnp.bfloa...]
    ppermute x1, starting transfers between devices: 3.06 us -> 0.07 us  [shards(): far_across = [swap_group(far[0])]]
  transfers between devices with their start and end apart: 34 -> 34, of which waited for: 11 -> 11; matrix products, arithmetic and copies ran while one was open for 3% -> 3% of each run, Pallas kernels for 18% -> 21%
where the time goes in v11:
time: 209 us; the launch traced here: 206 us
  waiting for transfers between devices  91.3 us (44%)
  starting transfers between devices  49.6 us (24%)
  Pallas kernels  46.1 us (22%)
  blocking collectives  10.9 us (5%)
  other arithmetic  3.92 us (2%)
  local copies, waits for them, and re-layouts  3.68 us (2%)
    ppermute x2, waiting for transfers between devices, shards(): next_shard = [jnp.where(middle, part, forward(part)) for part in inner]  59.4 us
    pallas_call x2, Pallas kernels, attend(): pl.pallas_call(functools.partial(attend_kernel, fresh_base, side), out_sh...  19.9 us
    ppermute x4, waiting for transfers between devices, shards(): came.append(swap_tp(sent[-1]))  18.1 us
    pallas_call x6, Pallas kernels, project(): pl.pallas_call(project_kernel if stay is None else project_both_kernel, o...  13.3 us
    all_to_all x1, blocking collectives, shards(): lax.all_to_all(wanted, 'seq', split_axis=0, concat_axis=0, tiled=True)  10.9 us
    ppermute x1, starting transfers between devices, shards(): far_on = [forward(after(far[0], left))]  8.74 us
    ppermute x2, starting transfers between devices, shards(): far = [cross(after(part, *next_across)) for part in near]  5.85 us
    ppermute x2, waiting for transfers between devices, shards(): next_across = [swap_group(part) for part in next_shard]  5.66 us
  transfers between devices with their start and end apart: 34, of which 11 were waited for; matrix products, arithmetic and copies ran while one was open for 3% of the time, Pallas kernels for 21%

profile of v11, /device:TPU:16, one launch (start us, length us, event | category | flops | bytes accessed | tf_op | source)
XLA Modules:
  0.0 206.2 jit_solution(4926902136810232366)
XLA Ops:
  0.0 1.3 fusion.5
  1.3 1.6 collective-permute-start
  2.9 1.9 collective-permute-start.1
  4.8 2.6 %rank.1 = (s32[128]{0:T(128)}, s32[4,64]{1,0:T(4,128)}) custom-call(s32[1,128]{1,0:T(1,128)} %owner.1, s32[1,128]{1,0:T(1,128)} %page.1), custom_call_target="tpu_custom_call" | custom-call | flops 3000000000 | bytes 1000 | tf_op jit(solution)/shard_map/rank/pallas_call | solution.py:49
  7.5 10.9 %all_to_all.17 = s32[4,1,64]{2,1,0:T(1,128)} all-to-all(s32[4,1,64]{2,1,0:T(1,128)} %bitcast.39), channel_id=1, replica_groups=mesh['group'=2,'seq'=4,'tp'=2,'role'=2] {'seq'}, dimensions={0} | all-to-all | bytes 2048 | tf_op jit(solution)/shard_map/all_to_all | solution.py:402
  18.4 1.4 collective-permute-start.2
  19.8 2.2 %collective-permute-start.3 = (bf16[512,512]{1,0:T(8,128)(2,1)S(1)}, bf16[512,512]{1,0:T(8,128)(2,1)}, u32[]{:S(2)}, u32[]{:S(2)}) collective-permute-start(bf16[512,512]{1,0:T(8,128)(2,1)S(1)} %get-tuple-element.46), channel_id=1, source_target_pairs={{4,8},{8,4},{5,9},{9,5},{6,10},{10,6},{7,11},{11,7},{20,24},{24,20... | collective-permute-start | bytes 1572872 | tf_op jit(solution)/shard_map/ppermute | solution.py:407
  22.0 5.1 %pick.1 = bf16[4,64,2,16,256]{4,3,2,1,0:T(8,128)(2,1)} custom-call(s32[4,64]{1,0:T(4,128)} %bitcast.38, bf16[256,2,16,256]{3,2,1,0:T(8,128)(2,1)} %bitcast.41), custom_call_target="tpu_custom_call" | custom-call | flops 3000000000 | bytes 1000 | tf_op jit(solution)/shard_map/pick/pallas_call | solution.py:339
  27.1 3.6 %collective-permute-done.2.refs_4_ = bf16[512,512]{1,0:T(8,128)(2,1)S(1)} collective-permute-done((bf16[512,512]{1,0:T(8,128)(2,1)S(1)}, bf16[512,512]{1,0:T(8,128)(2,1)S(1)}, u32[]{:S(2)}, u32[]{:S(2)}) %collective-permute-start.2) | collective-permute-done | bytes 524320 | tf_op jit(solution)/shard_map/ppermute | solution.py:406
  30.7 2.8 %collective-permute-done.3 = bf16[512,512]{1,0:T(8,128)(2,1)} collective-permute-done((bf16[512,512]{1,0:T(8,128)(2,1)S(1)}, bf16[512,512]{1,0:T(8,128)(2,1)}, u32[]{:S(2)}, u32[]{:S(2)}) %collective-permute-start.3) | collective-permute-done | bytes 524320 | tf_op jit(solution)/shard_map/ppermute | solution.py:407
  33.5 4.9 %all-to-all-start.1 = ((bf16[4,64,2,16,256]{4,3,2,1,0:T(8,128)(2,1)}), bf16[4,64,2,16,256]{4,3,2,1,0:T(8,128)(2,1)}, u32[]{:S(2)}, u32[]{:S(2)}) async-start(bf16[4,64,2,16,256]{4,3,2,1,0:T(8,128)(2,1)} %pick.1), calls=%async_computation.1 | async-start | bytes 8388608 | tf_op jit(solution)/shard_map/all_to_all | solution.py:413
  38.4 2.8 %collective-permute-start.10 = (bf16[512,512]{1,0:T(8,128)(2,1)S(1)}, bf16[512,512]{1,0:T(8,128)(2,1)S(1)}, u32[]{:S(2)}, u32[]{:S(2)}) collective-permute-start(bf16[512,512]{1,0:T(8,128)(2,1)S(1)} %collective-permute-done.1), channel_id=1, source_target_pairs={{4,0},{8,12},{5,1},{9,13},{6,2},{10,14},{7,3},{11,15},{20,16},{24,... | collective-permute-start | bytes 1572872 | tf_op jit(solution)/shard_map/ppermute | solution.py:440
  41.2 2.1 %collective-permute-start.14 = (bf16[512,512]{1,0:T(8,128)(2,1)}, bf16[512,512]{1,0:T(8,128)(2,1)}, u32[]{:S(2)}, u32[]{:S(2)}) collective-permute-start(bf16[512,512]{1,0:T(8,128)(2,1)} %collective-permute-done.3), channel_id=1, source_target_pairs={{4,0},{8,12},{5,1},{9,13},{6,2},{10,14},{7,3},{11,15},{20,16},{24,... | collective-permute-start | bytes 1572872 | tf_op jit(solution)/shard_map/ppermute | solution.py:440
  43.3 1.5 collective-permute-start.4
  45.4 51.4 %collective-permute-done.10 = bf16[512,512]{1,0:T(8,128)(2,1)S(1)} collective-permute-done((bf16[512,512]{1,0:T(8,128)(2,1)S(1)}, bf16[512,512]{1,0:T(8,128)(2,1)S(1)}, u32[]{:S(2)}, u32[]{:S(2)}) %collective-permute-start.10) | collective-permute-done | bytes 524320 | tf_op jit(solution)/shard_map/ppermute | solution.py:440
  96.8 1.6 collective-permute-start.11
  98.4 8.0 %collective-permute-done.14 = bf16[512,512]{1,0:T(8,128)(2,1)} collective-permute-done((bf16[512,512]{1,0:T(8,128)(2,1)}, bf16[512,512]{1,0:T(8,128)(2,1)}, u32[]{:S(2)}, u32[]{:S(2)}) %collective-permute-start.14) | collective-permute-done | bytes 524320 | tf_op jit(solution)/shard_map/ppermute | solution.py:440
  106.4 1.1 broadcast_select_fusion.2.refs_4_
  107.5 1.6 collective-permute-start.15
  109.6 0.8 copy-done.5
  111.2 0.6 collective-permute-start.12
  111.7 5.7 %collective-permute-done.15.refs_5_ = bf16[512,512]{1,0:T(8,128)(2,1)} collective-permute-done((bf16[512,512]{1,0:T(8,128)(2,1)S(1)}, bf16[512,512]{1,0:T(8,128)(2,1)}, u32[]{:S(2)}, u32[]{:S(2)}) %collective-permute-start.15) | collective-permute-done | bytes 524320 | tf_op jit(solution)/shard_map/ppermute | solution.py:441
  118.6 3.8 %collective-permute-start.18 = (bf16[512,512]{1,0:T(8,128)(2,1)}, bf16[512,512]{1,0:T(8,128)(2,1)}, u32[]{:S(2)}, u32[]{:S(2)}) collective-permute-start(bf16[512,512]{1,0:T(8,128)(2,1)} %collective-permute-done.refs_0_), channel_id=1, source_target_pairs={{4,8},{8,4},{5,9},{9,5},{6,10},{10,6},{7,11},{11,7},{20,24},{24,20... | collective-permute-start | bytes 1572872 | tf_op jit(solution)/shard_map/ppermute | solution.py:444
  122.6 1.1 copy.18
  123.9 2.1 collective-permute-start.20
  126.1 3.1 %place.1 = (bf16[2,3072,128]{2,1,0:T(8,128)(2,1)S(1)}, bf16[2,3072,256]{2,1,0:T(8,128)(2,1)S(1)}) custom-call(s32[128]{0:T(128)S(1)} %copy-done.2, bf16[256,2,16,256]{3,2,1,0:T(8,128)(2,1)} %bitcast.21.pages, bf16[384,512]{1,0:T(8,128)(2,1)S(1)} %bitcast.31), custom_call_target="tpu_custom_call" | custom-call | flops 1000000000 | bytes 1000 | tf_op jit(solution)/shard_map/place/pallas_call | solution.py:95
  129.2 10.3 %attend.2.left = bf16[4,192,512]{2,1,0:T(8,128)(2,1)S(1)} custom-call(s32[15]{0:T(128)S(1)} %stack.63.control, s32[6]{0:T(128)S(1)} %get-tuple-element.86.hist_at, s32[6]{0:T(128)S(1)} %get-tuple-element.85.hist_steps, s32[6]{0:T(128)S(1)} %get-tuple-element.80.fresh_at, s32[6]{0:T(128)S(1)} %get-tuple-element.79.fresh_steps, ...), custom_call_target="tpu_custom_call" | custom-call | flops 1000000000 | bytes 1000 | tf_op jit(solution)/shard_map/attend/pallas_call | solution.py:221
  139.5 1.5 project.6
  141.1 0.9 collective-permute-start.22
  142.0 8.7 %collective-permute-start.19 = (bf16[512,512]{1,0:T(8,128)(2,1)}, bf16[512,512]{1,0:T(8,128)(2,1)S(1)}, u32[]{:S(2)}, u32[]{:S(2)}) collective-permute-start(bf16[512,512]{1,0:T(8,128)(2,1)} %collective-permute-done.18), channel_id=1, source_target_pairs={{4,0},{8,12},{5,1},{9,13},{6,2},{10,14},{7,3},{11,15},{20,16},{24,... | collective-permute-start | bytes 1572872 | tf_op jit(solution)/shard_map/ppermute | solution.py:448
  150.7 9.6 %attend.3.stay.left = bf16[4,192,512]{2,1,0:T(8,128)(2,1)S(1)} custom-call(s32[15]{0:T(128)S(1)} %stack.63.control, s32[6]{0:T(128)S(1)} %get-tuple-element.86.hist_at, s32[6]{0:T(128)S(1)} %get-tuple-element.85.hist_steps, s32[6]{0:T(128)S(1)} %get-tuple-element.80.fresh_at, s32[6]{0:T(128)S(1)} %get-tuple-element.79.fresh_steps, ...), custom_call_target="tpu_custom_call" | custom-call | flops 16000000000 | bytes 1000 | tf_op jit(solution)/shard_map/attend/pallas_call | solution.py:221
  160.3 2.0 collective-permute-start.21
  162.5 1.1 broadcast_select_fusion.1.refs_0_
  163.8 3.6 %project.7 = (bf16[192,1024]{1,0:T(8,128)(2,1)S(1)}, bf16[192,1024]{1,0:T(8,128)(2,1)S(1)}) custom-call(s32[15]{0:T(128)S(1)} %stack.63.control, bf16[4,192,512]{2,1,0:T(8,128)(2,1)S(1)} %attend.2.left, bf16[4,192,512]{2,1,0:T(8,128)(2,1)S(1)} %attend.3.stay.left, bf16[512,512]{1,0:T(8,128)(2,1)} %collective-permute-done.refs_0_, ...), custom_call_target="tpu_custom_call" | custom-call | flops 6000000000 | bytes 1000 | tf_op jit(solution)/shard_map/project/pallas_call | solution.py:283
  167.4 1.8 collective-permute-start.23
  169.3 1.1 broadcast_select_fusion.refs_0_
  170.4 3.6 %project.8 = (bf16[192,1024]{1,0:T(8,128)(2,1)S(1)}, bf16[192,1024]{1,0:T(8,128)(2,1)S(1)}) custom-call(s32[15]{0:T(128)S(1)} %stack.63.control, bf16[4,192,512]{2,1,0:T(8,128)(2,1)S(1)} %attend.2.left, bf16[4,192,512]{2,1,0:T(8,128)(2,1)S(1)} %attend.3.stay.left, bf16[512,512]{1,0:T(8,128)(2,1)S(1)} %broadcast_select_fusion.3.refs_0_, ...), custom_call_target="tpu_custom_call" | custom-call | flops 6000000000 | bytes 1000 | tf_op jit(solution)/shard_map/project/pallas_call | solution.py:283
  174.8 2.0 collective-permute-start.29
  176.8 1.5 project.9.refs_0_
  178.3 7.4 %collective-permute-done.25.refs_7_ = bf16[192,1024]{1,0:T(8,128)(2,1)S(1)} collective-permute-done((bf16[192,1024]{1,0:T(8,128)(2,1)S(1)}, bf16[192,1024]{1,0:T(8,128)(2,1)S(1)}, u32[]{:S(2)}, u32[]{:S(2)}) %collective-permute-start.25) | collective-permute-done | bytes 393248 | tf_op jit(solution)/shard_map/ppermute | solution.py:459
  185.7 1.5 project.10
  187.3 1.4 collective-permute-done.29.refs_1_
  188.7 1.6 collective-permute-start.28
  190.3 5.7 %collective-permute-done.28.refs_8_ = bf16[192,512]{1,0:T(8,128)(2,1)S(1)} collective-permute-done((bf16[192,512]{1,0:T(8,128)(2,1)S(1)}, bf16[192,512]{1,0:T(8,128)(2,1)S(1)}, u32[]{:S(2)}, u32[]{:S(2)}) %collective-permute-start.28) | collective-permute-done | bytes 196640 | tf_op jit(solution)/shard_map/ppermute | solution.py:469
  196.0 1.5 project.11
  197.5 1.6 collective-permute-start.32
  199.2 5.0 %collective-permute-done.32.refs_9_ = bf16[192,512]{1,0:T(8,128)(2,1)S(1)} collective-permute-done((bf16[192,512]{1,0:T(8,128)(2,1)S(1)}, bf16[192,512]{1,0:T(8,128)(2,1)S(1)}, u32[]{:S(2)}, u32[]{:S(2)}) %collective-permute-start.32) | collective-permute-done | bytes 196640 | tf_op jit(solution)/shard_map/ppermute | solution.py:469
  204.1 2.0 join.1
  (73 shorter events, 4.5 us)
Async XLA Ops:
  1.3 17.1 %collective-permute-start = (bf16[512,512]{1,0:T(8,128)(2,1)S(1)}, bf16[512,512]{1,0:T(8,128)(2,1)}, u32[]{:S(2)}, u32[]{:S(2)}) collective-permute-start(bf16[512,512]{1,0:T(8,128)(2,1)S(1)} %get-tuple-element.84), channel_id=1, source_target_pairs={{0,4},{4,0},{8,12},{12,8},{1,5},{5,1},{9,13},{13,9},{2,6},{6,2},{1... | collective-permute-start | bytes 1572872 | tf_op jit(solution)/shard_map/ppermute | solution.py:399
  2.9 15.5 %collective-permute-start.1 = (bf16[512,512]{1,0:T(8,128)(2,1)S(1)}, bf16[512,512]{1,0:T(8,128)(2,1)S(1)}, u32[]{:S(2)}, u32[]{:S(2)}) collective-permute-start(bf16[512,512]{1,0:T(8,128)(2,1)S(1)} %get-tuple-element.84), channel_id=1, source_target_pairs={{4,8},{8,4},{5,9},{9,5},{6,10},{10,6},{7,11},{11,7},{20,24},{24,20... | collective-permute-start | bytes 1572872 | tf_op jit(solution)/shard_map/ppermute | solution.py:399
  18.4 12.3 %collective-permute-start.2 = (bf16[512,512]{1,0:T(8,128)(2,1)S(1)}, bf16[512,512]{1,0:T(8,128)(2,1)S(1)}, u32[]{:S(2)}, u32[]{:S(2)}) collective-permute-start(bf16[512,512]{1,0:T(8,128)(2,1)S(1)} %get-tuple-element.46), channel_id=1, source_target_pairs={{0,4},{4,0},{8,12},{12,8},{1,5},{5,1},{9,13},{13,9},{2,6},{6,2},{1... | collective-permute-start | bytes 1572872 | tf_op jit(solution)/shard_map/ppermute | solution.py:406
  19.8 13.7 %collective-permute-start.3 = (bf16[512,512]{1,0:T(8,128)(2,1)S(1)}, bf16[512,512]{1,0:T(8,128)(2,1)}, u32[]{:S(2)}, u32[]{:S(2)}) collective-permute-start(bf16[512,512]{1,0:T(8,128)(2,1)S(1)} %get-tuple-element.46), channel_id=1, source_target_pairs={{4,8},{8,4},{5,9},{9,5},{6,10},{10,6},{7,11},{11,7},{20,24},{24,20... | collective-permute-start | bytes 1572872 | tf_op jit(solution)/shard_map/ppermute | solution.py:407
  27.0 83.4 %copy-start.7 = (s32[1,384]{1,0:T(1,128)S(1)}, s32[1,384]{1,0:T(1,128)}, u32[]{:S(2)}) copy-start(s32[1,384]{1,0:T(1,128)} %param.13) | copy-start | bytes 4612
  27.0 83.8 %copy-start.8 = (s32[1,128]{1,0:T(1,128)S(1)}, s32[1,128]{1,0:T(1,128)}, u32[]{:S(2)}) copy-start(s32[1,128]{1,0:T(1,128)} %param.14) | copy-start | bytes 1540
  27.1 84.0 %copy-start.9 = (s32[1,128]{1,0:T(1,128)S(1)}, s32[1,128]{1,0:T(1,128)}, u32[]{:S(2)}) copy-start(s32[1,128]{1,0:T(1,128)} %param.15) | copy-start | bytes 1540
  30.7 78.9 %copy-start.3 = (bf16[512,512]{1,0:T(8,128)(2,1)}, bf16[512,512]{1,0:T(8,128)(2,1)S(1)}, u32[]{:S(2)}) copy-start(bf16[512,512]{1,0:T(8,128)(2,1)S(1)} %collective-permute-done.2.refs_4_) | copy-start | bytes 1572868
  33.5 92.5 %all-to-all-start.1 = ((bf16[4,64,2,16,256]{4,3,2,1,0:T(8,128)(2,1)}), bf16[4,64,2,16,256]{4,3,2,1,0:T(8,128)(2,1)}, u32[]{:S(2)}, u32[]{:S(2)}) async-start(bf16[4,64,2,16,256]{4,3,2,1,0:T(8,128)(2,1)} %pick.1), calls=%async_computation.1 | async-start | bytes 8388608 | tf_op jit(solution)/shard_map/all_to_all | solution.py:413
  38.4 87.7 %copy-start.2 = (s32[128]{0:T(128)S(1)}, s32[128]{0:T(128)}, u32[]{:S(2)}) copy-start(s32[128]{0:T(128)} %get-tuple-element.41.position) | copy-start | bytes 1540
  38.4 58.4 %collective-permute-start.10 = (bf16[512,512]{1,0:T(8,128)(2,1)S(1)}, bf16[512,512]{1,0:T(8,128)(2,1)S(1)}, u32[]{:S(2)}, u32[]{:S(2)}) collective-permute-start(bf16[512,512]{1,0:T(8,128)(2,1)S(1)} %collective-permute-done.1), channel_id=1, source_target_pairs={{4,0},{8,12},{5,1},{9,13},{6,2},{10,14},{7,3},{11,15},{20,16},{24,... | collective-permute-start | bytes 1572872 | tf_op jit(solution)/shard_map/ppermute | solution.py:440
  41.2 65.2 %collective-permute-start.14 = (bf16[512,512]{1,0:T(8,128)(2,1)}, bf16[512,512]{1,0:T(8,128)(2,1)}, u32[]{:S(2)}, u32[]{:S(2)}) collective-permute-start(bf16[512,512]{1,0:T(8,128)(2,1)} %collective-permute-done.3), channel_id=1, source_target_pairs={{4,0},{8,12},{5,1},{9,13},{6,2},{10,14},{7,3},{11,15},{20,16},{24,... | collective-permute-start | bytes 1572872 | tf_op jit(solution)/shard_map/ppermute | solution.py:440
  43.3 65.8 %collective-permute-start.4 = (bf16[512,512]{1,0:T(8,128)(2,1)}, bf16[512,512]{1,0:T(8,128)(2,1)}, u32[]{:S(2)}, u32[]{:S(2)}) collective-permute-start(bf16[512,512]{1,0:T(8,128)(2,1)} %collective-permute-done.refs_0_), channel_id=1, source_target_pairs={{0,16},{16,0},{1,17},{17,1},{2,18},{18,2},{3,19},{19,3},{4,20},{20... | collective-permute-start | bytes 1572872 | tf_op jit(solution)/shard_map/ppermute | solution.py:439
  44.8 64.8 %collective-permute-start.7 = (bf16[512,512]{1,0:T(8,128)(2,1)S(1)}, bf16[512,512]{1,0:T(8,128)(2,1)S(1)}, u32[]{:S(2)}, u32[]{:S(2)}) collective-permute-start(bf16[512,512]{1,0:T(8,128)(2,1)S(1)} %collective-permute-done.2.refs_4_), channel_id=1, source_target_pairs={{0,16},{16,0},{1,17},{17,1},{2,18},{18,2},{3,19},{19,3},{4,20},{20... | collective-permute-start | bytes 1572872 | tf_op jit(solution)/shard_map/ppermute | solution.py:439
  96.8 32.4 %copy-start = (bf16[1,384,2048]{2,1,0:T(8,128)(2,1)S(1)}, bf16[1,384,2048]{2,1,0:T(8,128)(2,1)}, u32[]{:S(2)}) copy-start(bf16[1,384,2048]{2,1,0:T(8,128)(2,1)} %param.9) | copy-start | bytes 4718596
  96.8 14.4 %collective-permute-start.11 = (bf16[512,512]{1,0:T(8,128)(2,1)S(1)}, bf16[512,512]{1,0:T(8,128)(2,1)}, u32[]{:S(2)}, u32[]{:S(2)}) collective-permute-start(bf16[512,512]{1,0:T(8,128)(2,1)S(1)} %broadcast_select_fusion.3.refs_0_), channel_id=1, source_target_pairs={{0,16},{16,0},{1,17},{17,1},{2,18},{18,2},{3,19},{19,3},{4,20},{20... | collective-permute-start | bytes 1572872 | tf_op jit(solution)/shard_map/ppermute | solution.py:441
  107.5 9.9 %collective-permute-start.15 = (bf16[512,512]{1,0:T(8,128)(2,1)S(1)}, bf16[512,512]{1,0:T(8,128)(2,1)}, u32[]{:S(2)}, u32[]{:S(2)}) collective-permute-start(bf16[512,512]{1,0:T(8,128)(2,1)S(1)} %broadcast_select_fusion.2.refs_4_), channel_id=1, source_target_pairs={{0,16},{16,0},{1,17},{17,1},{2,18},{18,2},{3,19},{19,3},{4,20},{20... | collective-permute-start | bytes 1572872 | tf_op jit(solution)/shard_map/ppermute | solution.py:441
  109.1 8.3 %collective-permute-start.5 = (bf16[512,512]{1,0:T(8,128)(2,1)}, bf16[512,512]{1,0:T(8,128)(2,1)}, u32[]{:S(2)}, u32[]{:S(2)}) collective-permute-start(bf16[512,512]{1,0:T(8,128)(2,1)} %collective-permute-done.refs_0_), channel_id=1, source_target_pairs={{0,1},{1,0},{2,3},{3,2},{4,5},{5,4},{6,7},{7,6},{8,9},{9,8},{10,11... | collective-permute-start | bytes 1572872 | tf_op jit(solution)/shard_map/ppermute | solution.py:437
  109.1 8.8 %collective-permute-start.6 = (bf16[512,512]{1,0:T(8,128)(2,1)}, bf16[512,512]{1,0:T(8,128)(2,1)}, u32[]{:S(2)}, u32[]{:S(2)}) collective-permute-start(bf16[512,512]{1,0:T(8,128)(2,1)} %collective-permute-done.4.refs_1_), channel_id=1, source_target_pairs={{0,1},{1,0},{2,3},{3,2},{4,5},{5,4},{6,7},{7,6},{8,9},{9,8},{10,11... | collective-permute-start | bytes 1572872 | tf_op jit(solution)/shard_map/ppermute | solution.py:437
  109.6 0.8 copy-start.5
  110.4 7.6 %collective-permute-start.8 = (bf16[512,512]{1,0:T(8,128)(2,1)S(1)}, bf16[512,512]{1,0:T(8,128)(2,1)}, u32[]{:S(2)}, u32[]{:S(2)}) collective-permute-start(bf16[512,512]{1,0:T(8,128)(2,1)S(1)} %collective-permute-done.2.refs_4_), channel_id=1, source_target_pairs={{0,1},{1,0},{2,3},{3,2},{4,5},{5,4},{6,7},{7,6},{8,9},{9,8},{10,11... | collective-permute-start | bytes 1572872 | tf_op jit(solution)/shard_map/ppermute | solution.py:437
  111.2 7.4 %collective-permute-start.12 = (bf16[512,512]{1,0:T(8,128)(2,1)S(1)}, bf16[512,512]{1,0:T(8,128)(2,1)}, u32[]{:S(2)}, u32[]{:S(2)}) collective-permute-start(bf16[512,512]{1,0:T(8,128)(2,1)S(1)} %broadcast_select_fusion.3.refs_0_), channel_id=1, source_target_pairs={{0,1},{1,0},{2,3},{3,2},{4,5},{5,4},{6,7},{7,6},{8,9},{9,8},{10,11... | collective-permute-start | bytes 1572872 | tf_op jit(solution)/shard_map/ppermute | solution.py:437
  117.4 6.5 %collective-permute-start.9 = (bf16[512,512]{1,0:T(8,128)(2,1)}, bf16[512,512]{1,0:T(8,128)(2,1)}, u32[]{:S(2)}, u32[]{:S(2)}) collective-permute-start(bf16[512,512]{1,0:T(8,128)(2,1)} %copy-done.5), channel_id=1, source_target_pairs={{0,1},{1,0},{2,3},{3,2},{4,5},{5,4},{6,7},{7,6},{8,9},{9,8},{10,11... | collective-permute-start | bytes 1572872 | tf_op jit(solution)/shard_map/ppermute | solution.py:437
  117.4 8.6 %collective-permute-start.13 = (bf16[512,512]{1,0:T(8,128)(2,1)}, bf16[512,512]{1,0:T(8,128)(2,1)}, u32[]{:S(2)}, u32[]{:S(2)}) collective-permute-start(bf16[512,512]{1,0:T(8,128)(2,1)} %collective-permute-done.11.refs_1_), channel_id=1, source_target_pairs={{0,1},{1,0},{2,3},{3,2},{4,5},{5,4},{6,7},{7,6},{8,9},{9,8},{10,11... | collective-permute-start | bytes 1572872 | tf_op jit(solution)/shard_map/ppermute | solution.py:437
  117.9 8.1 %collective-permute-start.16 = (bf16[512,512]{1,0:T(8,128)(2,1)S(1)}, bf16[512,512]{1,0:T(8,128)(2,1)}, u32[]{:S(2)}, u32[]{:S(2)}) collective-permute-start(bf16[512,512]{1,0:T(8,128)(2,1)S(1)} %broadcast_select_fusion.2.refs_4_), channel_id=1, source_target_pairs={{0,1},{1,0},{2,3},{3,2},{4,5},{5,4},{6,7},{7,6},{8,9},{9,8},{10,11... | collective-permute-start | bytes 1572872 | tf_op jit(solution)/shard_map/ppermute | solution.py:437
  118.0 8.0 %collective-permute-start.17 = (bf16[512,512]{1,0:T(8,128)(2,1)}, bf16[512,512]{1,0:T(8,128)(2,1)}, u32[]{:S(2)}, u32[]{:S(2)}) collective-permute-start(bf16[512,512]{1,0:T(8,128)(2,1)} %collective-permute-done.15.refs_5_), channel_id=1, source_target_pairs={{0,1},{1,0},{2,3},{3,2},{4,5},{5,4},{6,7},{7,6},{8,9},{9,8},{10,11... | collective-permute-start | bytes 1572872 | tf_op jit(solution)/shard_map/ppermute | solution.py:437
  118.6 23.4 %collective-permute-start.18 = (bf16[512,512]{1,0:T(8,128)(2,1)}, bf16[512,512]{1,0:T(8,128)(2,1)}, u32[]{:S(2)}, u32[]{:S(2)}) collective-permute-start(bf16[512,512]{1,0:T(8,128)(2,1)} %collective-permute-done.refs_0_), channel_id=1, source_target_pairs={{4,8},{8,4},{5,9},{9,5},{6,10},{10,6},{7,11},{11,7},{20,24},{24,20... | collective-permute-start | bytes 1572872 | tf_op jit(solution)/shard_map/ppermute | solution.py:444
  123.9 36.4 %collective-permute-start.20 = (bf16[512,512]{1,0:T(8,128)(2,1)}, bf16[512,512]{1,0:T(8,128)(2,1)}, u32[]{:S(2)}, u32[]{:S(2)}) collective-permute-start(bf16[512,512]{1,0:T(8,128)(2,1)} %copy-done.3), channel_id=1, source_target_pairs={{4,8},{8,4},{5,9},{9,5},{6,10},{10,6},{7,11},{11,7},{20,24},{24,20... | collective-permute-start | bytes 1572872 | tf_op jit(solution)/shard_map/ppermute | solution.py:444
  129.2 10.3 %copy-start.1 = (bf16[2048,1024]{1,0:T(8,128)(2,1)S(1)}, bf16[2048,1024]{1,0:T(8,128)(2,1)}, u32[]{:S(2)}) copy-start(bf16[2048,1024]{1,0:T(8,128)(2,1)} %refs_0_.3) | copy-start | bytes 12582916
  141.1 22.7 %copy-start.4 = (bf16[512,512]{1,0:T(8,128)(2,1)S(1)}, bf16[512,512]{1,0:T(8,128)(2,1)}, u32[]{:S(2)}) copy-start(bf16[512,512]{1,0:T(8,128)(2,1)} %copy-done.3) | copy-start | bytes 1572868
  141.1 22.7 %copy-start.6 = (bf16[512,512]{1,0:T(8,128)(2,1)S(1)}, bf16[512,512]{1,0:T(8,128)(2,1)}, u32[]{:S(2)}) copy-start(bf16[512,512]{1,0:T(8,128)(2,1)} %copy-done.5) | copy-start | bytes 1572868
  141.1 22.6 %collective-permute-start.22 = (bf16[192,1024]{1,0:T(8,128)(2,1)S(1)}, bf16[192,1024]{1,0:T(8,128)(2,1)S(1)}, u32[]{:S(2)}, u32[]{:S(2)}) collective-permute-start(bf16[192,1024]{1,0:T(8,128)(2,1)S(1)} %project.6), channel_id=1, source_target_pairs={{0,2},{2,0},{1,3},{3,1},{4,6},{6,4},{5,7},{7,5},{8,10},{10,8},{9,1... | collective-permute-start | bytes 1179656 | tf_op jit(solution)/shard_map/ppermute | solution.py:450
  142.0 20.6 %collective-permute-start.19 = (bf16[512,512]{1,0:T(8,128)(2,1)}, bf16[512,512]{1,0:T(8,128)(2,1)S(1)}, u32[]{:S(2)}, u32[]{:S(2)}) collective-permute-start(bf16[512,512]{1,0:T(8,128)(2,1)} %collective-permute-done.18), channel_id=1, source_target_pairs={{4,0},{8,12},{5,1},{9,13},{6,2},{10,14},{7,3},{11,15},{20,16},{24,... | collective-permute-start | bytes 1572872 | tf_op jit(solution)/shard_map/ppermute | solution.py:448
  160.3 8.9 %collective-permute-start.21 = (bf16[512,512]{1,0:T(8,128)(2,1)}, bf16[512,512]{1,0:T(8,128)(2,1)S(1)}, u32[]{:S(2)}, u32[]{:S(2)}) collective-permute-start(bf16[512,512]{1,0:T(8,128)(2,1)} %collective-permute-done.20), channel_id=1, source_target_pairs={{4,0},{8,12},{5,1},{9,13},{6,2},{10,14},{7,3},{11,15},{20,16},{24,... | collective-permute-start | bytes 1572872 | tf_op jit(solution)/shard_map/ppermute | solution.py:452
  163.6 10.5 %collective-permute-start.24 = (bf16[512,512]{1,0:T(8,128)(2,1)S(1)}, bf16[512,512]{1,0:T(8,128)(2,1)S(1)}, u32[]{:S(2)}, u32[]{:S(2)}) collective-permute-start(bf16[512,512]{1,0:T(8,128)(2,1)S(1)} %broadcast_select_fusion.1.refs_0_), channel_id=1, source_target_pairs={{0,16},{16,0},{1,17},{17,1},{2,18},{18,2},{3,19},{19,3},{4,20},{20... | collective-permute-start | bytes 1572872 | tf_op jit(solution)/shard_map/ppermute | solution.py:454
  167.4 9.4 %collective-permute-start.23 = (bf16[192,1024]{1,0:T(8,128)(2,1)S(1)}, bf16[192,1024]{1,0:T(8,128)(2,1)S(1)}, u32[]{:S(2)}, u32[]{:S(2)}) collective-permute-start(bf16[192,1024]{1,0:T(8,128)(2,1)S(1)} %get-tuple-element.60), channel_id=1, source_target_pairs={{0,2},{2,0},{1,3},{3,1},{4,6},{6,4},{5,7},{7,5},{8,10},{10,8},{9,1... | collective-permute-start | bytes 1179656 | tf_op jit(solution)/shard_map/ppermute | solution.py:459
  174.0 11.7 %collective-permute-start.26 = (bf16[512,512]{1,0:T(8,128)(2,1)S(1)}, bf16[512,512]{1,0:T(8,128)(2,1)S(1)}, u32[]{:S(2)}, u32[]{:S(2)}) collective-permute-start(bf16[512,512]{1,0:T(8,128)(2,1)S(1)} %broadcast_select_fusion.1.refs_0_), channel_id=1, source_target_pairs={{0,1},{1,0},{2,3},{3,2},{4,5},{5,4},{6,7},{7,6},{8,9},{9,8},{10,11... | collective-permute-start | bytes 1572872 | tf_op jit(solution)/shard_map/ppermute | solution.py:437
  174.1 11.6 %collective-permute-start.27 = (bf16[512,512]{1,0:T(8,128)(2,1)S(1)}, bf16[512,512]{1,0:T(8,128)(2,1)S(1)}, u32[]{:S(2)}, u32[]{:S(2)}) collective-permute-start(bf16[512,512]{1,0:T(8,128)(2,1)S(1)} %collective-permute-done.24.refs_1_), channel_id=1, source_target_pairs={{0,1},{1,0},{2,3},{3,2},{4,5},{5,4},{6,7},{7,6},{8,9},{9,8},{10,11... | collective-permute-start | bytes 1572872 | tf_op jit(solution)/shard_map/ppermute | solution.py:437
  174.6 11.1 %collective-permute-start.25 = (bf16[192,1024]{1,0:T(8,128)(2,1)S(1)}, bf16[192,1024]{1,0:T(8,128)(2,1)S(1)}, u32[]{:S(2)}, u32[]{:S(2)}) collective-permute-start(bf16[192,1024]{1,0:T(8,128)(2,1)S(1)} %get-tuple-element.63), channel_id=1, source_target_pairs={{0,2},{2,0},{1,3},{3,1},{4,6},{6,4},{5,7},{7,5},{8,10},{10,8},{9,1... | collective-permute-start | bytes 1179656 | tf_op jit(solution)/shard_map/ppermute | solution.py:459
  174.8 13.9 %collective-permute-start.29 = (bf16[512,512]{1,0:T(8,128)(2,1)S(1)}, bf16[512,512]{1,0:T(8,128)(2,1)S(1)}, u32[]{:S(2)}, u32[]{:S(2)}) collective-permute-start(bf16[512,512]{1,0:T(8,128)(2,1)S(1)} %broadcast_select_fusion.refs_0_), channel_id=1, source_target_pairs={{0,16},{16,0},{1,17},{17,1},{2,18},{18,2},{3,19},{19,3},{4,20},{20... | collective-permute-start | bytes 1572872 | tf_op jit(solution)/shard_map/ppermute | solution.py:462
  187.2 8.8 %collective-permute-start.30 = (bf16[512,512]{1,0:T(8,128)(2,1)S(1)}, bf16[512,512]{1,0:T(8,128)(2,1)S(1)}, u32[]{:S(2)}, u32[]{:S(2)}) collective-permute-start(bf16[512,512]{1,0:T(8,128)(2,1)S(1)} %broadcast_select_fusion.refs_0_), channel_id=1, source_target_pairs={{0,1},{1,0},{2,3},{3,2},{4,5},{5,4},{6,7},{7,6},{8,9},{9,8},{10,11... | collective-permute-start | bytes 1572872 | tf_op jit(solution)/shard_map/ppermute | solution.py:437
  188.7 7.3 %collective-permute-start.31 = (bf16[512,512]{1,0:T(8,128)(2,1)S(1)}, bf16[512,512]{1,0:T(8,128)(2,1)S(1)}, u32[]{:S(2)}, u32[]{:S(2)}) collective-permute-start(bf16[512,512]{1,0:T(8,128)(2,1)S(1)} %collective-permute-done.29.refs_1_), channel_id=1, source_target_pairs={{0,1},{1,0},{2,3},{3,2},{4,5},{5,4},{6,7},{7,6},{8,9},{9,8},{10,11... | collective-permute-start | bytes 1572872 | tf_op jit(solution)/shard_map/ppermute | solution.py:437
  188.7 7.3 %collective-permute-start.28 = (bf16[192,512]{1,0:T(8,128)(2,1)S(1)}, bf16[192,512]{1,0:T(8,128)(2,1)S(1)}, u32[]{:S(2)}, u32[]{:S(2)}) collective-permute-start(bf16[192,512]{1,0:T(8,128)(2,1)S(1)} %get-tuple-element.71), channel_id=1, source_target_pairs={{0,2},{2,0},{1,3},{3,1},{4,6},{6,4},{5,7},{7,5},{8,10},{10,8},{9,1... | collective-permute-start | bytes 589832 | tf_op jit(solution)/shard_map/ppermute | solution.py:469
  197.5 6.6 %collective-permute-start.32 = (bf16[192,512]{1,0:T(8,128)(2,1)S(1)}, bf16[192,512]{1,0:T(8,128)(2,1)S(1)}, u32[]{:S(2)}, u32[]{:S(2)}) collective-permute-start(bf16[192,512]{1,0:T(8,128)(2,1)S(1)} %get-tuple-element.76), channel_id=1, source_target_pairs={{0,2},{2,0},{1,3},{3,1},{4,6},{6,4},{5,7},{7,5},{8,10},{10,8},{9,1... | collective-permute-start | bytes 589832 | tf_op jit(solution)/shard_map/ppermute | solution.py:469

commit v12 on v11

--- a/solution.py
+++ b/solution.py
@@ -441,9 +441,10 @@
     next_across = [swap_group(part) for part in next_shard]
     near_all = four(near[0], near_across[0]) + four(near[1], near_across[1])
     next_all = four(next_shard[0], next_across[0]) + four(next_shard[1], next_across[1])
-    far = [cross(after(part, *next_across)) for part in near]
+    far = [cross(after(near[0], *next_across))]
 
     keys, values = place(position, after(pages, *near_all, *next_all), fresh)
+    far.append(cross(after(near[1], keys)))
     left = attend(1, control, tables, queries[0], keys, values, slots)
     far_on = [forward(after(far[0], left))]
     sent, kept = [project(control, left, [out_weight])], []
@@ -460,13 +461,14 @@
         if len(far_across) == 1:
             far[1] = jnp.where(middle, far[1], after(far_on[1], sent[1]))
             far_across.append(swap_group(far[1]))
-    kept.insert(0, project(control, after(stay, sent[2], came[1], far_across[0]), [out_weight]))
     for n in range(2):
-        pieces = four(far[n], far_across[n], sent[-1])
-        both = project(control, after(left, kept[0], *came[2 : 3 + n]), pieces, stay)
+        pieces = four(far[n], far_across[n], sent[-1], came[1])
+        both = project(control, after(left, *kept), pieces, stay)
         sent.append(both[0])
         kept.append(both[1])
         came.append(swap_tp(sent[-1]))
+        if n == 0:
+            kept.insert(0, project(control, after(stay, sent[3], came[2]), [out_weight]))
     return join(control, kept, came)
 
 

time: 209 us -> 207 us (level)
  waiting for transfers between devices: 91.3 us -> 97.1 us
  starting transfers between devices: 49.6 us -> 45.7 us
    ppermute x1, waiting for transfers between devices: 1.38 us -> 10.2 us  [shards(): far_across.append(swap_group(far[1]))]
    ppermute x4, waiting for transfers between devices: 18.1 us -> 9.46 us  [shards(): came.append(swap_tp(sent[-1]))]
    ppermute x1, starting transfers between devices: 8.74 us -> 1.8 us  [shards(): far_on = [forward(after(far[0], left))]]
    all_to_all x1, waiting for transfers between devices: 0.01 us -> 3.94 us  [shards(): lax.all_to_all(found, 'seq', split_axis=0, concat_axis=0, tiled=True)]
    ppermute x1, waiting for transfers between devices: 2.82 us -> 6.56 us  [shards(): inner.append(cross(later))]
    ppermute x1, starting transfers between devices: 0.07 us -> 3.67 us  [shards(): far_across = [swap_group(far[0])]]
    ppermute x1, waiting for transfers between devices: 3.62 us -> 0.31 us  [shards(): near.append(pair(later))]
    ppermute x4, starting transfers between devices: 5.24 us -> 2.95 us  [shards(): came.append(swap_tp(sent[-1]))]
  transfers between devices with their start and end apart: 34 -> 34, of which waited for: 11 -> 13; matrix products, arithmetic and copies ran while one was open for 3% -> 2% of each run, Pallas kernels for 21% -> 21%
where the time goes in v12:
time: 207 us; the launch traced here: 206 us
  waiting for transfers between devices  97.1 us (47%)
  starting transfers between devices  45.7 us (22%)
  Pallas kernels  44.5 us (21%)
  blocking collectives  10.7 us (5%)
  local copies, waits for them, and re-layouts  3.93 us (2%)
  other arithmetic  2.88 us (1%)
    ppermute x2, waiting for transfers between devices, shards(): next_shard = [jnp.where(middle, part, forward(part)) for part in inner]  59.4 us
    pallas_call x2, Pallas kernels, attend(): pl.pallas_call(functools.partial(attend_kernel, fresh_base, side), out_sh...  18.5 us
    pallas_call x6, Pallas kernels, project(): pl.pallas_call(project_kernel if stay is None else project_both_kernel, o...  13.2 us
    all_to_all x1, blocking collectives, shards(): lax.all_to_all(wanted, 'seq', split_axis=0, concat_axis=0, tiled=True)  10.7 us
    ppermute x1, waiting for transfers between devices, shards(): far_across.append(swap_group(far[1]))  10.2 us
    ppermute x4, waiting for transfers between devices, shards(): came.append(swap_tp(sent[-1]))  9.46 us
    ppermute x1, waiting for transfers between devices, shards(): inner.append(cross(later))  6.56 us
    all_to_all x1, starting transfers between devices, shards(): lax.all_to_all(found, 'seq', split_axis=0, concat_axis=0, tiled=True)  5.96 us
  transfers between devices with their start and end apart: 34, of which 13 were waited for; matrix products, arithmetic and copies ran while one was open for 2% of the time, Pallas kernels for 21%

profile of v12, /device:TPU:16, one launch (start us, length us, event | category | flops | bytes accessed | tf_op | source)
XLA Modules:
  0.0 205.6 jit_solution(17586406410471549548)
XLA Ops:
  0.0 1.3 fusion.5
  1.3 1.6 collective-permute-start
  2.9 1.9 collective-permute-start.1
  4.8 2.6 %rank.1 = (s32[128]{0:T(128)}, s32[4,64]{1,0:T(4,128)}) custom-call(s32[1,128]{1,0:T(1,128)} %owner.1, s32[1,128]{1,0:T(1,128)} %page.1), custom_call_target="tpu_custom_call" | custom-call | flops 3000000000 | bytes 1000 | tf_op jit(solution)/shard_map/rank/pallas_call | solution.py:49
  7.5 10.7 %all_to_all.17 = s32[4,1,64]{2,1,0:T(1,128)} all-to-all(s32[4,1,64]{2,1,0:T(1,128)} %bitcast.39), channel_id=1, replica_groups=mesh['group'=2,'seq'=4,'tp'=2,'role'=2] {'seq'}, dimensions={0} | all-to-all | bytes 2048 | tf_op jit(solution)/shard_map/all_to_all | solution.py:402
  18.2 2.2 %collective-permute-start.3 = (bf16[512,512]{1,0:T(8,128)(2,1)S(1)}, bf16[512,512]{1,0:T(8,128)(2,1)}, u32[]{:S(2)}, u32[]{:S(2)}) collective-permute-start(bf16[512,512]{1,0:T(8,128)(2,1)S(1)} %get-tuple-element.46), channel_id=1, source_target_pairs={{4,8},{8,4},{5,9},{9,5},{6,10},{10,6},{7,11},{11,7},{20,24},{24,20... | collective-permute-start | bytes 1572872 | tf_op jit(solution)/shard_map/ppermute | solution.py:407
  20.4 0.7 collective-permute-start.2
  21.1 5.0 %pick.1 = bf16[4,64,2,16,256]{4,3,2,1,0:T(8,128)(2,1)} custom-call(s32[4,64]{1,0:T(4,128)} %bitcast.38, bf16[256,2,16,256]{3,2,1,0:T(8,128)(2,1)} %bitcast.41), custom_call_target="tpu_custom_call" | custom-call | flops 3000000000 | bytes 1000 | tf_op jit(solution)/shard_map/pick/pallas_call | solution.py:339
  26.1 6.6 %collective-permute-done.3 = bf16[512,512]{1,0:T(8,128)(2,1)} collective-permute-done((bf16[512,512]{1,0:T(8,128)(2,1)S(1)}, bf16[512,512]{1,0:T(8,128)(2,1)}, u32[]{:S(2)}, u32[]{:S(2)}) %collective-permute-start.3) | collective-permute-done | bytes 524320 | tf_op jit(solution)/shard_map/ppermute | solution.py:407
  33.0 6.0 %all-to-all-start.1 = ((bf16[4,64,2,16,256]{4,3,2,1,0:T(8,128)(2,1)}), bf16[4,64,2,16,256]{4,3,2,1,0:T(8,128)(2,1)}, u32[]{:S(2)}, u32[]{:S(2)}) async-start(bf16[4,64,2,16,256]{4,3,2,1,0:T(8,128)(2,1)} %pick.1), calls=%async_computation.1 | async-start | bytes 8388608 | tf_op jit(solution)/shard_map/all_to_all | solution.py:413
  39.0 3.5 %collective-permute-start.10 = (bf16[512,512]{1,0:T(8,128)(2,1)S(1)}, bf16[512,512]{1,0:T(8,128)(2,1)S(1)}, u32[]{:S(2)}, u32[]{:S(2)}) collective-permute-start(bf16[512,512]{1,0:T(8,128)(2,1)S(1)} %collective-permute-done.1), channel_id=1, source_target_pairs={{4,0},{8,12},{5,1},{9,13},{6,2},{10,14},{7,3},{11,15},{20,16},{24,... | collective-permute-start | bytes 1572872 | tf_op jit(solution)/shard_map/ppermute | solution.py:440
  42.5 2.1 %collective-permute-start.14 = (bf16[512,512]{1,0:T(8,128)(2,1)}, bf16[512,512]{1,0:T(8,128)(2,1)}, u32[]{:S(2)}, u32[]{:S(2)}) collective-permute-start(bf16[512,512]{1,0:T(8,128)(2,1)} %collective-permute-done.3), channel_id=1, source_target_pairs={{4,0},{8,12},{5,1},{9,13},{6,2},{10,14},{7,3},{11,15},{20,16},{24,... | collective-permute-start | bytes 1572872 | tf_op jit(solution)/shard_map/ppermute | solution.py:440
  44.6 1.5 collective-permute-start.4
  46.6 51.5 %collective-permute-done.10 = bf16[512,512]{1,0:T(8,128)(2,1)S(1)} collective-permute-done((bf16[512,512]{1,0:T(8,128)(2,1)S(1)}, bf16[512,512]{1,0:T(8,128)(2,1)S(1)}, u32[]{:S(2)}, u32[]{:S(2)}) %collective-permute-start.10) | collective-permute-done | bytes 524320 | tf_op jit(solution)/shard_map/ppermute | solution.py:440
  98.1 1.6 collective-permute-start.11
  99.7 8.0 %collective-permute-done.14 = bf16[512,512]{1,0:T(8,128)(2,1)} collective-permute-done((bf16[512,512]{1,0:T(8,128)(2,1)}, bf16[512,512]{1,0:T(8,128)(2,1)}, u32[]{:S(2)}, u32[]{:S(2)}) %collective-permute-start.14) | collective-permute-done | bytes 524320 | tf_op jit(solution)/shard_map/ppermute | solution.py:440
  107.7 1.1 broadcast_select_fusion.2.refs_4_
  108.8 1.6 collective-permute-start.15
  110.4 0.6 collective-permute-start.8
  111.2 0.8 copy-done.7
  113.3 5.4 %collective-permute-done.15.refs_5_ = bf16[512,512]{1,0:T(8,128)(2,1)} collective-permute-done((bf16[512,512]{1,0:T(8,128)(2,1)S(1)}, bf16[512,512]{1,0:T(8,128)(2,1)}, u32[]{:S(2)}, u32[]{:S(2)}) %collective-permute-start.15) | collective-permute-done | bytes 524320 | tf_op jit(solution)/shard_map/ppermute | solution.py:441
  119.9 2.5 %collective-permute-start.18 = (bf16[512,512]{1,0:T(8,128)(2,1)}, bf16[512,512]{1,0:T(8,128)(2,1)}, u32[]{:S(2)}, u32[]{:S(2)}) collective-permute-start(bf16[512,512]{1,0:T(8,128)(2,1)} %collective-permute-done.refs_0_), channel_id=1, source_target_pairs={{4,8},{8,4},{5,9},{9,5},{6,10},{10,6},{7,11},{11,7},{20,24},{24,20... | collective-permute-start | bytes 1572872 | tf_op jit(solution)/shard_map/ppermute | solution.py:444
  122.5 1.1 copy.18
  124.1 3.9 %all-to-all-done.1 = bf16[4,64,2,16,256]{4,3,2,1,0:T(8,128)(2,1)} async-done(((bf16[4,64,2,16,256]{4,3,2,1,0:T(8,128)(2,1)}), bf16[4,64,2,16,256]{4,3,2,1,0:T(8,128)(2,1)}, u32[]{:S(2)}, u32[]{:S(2)}) %all-to-all-start.1) | async-done | bytes 4194336 | tf_op jit(solution)/shard_map/all_to_all | solution.py:413
  128.0 3.2 %place.1 = (bf16[2,3072,128]{2,1,0:T(8,128)(2,1)S(1)}, bf16[2,3072,256]{2,1,0:T(8,128)(2,1)S(1)}) custom-call(s32[128]{0:T(128)S(1)} %copy-done.2, bf16[256,2,16,256]{3,2,1,0:T(8,128)(2,1)} %bitcast.21.pages, bf16[384,512]{1,0:T(8,128)(2,1)S(1)} %bitcast.31), custom_call_target="tpu_custom_call" | custom-call | flops 1000000000 | bytes 1000 | tf_op jit(solution)/shard_map/place/pallas_call | solution.py:95
  131.3 4.8 %collective-permute-start.20 = (bf16[512,512]{1,0:T(8,128)(2,1)S(1)}, bf16[512,512]{1,0:T(8,128)(2,1)S(1)}, u32[]{:S(2)}, u32[]{:S(2)}) collective-permute-start(bf16[512,512]{1,0:T(8,128)(2,1)S(1)} %copy-done.4), channel_id=1, source_target_pairs={{4,8},{8,4},{5,9},{9,5},{6,10},{10,6},{7,11},{11,7},{20,24},{24,20... | collective-permute-start | bytes 1572872 | tf_op jit(solution)/shard_map/ppermute | solution.py:447
  136.1 8.9 %attend.2.left = bf16[4,192,512]{2,1,0:T(8,128)(2,1)S(1)} custom-call(s32[15]{0:T(128)S(1)} %stack.63.control, s32[6]{0:T(128)S(1)} %get-tuple-element.86.hist_at, s32[6]{0:T(128)S(1)} %get-tuple-element.85.hist_steps, s32[6]{0:T(128)S(1)} %get-tuple-element.80.fresh_at, s32[6]{0:T(128)S(1)} %get-tuple-element.79.fresh_steps, ...), custom_call_target="tpu_custom_call" | custom-call | flops 1000000000 | bytes 1000 | tf_op jit(solution)/shard_map/attend/pallas_call | solution.py:221
  145.0 1.5 project.6
  146.6 2.2 %collective-permute-start.21 = (bf16[192,1024]{1,0:T(8,128)(2,1)S(1)}, bf16[192,1024]{1,0:T(8,128)(2,1)S(1)}, u32[]{:S(2)}, u32[]{:S(2)}) collective-permute-start(bf16[192,1024]{1,0:T(8,128)(2,1)S(1)} %project.6), channel_id=1, source_target_pairs={{0,2},{2,0},{1,3},{3,1},{4,6},{6,4},{5,7},{7,5},{8,10},{10,8},{9,1... | collective-permute-start | bytes 1179656 | tf_op jit(solution)/shard_map/ppermute | solution.py:451
  148.8 1.8 collective-permute-start.19
  150.6 9.6 %attend.3.stay.left = bf16[4,192,512]{2,1,0:T(8,128)(2,1)S(1)} custom-call(s32[15]{0:T(128)S(1)} %stack.63.control, s32[6]{0:T(128)S(1)} %get-tuple-element.86.hist_at, s32[6]{0:T(128)S(1)} %get-tuple-element.85.hist_steps, s32[6]{0:T(128)S(1)} %get-tuple-element.80.fresh_at, s32[6]{0:T(128)S(1)} %get-tuple-element.79.fresh_steps, ...), custom_call_target="tpu_custom_call" | custom-call | flops 16000000000 | bytes 1000 | tf_op jit(solution)/shard_map/attend/pallas_call | solution.py:221
  160.2 1.3 collective-permute-start.22
  161.6 1.1 broadcast_select_fusion.1.refs_0_
  162.7 3.7 %collective-permute-start.23 = (bf16[512,512]{1,0:T(8,128)(2,1)S(1)}, bf16[512,512]{1,0:T(8,128)(2,1)S(1)}, u32[]{:S(2)}, u32[]{:S(2)}) collective-permute-start(bf16[512,512]{1,0:T(8,128)(2,1)S(1)} %broadcast_select_fusion.1.refs_0_), channel_id=1, source_target_pairs={{0,16},{16,0},{1,17},{17,1},{2,18},{18,2},{3,19},{19,3},{4,20},{20... | collective-permute-start | bytes 1572872 | tf_op jit(solution)/shard_map/ppermute | solution.py:455
  166.4 3.5 %project.7 = (bf16[192,1024]{1,0:T(8,128)(2,1)S(1)}, bf16[192,1024]{1,0:T(8,128)(2,1)S(1)}) custom-call(s32[15]{0:T(128)S(1)} %stack.63.control, bf16[4,192,512]{2,1,0:T(8,128)(2,1)S(1)} %attend.2.left, bf16[4,192,512]{2,1,0:T(8,128)(2,1)S(1)} %attend.3.stay.left, bf16[512,512]{1,0:T(8,128)(2,1)} %collective-permute-done.refs_0_, ...), custom_call_target="tpu_custom_call" | custom-call | flops 6000000000 | bytes 1000 | tf_op jit(solution)/shard_map/project/pallas_call | solution.py:283
  169.8 0.5 collective-permute-start.24
  170.4 3.6 %project.8 = (bf16[192,1024]{1,0:T(8,128)(2,1)S(1)}, bf16[192,1024]{1,0:T(8,128)(2,1)S(1)}) custom-call(s32[15]{0:T(128)S(1)} %stack.63.control, bf16[4,192,512]{2,1,0:T(8,128)(2,1)S(1)} %attend.2.left, bf16[4,192,512]{2,1,0:T(8,128)(2,1)S(1)} %attend.3.stay.left, bf16[512,512]{1,0:T(8,128)(2,1)S(1)} %broadcast_select_fusion.3.refs_0_, ...), custom_call_target="tpu_custom_call" | custom-call | flops 6000000000 | bytes 1000 | tf_op jit(solution)/shard_map/project/pallas_call | solution.py:283
  174.1 3.6 %collective-permute-done.24.refs_6_ = bf16[192,1024]{1,0:T(8,128)(2,1)S(1)} collective-permute-done((bf16[192,1024]{1,0:T(8,128)(2,1)S(1)}, bf16[192,1024]{1,0:T(8,128)(2,1)S(1)}, u32[]{:S(2)}, u32[]{:S(2)}) %collective-permute-start.24) | collective-permute-done | bytes 393248 | tf_op jit(solution)/shard_map/ppermute | solution.py:460
  178.7 0.9 collective-permute-done.26.refs_3_
  179.6 0.7 collective-permute-done.25.refs_2_
  180.3 1.5 project.9
  181.9 10.2 %collective-permute-done.28.refs_1_ = bf16[512,512]{1,0:T(8,128)(2,1)S(1)} collective-permute-done((bf16[512,512]{1,0:T(8,128)(2,1)S(1)}, bf16[512,512]{1,0:T(8,128)(2,1)S(1)}, u32[]{:S(2)}, u32[]{:S(2)}) %collective-permute-start.28) | collective-permute-done | bytes 524320 | tf_op jit(solution)/shard_map/ppermute | solution.py:463
  193.0 1.5 project.10.refs_0_
  194.7 1.5 project.11
  196.2 1.5 collective-permute-start.32
  197.7 1.9 collective-permute-done.31.refs_8_
  199.6 3.9 %collective-permute-done.32.refs_9_ = bf16[192,512]{1,0:T(8,128)(2,1)S(1)} collective-permute-done((bf16[192,512]{1,0:T(8,128)(2,1)S(1)}, bf16[192,512]{1,0:T(8,128)(2,1)S(1)}, u32[]{:S(2)}, u32[]{:S(2)}) %collective-permute-start.32) | collective-permute-done | bytes 196640 | tf_op jit(solution)/shard_map/ppermute | solution.py:469
  203.6 2.0 join.1
  (77 shorter events, 6.0 us)
Async XLA Ops:
  1.3 17.0 %collective-permute-start = (bf16[512,512]{1,0:T(8,128)(2,1)S(1)}, bf16[512,512]{1,0:T(8,128)(2,1)}, u32[]{:S(2)}, u32[]{:S(2)}) collective-permute-start(bf16[512,512]{1,0:T(8,128)(2,1)S(1)} %get-tuple-element.84), channel_id=1, source_target_pairs={{0,4},{4,0},{8,12},{12,8},{1,5},{5,1},{9,13},{13,9},{2,6},{6,2},{1... | collective-permute-start | bytes 1572872 | tf_op jit(solution)/shard_map/ppermute | solution.py:399
  2.9 15.3 %collective-permute-start.1 = (bf16[512,512]{1,0:T(8,128)(2,1)S(1)}, bf16[512,512]{1,0:T(8,128)(2,1)S(1)}, u32[]{:S(2)}, u32[]{:S(2)}) collective-permute-start(bf16[512,512]{1,0:T(8,128)(2,1)S(1)} %get-tuple-element.84), channel_id=1, source_target_pairs={{4,8},{8,4},{5,9},{9,5},{6,10},{10,6},{7,11},{11,7},{20,24},{24,20... | collective-permute-start | bytes 1572872 | tf_op jit(solution)/shard_map/ppermute | solution.py:399
  18.2 14.4 %collective-permute-start.3 = (bf16[512,512]{1,0:T(8,128)(2,1)S(1)}, bf16[512,512]{1,0:T(8,128)(2,1)}, u32[]{:S(2)}, u32[]{:S(2)}) collective-permute-start(bf16[512,512]{1,0:T(8,128)(2,1)S(1)} %get-tuple-element.46), channel_id=1, source_target_pairs={{4,8},{8,4},{5,9},{9,5},{6,10},{10,6},{7,11},{11,7},{20,24},{24,20... | collective-permute-start | bytes 1572872 | tf_op jit(solution)/shard_map/ppermute | solution.py:407
  20.4 12.6 %collective-permute-start.2 = (bf16[512,512]{1,0:T(8,128)(2,1)S(1)}, bf16[512,512]{1,0:T(8,128)(2,1)S(1)}, u32[]{:S(2)}, u32[]{:S(2)}) collective-permute-start(bf16[512,512]{1,0:T(8,128)(2,1)S(1)} %get-tuple-element.46), channel_id=1, source_target_pairs={{0,4},{4,0},{8,12},{12,8},{1,5},{5,1},{9,13},{13,9},{2,6},{6,2},{1... | collective-permute-start | bytes 1572872 | tf_op jit(solution)/shard_map/ppermute | solution.py:406
  26.1 86.4 %copy-start.9 = (s32[1,384]{1,0:T(1,128)S(1)}, s32[1,384]{1,0:T(1,128)}, u32[]{:S(2)}) copy-start(s32[1,384]{1,0:T(1,128)} %param.13) | copy-start | bytes 4612
  26.1 86.8 %copy-start.10 = (s32[1,128]{1,0:T(1,128)S(1)}, s32[1,128]{1,0:T(1,128)}, u32[]{:S(2)}) copy-start(s32[1,128]{1,0:T(1,128)} %param.14) | copy-start | bytes 1540
  26.1 87.0 %copy-start.11 = (s32[1,128]{1,0:T(1,128)S(1)}, s32[1,128]{1,0:T(1,128)}, u32[]{:S(2)}) copy-start(s32[1,128]{1,0:T(1,128)} %param.15) | copy-start | bytes 1540
  33.0 77.4 %copy-start.3 = (bf16[512,512]{1,0:T(8,128)(2,1)}, bf16[512,512]{1,0:T(8,128)(2,1)S(1)}, u32[]{:S(2)}) copy-start(bf16[512,512]{1,0:T(8,128)(2,1)S(1)} %collective-permute-done.2.refs_4_) | copy-start | bytes 1572868
  33.0 95.0 %all-to-all-start.1 = ((bf16[4,64,2,16,256]{4,3,2,1,0:T(8,128)(2,1)}), bf16[4,64,2,16,256]{4,3,2,1,0:T(8,128)(2,1)}, u32[]{:S(2)}, u32[]{:S(2)}) async-start(bf16[4,64,2,16,256]{4,3,2,1,0:T(8,128)(2,1)} %pick.1), calls=%async_computation.1 | async-start | bytes 8388608 | tf_op jit(solution)/shard_map/all_to_all | solution.py:413
  39.0 89.1 %copy-start.2 = (s32[128]{0:T(128)S(1)}, s32[128]{0:T(128)}, u32[]{:S(2)}) copy-start(s32[128]{0:T(128)} %get-tuple-element.41.position) | copy-start | bytes 1540
  39.0 59.1 %collective-permute-start.10 = (bf16[512,512]{1,0:T(8,128)(2,1)S(1)}, bf16[512,512]{1,0:T(8,128)(2,1)S(1)}, u32[]{:S(2)}, u32[]{:S(2)}) collective-permute-start(bf16[512,512]{1,0:T(8,128)(2,1)S(1)} %collective-permute-done.1), channel_id=1, source_target_pairs={{4,0},{8,12},{5,1},{9,13},{6,2},{10,14},{7,3},{11,15},{20,16},{24,... | collective-permute-start | bytes 1572872 | tf_op jit(solution)/shard_map/ppermute | solution.py:440
  42.5 65.2 %collective-permute-start.14 = (bf16[512,512]{1,0:T(8,128)(2,1)}, bf16[512,512]{1,0:T(8,128)(2,1)}, u32[]{:S(2)}, u32[]{:S(2)}) collective-permute-start(bf16[512,512]{1,0:T(8,128)(2,1)} %collective-permute-done.3), channel_id=1, source_target_pairs={{4,0},{8,12},{5,1},{9,13},{6,2},{10,14},{7,3},{11,15},{20,16},{24,... | collective-permute-start | bytes 1572872 | tf_op jit(solution)/shard_map/ppermute | solution.py:440
  44.6 65.8 %collective-permute-start.4 = (bf16[512,512]{1,0:T(8,128)(2,1)}, bf16[512,512]{1,0:T(8,128)(2,1)S(1)}, u32[]{:S(2)}, u32[]{:S(2)}) collective-permute-start(bf16[512,512]{1,0:T(8,128)(2,1)} %collective-permute-done.refs_0_), channel_id=1, source_target_pairs={{0,16},{16,0},{1,17},{17,1},{2,18},{18,2},{3,19},{19,3},{4,20},{20... | collective-permute-start | bytes 1572872 | tf_op jit(solution)/shard_map/ppermute | solution.py:439
  46.1 64.9 %collective-permute-start.7 = (bf16[512,512]{1,0:T(8,128)(2,1)S(1)}, bf16[512,512]{1,0:T(8,128)(2,1)S(1)}, u32[]{:S(2)}, u32[]{:S(2)}) collective-permute-start(bf16[512,512]{1,0:T(8,128)(2,1)S(1)} %collective-permute-done.2.refs_4_), channel_id=1, source_target_pairs={{0,16},{16,0},{1,17},{17,1},{2,18},{18,2},{3,19},{19,3},{4,20},{20... | collective-permute-start | bytes 1572872 | tf_op jit(solution)/shard_map/ppermute | solution.py:439
  98.1 37.9 %copy-start = (bf16[1,384,2048]{2,1,0:T(8,128)(2,1)S(1)}, bf16[1,384,2048]{2,1,0:T(8,128)(2,1)}, u32[]{:S(2)}) copy-start(bf16[1,384,2048]{2,1,0:T(8,128)(2,1)} %param.9) | copy-start | bytes 4718596
  98.1 15.1 %collective-permute-start.11 = (bf16[512,512]{1,0:T(8,128)(2,1)S(1)}, bf16[512,512]{1,0:T(8,128)(2,1)}, u32[]{:S(2)}, u32[]{:S(2)}) collective-permute-start(bf16[512,512]{1,0:T(8,128)(2,1)S(1)} %broadcast_select_fusion.3.refs_0_), channel_id=1, source_target_pairs={{0,16},{16,0},{1,17},{17,1},{2,18},{18,2},{3,19},{19,3},{4,20},{20... | collective-permute-start | bytes 1572872 | tf_op jit(solution)/shard_map/ppermute | solution.py:441
  108.8 9.9 %collective-permute-start.15 = (bf16[512,512]{1,0:T(8,128)(2,1)S(1)}, bf16[512,512]{1,0:T(8,128)(2,1)}, u32[]{:S(2)}, u32[]{:S(2)}) collective-permute-start(bf16[512,512]{1,0:T(8,128)(2,1)S(1)} %broadcast_select_fusion.2.refs_4_), channel_id=1, source_target_pairs={{0,16},{16,0},{1,17},{17,1},{2,18},{18,2},{3,19},{19,3},{4,20},{20... | collective-permute-start | bytes 1572872 | tf_op jit(solution)/shard_map/ppermute | solution.py:441
  110.4 8.4 %collective-permute-start.5 = (bf16[512,512]{1,0:T(8,128)(2,1)}, bf16[512,512]{1,0:T(8,128)(2,1)}, u32[]{:S(2)}, u32[]{:S(2)}) collective-permute-start(bf16[512,512]{1,0:T(8,128)(2,1)} %collective-permute-done.refs_0_), channel_id=1, source_target_pairs={{0,1},{1,0},{2,3},{3,2},{4,5},{5,4},{6,7},{7,6},{8,9},{9,8},{10,11... | collective-permute-start | bytes 1572872 | tf_op jit(solution)/shard_map/ppermute | solution.py:437
  110.4 0.8 copy-start.5
  110.4 8.9 %collective-permute-start.8 = (bf16[512,512]{1,0:T(8,128)(2,1)S(1)}, bf16[512,512]{1,0:T(8,128)(2,1)}, u32[]{:S(2)}, u32[]{:S(2)}) collective-permute-start(bf16[512,512]{1,0:T(8,128)(2,1)S(1)} %collective-permute-done.2.refs_4_), channel_id=1, source_target_pairs={{0,1},{1,0},{2,3},{3,2},{4,5},{5,4},{6,7},{7,6},{8,9},{9,8},{10,11... | collective-permute-start | bytes 1572872 | tf_op jit(solution)/shard_map/ppermute | solution.py:437
  111.2 0.8 copy-start.7
  112.0 7.3 %collective-permute-start.12 = (bf16[512,512]{1,0:T(8,128)(2,1)S(1)}, bf16[512,512]{1,0:T(8,128)(2,1)}, u32[]{:S(2)}, u32[]{:S(2)}) collective-permute-start(bf16[512,512]{1,0:T(8,128)(2,1)S(1)} %broadcast_select_fusion.3.refs_0_), channel_id=1, source_target_pairs={{0,1},{1,0},{2,3},{3,2},{4,5},{5,4},{6,7},{7,6},{8,9},{9,8},{10,11... | collective-permute-start | bytes 1572872 | tf_op jit(solution)/shard_map/ppermute | solution.py:437
  113.2 6.6 %collective-permute-start.6 = (bf16[512,512]{1,0:T(8,128)(2,1)}, bf16[512,512]{1,0:T(8,128)(2,1)}, u32[]{:S(2)}, u32[]{:S(2)}) collective-permute-start(bf16[512,512]{1,0:T(8,128)(2,1)} %copy-done.5), channel_id=1, source_target_pairs={{0,1},{1,0},{2,3},{3,2},{4,5},{5,4},{6,7},{7,6},{8,9},{9,8},{10,11... | collective-permute-start | bytes 1572872 | tf_op jit(solution)/shard_map/ppermute | solution.py:437
  118.7 5.3 %collective-permute-start.16 = (bf16[512,512]{1,0:T(8,128)(2,1)S(1)}, bf16[512,512]{1,0:T(8,128)(2,1)}, u32[]{:S(2)}, u32[]{:S(2)}) collective-permute-start(bf16[512,512]{1,0:T(8,128)(2,1)S(1)} %broadcast_select_fusion.2.refs_4_), channel_id=1, source_target_pairs={{0,1},{1,0},{2,3},{3,2},{4,5},{5,4},{6,7},{7,6},{8,9},{9,8},{10,11... | collective-permute-start | bytes 1572872 | tf_op jit(solution)/shard_map/ppermute | solution.py:437
  118.7 5.3 %collective-permute-start.9 = (bf16[512,512]{1,0:T(8,128)(2,1)}, bf16[512,512]{1,0:T(8,128)(2,1)}, u32[]{:S(2)}, u32[]{:S(2)}) collective-permute-start(bf16[512,512]{1,0:T(8,128)(2,1)} %copy-done.7), channel_id=1, source_target_pairs={{0,1},{1,0},{2,3},{3,2},{4,5},{5,4},{6,7},{7,6},{8,9},{9,8},{10,11... | collective-permute-start | bytes 1572872 | tf_op jit(solution)/shard_map/ppermute | solution.py:437
  119.2 4.8 %collective-permute-start.13 = (bf16[512,512]{1,0:T(8,128)(2,1)}, bf16[512,512]{1,0:T(8,128)(2,1)}, u32[]{:S(2)}, u32[]{:S(2)}) collective-permute-start(bf16[512,512]{1,0:T(8,128)(2,1)} %collective-permute-done.11.refs_1_), channel_id=1, source_target_pairs={{0,1},{1,0},{2,3},{3,2},{4,5},{5,4},{6,7},{7,6},{8,9},{9,8},{10,11... | collective-permute-start | bytes 1572872 | tf_op jit(solution)/shard_map/ppermute | solution.py:437
  119.3 4.8 %collective-permute-start.17 = (bf16[512,512]{1,0:T(8,128)(2,1)}, bf16[512,512]{1,0:T(8,128)(2,1)}, u32[]{:S(2)}, u32[]{:S(2)}) collective-permute-start(bf16[512,512]{1,0:T(8,128)(2,1)} %collective-permute-done.15.refs_5_), channel_id=1, source_target_pairs={{0,1},{1,0},{2,3},{3,2},{4,5},{5,4},{6,7},{7,6},{8,9},{9,8},{10,11... | collective-permute-start | bytes 1572872 | tf_op jit(solution)/shard_map/ppermute | solution.py:437
  119.9 28.9 %collective-permute-start.18 = (bf16[512,512]{1,0:T(8,128)(2,1)}, bf16[512,512]{1,0:T(8,128)(2,1)}, u32[]{:S(2)}, u32[]{:S(2)}) collective-permute-start(bf16[512,512]{1,0:T(8,128)(2,1)} %collective-permute-done.refs_0_), channel_id=1, source_target_pairs={{4,8},{8,4},{5,9},{9,5},{6,10},{10,6},{7,11},{11,7},{20,24},{24,20... | collective-permute-start | bytes 1572872 | tf_op jit(solution)/shard_map/ppermute | solution.py:444
  128.0 3.2 %copy-start.4 = (bf16[512,512]{1,0:T(8,128)(2,1)S(1)}, bf16[512,512]{1,0:T(8,128)(2,1)}, u32[]{:S(2)}) copy-start(bf16[512,512]{1,0:T(8,128)(2,1)} %copy-done.3) | copy-start | bytes 1572868
  131.2 13.7 %copy-start.1 = (bf16[2048,1024]{1,0:T(8,128)(2,1)S(1)}, bf16[2048,1024]{1,0:T(8,128)(2,1)}, u32[]{:S(2)}) copy-start(bf16[2048,1024]{1,0:T(8,128)(2,1)} %refs_0_.3) | copy-start | bytes 12582916
  131.3 28.9 %collective-permute-start.20 = (bf16[512,512]{1,0:T(8,128)(2,1)S(1)}, bf16[512,512]{1,0:T(8,128)(2,1)S(1)}, u32[]{:S(2)}, u32[]{:S(2)}) collective-permute-start(bf16[512,512]{1,0:T(8,128)(2,1)S(1)} %copy-done.4), channel_id=1, source_target_pairs={{4,8},{8,4},{5,9},{9,5},{6,10},{10,6},{7,11},{11,7},{20,24},{24,20... | collective-permute-start | bytes 1572872 | tf_op jit(solution)/shard_map/ppermute | solution.py:447
  146.5 19.8 %copy-start.6 = (bf16[512,512]{1,0:T(8,128)(2,1)S(1)}, bf16[512,512]{1,0:T(8,128)(2,1)}, u32[]{:S(2)}) copy-start(bf16[512,512]{1,0:T(8,128)(2,1)} %copy-done.5) | copy-start | bytes 1572868
  146.6 19.8 %copy-start.8 = (bf16[512,512]{1,0:T(8,128)(2,1)S(1)}, bf16[512,512]{1,0:T(8,128)(2,1)}, u32[]{:S(2)}) copy-start(bf16[512,512]{1,0:T(8,128)(2,1)} %copy-done.7) | copy-start | bytes 1572868
  146.6 19.8 %collective-permute-start.21 = (bf16[192,1024]{1,0:T(8,128)(2,1)S(1)}, bf16[192,1024]{1,0:T(8,128)(2,1)S(1)}, u32[]{:S(2)}, u32[]{:S(2)}) collective-permute-start(bf16[192,1024]{1,0:T(8,128)(2,1)S(1)} %project.6), channel_id=1, source_target_pairs={{0,2},{2,0},{1,3},{3,1},{4,6},{6,4},{5,7},{7,5},{8,10},{10,8},{9,1... | collective-permute-start | bytes 1179656 | tf_op jit(solution)/shard_map/ppermute | solution.py:451
  148.8 12.7 %collective-permute-start.19 = (bf16[512,512]{1,0:T(8,128)(2,1)}, bf16[512,512]{1,0:T(8,128)(2,1)S(1)}, u32[]{:S(2)}, u32[]{:S(2)}) collective-permute-start(bf16[512,512]{1,0:T(8,128)(2,1)} %collective-permute-done.18), channel_id=1, source_target_pairs={{4,0},{8,12},{5,1},{9,13},{6,2},{10,14},{7,3},{11,15},{20,16},{24,... | collective-permute-start | bytes 1572872 | tf_op jit(solution)/shard_map/ppermute | solution.py:449
  160.2 10.1 %collective-permute-start.22 = (bf16[512,512]{1,0:T(8,128)(2,1)S(1)}, bf16[512,512]{1,0:T(8,128)(2,1)S(1)}, u32[]{:S(2)}, u32[]{:S(2)}) collective-permute-start(bf16[512,512]{1,0:T(8,128)(2,1)S(1)} %collective-permute-done.20), channel_id=1, source_target_pairs={{4,0},{8,12},{5,1},{9,13},{6,2},{10,14},{7,3},{11,15},{20,16},{24,... | collective-permute-start | bytes 1572872 | tf_op jit(solution)/shard_map/ppermute | solution.py:453
  162.7 15.0 %collective-permute-start.23 = (bf16[512,512]{1,0:T(8,128)(2,1)S(1)}, bf16[512,512]{1,0:T(8,128)(2,1)S(1)}, u32[]{:S(2)}, u32[]{:S(2)}) collective-permute-start(bf16[512,512]{1,0:T(8,128)(2,1)S(1)} %broadcast_select_fusion.1.refs_0_), channel_id=1, source_target_pairs={{0,16},{16,0},{1,17},{17,1},{2,18},{18,2},{3,19},{19,3},{4,20},{20... | collective-permute-start | bytes 1572872 | tf_op jit(solution)/shard_map/ppermute | solution.py:455
  169.8 7.8 %collective-permute-start.24 = (bf16[192,1024]{1,0:T(8,128)(2,1)S(1)}, bf16[192,1024]{1,0:T(8,128)(2,1)S(1)}, u32[]{:S(2)}, u32[]{:S(2)}) collective-permute-start(bf16[192,1024]{1,0:T(8,128)(2,1)S(1)} %get-tuple-element.61), channel_id=1, source_target_pairs={{0,2},{2,0},{1,3},{3,1},{4,6},{6,4},{5,7},{7,5},{8,10},{10,8},{9,1... | collective-permute-start | bytes 1179656 | tf_op jit(solution)/shard_map/ppermute | solution.py:460
  177.7 1.9 collective-permute-start.26
  177.7 2.7 %collective-permute-start.25 = (bf16[512,512]{1,0:T(8,128)(2,1)S(1)}, bf16[512,512]{1,0:T(8,128)(2,1)S(1)}, u32[]{:S(2)}, u32[]{:S(2)}) collective-permute-start(bf16[512,512]{1,0:T(8,128)(2,1)S(1)} %broadcast_select_fusion.1.refs_0_), channel_id=1, source_target_pairs={{0,1},{1,0},{2,3},{3,2},{4,5},{5,4},{6,7},{7,6},{8,9},{9,8},{10,11... | collective-permute-start | bytes 1572872 | tf_op jit(solution)/shard_map/ppermute | solution.py:437
  178.2 13.8 %collective-permute-start.28 = (bf16[512,512]{1,0:T(8,128)(2,1)S(1)}, bf16[512,512]{1,0:T(8,128)(2,1)S(1)}, u32[]{:S(2)}, u32[]{:S(2)}) collective-permute-start(bf16[512,512]{1,0:T(8,128)(2,1)S(1)} %broadcast_select_fusion.refs_0_), channel_id=1, source_target_pairs={{0,16},{16,0},{1,17},{17,1},{2,18},{18,2},{3,19},{19,3},{4,20},{20... | collective-permute-start | bytes 1572872 | tf_op jit(solution)/shard_map/ppermute | solution.py:463
  178.2 14.8 %collective-permute-start.27 = (bf16[192,1024]{1,0:T(8,128)(2,1)S(1)}, bf16[192,1024]{1,0:T(8,128)(2,1)S(1)}, u32[]{:S(2)}, u32[]{:S(2)}) collective-permute-start(bf16[192,1024]{1,0:T(8,128)(2,1)S(1)} %get-tuple-element.66), channel_id=1, source_target_pairs={{0,2},{2,0},{1,3},{3,1},{4,6},{6,4},{5,7},{7,5},{8,10},{10,8},{9,1... | collective-permute-start | bytes 1179656 | tf_op jit(solution)/shard_map/ppermute | solution.py:460
  192.0 2.5 %collective-permute-start.30 = (bf16[512,512]{1,0:T(8,128)(2,1)S(1)}, bf16[512,512]{1,0:T(8,128)(2,1)S(1)}, u32[]{:S(2)}, u32[]{:S(2)}) collective-permute-start(bf16[512,512]{1,0:T(8,128)(2,1)S(1)} %collective-permute-done.28.refs_1_), channel_id=1, source_target_pairs={{0,1},{1,0},{2,3},{3,2},{4,5},{5,4},{6,7},{7,6},{8,9},{9,8},{10,11... | collective-permute-start | bytes 1572872 | tf_op jit(solution)/shard_map/ppermute | solution.py:437
  192.0 2.7 %collective-permute-start.29 = (bf16[512,512]{1,0:T(8,128)(2,1)S(1)}, bf16[512,512]{1,0:T(8,128)(2,1)S(1)}, u32[]{:S(2)}, u32[]{:S(2)}) collective-permute-start(bf16[512,512]{1,0:T(8,128)(2,1)S(1)} %broadcast_select_fusion.refs_0_), channel_id=1, source_target_pairs={{0,1},{1,0},{2,3},{3,2},{4,5},{5,4},{6,7},{7,6},{8,9},{9,8},{10,11... | collective-permute-start | bytes 1572872 | tf_op jit(solution)/shard_map/ppermute | solution.py:437
  192.5 7.1 %collective-permute-start.31 = (bf16[192,512]{1,0:T(8,128)(2,1)S(1)}, bf16[192,512]{1,0:T(8,128)(2,1)S(1)}, u32[]{:S(2)}, u32[]{:S(2)}) collective-permute-start(bf16[192,512]{1,0:T(8,128)(2,1)S(1)} %get-tuple-element.69), channel_id=1, source_target_pairs={{0,2},{2,0},{1,3},{3,1},{4,6},{6,4},{5,7},{7,5},{8,10},{10,8},{9,1... | collective-permute-start | bytes 589832 | tf_op jit(solution)/shard_map/ppermute | solution.py:469
  196.2 7.4 %collective-permute-start.32 = (bf16[192,512]{1,0:T(8,128)(2,1)S(1)}, bf16[192,512]{1,0:T(8,128)(2,1)S(1)}, u32[]{:S(2)}, u32[]{:S(2)}) collective-permute-start(bf16[192,512]{1,0:T(8,128)(2,1)S(1)} %get-tuple-element.76), channel_id=1, source_target_pairs={{0,2},{2,0},{1,3},{3,1},{4,6},{6,4},{5,7},{7,5},{8,10},{10,8},{9,1... | collective-permute-start | bytes 589832 | tf_op jit(solution)/shard_map/ppermute | solution.py:469

commit v13 on v9

--- a/solution.py
+++ b/solution.py
@@ -309,26 +309,37 @@
     )(control, *operands)
 
 
-def pick_kernel(asked, pool, out, sem):
+def pick_kernel(asked, pool, out, held, rows, sem):
     owners, bucket = asked.shape
+    whole = pltpu.make_async_copy(pool, held, sem.at[owners])
+    whole.start()
+    whole.wait()
     for owner in range(owners):
 
-        def start(n, carry):
-            pltpu.make_async_copy(pool.at[asked[owner, n]], out.at[owner, n], sem).start()
+        def copy(n, carry):
+            rows[owner, n] = held[asked[owner, n]]
             return carry
 
-        lax.fori_loop(0, bucket, start, 0, unroll=8)
-    pltpu.make_async_copy(out, out, sem).wait()
+        lax.fori_loop(0, bucket, copy, 0, unroll=8)
+        pltpu.make_async_copy(rows.at[owner], out.at[owner], sem.at[owner]).start()
+    for owner in range(owners):
+        pltpu.make_async_copy(rows.at[owner], out.at[owner], sem.at[owner]).wait()
 
 
 def pick(pool, asked):
     hbm = pl.BlockSpec(memory_space=pltpu.HBM)
+    out = asked.shape + pool.shape[1:]
     return pl.pallas_call(
         pick_kernel,
-        out_shape=jax.ShapeDtypeStruct(asked.shape + pool.shape[1:], jnp.bfloat16),
+        out_shape=jax.ShapeDtypeStruct(out, jnp.bfloat16),
         in_specs=[pl.BlockSpec(memory_space=pltpu.SMEM), hbm],
         out_specs=hbm,
-        scratch_shapes=[pltpu.SemaphoreType.DMA],
+        scratch_shapes=[
+            pltpu.VMEM(pool.shape, jnp.bfloat16),
+            pltpu.VMEM(out, jnp.bfloat16),
+            pltpu.SemaphoreType.DMA((asked.shape[0] + 1,)),
+        ],
+        compiler_params=pltpu.CompilerParams(vmem_limit_bytes=56 * MIB),
         cost_estimate=cost(),
         name="pick",
     )(asked, pool)
@@ -371,8 +382,8 @@
 
     if owner_count == 4:
         middle = (seq == 1) | (seq == 2)
-        cut, early = columns // 2, columns // LANES * 5 // 8 * LANES
-        parts = [quarter[:, :early], quarter[:, early:]]
+        cut = columns // 2
+        parts = [quarter[:, :cut], quarter[:, cut:]]
         pair = functools.partial(lax.ppermute, axis_name="seq", perm=[(0, 1), (1, 0), (2, 3), (3, 2)])
         cross = functools.partial(lax.ppermute, axis_name="seq", perm=[(1, 2), (2, 1)])
         forward = functools.partial(lax.ppermute, axis_name="seq", perm=[(1, 0), (2, 3)])
@@ -421,8 +432,7 @@
     next_across = [swap_group(part) for part in next_shard]
     near_all = four(near[0], near_across[0]) + four(near[1], near_across[1])
     next_all = four(next_shard[0], next_across[0]) + four(next_shard[1], next_across[1])
-    far = [near[0][:, :cut], jnp.concatenate([near[0][:, cut:], near[1]], axis=1)]
-    far = [cross(after(part, *next_across)) for part in far]
+    far = [cross(after(part, *next_across)) for part in near]
 
     keys, values = place(position, after(pages, *near_all, *next_all), fresh)
     left = attend(1, control, tables, queries[0], keys, values, slots)

time: 332 us -> 203 us (0.61)
  Pallas kernels: 179 us -> 54.8 us
  blocking collectives: 0 us -> 10.9 us
  waiting for transfers between devices: 88 us -> 79 us
    pallas_call x1, Pallas kernels: 129 us -> 5.04 us  [pick(): pl.pallas_call(pick_kernel, out_shape=jax.ShapeDtypeStruct(out, jnp.bfloa...]
    all_to_all x0 -> x1, blocking collectives: none -> 10.9 us  [shards(): lax.all_to_all(wanted, 'seq', split_axis=0, concat_axis=0, tiled=True)]
    ppermute x2, waiting for transfers between devices: 17.1 us -> 7.72 us  [shards(): next_across = [swap_group(part) for part in next_shard]]
    all_to_all x1 -> x0, waiting for transfers between devices: 7.8 us -> none  [shards(): lax.all_to_all(wanted, 'seq', split_axis=0, concat_axis=0, tiled=True)]
    ppermute x1, waiting for transfers between devices: 0.01 us -> 6.99 us  [shards(): inner.append(cross(later))]
    all_to_all x1 -> x0, starting transfers between devices: 4.76 us -> none  [shards(): lax.all_to_all(wanted, 'seq', split_axis=0, concat_axis=0, tiled=True)]
  transfers between devices with their start and end apart: 35 -> 34, of which waited for: 7 -> 8; matrix products, arithmetic and copies ran while one was open for 3% -> 2% of each run, Pallas kernels for 54% -> 26%
where the time goes in v13:
time: 203 us; the launch traced here: 202 us
  waiting for transfers between devices  79 us (39%)
  Pallas kernels  54.8 us (27%)
  starting transfers between devices  49.9 us (25%)
  blocking collectives  10.9 us (5%)
  local copies, waits for them, and re-layouts  3.66 us (2%)
  other arithmetic  2.92 us (1%)
    ppermute x2, waiting for transfers between devices, shards(): next_shard = [jnp.where(middle, part, forward(part)) for part in inner]  58.7 us
    pallas_call x10, Pallas kernels, project(): pl.pallas_call(kernel, out_shape=out_shape, grid_spec=pltpu.PrefetchScala...  24 us
    pallas_call x2, Pallas kernels, attend(): pl.pallas_call(functools.partial(attend_kernel, fresh_base, side), out_sh...  19.9 us
    all_to_all x1, blocking collectives, shards(): lax.all_to_all(wanted, 'seq', split_axis=0, concat_axis=0, tiled=True)  10.9 us
    ppermute x2, waiting for transfers between devices, shards(): next_across = [swap_group(part) for part in next_shard]  7.72 us
    ppermute x1, waiting for transfers between devices, shards(): inner.append(cross(later))  6.99 us
    ppermute x2, starting transfers between devices, shards(): next_shard = [jnp.where(middle, part, forward(part)) for part in inner]  6.27 us
    all_to_all x1, starting transfers between devices, shards(): lax.all_to_all(found, 'seq', split_axis=0, concat_axis=0, tiled=True)  5.94 us
  transfers between devices with their start and end apart: 34, of which 8 were waited for; matrix products, arithmetic and copies ran while one was open for 2% of the time, Pallas kernels for 26%

profile of v13, /device:TPU:16, one launch (start us, length us, event | category | flops | bytes accessed | tf_op | source)
XLA Modules:
  0.0 201.8 jit_solution(2690745986800809908)
XLA Ops:
  0.0 1.3 fusion.5
  1.3 1.6 collective-permute-start
  2.9 1.9 collective-permute-start.1
  4.8 2.6 %rank.1 = (s32[128]{0:T(128)}, s32[4,64]{1,0:T(4,128)}) custom-call(s32[1,128]{1,0:T(1,128)} %owner.1, s32[1,128]{1,0:T(1,128)} %page.1), custom_call_target="tpu_custom_call" | custom-call | flops 3000000000 | bytes 1000 | tf_op jit(solution)/shard_map/rank/pallas_call | solution.py:49
  7.5 10.9 %all_to_all.17 = s32[4,1,64]{2,1,0:T(1,128)} all-to-all(s32[4,1,64]{2,1,0:T(1,128)} %bitcast.39), channel_id=1, replica_groups=mesh['group'=2,'seq'=4,'tp'=2,'role'=2] {'seq'}, dimensions={0} | all-to-all | bytes 2048 | tf_op jit(solution)/shard_map/all_to_all | solution.py:393
  18.4 2.0 %collective-permute-start.3 = (bf16[512,512]{1,0:T(8,128)(2,1)S(1)}, bf16[512,512]{1,0:T(8,128)(2,1)S(1)}, u32[]{:S(2)}, u32[]{:S(2)}) collective-permute-start(bf16[512,512]{1,0:T(8,128)(2,1)S(1)} %get-tuple-element.38), channel_id=1, source_target_pairs={{4,8},{8,4},{5,9},{9,5},{6,10},{10,6},{7,11},{11,7},{20,24},{24,20... | collective-permute-start | bytes 1572872 | tf_op jit(solution)/shard_map/ppermute | solution.py:398
  20.5 5.0 %pick.1 = bf16[4,64,2,16,256]{4,3,2,1,0:T(8,128)(2,1)} custom-call(s32[4,64]{1,0:T(4,128)} %bitcast.38, bf16[256,2,16,256]{3,2,1,0:T(8,128)(2,1)} %bitcast.41), custom_call_target="tpu_custom_call" | custom-call | flops 3000000000 | bytes 1000 | tf_op jit(solution)/shard_map/pick/pallas_call | solution.py:332
  25.6 7.0 %collective-permute-done.3 = bf16[512,512]{1,0:T(8,128)(2,1)S(1)} collective-permute-done((bf16[512,512]{1,0:T(8,128)(2,1)S(1)}, bf16[512,512]{1,0:T(8,128)(2,1)S(1)}, u32[]{:S(2)}, u32[]{:S(2)}) %collective-permute-start.3) | collective-permute-done | bytes 524320 | tf_op jit(solution)/shard_map/ppermute | solution.py:398
  33.0 5.9 %all-to-all-start.1 = ((bf16[4,64,2,16,256]{4,3,2,1,0:T(8,128)(2,1)}), bf16[4,64,2,16,256]{4,3,2,1,0:T(8,128)(2,1)}, u32[]{:S(2)}, u32[]{:S(2)}) async-start(bf16[4,64,2,16,256]{4,3,2,1,0:T(8,128)(2,1)} %pick.1), calls=%async_computation.1 | async-start | bytes 8388608 | tf_op jit(solution)/shard_map/all_to_all | solution.py:404
  38.9 4.2 %collective-permute-start.10 = (bf16[512,512]{1,0:T(8,128)(2,1)S(1)}, bf16[512,512]{1,0:T(8,128)(2,1)}, u32[]{:S(2)}, u32[]{:S(2)}) collective-permute-start(bf16[512,512]{1,0:T(8,128)(2,1)S(1)} %collective-permute-done.1), channel_id=1, source_target_pairs={{4,0},{8,12},{5,1},{9,13},{6,2},{10,14},{7,3},{11,15},{20,16},{24,... | collective-permute-start | bytes 1572872 | tf_op jit(solution)/shard_map/ppermute | solution.py:431
  43.1 2.1 %collective-permute-start.14 = (bf16[512,512]{1,0:T(8,128)(2,1)S(1)}, bf16[512,512]{1,0:T(8,128)(2,1)}, u32[]{:S(2)}, u32[]{:S(2)}) collective-permute-start(bf16[512,512]{1,0:T(8,128)(2,1)S(1)} %collective-permute-done.3), channel_id=1, source_target_pairs={{4,0},{8,12},{5,1},{9,13},{6,2},{10,14},{7,3},{11,15},{20,16},{24,... | collective-permute-start | bytes 1572872 | tf_op jit(solution)/shard_map/ppermute | solution.py:431
  45.2 1.5 collective-permute-start.4
  47.2 50.9 %collective-permute-done.10 = bf16[512,512]{1,0:T(8,128)(2,1)} collective-permute-done((bf16[512,512]{1,0:T(8,128)(2,1)S(1)}, bf16[512,512]{1,0:T(8,128)(2,1)}, u32[]{:S(2)}, u32[]{:S(2)}) %collective-permute-start.10) | collective-permute-done | bytes 524320 | tf_op jit(solution)/shard_map/ppermute | solution.py:431
  98.2 1.6 collective-permute-start.11
  99.8 7.8 %collective-permute-done.14 = bf16[512,512]{1,0:T(8,128)(2,1)} collective-permute-done((bf16[512,512]{1,0:T(8,128)(2,1)S(1)}, bf16[512,512]{1,0:T(8,128)(2,1)}, u32[]{:S(2)}, u32[]{:S(2)}) %collective-permute-start.14) | collective-permute-done | bytes 524320 | tf_op jit(solution)/shard_map/ppermute | solution.py:431
  107.6 1.6 collective-permute-start.15
  109.2 0.5 collective-permute-start.8
  111.1 7.7 %collective-permute-done.15.refs_5_ = bf16[512,512]{1,0:T(8,128)(2,1)} collective-permute-done((bf16[512,512]{1,0:T(8,128)(2,1)S(1)}, bf16[512,512]{1,0:T(8,128)(2,1)}, u32[]{:S(2)}, u32[]{:S(2)}) %collective-permute-start.15) | collective-permute-done | bytes 524320 | tf_op jit(solution)/shard_map/ppermute | solution.py:432
  119.4 0.8 copy-done.3
  120.7 1.9 collective-permute-start.18
  122.8 1.1 copy.22
  124.3 3.9 %collective-permute-start.20 = (bf16[512,512]{1,0:T(8,128)(2,1)S(1)}, bf16[512,512]{1,0:T(8,128)(2,1)}, u32[]{:S(2)}, u32[]{:S(2)}) collective-permute-start(bf16[512,512]{1,0:T(8,128)(2,1)S(1)} %collective-permute-done.2.refs_4_), channel_id=1, source_target_pairs={{4,8},{8,4},{5,9},{9,5},{6,10},{10,6},{7,11},{11,7},{20,24},{24,20... | collective-permute-start | bytes 1572872 | tf_op jit(solution)/shard_map/ppermute | solution.py:435
  128.2 3.3 %place.1 = (bf16[2,3072,128]{2,1,0:T(8,128)(2,1)S(1)}, bf16[2,3072,256]{2,1,0:T(8,128)(2,1)S(1)}) custom-call(s32[128]{0:T(128)S(1)} %copy-done.2, bf16[256,2,16,256]{3,2,1,0:T(8,128)(2,1)} %bitcast.21.pages, bf16[384,512]{1,0:T(8,128)(2,1)S(1)} %bitcast.31), custom_call_target="tpu_custom_call" | custom-call | flops 1000000000 | bytes 1000 | tf_op jit(solution)/shard_map/place/pallas_call | solution.py:95
  131.5 11.0 %attend.2.left = bf16[4,192,512]{2,1,0:T(8,128)(2,1)S(1)} custom-call(s32[15]{0:T(128)S(1)} %stack.63.control, s32[6]{0:T(128)S(1)} %get-tuple-element.70.hist_at, s32[6]{0:T(128)S(1)} %get-tuple-element.69.hist_steps, s32[6]{0:T(128)S(1)} %get-tuple-element.64.fresh_at, s32[6]{0:T(128)S(1)} %get-tuple-element.63.fresh_steps, ...), custom_call_target="tpu_custom_call" | custom-call | flops 1000000000 | bytes 1000 | tf_op jit(solution)/shard_map/attend/pallas_call | solution.py:221
  142.5 1.5 project.5
  144.1 3.3 %collective-permute-start.19 = (bf16[512,512]{1,0:T(8,128)(2,1)}, bf16[512,512]{1,0:T(8,128)(2,1)S(1)}, u32[]{:S(2)}, u32[]{:S(2)}) collective-permute-start(bf16[512,512]{1,0:T(8,128)(2,1)} %collective-permute-done.18), channel_id=1, source_target_pairs={{4,0},{8,12},{5,1},{9,13},{6,2},{10,14},{7,3},{11,15},{20,16},{24,... | collective-permute-start | bytes 1572872 | tf_op jit(solution)/shard_map/ppermute | solution.py:439
  147.4 3.2 %project.6 = bf16[192,1024]{1,0:T(8,128)(2,1)S(1)} custom-call(s32[15]{0:T(128)S(1)} %stack.63.control, bf16[4,192,512]{2,1,0:T(8,128)(2,1)S(1)} %attend.2.left, bf16[512,512]{1,0:T(8,128)(2,1)S(1)} %collective-permute-done.refs_0_, bf16[512,512]{1,0:T(8,128)(2,1)S(1)} %collective-permute-done.4.refs_1_, bf16[512,512]{1,0:T(8,128)(2,1)} %collective-permute-done.5.refs_2_, ...), custom_call_target="tpu_custom_call" | custom-call | flops 3000000000 | bytes 1000 | tf_op jit(solution)/shard_map/project/pallas_call | solution.py:299
  150.6 3.6 %collective-permute-start.24 = (bf16[192,1024]{1,0:T(8,128)(2,1)S(1)}, bf16[192,1024]{1,0:T(8,128)(2,1)S(1)}, u32[]{:S(2)}, u32[]{:S(2)}) collective-permute-start(bf16[192,1024]{1,0:T(8,128)(2,1)S(1)} %project.6), channel_id=1, source_target_pairs={{0,2},{2,0},{1,3},{3,1},{4,6},{6,4},{5,7},{7,5},{8,10},{10,8},{9,1... | collective-permute-start | bytes 1179656 | tf_op jit(solution)/shard_map/ppermute | solution.py:446
  154.4 3.2 %project.7 = bf16[192,1024]{1,0:T(8,128)(2,1)S(1)} custom-call(s32[15]{0:T(128)S(1)} %stack.63.control, bf16[4,192,512]{2,1,0:T(8,128)(2,1)S(1)} %attend.2.left, bf16[512,512]{1,0:T(8,128)(2,1)S(1)} %broadcast_select_fusion.3.refs_0_, bf16[512,512]{1,0:T(8,128)(2,1)} %collective-permute-done.11.refs_1_, bf16[512,512]{1,0:T(8,128)(2,1)S(1)} %copy-done.4, ...), custom_call_target="tpu_custom_call" | custom-call | flops 3000000000 | bytes 1000 | tf_op jit(solution)/shard_map/project/pallas_call | solution.py:299
  157.6 2.0 collective-permute-start.23
  159.6 1.5 collective-permute-start.21
  161.1 1.1 broadcast_select_fusion.1.refs_0_
  162.2 0.9 collective-permute-start.26
  163.1 8.9 %attend.3.left = bf16[4,192,512]{2,1,0:T(8,128)(2,1)S(1)} custom-call(s32[15]{0:T(128)S(1)} %stack.63.control, s32[6]{0:T(128)S(1)} %get-tuple-element.70.hist_at, s32[6]{0:T(128)S(1)} %get-tuple-element.69.hist_steps, s32[6]{0:T(128)S(1)} %get-tuple-element.64.fresh_at, s32[6]{0:T(128)S(1)} %get-tuple-element.63.fresh_steps, ...), custom_call_target="tpu_custom_call" | custom-call | flops 16000000000 | bytes 1000 | tf_op jit(solution)/shard_map/attend/pallas_call | solution.py:221
  172.1 1.1 broadcast_select_fusion.refs_0_
  173.2 1.9 collective-permute-start.22
  175.2 2.3 %finish.5.refs_8_ = bf16[1,192,4096]{2,1,0:T(8,128)(2,1)} custom-call(s32[15]{0:T(128)S(1)} %stack.63.control, bf16[4,192,512]{2,1,0:T(8,128)(2,1)S(1)} %attend.3.left, bf16[192,1024]{1,0:T(8,128)(2,1)S(1)} %collective-permute-done.25.came, bf16[2048,1024]{1,0:T(8,128)(2,1)S(1)} %copy-done.1), custom_call_target="tpu_custom_call" | custom-call | flops 3000000000 | bytes 1000 | tf_op jit(solution)/shard_map/finish/pallas_call | solution.py:299
  177.7 4.0 %finish.6.refs_8_ = bf16[1,192,4096]{2,1,0:T(8,128)(2,1)} custom-call(s32[15]{0:T(128)S(1)} %stack.63.control, bf16[4,192,512]{2,1,0:T(8,128)(2,1)S(1)} %attend.3.left, bf16[192,1024]{1,0:T(8,128)(2,1)S(1)} %collective-permute-done.24.came, bf16[512,512]{1,0:T(8,128)(2,1)S(1)} %collective-permute-done.refs_0_, ...), custom_call_target="tpu_custom_call", output_to_operand_aliasing={{}: (11, {})} | custom-call | flops 3000000000 | bytes 1000 | tf_op jit(solution)/shard_map/finish/pallas_call | solution.py:299
  181.6 4.0 %finish.7.refs_4_ = bf16[1,192,4096]{2,1,0:T(8,128)(2,1)} custom-call(s32[15]{0:T(128)S(1)} %stack.63.control, bf16[4,192,512]{2,1,0:T(8,128)(2,1)S(1)} %attend.3.left, bf16[192,1024]{1,0:T(8,128)(2,1)S(1)} %collective-permute-done.23.came, bf16[512,512]{1,0:T(8,128)(2,1)S(1)} %broadcast_select_fusion.3.refs_0_, ...), custom_call_target="tpu_custom_call", output_to_operand_aliasing={{}: (11, {})} | custom-call | flops 3000000000 | bytes 1000 | tf_op jit(solution)/shard_map/finish/pallas_call | solution.py:299
  185.6 1.1 project.8
  186.7 1.0 collective-permute-done.22.refs_1_
  188.2 2.5 %collective-permute-start.32 = (bf16[192,512]{1,0:T(8,128)(2,1)S(1)}, bf16[192,512]{1,0:T(8,128)(2,1)S(1)}, u32[]{:S(2)}, u32[]{:S(2)}) collective-permute-start(bf16[192,512]{1,0:T(8,128)(2,1)S(1)} %project.8), channel_id=1, source_target_pairs={{0,2},{2,0},{1,3},{3,1},{4,6},{6,4},{5,7},{7,5},{8,10},{10,8},{9,1... | collective-permute-start | bytes 589832 | tf_op jit(solution)/shard_map/ppermute | solution.py:456
  190.7 1.1 project.9
  191.8 2.2 %collective-permute-start.31 = (bf16[192,512]{1,0:T(8,128)(2,1)S(1)}, bf16[192,512]{1,0:T(8,128)(2,1)S(1)}, u32[]{:S(2)}, u32[]{:S(2)}) collective-permute-start(bf16[192,512]{1,0:T(8,128)(2,1)S(1)} %project.9), channel_id=1, source_target_pairs={{0,2},{2,0},{1,3},{3,1},{4,6},{6,4},{5,7},{7,5},{8,10},{10,8},{9,1... | collective-permute-start | bytes 589832 | tf_op jit(solution)/shard_map/ppermute | solution.py:459
  194.0 2.4 %collective-permute-done.32.came = bf16[192,512]{1,0:T(8,128)(2,1)S(1)} collective-permute-done((bf16[192,512]{1,0:T(8,128)(2,1)S(1)}, bf16[192,512]{1,0:T(8,128)(2,1)S(1)}, u32[]{:S(2)}, u32[]{:S(2)}) %collective-permute-start.32) | collective-permute-done | bytes 196640 | tf_op jit(solution)/shard_map/ppermute | solution.py:456
  196.4 1.8 finish.8.refs_4_
  198.2 1.8 collective-permute-done.31.came
  200.0 1.8 finish.9
  (72 shorter events, 4.8 us)
Async XLA Ops:
  1.3 17.1 %collective-permute-start = (bf16[512,512]{1,0:T(8,128)(2,1)S(1)}, bf16[512,512]{1,0:T(8,128)(2,1)S(1)}, u32[]{:S(2)}, u32[]{:S(2)}) collective-permute-start(bf16[512,512]{1,0:T(8,128)(2,1)S(1)} %get-tuple-element.68), channel_id=1, source_target_pairs={{0,4},{4,0},{8,12},{12,8},{1,5},{5,1},{9,13},{13,9},{2,6},{6,2},{1... | collective-permute-start | bytes 1572872 | tf_op jit(solution)/shard_map/ppermute | solution.py:390
  2.9 15.5 %collective-permute-start.1 = (bf16[512,512]{1,0:T(8,128)(2,1)S(1)}, bf16[512,512]{1,0:T(8,128)(2,1)S(1)}, u32[]{:S(2)}, u32[]{:S(2)}) collective-permute-start(bf16[512,512]{1,0:T(8,128)(2,1)S(1)} %get-tuple-element.68), channel_id=1, source_target_pairs={{4,8},{8,4},{5,9},{9,5},{6,10},{10,6},{7,11},{11,7},{20,24},{24,20... | collective-permute-start | bytes 1572872 | tf_op jit(solution)/shard_map/ppermute | solution.py:390
  18.4 14.2 %collective-permute-start.3 = (bf16[512,512]{1,0:T(8,128)(2,1)S(1)}, bf16[512,512]{1,0:T(8,128)(2,1)S(1)}, u32[]{:S(2)}, u32[]{:S(2)}) collective-permute-start(bf16[512,512]{1,0:T(8,128)(2,1)S(1)} %get-tuple-element.38), channel_id=1, source_target_pairs={{4,8},{8,4},{5,9},{9,5},{6,10},{10,6},{7,11},{11,7},{20,24},{24,20... | collective-permute-start | bytes 1572872 | tf_op jit(solution)/shard_map/ppermute | solution.py:398
  20.4 12.6 %collective-permute-start.2 = (bf16[512,512]{1,0:T(8,128)(2,1)S(1)}, bf16[512,512]{1,0:T(8,128)(2,1)S(1)}, u32[]{:S(2)}, u32[]{:S(2)}) collective-permute-start(bf16[512,512]{1,0:T(8,128)(2,1)S(1)} %get-tuple-element.38), channel_id=1, source_target_pairs={{0,4},{4,0},{8,12},{12,8},{1,5},{5,1},{9,13},{13,9},{2,6},{6,2},{1... | collective-permute-start | bytes 1572872 | tf_op jit(solution)/shard_map/ppermute | solution.py:397
  33.0 95.2 %all-to-all-start.1 = ((bf16[4,64,2,16,256]{4,3,2,1,0:T(8,128)(2,1)}), bf16[4,64,2,16,256]{4,3,2,1,0:T(8,128)(2,1)}, u32[]{:S(2)}, u32[]{:S(2)}) async-start(bf16[4,64,2,16,256]{4,3,2,1,0:T(8,128)(2,1)} %pick.1), calls=%async_computation.1 | async-start | bytes 8388608 | tf_op jit(solution)/shard_map/all_to_all | solution.py:404
  38.9 59.2 %collective-permute-start.10 = (bf16[512,512]{1,0:T(8,128)(2,1)S(1)}, bf16[512,512]{1,0:T(8,128)(2,1)}, u32[]{:S(2)}, u32[]{:S(2)}) collective-permute-start(bf16[512,512]{1,0:T(8,128)(2,1)S(1)} %collective-permute-done.1), channel_id=1, source_target_pairs={{4,0},{8,12},{5,1},{9,13},{6,2},{10,14},{7,3},{11,15},{20,16},{24,... | collective-permute-start | bytes 1572872 | tf_op jit(solution)/shard_map/ppermute | solution.py:431
  43.1 64.4 %collective-permute-start.14 = (bf16[512,512]{1,0:T(8,128)(2,1)S(1)}, bf16[512,512]{1,0:T(8,128)(2,1)}, u32[]{:S(2)}, u32[]{:S(2)}) collective-permute-start(bf16[512,512]{1,0:T(8,128)(2,1)S(1)} %collective-permute-done.3), channel_id=1, source_target_pairs={{4,0},{8,12},{5,1},{9,13},{6,2},{10,14},{7,3},{11,15},{20,16},{24,... | collective-permute-start | bytes 1572872 | tf_op jit(solution)/shard_map/ppermute | solution.py:431
  45.2 64.6 %copy-start.5 = (s32[1,384]{1,0:T(1,128)S(1)}, s32[1,384]{1,0:T(1,128)}, u32[]{:S(2)}) copy-start(s32[1,384]{1,0:T(1,128)} %param.13) | copy-start | bytes 4612
  45.2 65.0 %copy-start.6 = (s32[1,128]{1,0:T(1,128)S(1)}, s32[1,128]{1,0:T(1,128)}, u32[]{:S(2)}) copy-start(s32[1,128]{1,0:T(1,128)} %param.14) | copy-start | bytes 1540
  45.2 65.2 %copy-start.7 = (s32[1,128]{1,0:T(1,128)S(1)}, s32[1,128]{1,0:T(1,128)}, u32[]{:S(2)}) copy-start(s32[1,128]{1,0:T(1,128)} %param.15) | copy-start | bytes 1540
  45.2 64.0 %collective-permute-start.4 = (bf16[512,512]{1,0:T(8,128)(2,1)S(1)}, bf16[512,512]{1,0:T(8,128)(2,1)S(1)}, u32[]{:S(2)}, u32[]{:S(2)}) collective-permute-start(bf16[512,512]{1,0:T(8,128)(2,1)S(1)} %collective-permute-done.refs_0_), channel_id=1, source_target_pairs={{0,16},{16,0},{1,17},{17,1},{2,18},{18,2},{3,19},{19,3},{4,20},{20... | collective-permute-start | bytes 1572872 | tf_op jit(solution)/shard_map/ppermute | solution.py:430
  46.7 63.0 %collective-permute-start.7 = (bf16[512,512]{1,0:T(8,128)(2,1)S(1)}, bf16[512,512]{1,0:T(8,128)(2,1)}, u32[]{:S(2)}, u32[]{:S(2)}) collective-permute-start(bf16[512,512]{1,0:T(8,128)(2,1)S(1)} %collective-permute-done.2.refs_4_), channel_id=1, source_target_pairs={{0,16},{16,0},{1,17},{17,1},{2,18},{18,2},{3,19},{19,3},{4,20},{20... | collective-permute-start | bytes 1572872 | tf_op jit(solution)/shard_map/ppermute | solution.py:430
  98.2 30.0 %copy-start.2 = (s32[128]{0:T(128)S(1)}, s32[128]{0:T(128)}, u32[]{:S(2)}) copy-start(s32[128]{0:T(128)} %get-tuple-element.33.position) | copy-start | bytes 1540
  98.2 12.4 %collective-permute-start.11 = (bf16[512,512]{1,0:T(8,128)(2,1)S(1)}, bf16[512,512]{1,0:T(8,128)(2,1)}, u32[]{:S(2)}, u32[]{:S(2)}) collective-permute-start(bf16[512,512]{1,0:T(8,128)(2,1)S(1)} %broadcast_select_fusion.3.refs_0_), channel_id=1, source_target_pairs={{0,16},{16,0},{1,17},{17,1},{2,18},{18,2},{3,19},{19,3},{4,20},{20... | collective-permute-start | bytes 1572872 | tf_op jit(solution)/shard_map/ppermute | solution.py:432
  107.6 11.1 %collective-permute-start.15 = (bf16[512,512]{1,0:T(8,128)(2,1)S(1)}, bf16[512,512]{1,0:T(8,128)(2,1)}, u32[]{:S(2)}, u32[]{:S(2)}) collective-permute-start(bf16[512,512]{1,0:T(8,128)(2,1)S(1)} %broadcast_select_fusion.2.refs_4_), channel_id=1, source_target_pairs={{0,16},{16,0},{1,17},{17,1},{2,18},{18,2},{3,19},{19,3},{4,20},{20... | collective-permute-start | bytes 1572872 | tf_op jit(solution)/shard_map/ppermute | solution.py:432
  109.2 9.6 %collective-permute-start.5 = (bf16[512,512]{1,0:T(8,128)(2,1)S(1)}, bf16[512,512]{1,0:T(8,128)(2,1)}, u32[]{:S(2)}, u32[]{:S(2)}) collective-permute-start(bf16[512,512]{1,0:T(8,128)(2,1)S(1)} %collective-permute-done.refs_0_), channel_id=1, source_target_pairs={{0,1},{1,0},{2,3},{3,2},{4,5},{5,4},{6,7},{7,6},{8,9},{9,8},{10,11... | collective-permute-start | bytes 1572872 | tf_op jit(solution)/shard_map/ppermute | solution.py:428
  109.2 10.1 %collective-permute-start.8 = (bf16[512,512]{1,0:T(8,128)(2,1)S(1)}, bf16[512,512]{1,0:T(8,128)(2,1)}, u32[]{:S(2)}, u32[]{:S(2)}) collective-permute-start(bf16[512,512]{1,0:T(8,128)(2,1)S(1)} %collective-permute-done.2.refs_4_), channel_id=1, source_target_pairs={{0,1},{1,0},{2,3},{3,2},{4,5},{5,4},{6,7},{7,6},{8,9},{9,8},{10,11... | collective-permute-start | bytes 1572872 | tf_op jit(solution)/shard_map/ppermute | solution.py:428
  109.7 9.6 %collective-permute-start.12 = (bf16[512,512]{1,0:T(8,128)(2,1)S(1)}, bf16[512,512]{1,0:T(8,128)(2,1)S(1)}, u32[]{:S(2)}, u32[]{:S(2)}) collective-permute-start(bf16[512,512]{1,0:T(8,128)(2,1)S(1)} %broadcast_select_fusion.3.refs_0_), channel_id=1, source_target_pairs={{0,1},{1,0},{2,3},{3,2},{4,5},{5,4},{6,7},{7,6},{8,9},{9,8},{10,11... | collective-permute-start | bytes 1572872 | tf_op jit(solution)/shard_map/ppermute | solution.py:428
  110.6 10.2 %collective-permute-start.6 = (bf16[512,512]{1,0:T(8,128)(2,1)S(1)}, bf16[512,512]{1,0:T(8,128)(2,1)}, u32[]{:S(2)}, u32[]{:S(2)}) collective-permute-start(bf16[512,512]{1,0:T(8,128)(2,1)S(1)} %collective-permute-done.4.refs_1_), channel_id=1, source_target_pairs={{0,1},{1,0},{2,3},{3,2},{4,5},{5,4},{6,7},{7,6},{8,9},{9,8},{10,11... | collective-permute-start | bytes 1572872 | tf_op jit(solution)/shard_map/ppermute | solution.py:428
  118.8 5.5 %collective-permute-start.16 = (bf16[512,512]{1,0:T(8,128)(2,1)S(1)}, bf16[512,512]{1,0:T(8,128)(2,1)}, u32[]{:S(2)}, u32[]{:S(2)}) collective-permute-start(bf16[512,512]{1,0:T(8,128)(2,1)S(1)} %broadcast_select_fusion.2.refs_4_), channel_id=1, source_target_pairs={{0,1},{1,0},{2,3},{3,2},{4,5},{5,4},{6,7},{7,6},{8,9},{9,8},{10,11... | collective-permute-start | bytes 1572872 | tf_op jit(solution)/shard_map/ppermute | solution.py:428
  118.8 9.4 %collective-permute-start.9 = (bf16[512,512]{1,0:T(8,128)(2,1)}, bf16[512,512]{1,0:T(8,128)(2,1)}, u32[]{:S(2)}, u32[]{:S(2)}) collective-permute-start(bf16[512,512]{1,0:T(8,128)(2,1)} %collective-permute-done.7.refs_5_), channel_id=1, source_target_pairs={{0,1},{1,0},{2,3},{3,2},{4,5},{5,4},{6,7},{7,6},{8,9},{9,8},{10,11... | collective-permute-start | bytes 1572872 | tf_op jit(solution)/shard_map/ppermute | solution.py:428
  119.3 8.9 %collective-permute-start.13 = (bf16[512,512]{1,0:T(8,128)(2,1)}, bf16[512,512]{1,0:T(8,128)(2,1)}, u32[]{:S(2)}, u32[]{:S(2)}) collective-permute-start(bf16[512,512]{1,0:T(8,128)(2,1)} %collective-permute-done.11.refs_1_), channel_id=1, source_target_pairs={{0,1},{1,0},{2,3},{3,2},{4,5},{5,4},{6,7},{7,6},{8,9},{9,8},{10,11... | collective-permute-start | bytes 1572872 | tf_op jit(solution)/shard_map/ppermute | solution.py:428
  119.4 0.8 copy-start.3
  120.2 8.0 %collective-permute-start.17 = (bf16[512,512]{1,0:T(8,128)(2,1)}, bf16[512,512]{1,0:T(8,128)(2,1)}, u32[]{:S(2)}, u32[]{:S(2)}) collective-permute-start(bf16[512,512]{1,0:T(8,128)(2,1)} %collective-permute-done.15.refs_5_), channel_id=1, source_target_pairs={{0,1},{1,0},{2,3},{3,2},{4,5},{5,4},{6,7},{7,6},{8,9},{9,8},{10,11... | collective-permute-start | bytes 1572872 | tf_op jit(solution)/shard_map/ppermute | solution.py:428
  120.7 23.3 %collective-permute-start.18 = (bf16[512,512]{1,0:T(8,128)(2,1)S(1)}, bf16[512,512]{1,0:T(8,128)(2,1)}, u32[]{:S(2)}, u32[]{:S(2)}) collective-permute-start(bf16[512,512]{1,0:T(8,128)(2,1)S(1)} %collective-permute-done.refs_0_), channel_id=1, source_target_pairs={{4,8},{8,4},{5,9},{9,5},{6,10},{10,6},{7,11},{11,7},{20,24},{24,20... | collective-permute-start | bytes 1572872 | tf_op jit(solution)/shard_map/ppermute | solution.py:435
  124.3 35.3 %collective-permute-start.20 = (bf16[512,512]{1,0:T(8,128)(2,1)S(1)}, bf16[512,512]{1,0:T(8,128)(2,1)}, u32[]{:S(2)}, u32[]{:S(2)}) collective-permute-start(bf16[512,512]{1,0:T(8,128)(2,1)S(1)} %collective-permute-done.2.refs_4_), channel_id=1, source_target_pairs={{4,8},{8,4},{5,9},{9,5},{6,10},{10,6},{7,11},{11,7},{20,24},{24,20... | collective-permute-start | bytes 1572872 | tf_op jit(solution)/shard_map/ppermute | solution.py:435
  128.2 3.3 %copy-start = (bf16[1,384,2048]{2,1,0:T(8,128)(2,1)S(1)}, bf16[1,384,2048]{2,1,0:T(8,128)(2,1)}, u32[]{:S(2)}) copy-start(bf16[1,384,2048]{2,1,0:T(8,128)(2,1)} %param.9) | copy-start | bytes 4718596
  131.5 11.0 %copy-start.1 = (bf16[2048,1024]{1,0:T(8,128)(2,1)S(1)}, bf16[2048,1024]{1,0:T(8,128)(2,1)}, u32[]{:S(2)}) copy-start(bf16[2048,1024]{1,0:T(8,128)(2,1)} %refs_0_.3) | copy-start | bytes 12582916
  144.1 10.3 %copy-start.4 = (bf16[512,512]{1,0:T(8,128)(2,1)S(1)}, bf16[512,512]{1,0:T(8,128)(2,1)}, u32[]{:S(2)}) copy-start(bf16[512,512]{1,0:T(8,128)(2,1)} %copy-done.3) | copy-start | bytes 1572868
  144.1 17.0 %collective-permute-start.19 = (bf16[512,512]{1,0:T(8,128)(2,1)}, bf16[512,512]{1,0:T(8,128)(2,1)S(1)}, u32[]{:S(2)}, u32[]{:S(2)}) collective-permute-start(bf16[512,512]{1,0:T(8,128)(2,1)} %collective-permute-done.18), channel_id=1, source_target_pairs={{4,0},{8,12},{5,1},{9,13},{6,2},{10,14},{7,3},{11,15},{20,16},{24,... | collective-permute-start | bytes 1572872 | tf_op jit(solution)/shard_map/ppermute | solution.py:439
  150.6 21.4 %collective-permute-start.24 = (bf16[192,1024]{1,0:T(8,128)(2,1)S(1)}, bf16[192,1024]{1,0:T(8,128)(2,1)S(1)}, u32[]{:S(2)}, u32[]{:S(2)}) collective-permute-start(bf16[192,1024]{1,0:T(8,128)(2,1)S(1)} %project.6), channel_id=1, source_target_pairs={{0,2},{2,0},{1,3},{3,1},{4,6},{6,4},{5,7},{7,5},{8,10},{10,8},{9,1... | collective-permute-start | bytes 1179656 | tf_op jit(solution)/shard_map/ppermute | solution.py:446
  154.3 17.8 %collective-permute-start.25 = (bf16[192,1024]{1,0:T(8,128)(2,1)S(1)}, bf16[192,1024]{1,0:T(8,128)(2,1)S(1)}, u32[]{:S(2)}, u32[]{:S(2)}) collective-permute-start(bf16[192,1024]{1,0:T(8,128)(2,1)S(1)} %project.5), channel_id=1, source_target_pairs={{0,2},{2,0},{1,3},{3,1},{4,6},{6,4},{5,7},{7,5},{8,10},{10,8},{9,1... | collective-permute-start | bytes 1179656 | tf_op jit(solution)/shard_map/ppermute | solution.py:446
  157.6 24.1 %collective-permute-start.23 = (bf16[192,1024]{1,0:T(8,128)(2,1)S(1)}, bf16[192,1024]{1,0:T(8,128)(2,1)S(1)}, u32[]{:S(2)}, u32[]{:S(2)}) collective-permute-start(bf16[192,1024]{1,0:T(8,128)(2,1)S(1)} %project.7), channel_id=1, source_target_pairs={{0,2},{2,0},{1,3},{3,1},{4,6},{6,4},{5,7},{7,5},{8,10},{10,8},{9,1... | collective-permute-start | bytes 1179656 | tf_op jit(solution)/shard_map/ppermute | solution.py:446
  159.6 12.5 %collective-permute-start.21 = (bf16[512,512]{1,0:T(8,128)(2,1)}, bf16[512,512]{1,0:T(8,128)(2,1)S(1)}, u32[]{:S(2)}, u32[]{:S(2)}) collective-permute-start(bf16[512,512]{1,0:T(8,128)(2,1)} %collective-permute-done.20), channel_id=1, source_target_pairs={{4,0},{8,12},{5,1},{9,13},{6,2},{10,14},{7,3},{11,15},{20,16},{24,... | collective-permute-start | bytes 1572872 | tf_op jit(solution)/shard_map/ppermute | solution.py:441
  162.2 15.3 %collective-permute-start.26 = (bf16[512,512]{1,0:T(8,128)(2,1)S(1)}, bf16[512,512]{1,0:T(8,128)(2,1)S(1)}, u32[]{:S(2)}, u32[]{:S(2)}) collective-permute-start(bf16[512,512]{1,0:T(8,128)(2,1)S(1)} %broadcast_select_fusion.1.refs_0_), channel_id=1, source_target_pairs={{0,16},{16,0},{1,17},{17,1},{2,18},{18,2},{3,19},{19,3},{4,20},{20... | collective-permute-start | bytes 1572872 | tf_op jit(solution)/shard_map/ppermute | solution.py:444
  172.0 13.6 %collective-permute-start.27 = (bf16[512,512]{1,0:T(8,128)(2,1)S(1)}, bf16[512,512]{1,0:T(8,128)(2,1)S(1)}, u32[]{:S(2)}, u32[]{:S(2)}) collective-permute-start(bf16[512,512]{1,0:T(8,128)(2,1)S(1)} %broadcast_select_fusion.1.refs_0_), channel_id=1, source_target_pairs={{0,1},{1,0},{2,3},{3,2},{4,5},{5,4},{6,7},{7,6},{8,9},{9,8},{10,11... | collective-permute-start | bytes 1572872 | tf_op jit(solution)/shard_map/ppermute | solution.py:428
  173.2 14.5 %collective-permute-start.22 = (bf16[512,512]{1,0:T(8,128)(2,1)S(1)}, bf16[512,512]{1,0:T(8,128)(2,1)S(1)}, u32[]{:S(2)}, u32[]{:S(2)}) collective-permute-start(bf16[512,512]{1,0:T(8,128)(2,1)S(1)} %broadcast_select_fusion.refs_0_), channel_id=1, source_target_pairs={{0,16},{16,0},{1,17},{17,1},{2,18},{18,2},{3,19},{19,3},{4,20},{20... | collective-permute-start | bytes 1572872 | tf_op jit(solution)/shard_map/ppermute | solution.py:449
  177.5 8.1 %collective-permute-start.28 = (bf16[512,512]{1,0:T(8,128)(2,1)S(1)}, bf16[512,512]{1,0:T(8,128)(2,1)S(1)}, u32[]{:S(2)}, u32[]{:S(2)}) collective-permute-start(bf16[512,512]{1,0:T(8,128)(2,1)S(1)} %collective-permute-done.26.refs_1_), channel_id=1, source_target_pairs={{0,1},{1,0},{2,3},{3,2},{4,5},{5,4},{6,7},{7,6},{8,9},{9,8},{10,11... | collective-permute-start | bytes 1572872 | tf_op jit(solution)/shard_map/ppermute | solution.py:428
  187.7 3.0 %collective-permute-start.30 = (bf16[512,512]{1,0:T(8,128)(2,1)S(1)}, bf16[512,512]{1,0:T(8,128)(2,1)S(1)}, u32[]{:S(2)}, u32[]{:S(2)}) collective-permute-start(bf16[512,512]{1,0:T(8,128)(2,1)S(1)} %collective-permute-done.22.refs_1_), channel_id=1, source_target_pairs={{0,1},{1,0},{2,3},{3,2},{4,5},{5,4},{6,7},{7,6},{8,9},{9,8},{10,11... | collective-permute-start | bytes 1572872 | tf_op jit(solution)/shard_map/ppermute | solution.py:428
  187.7 3.0 %collective-permute-start.29 = (bf16[512,512]{1,0:T(8,128)(2,1)S(1)}, bf16[512,512]{1,0:T(8,128)(2,1)S(1)}, u32[]{:S(2)}, u32[]{:S(2)}) collective-permute-start(bf16[512,512]{1,0:T(8,128)(2,1)S(1)} %broadcast_select_fusion.refs_0_), channel_id=1, source_target_pairs={{0,1},{1,0},{2,3},{3,2},{4,5},{5,4},{6,7},{7,6},{8,9},{9,8},{10,11... | collective-permute-start | bytes 1572872 | tf_op jit(solution)/shard_map/ppermute | solution.py:428
  188.2 8.2 %collective-permute-start.32 = (bf16[192,512]{1,0:T(8,128)(2,1)S(1)}, bf16[192,512]{1,0:T(8,128)(2,1)S(1)}, u32[]{:S(2)}, u32[]{:S(2)}) collective-permute-start(bf16[192,512]{1,0:T(8,128)(2,1)S(1)} %project.8), channel_id=1, source_target_pairs={{0,2},{2,0},{1,3},{3,1},{4,6},{6,4},{5,7},{7,5},{8,10},{10,8},{9,1... | collective-permute-start | bytes 589832 | tf_op jit(solution)/shard_map/ppermute | solution.py:456
  191.8 8.2 %collective-permute-start.31 = (bf16[192,512]{1,0:T(8,128)(2,1)S(1)}, bf16[192,512]{1,0:T(8,128)(2,1)S(1)}, u32[]{:S(2)}, u32[]{:S(2)}) collective-permute-start(bf16[192,512]{1,0:T(8,128)(2,1)S(1)} %project.9), channel_id=1, source_target_pairs={{0,2},{2,0},{1,3},{3,1},{4,6},{6,4},{5,7},{7,5},{8,10},{10,8},{9,1... | collective-permute-start | bytes 589832 | tf_op jit(solution)/shard_map/ppermute | solution.py:459

commit v14 on v13

--- a/solution.py
+++ b/solution.py
@@ -304,7 +304,7 @@
         ),
         input_output_aliases=aliases,
         compiler_params=pltpu.CompilerParams(vmem_limit_bytes=16 * MIB),
-        cost_estimate=cost(),
+        cost_estimate=cost(10**8 if base == 12 else 3 * 10**9),
         name="project" if came is None else "finish",
     )(control, *operands)
 
@@ -451,11 +451,11 @@
     total = columns * owner_count
     out = project(control, after(stay, *came[:2]), [out_weight], came[0], 10, None, total)
     out = project(control, stay, near_all, came[1], 11, out, total)
-    out = project(control, stay, next_all, came[2], 12, out, total)
     sent.append(project(control, after(left, out), far_all[0]))
     came.append(swap_tp(sent[3]))
-    far_all.append(four(far[1], far_across[1], sent[3]))
-    sent.append(project(control, left, far_all[1]))
+    out = project(control, after(stay, sent[3]), next_all, came[2], 12, out, total)
+    far_all.append(four(far[1], far_across[1], out, came[3]))
+    sent.append(project(control, after(left, out), far_all[1]))
     came.append(swap_tp(sent[4]))
     out = project(control, after(stay, sent[4]), far_all[0], came[3], 13, out, total)
     return project(control, stay, far_all[1], came[4], 14, out, total)

time: 203 us -> 205 us (level)
  waiting for transfers between devices: 79 us -> 81.8 us
    ppermute x1, waiting for transfers between devices: 6.99 us -> 2.87 us  [shards(): inner.append(cross(later))]
    ppermute x1, waiting for transfers between devices: 0.42 us -> 3.83 us  [shards(): near.append(pair(later))]
    ppermute x1, starting transfers between devices: 3.35 us -> 6.63 us  [shards(): far_on = [forward(after(far[0], left))]]
  transfers between devices with their start and end apart: 34 -> 34, of which waited for: 8 -> 11; matrix products, arithmetic and copies ran while one was open for 2% -> 2% of each run, Pallas kernels for 26% -> 26%
where the time goes in v14:
time: 205 us; the launch traced here: 203 us
  waiting for transfers between devices  81.8 us (40%)
  Pallas kernels  55.1 us (27%)
  starting transfers between devices  49.2 us (24%)
  blocking collectives  10.7 us (5%)
  other arithmetic  2.89 us (1%)
  local copies, waits for them, and re-layouts  2.87 us (1%)
    ppermute x2, waiting for transfers between devices, shards(): next_shard = [jnp.where(middle, part, forward(part)) for part in inner]  59.4 us
    pallas_call x10, Pallas kernels, project(): pl.pallas_call(kernel, out_shape=out_shape, grid_spec=pltpu.PrefetchScala...  23.6 us
    pallas_call x2, Pallas kernels, attend(): pl.pallas_call(functools.partial(attend_kernel, fresh_base, side), out_sh...  20.5 us
    all_to_all x1, blocking collectives, shards(): lax.all_to_all(wanted, 'seq', split_axis=0, concat_axis=0, tiled=True)  10.7 us
    ppermute x2, waiting for transfers between devices, shards(): next_across = [swap_group(part) for part in next_shard]  7.29 us
    ppermute x1, starting transfers between devices, shards(): far_on = [forward(after(far[0], left))]  6.63 us
    ppermute x2, starting transfers between devices, shards(): far = [cross(after(part, *next_across)) for part in near]  5.85 us
    pallas_call x1, Pallas kernels, pick(): pl.pallas_call(pick_kernel, out_shape=jax.ShapeDtypeStruct(out, jnp.bfloa...  5.04 us
  transfers between devices with their start and end apart: 34, of which 11 were waited for; matrix products, arithmetic and copies ran while one was open for 2% of the time, Pallas kernels for 26%

profile of v14, /device:TPU:16, one launch (start us, length us, event | category | flops | bytes accessed | tf_op | source)
XLA Modules:
  0.0 203.3 jit_solution(17763663857093337308)
XLA Ops:
  0.0 1.3 fusion.5
  1.3 1.6 collective-permute-start
  2.9 1.9 collective-permute-start.1
  4.8 2.6 %rank.1 = (s32[128]{0:T(128)}, s32[4,64]{1,0:T(4,128)}) custom-call(s32[1,128]{1,0:T(1,128)} %owner.1, s32[1,128]{1,0:T(1,128)} %page.1), custom_call_target="tpu_custom_call" | custom-call | flops 3000000000 | bytes 1000 | tf_op jit(solution)/shard_map/rank/pallas_call | solution.py:49
  7.5 10.7 %all_to_all.17 = s32[4,1,64]{2,1,0:T(1,128)} all-to-all(s32[4,1,64]{2,1,0:T(1,128)} %bitcast.39), channel_id=1, replica_groups=mesh['group'=2,'seq'=4,'tp'=2,'role'=2] {'seq'}, dimensions={0} | all-to-all | bytes 2048 | tf_op jit(solution)/shard_map/all_to_all | solution.py:393
  18.2 1.4 collective-permute-start.2
  19.6 2.2 %collective-permute-start.3 = (bf16[512,512]{1,0:T(8,128)(2,1)S(1)}, bf16[512,512]{1,0:T(8,128)(2,1)S(1)}, u32[]{:S(2)}, u32[]{:S(2)}) collective-permute-start(bf16[512,512]{1,0:T(8,128)(2,1)S(1)} %get-tuple-element.40), channel_id=1, source_target_pairs={{4,8},{8,4},{5,9},{9,5},{6,10},{10,6},{7,11},{11,7},{20,24},{24,20... | collective-permute-start | bytes 1572872 | tf_op jit(solution)/shard_map/ppermute | solution.py:398
  21.8 5.0 %pick.1 = bf16[4,64,2,16,256]{4,3,2,1,0:T(8,128)(2,1)} custom-call(s32[4,64]{1,0:T(4,128)} %bitcast.38, bf16[256,2,16,256]{3,2,1,0:T(8,128)(2,1)} %bitcast.41), custom_call_target="tpu_custom_call" | custom-call | flops 3000000000 | bytes 1000 | tf_op jit(solution)/shard_map/pick/pallas_call | solution.py:332
  26.9 3.8 %collective-permute-done.2.refs_4_ = bf16[512,512]{1,0:T(8,128)(2,1)S(1)} collective-permute-done((bf16[512,512]{1,0:T(8,128)(2,1)S(1)}, bf16[512,512]{1,0:T(8,128)(2,1)S(1)}, u32[]{:S(2)}, u32[]{:S(2)}) %collective-permute-start.2) | collective-permute-done | bytes 524320 | tf_op jit(solution)/shard_map/ppermute | solution.py:397
  30.7 2.9 %collective-permute-done.3 = bf16[512,512]{1,0:T(8,128)(2,1)S(1)} collective-permute-done((bf16[512,512]{1,0:T(8,128)(2,1)S(1)}, bf16[512,512]{1,0:T(8,128)(2,1)S(1)}, u32[]{:S(2)}, u32[]{:S(2)}) %collective-permute-start.3) | collective-permute-done | bytes 524320 | tf_op jit(solution)/shard_map/ppermute | solution.py:398
  33.6 4.8 %all-to-all-start.1 = ((bf16[4,64,2,16,256]{4,3,2,1,0:T(8,128)(2,1)}), bf16[4,64,2,16,256]{4,3,2,1,0:T(8,128)(2,1)}, u32[]{:S(2)}, u32[]{:S(2)}) async-start(bf16[4,64,2,16,256]{4,3,2,1,0:T(8,128)(2,1)} %pick.1), calls=%async_computation.1 | async-start | bytes 8388608 | tf_op jit(solution)/shard_map/all_to_all | solution.py:404
  38.4 2.7 %collective-permute-start.10 = (bf16[512,512]{1,0:T(8,128)(2,1)S(1)}, bf16[512,512]{1,0:T(8,128)(2,1)S(1)}, u32[]{:S(2)}, u32[]{:S(2)}) collective-permute-start(bf16[512,512]{1,0:T(8,128)(2,1)S(1)} %collective-permute-done.1), channel_id=1, source_target_pairs={{4,0},{8,12},{5,1},{9,13},{6,2},{10,14},{7,3},{11,15},{20,16},{24,... | collective-permute-start | bytes 1572872 | tf_op jit(solution)/shard_map/ppermute | solution.py:431
  41.1 2.1 %collective-permute-start.14 = (bf16[512,512]{1,0:T(8,128)(2,1)S(1)}, bf16[512,512]{1,0:T(8,128)(2,1)}, u32[]{:S(2)}, u32[]{:S(2)}) collective-permute-start(bf16[512,512]{1,0:T(8,128)(2,1)S(1)} %collective-permute-done.3), channel_id=1, source_target_pairs={{4,0},{8,12},{5,1},{9,13},{6,2},{10,14},{7,3},{11,15},{20,16},{24,... | collective-permute-start | bytes 1572872 | tf_op jit(solution)/shard_map/ppermute | solution.py:431
  43.2 1.5 collective-permute-start.4
  45.3 51.3 %collective-permute-done.10 = bf16[512,512]{1,0:T(8,128)(2,1)S(1)} collective-permute-done((bf16[512,512]{1,0:T(8,128)(2,1)S(1)}, bf16[512,512]{1,0:T(8,128)(2,1)S(1)}, u32[]{:S(2)}, u32[]{:S(2)}) %collective-permute-start.10) | collective-permute-done | bytes 524320 | tf_op jit(solution)/shard_map/ppermute | solution.py:431
  96.7 1.6 collective-permute-start.11
  98.3 8.1 %collective-permute-done.14 = bf16[512,512]{1,0:T(8,128)(2,1)} collective-permute-done((bf16[512,512]{1,0:T(8,128)(2,1)S(1)}, bf16[512,512]{1,0:T(8,128)(2,1)}, u32[]{:S(2)}, u32[]{:S(2)}) %collective-permute-start.14) | collective-permute-done | bytes 524320 | tf_op jit(solution)/shard_map/ppermute | solution.py:431
  106.4 1.6 collective-permute-start.15
  109.9 7.3 %collective-permute-done.15.refs_5_ = bf16[512,512]{1,0:T(8,128)(2,1)S(1)} collective-permute-done((bf16[512,512]{1,0:T(8,128)(2,1)S(1)}, bf16[512,512]{1,0:T(8,128)(2,1)S(1)}, u32[]{:S(2)}, u32[]{:S(2)}) %collective-permute-start.15) | collective-permute-done | bytes 524320 | tf_op jit(solution)/shard_map/ppermute | solution.py:432
  118.3 3.1 %collective-permute-start.18 = (bf16[512,512]{1,0:T(8,128)(2,1)}, bf16[512,512]{1,0:T(8,128)(2,1)}, u32[]{:S(2)}, u32[]{:S(2)}) collective-permute-start(bf16[512,512]{1,0:T(8,128)(2,1)} %collective-permute-done.refs_0_), channel_id=1, source_target_pairs={{4,8},{8,4},{5,9},{9,5},{6,10},{10,6},{7,11},{11,7},{20,24},{24,20... | collective-permute-start | bytes 1572872 | tf_op jit(solution)/shard_map/ppermute | solution.py:435
  121.6 1.1 copy.22
  123.0 2.7 %collective-permute-start.26 = (bf16[512,512]{1,0:T(8,128)(2,1)}, bf16[512,512]{1,0:T(8,128)(2,1)}, u32[]{:S(2)}, u32[]{:S(2)}) collective-permute-start(bf16[512,512]{1,0:T(8,128)(2,1)} %copy-done.3), channel_id=1, source_target_pairs={{4,8},{8,4},{5,9},{9,5},{6,10},{10,6},{7,11},{11,7},{20,24},{24,20... | collective-permute-start | bytes 1572872 | tf_op jit(solution)/shard_map/ppermute | solution.py:435
  126.1 3.3 %place.1 = (bf16[2,3072,128]{2,1,0:T(8,128)(2,1)S(1)}, bf16[2,3072,256]{2,1,0:T(8,128)(2,1)S(1)}) custom-call(s32[128]{0:T(128)S(1)} %copy-done.2, bf16[256,2,16,256]{3,2,1,0:T(8,128)(2,1)} %bitcast.21.pages, bf16[384,512]{1,0:T(8,128)(2,1)S(1)} %bitcast.31), custom_call_target="tpu_custom_call" | custom-call | flops 1000000000 | bytes 1000 | tf_op jit(solution)/shard_map/place/pallas_call | solution.py:95
  129.4 10.3 %attend.2.left = bf16[4,192,512]{2,1,0:T(8,128)(2,1)S(1)} custom-call(s32[15]{0:T(128)S(1)} %stack.63.control, s32[6]{0:T(128)S(1)} %get-tuple-element.74.hist_at, s32[6]{0:T(128)S(1)} %get-tuple-element.73.hist_steps, s32[6]{0:T(128)S(1)} %get-tuple-element.68.fresh_at, s32[6]{0:T(128)S(1)} %get-tuple-element.67.fresh_steps, ...), custom_call_target="tpu_custom_call" | custom-call | flops 1000000000 | bytes 1000 | tf_op jit(solution)/shard_map/attend/pallas_call | solution.py:221
  139.7 1.6 project.5
  141.2 0.8 collective-permute-done.18
  142.0 6.6 %collective-permute-start.19 = (bf16[512,512]{1,0:T(8,128)(2,1)}, bf16[512,512]{1,0:T(8,128)(2,1)S(1)}, u32[]{:S(2)}, u32[]{:S(2)}) collective-permute-start(bf16[512,512]{1,0:T(8,128)(2,1)} %collective-permute-done.18), channel_id=1, source_target_pairs={{4,0},{8,12},{5,1},{9,13},{6,2},{10,14},{7,3},{11,15},{20,16},{24,... | collective-permute-start | bytes 1572872 | tf_op jit(solution)/shard_map/ppermute | solution.py:439
  148.7 3.4 %project.6 = bf16[192,1024]{1,0:T(8,128)(2,1)S(1)} custom-call(s32[15]{0:T(128)S(1)} %stack.63.control, bf16[4,192,512]{2,1,0:T(8,128)(2,1)S(1)} %attend.2.left, bf16[512,512]{1,0:T(8,128)(2,1)} %collective-permute-done.refs_0_, bf16[512,512]{1,0:T(8,128)(2,1)} %collective-permute-done.4.refs_1_, bf16[512,512]{1,0:T(8,128)(2,1)} %collective-permute-done.5.refs_2_, ...), custom_call_target="tpu_custom_call" | custom-call | flops 3000000000 | bytes 1000 | tf_op jit(solution)/shard_map/project/pallas_call | solution.py:299
  152.0 2.3 %collective-permute-start.20 = (bf16[192,1024]{1,0:T(8,128)(2,1)S(1)}, bf16[192,1024]{1,0:T(8,128)(2,1)S(1)}, u32[]{:S(2)}, u32[]{:S(2)}) collective-permute-start(bf16[192,1024]{1,0:T(8,128)(2,1)S(1)} %project.6), channel_id=1, source_target_pairs={{0,2},{2,0},{1,3},{3,1},{4,6},{6,4},{5,7},{7,5},{8,10},{10,8},{9,1... | collective-permute-start | bytes 1179656 | tf_op jit(solution)/shard_map/ppermute | solution.py:446
  154.4 2.9 %project.7 = bf16[192,1024]{1,0:T(8,128)(2,1)S(1)} custom-call(s32[15]{0:T(128)S(1)} %stack.63.control, bf16[4,192,512]{2,1,0:T(8,128)(2,1)S(1)} %attend.2.left, bf16[512,512]{1,0:T(8,128)(2,1)S(1)} %broadcast_select_fusion.3.refs_0_, bf16[512,512]{1,0:T(8,128)(2,1)S(1)} %collective-permute-done.11.refs_1_, ...), custom_call_target="tpu_custom_call" | custom-call | flops 3000000000 | bytes 1000 | tf_op jit(solution)/shard_map/project/pallas_call | solution.py:299
  157.3 2.0 collective-permute-start.25
  159.3 1.5 collective-permute-start.27
  160.8 1.1 broadcast_select_fusion.1.refs_0_
  161.9 1.5 collective-permute-start.22
  163.4 10.3 %attend.3.left = bf16[4,192,512]{2,1,0:T(8,128)(2,1)S(1)} custom-call(s32[15]{0:T(128)S(1)} %stack.63.control, s32[6]{0:T(128)S(1)} %get-tuple-element.74.hist_at, s32[6]{0:T(128)S(1)} %get-tuple-element.73.hist_steps, s32[6]{0:T(128)S(1)} %get-tuple-element.68.fresh_at, s32[6]{0:T(128)S(1)} %get-tuple-element.67.fresh_steps, ...), custom_call_target="tpu_custom_call" | custom-call | flops 16000000000 | bytes 1000 | tf_op jit(solution)/shard_map/attend/pallas_call | solution.py:221
  173.8 1.1 broadcast_select_fusion.refs_0_
  175.8 2.3 %finish.5.refs_8_ = bf16[1,192,4096]{2,1,0:T(8,128)(2,1)} custom-call(s32[15]{0:T(128)S(1)} %stack.63.control, bf16[4,192,512]{2,1,0:T(8,128)(2,1)S(1)} %attend.3.left, bf16[192,1024]{1,0:T(8,128)(2,1)S(1)} %collective-permute-done.21.came, bf16[2048,1024]{1,0:T(8,128)(2,1)S(1)} %copy-done.1), custom_call_target="tpu_custom_call" | custom-call | flops 3000000000 | bytes 1000 | tf_op jit(solution)/shard_map/finish/pallas_call | solution.py:299
  178.1 4.1 %finish.6.refs_8_ = bf16[1,192,4096]{2,1,0:T(8,128)(2,1)} custom-call(s32[15]{0:T(128)S(1)} %stack.63.control, bf16[4,192,512]{2,1,0:T(8,128)(2,1)S(1)} %attend.3.left, bf16[192,1024]{1,0:T(8,128)(2,1)S(1)} %collective-permute-done.20.came, bf16[512,512]{1,0:T(8,128)(2,1)} %collective-permute-done.refs_0_, ...), custom_call_target="tpu_custom_call", output_to_operand_aliasing={{}: (11, {})} | custom-call | flops 3000000000 | bytes 1000 | tf_op jit(solution)/shard_map/finish/pallas_call | solution.py:299
  182.2 1.1 project.8
  183.3 2.0 collective-permute-start.29
  185.4 3.6 %finish.7.refs_4_ = bf16[1,192,4096]{2,1,0:T(8,128)(2,1)} custom-call(s32[15]{0:T(128)S(1)} %stack.63.control, bf16[4,192,512]{2,1,0:T(8,128)(2,1)S(1)} %attend.3.left, bf16[192,1024]{1,0:T(8,128)(2,1)S(1)} %collective-permute-done.25.came, bf16[512,512]{1,0:T(8,128)(2,1)S(1)} %broadcast_select_fusion.3.refs_0_, ...), custom_call_target="tpu_custom_call", output_to_operand_aliasing={{}: (11, {})} | custom-call | flops 100000000 | bytes 1000 | tf_op jit(solution)/shard_map/finish/pallas_call | solution.py:299
  189.0 1.7 collective-permute-done.29.came
  191.2 1.4 collective-permute-done.30.refs_2_
  193.4 1.1 project.9
  194.5 1.8 collective-permute-start.32
  196.3 1.8 finish.8.refs_4_
  198.1 3.4 %collective-permute-done.32.came = bf16[192,512]{1,0:T(8,128)(2,1)S(1)} collective-permute-done((bf16[192,512]{1,0:T(8,128)(2,1)S(1)}, bf16[192,512]{1,0:T(8,128)(2,1)S(1)}, u32[]{:S(2)}, u32[]{:S(2)}) %collective-permute-start.32) | collective-permute-done | bytes 196640 | tf_op jit(solution)/shard_map/ppermute | solution.py:459
  201.5 1.8 finish.9
  (76 shorter events, 6.6 us)
Async XLA Ops:
  1.3 17.0 %collective-permute-start = (bf16[512,512]{1,0:T(8,128)(2,1)S(1)}, bf16[512,512]{1,0:T(8,128)(2,1)}, u32[]{:S(2)}, u32[]{:S(2)}) collective-permute-start(bf16[512,512]{1,0:T(8,128)(2,1)S(1)} %get-tuple-element.72), channel_id=1, source_target_pairs={{0,4},{4,0},{8,12},{12,8},{1,5},{5,1},{9,13},{13,9},{2,6},{6,2},{1... | collective-permute-start | bytes 1572872 | tf_op jit(solution)/shard_map/ppermute | solution.py:390
  2.9 15.3 %collective-permute-start.1 = (bf16[512,512]{1,0:T(8,128)(2,1)S(1)}, bf16[512,512]{1,0:T(8,128)(2,1)S(1)}, u32[]{:S(2)}, u32[]{:S(2)}) collective-permute-start(bf16[512,512]{1,0:T(8,128)(2,1)S(1)} %get-tuple-element.72), channel_id=1, source_target_pairs={{4,8},{8,4},{5,9},{9,5},{6,10},{10,6},{7,11},{11,7},{20,24},{24,20... | collective-permute-start | bytes 1572872 | tf_op jit(solution)/shard_map/ppermute | solution.py:390
  18.2 12.5 %collective-permute-start.2 = (bf16[512,512]{1,0:T(8,128)(2,1)S(1)}, bf16[512,512]{1,0:T(8,128)(2,1)S(1)}, u32[]{:S(2)}, u32[]{:S(2)}) collective-permute-start(bf16[512,512]{1,0:T(8,128)(2,1)S(1)} %get-tuple-element.40), channel_id=1, source_target_pairs={{0,4},{4,0},{8,12},{12,8},{1,5},{5,1},{9,13},{13,9},{2,6},{6,2},{1... | collective-permute-start | bytes 1572872 | tf_op jit(solution)/shard_map/ppermute | solution.py:397
  19.6 13.9 %collective-permute-start.3 = (bf16[512,512]{1,0:T(8,128)(2,1)S(1)}, bf16[512,512]{1,0:T(8,128)(2,1)S(1)}, u32[]{:S(2)}, u32[]{:S(2)}) collective-permute-start(bf16[512,512]{1,0:T(8,128)(2,1)S(1)} %get-tuple-element.40), channel_id=1, source_target_pairs={{4,8},{8,4},{5,9},{9,5},{6,10},{10,6},{7,11},{11,7},{20,24},{24,20... | collective-permute-start | bytes 1572872 | tf_op jit(solution)/shard_map/ppermute | solution.py:398
  30.7 77.8 %copy-start.3 = (bf16[512,512]{1,0:T(8,128)(2,1)}, bf16[512,512]{1,0:T(8,128)(2,1)S(1)}, u32[]{:S(2)}) copy-start(bf16[512,512]{1,0:T(8,128)(2,1)S(1)} %collective-permute-done.2.refs_4_) | copy-start | bytes 1572868
  33.6 92.5 %all-to-all-start.1 = ((bf16[4,64,2,16,256]{4,3,2,1,0:T(8,128)(2,1)}), bf16[4,64,2,16,256]{4,3,2,1,0:T(8,128)(2,1)}, u32[]{:S(2)}, u32[]{:S(2)}) async-start(bf16[4,64,2,16,256]{4,3,2,1,0:T(8,128)(2,1)} %pick.1), calls=%async_computation.1 | async-start | bytes 8388608 | tf_op jit(solution)/shard_map/all_to_all | solution.py:404
  38.4 58.2 %collective-permute-start.10 = (bf16[512,512]{1,0:T(8,128)(2,1)S(1)}, bf16[512,512]{1,0:T(8,128)(2,1)S(1)}, u32[]{:S(2)}, u32[]{:S(2)}) collective-permute-start(bf16[512,512]{1,0:T(8,128)(2,1)S(1)} %collective-permute-done.1), channel_id=1, source_target_pairs={{4,0},{8,12},{5,1},{9,13},{6,2},{10,14},{7,3},{11,15},{20,16},{24,... | collective-permute-start | bytes 1572872 | tf_op jit(solution)/shard_map/ppermute | solution.py:431
  41.1 65.2 %collective-permute-start.14 = (bf16[512,512]{1,0:T(8,128)(2,1)S(1)}, bf16[512,512]{1,0:T(8,128)(2,1)}, u32[]{:S(2)}, u32[]{:S(2)}) collective-permute-start(bf16[512,512]{1,0:T(8,128)(2,1)S(1)} %collective-permute-done.3), channel_id=1, source_target_pairs={{4,0},{8,12},{5,1},{9,13},{6,2},{10,14},{7,3},{11,15},{20,16},{24,... | collective-permute-start | bytes 1572872 | tf_op jit(solution)/shard_map/ppermute | solution.py:431
  43.2 65.3 %copy-start.7 = (s32[1,384]{1,0:T(1,128)S(1)}, s32[1,384]{1,0:T(1,128)}, u32[]{:S(2)}) copy-start(s32[1,384]{1,0:T(1,128)} %param.13) | copy-start | bytes 4612
  43.2 65.7 %copy-start.8 = (s32[1,128]{1,0:T(1,128)S(1)}, s32[1,128]{1,0:T(1,128)}, u32[]{:S(2)}) copy-start(s32[1,128]{1,0:T(1,128)} %param.14) | copy-start | bytes 1540
  43.2 66.0 %copy-start.9 = (s32[1,128]{1,0:T(1,128)S(1)}, s32[1,128]{1,0:T(1,128)}, u32[]{:S(2)}) copy-start(s32[1,128]{1,0:T(1,128)} %param.15) | copy-start | bytes 1540
  43.2 64.7 %collective-permute-start.4 = (bf16[512,512]{1,0:T(8,128)(2,1)}, bf16[512,512]{1,0:T(8,128)(2,1)}, u32[]{:S(2)}, u32[]{:S(2)}) collective-permute-start(bf16[512,512]{1,0:T(8,128)(2,1)} %collective-permute-done.refs_0_), channel_id=1, source_target_pairs={{0,16},{16,0},{1,17},{17,1},{2,18},{18,2},{3,19},{19,3},{4,20},{20... | collective-permute-start | bytes 1572872 | tf_op jit(solution)/shard_map/ppermute | solution.py:430
  44.7 63.7 %collective-permute-start.7 = (bf16[512,512]{1,0:T(8,128)(2,1)S(1)}, bf16[512,512]{1,0:T(8,128)(2,1)S(1)}, u32[]{:S(2)}, u32[]{:S(2)}) collective-permute-start(bf16[512,512]{1,0:T(8,128)(2,1)S(1)} %collective-permute-done.2.refs_4_), channel_id=1, source_target_pairs={{0,16},{16,0},{1,17},{17,1},{2,18},{18,2},{3,19},{19,3},{4,20},{20... | collective-permute-start | bytes 1572872 | tf_op jit(solution)/shard_map/ppermute | solution.py:430
  96.7 29.4 %copy-start.2 = (s32[128]{0:T(128)S(1)}, s32[128]{0:T(128)}, u32[]{:S(2)}) copy-start(s32[128]{0:T(128)} %get-tuple-element.35.position) | copy-start | bytes 1540
  96.7 12.6 %collective-permute-start.11 = (bf16[512,512]{1,0:T(8,128)(2,1)S(1)}, bf16[512,512]{1,0:T(8,128)(2,1)S(1)}, u32[]{:S(2)}, u32[]{:S(2)}) collective-permute-start(bf16[512,512]{1,0:T(8,128)(2,1)S(1)} %broadcast_select_fusion.3.refs_0_), channel_id=1, source_target_pairs={{0,16},{16,0},{1,17},{17,1},{2,18},{18,2},{3,19},{19,3},{4,20},{20... | collective-permute-start | bytes 1572872 | tf_op jit(solution)/shard_map/ppermute | solution.py:432
  106.4 10.8 %collective-permute-start.15 = (bf16[512,512]{1,0:T(8,128)(2,1)S(1)}, bf16[512,512]{1,0:T(8,128)(2,1)S(1)}, u32[]{:S(2)}, u32[]{:S(2)}) collective-permute-start(bf16[512,512]{1,0:T(8,128)(2,1)S(1)} %broadcast_select_fusion.2.refs_4_), channel_id=1, source_target_pairs={{0,16},{16,0},{1,17},{17,1},{2,18},{18,2},{3,19},{19,3},{4,20},{20... | collective-permute-start | bytes 1572872 | tf_op jit(solution)/shard_map/ppermute | solution.py:432
  108.0 9.2 %collective-permute-start.5 = (bf16[512,512]{1,0:T(8,128)(2,1)}, bf16[512,512]{1,0:T(8,128)(2,1)}, u32[]{:S(2)}, u32[]{:S(2)}) collective-permute-start(bf16[512,512]{1,0:T(8,128)(2,1)} %collective-permute-done.refs_0_), channel_id=1, source_target_pairs={{0,1},{1,0},{2,3},{3,2},{4,5},{5,4},{6,7},{7,6},{8,9},{9,8},{10,11... | collective-permute-start | bytes 1572872 | tf_op jit(solution)/shard_map/ppermute | solution.py:428
  108.0 9.7 %collective-permute-start.6 = (bf16[512,512]{1,0:T(8,128)(2,1)}, bf16[512,512]{1,0:T(8,128)(2,1)}, u32[]{:S(2)}, u32[]{:S(2)}) collective-permute-start(bf16[512,512]{1,0:T(8,128)(2,1)} %collective-permute-done.4.refs_1_), channel_id=1, source_target_pairs={{0,1},{1,0},{2,3},{3,2},{4,5},{5,4},{6,7},{7,6},{8,9},{9,8},{10,11... | collective-permute-start | bytes 1572872 | tf_op jit(solution)/shard_map/ppermute | solution.py:428
  108.5 0.8 copy-start.5
  108.5 9.3 %collective-permute-start.8 = (bf16[512,512]{1,0:T(8,128)(2,1)S(1)}, bf16[512,512]{1,0:T(8,128)(2,1)}, u32[]{:S(2)}, u32[]{:S(2)}) collective-permute-start(bf16[512,512]{1,0:T(8,128)(2,1)S(1)} %collective-permute-done.2.refs_4_), channel_id=1, source_target_pairs={{0,1},{1,0},{2,3},{3,2},{4,5},{5,4},{6,7},{7,6},{8,9},{9,8},{10,11... | collective-permute-start | bytes 1572872 | tf_op jit(solution)/shard_map/ppermute | solution.py:428
  109.3 9.0 %collective-permute-start.12 = (bf16[512,512]{1,0:T(8,128)(2,1)S(1)}, bf16[512,512]{1,0:T(8,128)(2,1)S(1)}, u32[]{:S(2)}, u32[]{:S(2)}) collective-permute-start(bf16[512,512]{1,0:T(8,128)(2,1)S(1)} %broadcast_select_fusion.3.refs_0_), channel_id=1, source_target_pairs={{0,1},{1,0},{2,3},{3,2},{4,5},{5,4},{6,7},{7,6},{8,9},{9,8},{10,11... | collective-permute-start | bytes 1572872 | tf_op jit(solution)/shard_map/ppermute | solution.py:428
  117.2 5.8 %collective-permute-start.9 = (bf16[512,512]{1,0:T(8,128)(2,1)}, bf16[512,512]{1,0:T(8,128)(2,1)}, u32[]{:S(2)}, u32[]{:S(2)}) collective-permute-start(bf16[512,512]{1,0:T(8,128)(2,1)} %copy-done.5), channel_id=1, source_target_pairs={{0,1},{1,0},{2,3},{3,2},{4,5},{5,4},{6,7},{7,6},{8,9},{9,8},{10,11... | collective-permute-start | bytes 1572872 | tf_op jit(solution)/shard_map/ppermute | solution.py:428
  117.2 8.5 %collective-permute-start.13 = (bf16[512,512]{1,0:T(8,128)(2,1)S(1)}, bf16[512,512]{1,0:T(8,128)(2,1)}, u32[]{:S(2)}, u32[]{:S(2)}) collective-permute-start(bf16[512,512]{1,0:T(8,128)(2,1)S(1)} %collective-permute-done.11.refs_1_), channel_id=1, source_target_pairs={{0,1},{1,0},{2,3},{3,2},{4,5},{5,4},{6,7},{7,6},{8,9},{9,8},{10,11... | collective-permute-start | bytes 1572872 | tf_op jit(solution)/shard_map/ppermute | solution.py:428
  117.7 8.0 %collective-permute-start.16 = (bf16[512,512]{1,0:T(8,128)(2,1)S(1)}, bf16[512,512]{1,0:T(8,128)(2,1)}, u32[]{:S(2)}, u32[]{:S(2)}) collective-permute-start(bf16[512,512]{1,0:T(8,128)(2,1)S(1)} %broadcast_select_fusion.2.refs_4_), channel_id=1, source_target_pairs={{0,1},{1,0},{2,3},{3,2},{4,5},{5,4},{6,7},{7,6},{8,9},{9,8},{10,11... | collective-permute-start | bytes 1572872 | tf_op jit(solution)/shard_map/ppermute | solution.py:428
  117.7 8.0 %collective-permute-start.17 = (bf16[512,512]{1,0:T(8,128)(2,1)S(1)}, bf16[512,512]{1,0:T(8,128)(2,1)}, u32[]{:S(2)}, u32[]{:S(2)}) collective-permute-start(bf16[512,512]{1,0:T(8,128)(2,1)S(1)} %collective-permute-done.15.refs_5_), channel_id=1, source_target_pairs={{0,1},{1,0},{2,3},{3,2},{4,5},{5,4},{6,7},{7,6},{8,9},{9,8},{10,11... | collective-permute-start | bytes 1572872 | tf_op jit(solution)/shard_map/ppermute | solution.py:428
  118.3 23.7 %collective-permute-start.18 = (bf16[512,512]{1,0:T(8,128)(2,1)}, bf16[512,512]{1,0:T(8,128)(2,1)}, u32[]{:S(2)}, u32[]{:S(2)}) collective-permute-start(bf16[512,512]{1,0:T(8,128)(2,1)} %collective-permute-done.refs_0_), channel_id=1, source_target_pairs={{4,8},{8,4},{5,9},{9,5},{6,10},{10,6},{7,11},{11,7},{20,24},{24,20... | collective-permute-start | bytes 1572872 | tf_op jit(solution)/shard_map/ppermute | solution.py:435
  123.0 36.3 %collective-permute-start.26 = (bf16[512,512]{1,0:T(8,128)(2,1)}, bf16[512,512]{1,0:T(8,128)(2,1)}, u32[]{:S(2)}, u32[]{:S(2)}) collective-permute-start(bf16[512,512]{1,0:T(8,128)(2,1)} %copy-done.3), channel_id=1, source_target_pairs={{4,8},{8,4},{5,9},{9,5},{6,10},{10,6},{7,11},{11,7},{20,24},{24,20... | collective-permute-start | bytes 1572872 | tf_op jit(solution)/shard_map/ppermute | solution.py:435
  126.1 3.3 %copy-start = (bf16[1,384,2048]{2,1,0:T(8,128)(2,1)S(1)}, bf16[1,384,2048]{2,1,0:T(8,128)(2,1)}, u32[]{:S(2)}) copy-start(bf16[1,384,2048]{2,1,0:T(8,128)(2,1)} %param.9) | copy-start | bytes 4718596
  129.4 10.3 %copy-start.1 = (bf16[2048,1024]{1,0:T(8,128)(2,1)S(1)}, bf16[2048,1024]{1,0:T(8,128)(2,1)}, u32[]{:S(2)}) copy-start(bf16[2048,1024]{1,0:T(8,128)(2,1)} %refs_0_.3) | copy-start | bytes 12582916
  139.7 9.0 %copy-start.4 = (bf16[512,512]{1,0:T(8,128)(2,1)S(1)}, bf16[512,512]{1,0:T(8,128)(2,1)}, u32[]{:S(2)}) copy-start(bf16[512,512]{1,0:T(8,128)(2,1)} %copy-done.3) | copy-start | bytes 1572868
  139.7 9.0 %copy-start.6 = (bf16[512,512]{1,0:T(8,128)(2,1)S(1)}, bf16[512,512]{1,0:T(8,128)(2,1)}, u32[]{:S(2)}) copy-start(bf16[512,512]{1,0:T(8,128)(2,1)} %copy-done.5) | copy-start | bytes 1572868
  142.0 18.8 %collective-permute-start.19 = (bf16[512,512]{1,0:T(8,128)(2,1)}, bf16[512,512]{1,0:T(8,128)(2,1)S(1)}, u32[]{:S(2)}, u32[]{:S(2)}) collective-permute-start(bf16[512,512]{1,0:T(8,128)(2,1)} %collective-permute-done.18), channel_id=1, source_target_pairs={{4,0},{8,12},{5,1},{9,13},{6,2},{10,14},{7,3},{11,15},{20,16},{24,... | collective-permute-start | bytes 1572872 | tf_op jit(solution)/shard_map/ppermute | solution.py:439
  152.0 21.7 %collective-permute-start.20 = (bf16[192,1024]{1,0:T(8,128)(2,1)S(1)}, bf16[192,1024]{1,0:T(8,128)(2,1)S(1)}, u32[]{:S(2)}, u32[]{:S(2)}) collective-permute-start(bf16[192,1024]{1,0:T(8,128)(2,1)S(1)} %project.6), channel_id=1, source_target_pairs={{0,2},{2,0},{1,3},{3,1},{4,6},{6,4},{5,7},{7,5},{8,10},{10,8},{9,1... | collective-permute-start | bytes 1179656 | tf_op jit(solution)/shard_map/ppermute | solution.py:446
  154.3 19.4 %collective-permute-start.21 = (bf16[192,1024]{1,0:T(8,128)(2,1)S(1)}, bf16[192,1024]{1,0:T(8,128)(2,1)S(1)}, u32[]{:S(2)}, u32[]{:S(2)}) collective-permute-start(bf16[192,1024]{1,0:T(8,128)(2,1)S(1)} %project.5), channel_id=1, source_target_pairs={{0,2},{2,0},{1,3},{3,1},{4,6},{6,4},{5,7},{7,5},{8,10},{10,8},{9,1... | collective-permute-start | bytes 1179656 | tf_op jit(solution)/shard_map/ppermute | solution.py:446
  157.3 28.1 %collective-permute-start.25 = (bf16[192,1024]{1,0:T(8,128)(2,1)S(1)}, bf16[192,1024]{1,0:T(8,128)(2,1)S(1)}, u32[]{:S(2)}, u32[]{:S(2)}) collective-permute-start(bf16[192,1024]{1,0:T(8,128)(2,1)S(1)} %project.7), channel_id=1, source_target_pairs={{0,2},{2,0},{1,3},{3,1},{4,6},{6,4},{5,7},{7,5},{8,10},{10,8},{9,1... | collective-permute-start | bytes 1179656 | tf_op jit(solution)/shard_map/ppermute | solution.py:446
  159.3 14.5 %collective-permute-start.27 = (bf16[512,512]{1,0:T(8,128)(2,1)}, bf16[512,512]{1,0:T(8,128)(2,1)S(1)}, u32[]{:S(2)}, u32[]{:S(2)}) collective-permute-start(bf16[512,512]{1,0:T(8,128)(2,1)} %collective-permute-done.26), channel_id=1, source_target_pairs={{4,0},{8,12},{5,1},{9,13},{6,2},{10,14},{7,3},{11,15},{20,16},{24,... | collective-permute-start | bytes 1572872 | tf_op jit(solution)/shard_map/ppermute | solution.py:441
  161.9 13.7 %collective-permute-start.22 = (bf16[512,512]{1,0:T(8,128)(2,1)S(1)}, bf16[512,512]{1,0:T(8,128)(2,1)S(1)}, u32[]{:S(2)}, u32[]{:S(2)}) collective-permute-start(bf16[512,512]{1,0:T(8,128)(2,1)S(1)} %broadcast_select_fusion.1.refs_0_), channel_id=1, source_target_pairs={{0,16},{16,0},{1,17},{17,1},{2,18},{18,2},{3,19},{19,3},{4,20},{20... | collective-permute-start | bytes 1572872 | tf_op jit(solution)/shard_map/ppermute | solution.py:444
  173.7 8.5 %collective-permute-start.23 = (bf16[512,512]{1,0:T(8,128)(2,1)S(1)}, bf16[512,512]{1,0:T(8,128)(2,1)S(1)}, u32[]{:S(2)}, u32[]{:S(2)}) collective-permute-start(bf16[512,512]{1,0:T(8,128)(2,1)S(1)} %broadcast_select_fusion.1.refs_0_), channel_id=1, source_target_pairs={{0,1},{1,0},{2,3},{3,2},{4,5},{5,4},{6,7},{7,6},{8,9},{9,8},{10,11... | collective-permute-start | bytes 1572872 | tf_op jit(solution)/shard_map/ppermute | solution.py:428
  174.9 15.8 %collective-permute-start.28 = (bf16[512,512]{1,0:T(8,128)(2,1)S(1)}, bf16[512,512]{1,0:T(8,128)(2,1)S(1)}, u32[]{:S(2)}, u32[]{:S(2)}) collective-permute-start(bf16[512,512]{1,0:T(8,128)(2,1)S(1)} %broadcast_select_fusion.refs_0_), channel_id=1, source_target_pairs={{0,16},{16,0},{1,17},{17,1},{2,18},{18,2},{3,19},{19,3},{4,20},{20... | collective-permute-start | bytes 1572872 | tf_op jit(solution)/shard_map/ppermute | solution.py:449
  175.6 6.6 %collective-permute-start.24 = (bf16[512,512]{1,0:T(8,128)(2,1)S(1)}, bf16[512,512]{1,0:T(8,128)(2,1)S(1)}, u32[]{:S(2)}, u32[]{:S(2)}) collective-permute-start(bf16[512,512]{1,0:T(8,128)(2,1)S(1)} %collective-permute-done.22.refs_1_), channel_id=1, source_target_pairs={{0,1},{1,0},{2,3},{3,2},{4,5},{5,4},{6,7},{7,6},{8,9},{9,8},{10,11... | collective-permute-start | bytes 1572872 | tf_op jit(solution)/shard_map/ppermute | solution.py:428
  183.3 7.4 %collective-permute-start.29 = (bf16[192,512]{1,0:T(8,128)(2,1)S(1)}, bf16[192,512]{1,0:T(8,128)(2,1)S(1)}, u32[]{:S(2)}, u32[]{:S(2)}) collective-permute-start(bf16[192,512]{1,0:T(8,128)(2,1)S(1)} %project.8), channel_id=1, source_target_pairs={{0,2},{2,0},{1,3},{3,1},{4,6},{6,4},{5,7},{7,5},{8,10},{10,8},{9,1... | collective-permute-start | bytes 589832 | tf_op jit(solution)/shard_map/ppermute | solution.py:455
  190.7 1.9 collective-permute-start.30
  190.7 2.7 %collective-permute-start.31 = (bf16[512,512]{1,0:T(8,128)(2,1)S(1)}, bf16[512,512]{1,0:T(8,128)(2,1)S(1)}, u32[]{:S(2)}, u32[]{:S(2)}) collective-permute-start(bf16[512,512]{1,0:T(8,128)(2,1)S(1)} %collective-permute-done.28.refs_1_), channel_id=1, source_target_pairs={{0,1},{1,0},{2,3},{3,2},{4,5},{5,4},{6,7},{7,6},{8,9},{9,8},{10,11... | collective-permute-start | bytes 1572872 | tf_op jit(solution)/shard_map/ppermute | solution.py:428
  194.5 7.0 %collective-permute-start.32 = (bf16[192,512]{1,0:T(8,128)(2,1)S(1)}, bf16[192,512]{1,0:T(8,128)(2,1)S(1)}, u32[]{:S(2)}, u32[]{:S(2)}) collective-permute-start(bf16[192,512]{1,0:T(8,128)(2,1)S(1)} %project.9), channel_id=1, source_target_pairs={{0,2},{2,0},{1,3},{3,1},{4,6},{6,4},{5,7},{7,5},{8,10},{10,8},{9,1... | collective-permute-start | bytes 589832 | tf_op jit(solution)/shard_map/ppermute | solution.py:459

commit v15 on v13

--- a/solution.py
+++ b/solution.py
@@ -9,7 +9,7 @@
 from jax.sharding import PartitionSpec as P
 
 HD = 128
-TILE = 64
+TILE = 96
 KEYS = 256
 LANES = 128
 HIDDEN = -1e30

time: 203 us -> 203 us (level)
  waiting for transfers between devices: 79 us -> 82.3 us
  starting transfers between devices: 49.9 us -> 46.8 us
    ppermute x3, starting transfers between devices: 5.71 us -> 2.22 us  [shards(): came = [swap_tp(each) for each in sent]]
    ppermute x1, starting transfers between devices: 3.35 us -> 6.3 us  [shards(): far_on = [forward(after(far[0], left))]]
  transfers between devices with their start and end apart: 34 -> 34, of which waited for: 8 -> 10; matrix products, arithmetic and copies ran while one was open for 2% -> 2% of each run, Pallas kernels for 26% -> 27%
where the time goes in v15:
time: 203 us
  waiting for transfers between devices  82.3 us (41%)
  Pallas kernels  56.2 us (28%)
  starting transfers between devices  46.8 us (23%)
  blocking collectives  10.9 us (5%)
  local copies, waits for them, and re-layouts  3.66 us (2%)
  other arithmetic  2.92 us (1%)
    ppermute x2, waiting for transfers between devices, shards(): next_shard = [jnp.where(middle, part, forward(part)) for part in inner]  58.7 us
    pallas_call x10, Pallas kernels, project(): pl.pallas_call(kernel, out_shape=out_shape, grid_spec=pltpu.PrefetchScala...  24 us
    pallas_call x2, Pallas kernels, attend(): pl.pallas_call(functools.partial(attend_kernel, fresh_base, side), out_sh...  21.3 us
    all_to_all x1, blocking collectives, shards(): lax.all_to_all(wanted, 'seq', split_axis=0, concat_axis=0, tiled=True)  10.9 us
    ppermute x2, waiting for transfers between devices, shards(): next_across = [swap_group(part) for part in next_shard]  7.73 us
    ppermute x1, waiting for transfers between devices, shards(): inner.append(cross(later))  6.99 us
    ppermute x1, starting transfers between devices, shards(): far_on = [forward(after(far[0], left))]  6.3 us
    ppermute x2, starting transfers between devices, shards(): next_shard = [jnp.where(middle, part, forward(part)) for part in inner]  6.27 us
  transfers between devices with their start and end apart: 34, of which 10 were waited for; matrix products, arithmetic and copies ran while one was open for 2% of the time, Pallas kernels for 27%

profile of v15, /device:TPU:16, one launch (start us, length us, event | category | flops | bytes accessed | tf_op | source)
XLA Modules:
  0.0 203.4 jit_solution(15365618755226202006)
XLA Ops:
  0.0 1.3 fusion.5
  1.3 1.6 collective-permute-start
  2.9 1.9 collective-permute-start.1
  4.8 2.6 %rank.1 = (s32[128]{0:T(128)}, s32[4,64]{1,0:T(4,128)}) custom-call(s32[1,128]{1,0:T(1,128)} %owner.1, s32[1,128]{1,0:T(1,128)} %page.1), custom_call_target="tpu_custom_call" | custom-call | flops 3000000000 | bytes 1000 | tf_op jit(solution)/shard_map/rank/pallas_call | solution.py:49
  7.5 10.9 %all_to_all.17 = s32[4,1,64]{2,1,0:T(1,128)} all-to-all(s32[4,1,64]{2,1,0:T(1,128)} %bitcast.39), channel_id=1, replica_groups=mesh['group'=2,'seq'=4,'tp'=2,'role'=2] {'seq'}, dimensions={0} | all-to-all | bytes 2048 | tf_op jit(solution)/shard_map/all_to_all | solution.py:393
  18.4 2.0 %collective-permute-start.3 = (bf16[512,512]{1,0:T(8,128)(2,1)S(1)}, bf16[512,512]{1,0:T(8,128)(2,1)S(1)}, u32[]{:S(2)}, u32[]{:S(2)}) collective-permute-start(bf16[512,512]{1,0:T(8,128)(2,1)S(1)} %get-tuple-element.38), channel_id=1, source_target_pairs={{4,8},{8,4},{5,9},{9,5},{6,10},{10,6},{7,11},{11,7},{20,24},{24,20... | collective-permute-start | bytes 1572872 | tf_op jit(solution)/shard_map/ppermute | solution.py:398
  20.5 5.0 %pick.1 = bf16[4,64,2,16,256]{4,3,2,1,0:T(8,128)(2,1)} custom-call(s32[4,64]{1,0:T(4,128)} %bitcast.38, bf16[256,2,16,256]{3,2,1,0:T(8,128)(2,1)} %bitcast.41), custom_call_target="tpu_custom_call" | custom-call | flops 3000000000 | bytes 1000 | tf_op jit(solution)/shard_map/pick/pallas_call | solution.py:332
  25.6 7.0 %collective-permute-done.3 = bf16[512,512]{1,0:T(8,128)(2,1)S(1)} collective-permute-done((bf16[512,512]{1,0:T(8,128)(2,1)S(1)}, bf16[512,512]{1,0:T(8,128)(2,1)S(1)}, u32[]{:S(2)}, u32[]{:S(2)}) %collective-permute-start.3) | collective-permute-done | bytes 524320 | tf_op jit(solution)/shard_map/ppermute | solution.py:398
  33.0 5.9 %all-to-all-start.1 = ((bf16[4,64,2,16,256]{4,3,2,1,0:T(8,128)(2,1)}), bf16[4,64,2,16,256]{4,3,2,1,0:T(8,128)(2,1)}, u32[]{:S(2)}, u32[]{:S(2)}) async-start(bf16[4,64,2,16,256]{4,3,2,1,0:T(8,128)(2,1)} %pick.1), calls=%async_computation.1 | async-start | bytes 8388608 | tf_op jit(solution)/shard_map/all_to_all | solution.py:404
  38.9 4.2 %collective-permute-start.10 = (bf16[512,512]{1,0:T(8,128)(2,1)S(1)}, bf16[512,512]{1,0:T(8,128)(2,1)}, u32[]{:S(2)}, u32[]{:S(2)}) collective-permute-start(bf16[512,512]{1,0:T(8,128)(2,1)S(1)} %collective-permute-done.1), channel_id=1, source_target_pairs={{4,0},{8,12},{5,1},{9,13},{6,2},{10,14},{7,3},{11,15},{20,16},{24,... | collective-permute-start | bytes 1572872 | tf_op jit(solution)/shard_map/ppermute | solution.py:431
  43.1 2.1 %collective-permute-start.14 = (bf16[512,512]{1,0:T(8,128)(2,1)S(1)}, bf16[512,512]{1,0:T(8,128)(2,1)}, u32[]{:S(2)}, u32[]{:S(2)}) collective-permute-start(bf16[512,512]{1,0:T(8,128)(2,1)S(1)} %collective-permute-done.3), channel_id=1, source_target_pairs={{4,0},{8,12},{5,1},{9,13},{6,2},{10,14},{7,3},{11,15},{20,16},{24,... | collective-permute-start | bytes 1572872 | tf_op jit(solution)/shard_map/ppermute | solution.py:431
  45.2 1.5 collective-permute-start.4
  47.2 50.9 %collective-permute-done.10 = bf16[512,512]{1,0:T(8,128)(2,1)} collective-permute-done((bf16[512,512]{1,0:T(8,128)(2,1)S(1)}, bf16[512,512]{1,0:T(8,128)(2,1)}, u32[]{:S(2)}, u32[]{:S(2)}) %collective-permute-start.10) | collective-permute-done | bytes 524320 | tf_op jit(solution)/shard_map/ppermute | solution.py:431
  98.2 1.6 collective-permute-start.11
  99.8 7.8 %collective-permute-done.14 = bf16[512,512]{1,0:T(8,128)(2,1)} collective-permute-done((bf16[512,512]{1,0:T(8,128)(2,1)S(1)}, bf16[512,512]{1,0:T(8,128)(2,1)}, u32[]{:S(2)}, u32[]{:S(2)}) %collective-permute-start.14) | collective-permute-done | bytes 524320 | tf_op jit(solution)/shard_map/ppermute | solution.py:431
  107.6 1.6 collective-permute-start.15
  109.2 0.5 collective-permute-start.8
  111.1 7.7 %collective-permute-done.15.refs_5_ = bf16[512,512]{1,0:T(8,128)(2,1)} collective-permute-done((bf16[512,512]{1,0:T(8,128)(2,1)S(1)}, bf16[512,512]{1,0:T(8,128)(2,1)}, u32[]{:S(2)}, u32[]{:S(2)}) %collective-permute-start.15) | collective-permute-done | bytes 524320 | tf_op jit(solution)/shard_map/ppermute | solution.py:432
  118.8 0.5 collective-permute-start.9
  119.4 0.8 copy-done.3
  120.7 1.9 collective-permute-start.18
  122.8 1.1 copy.22
  124.3 3.9 %collective-permute-start.20 = (bf16[512,512]{1,0:T(8,128)(2,1)S(1)}, bf16[512,512]{1,0:T(8,128)(2,1)}, u32[]{:S(2)}, u32[]{:S(2)}) collective-permute-start(bf16[512,512]{1,0:T(8,128)(2,1)S(1)} %collective-permute-done.2.refs_4_), channel_id=1, source_target_pairs={{4,8},{8,4},{5,9},{9,5},{6,10},{10,6},{7,11},{11,7},{20,24},{24,20... | collective-permute-start | bytes 1572872 | tf_op jit(solution)/shard_map/ppermute | solution.py:435
  128.2 3.3 %place.1 = (bf16[2,3072,128]{2,1,0:T(8,128)(2,1)S(1)}, bf16[2,3072,256]{2,1,0:T(8,128)(2,1)S(1)}) custom-call(s32[128]{0:T(128)S(1)} %copy-done.2, bf16[256,2,16,256]{3,2,1,0:T(8,128)(2,1)} %bitcast.21.pages, bf16[384,512]{1,0:T(8,128)(2,1)S(1)} %bitcast.31), custom_call_target="tpu_custom_call" | custom-call | flops 1000000000 | bytes 1000 | tf_op jit(solution)/shard_map/place/pallas_call | solution.py:95
  131.5 10.2 %attend.2.left = bf16[4,192,512]{2,1,0:T(8,128)(2,1)S(1)} custom-call(s32[15]{0:T(128)S(1)} %stack.63.control, s32[4]{0:T(128)S(1)} %get-tuple-element.70.hist_at, s32[4]{0:T(128)S(1)} %get-tuple-element.69.hist_steps, s32[4]{0:T(128)S(1)} %get-tuple-element.64.fresh_at, s32[4]{0:T(128)S(1)} %get-tuple-element.63.fresh_steps, ...), custom_call_target="tpu_custom_call" | custom-call | flops 1000000000 | bytes 1000 | tf_op jit(solution)/shard_map/attend/pallas_call | solution.py:221
  141.7 1.5 project.5
  143.3 6.3 %collective-permute-start.19 = (bf16[512,512]{1,0:T(8,128)(2,1)}, bf16[512,512]{1,0:T(8,128)(2,1)S(1)}, u32[]{:S(2)}, u32[]{:S(2)}) collective-permute-start(bf16[512,512]{1,0:T(8,128)(2,1)} %collective-permute-done.18), channel_id=1, source_target_pairs={{4,0},{8,12},{5,1},{9,13},{6,2},{10,14},{7,3},{11,15},{20,16},{24,... | collective-permute-start | bytes 1572872 | tf_op jit(solution)/shard_map/ppermute | solution.py:439
  149.6 3.2 %project.6 = bf16[192,1024]{1,0:T(8,128)(2,1)S(1)} custom-call(s32[15]{0:T(128)S(1)} %stack.63.control, bf16[4,192,512]{2,1,0:T(8,128)(2,1)S(1)} %attend.2.left, bf16[512,512]{1,0:T(8,128)(2,1)S(1)} %collective-permute-done.refs_0_, bf16[512,512]{1,0:T(8,128)(2,1)S(1)} %collective-permute-done.4.refs_1_, bf16[512,512]{1,0:T(8,128)(2,1)} %collective-permute-done.5.refs_2_, ...), custom_call_target="tpu_custom_call" | custom-call | flops 3000000000 | bytes 1000 | tf_op jit(solution)/shard_map/project/pallas_call | solution.py:299
  152.9 2.0 collective-permute-start.25
  154.9 3.2 %project.7 = bf16[192,1024]{1,0:T(8,128)(2,1)S(1)} custom-call(s32[15]{0:T(128)S(1)} %stack.63.control, bf16[4,192,512]{2,1,0:T(8,128)(2,1)S(1)} %attend.2.left, bf16[512,512]{1,0:T(8,128)(2,1)S(1)} %broadcast_select_fusion.3.refs_0_, bf16[512,512]{1,0:T(8,128)(2,1)} %collective-permute-done.11.refs_1_, bf16[512,512]{1,0:T(8,128)(2,1)S(1)} %copy-done.4, ...), custom_call_target="tpu_custom_call" | custom-call | flops 3000000000 | bytes 1000 | tf_op jit(solution)/shard_map/project/pallas_call | solution.py:299
  158.3 1.5 collective-permute-start.21
  159.8 1.1 broadcast_select_fusion.1.refs_0_
  160.9 2.5 %collective-permute-start.26 = (bf16[512,512]{1,0:T(8,128)(2,1)S(1)}, bf16[512,512]{1,0:T(8,128)(2,1)S(1)}, u32[]{:S(2)}, u32[]{:S(2)}) collective-permute-start(bf16[512,512]{1,0:T(8,128)(2,1)S(1)} %broadcast_select_fusion.1.refs_0_), channel_id=1, source_target_pairs={{0,16},{16,0},{1,17},{17,1},{2,18},{18,2},{3,19},{19,3},{4,20},{20... | collective-permute-start | bytes 1572872 | tf_op jit(solution)/shard_map/ppermute | solution.py:444
  163.4 11.1 %attend.3.left = bf16[4,192,512]{2,1,0:T(8,128)(2,1)S(1)} custom-call(s32[15]{0:T(128)S(1)} %stack.63.control, s32[4]{0:T(128)S(1)} %get-tuple-element.70.hist_at, s32[4]{0:T(128)S(1)} %get-tuple-element.69.hist_steps, s32[4]{0:T(128)S(1)} %get-tuple-element.64.fresh_at, s32[4]{0:T(128)S(1)} %get-tuple-element.63.fresh_steps, ...), custom_call_target="tpu_custom_call" | custom-call | flops 16000000000 | bytes 1000 | tf_op jit(solution)/shard_map/attend/pallas_call | solution.py:221
  174.6 1.1 broadcast_select_fusion.refs_0_
  175.8 2.3 %finish.5.refs_8_ = bf16[1,192,4096]{2,1,0:T(8,128)(2,1)} custom-call(s32[15]{0:T(128)S(1)} %stack.63.control, bf16[4,192,512]{2,1,0:T(8,128)(2,1)S(1)} %attend.3.left, bf16[192,1024]{1,0:T(8,128)(2,1)S(1)} %collective-permute-done.25.came, bf16[2048,1024]{1,0:T(8,128)(2,1)S(1)} %copy-done.1), custom_call_target="tpu_custom_call" | custom-call | flops 3000000000 | bytes 1000 | tf_op jit(solution)/shard_map/finish/pallas_call | solution.py:299
  178.6 4.0 %finish.6.refs_8_ = bf16[1,192,4096]{2,1,0:T(8,128)(2,1)} custom-call(s32[15]{0:T(128)S(1)} %stack.63.control, bf16[4,192,512]{2,1,0:T(8,128)(2,1)S(1)} %attend.3.left, bf16[192,1024]{1,0:T(8,128)(2,1)S(1)} %collective-permute-done.24.came, bf16[512,512]{1,0:T(8,128)(2,1)S(1)} %collective-permute-done.refs_0_, ...), custom_call_target="tpu_custom_call", output_to_operand_aliasing={{}: (11, {})} | custom-call | flops 3000000000 | bytes 1000 | tf_op jit(solution)/shard_map/finish/pallas_call | solution.py:299
  182.6 4.0 %finish.7.refs_4_ = bf16[1,192,4096]{2,1,0:T(8,128)(2,1)} custom-call(s32[15]{0:T(128)S(1)} %stack.63.control, bf16[4,192,512]{2,1,0:T(8,128)(2,1)S(1)} %attend.3.left, bf16[192,1024]{1,0:T(8,128)(2,1)S(1)} %collective-permute-done.23.came, bf16[512,512]{1,0:T(8,128)(2,1)S(1)} %broadcast_select_fusion.3.refs_0_, ...), custom_call_target="tpu_custom_call", output_to_operand_aliasing={{}: (11, {})} | custom-call | flops 3000000000 | bytes 1000 | tf_op jit(solution)/shard_map/finish/pallas_call | solution.py:299
  186.5 1.1 project.8
  187.6 2.5 %collective-permute-done.22.refs_1_ = bf16[512,512]{1,0:T(8,128)(2,1)S(1)} collective-permute-done((bf16[512,512]{1,0:T(8,128)(2,1)S(1)}, bf16[512,512]{1,0:T(8,128)(2,1)S(1)}, u32[]{:S(2)}, u32[]{:S(2)}) %collective-permute-start.22) | collective-permute-done | bytes 524320 | tf_op jit(solution)/shard_map/ppermute | solution.py:449
  190.6 1.0 collective-permute-start.32
  192.0 0.7 collective-permute-done.29.refs_2_
  192.8 1.1 project.9
  193.9 1.1 collective-permute-start.31
  195.0 3.1 %collective-permute-done.32.came = bf16[192,512]{1,0:T(8,128)(2,1)S(1)} collective-permute-done((bf16[192,512]{1,0:T(8,128)(2,1)S(1)}, bf16[192,512]{1,0:T(8,128)(2,1)S(1)}, u32[]{:S(2)}, u32[]{:S(2)}) %collective-permute-start.32) | collective-permute-done | bytes 196640 | tf_op jit(solution)/shard_map/ppermute | solution.py:456
  198.1 1.8 finish.8.refs_4_
  199.9 1.7 collective-permute-done.31.came
  201.6 1.8 finish.9
  (72 shorter events, 5.1 us)
Async XLA Ops:
  1.3 17.1 %collective-permute-start = (bf16[512,512]{1,0:T(8,128)(2,1)S(1)}, bf16[512,512]{1,0:T(8,128)(2,1)S(1)}, u32[]{:S(2)}, u32[]{:S(2)}) collective-permute-start(bf16[512,512]{1,0:T(8,128)(2,1)S(1)} %get-tuple-element.68), channel_id=1, source_target_pairs={{0,4},{4,0},{8,12},{12,8},{1,5},{5,1},{9,13},{13,9},{2,6},{6,2},{1... | collective-permute-start | bytes 1572872 | tf_op jit(solution)/shard_map/ppermute | solution.py:390
  2.9 15.5 %collective-permute-start.1 = (bf16[512,512]{1,0:T(8,128)(2,1)S(1)}, bf16[512,512]{1,0:T(8,128)(2,1)S(1)}, u32[]{:S(2)}, u32[]{:S(2)}) collective-permute-start(bf16[512,512]{1,0:T(8,128)(2,1)S(1)} %get-tuple-element.68), channel_id=1, source_target_pairs={{4,8},{8,4},{5,9},{9,5},{6,10},{10,6},{7,11},{11,7},{20,24},{24,20... | collective-permute-start | bytes 1572872 | tf_op jit(solution)/shard_map/ppermute | solution.py:390
  18.4 14.2 %collective-permute-start.3 = (bf16[512,512]{1,0:T(8,128)(2,1)S(1)}, bf16[512,512]{1,0:T(8,128)(2,1)S(1)}, u32[]{:S(2)}, u32[]{:S(2)}) collective-permute-start(bf16[512,512]{1,0:T(8,128)(2,1)S(1)} %get-tuple-element.38), channel_id=1, source_target_pairs={{4,8},{8,4},{5,9},{9,5},{6,10},{10,6},{7,11},{11,7},{20,24},{24,20... | collective-permute-start | bytes 1572872 | tf_op jit(solution)/shard_map/ppermute | solution.py:398
  20.4 12.6 %collective-permute-start.2 = (bf16[512,512]{1,0:T(8,128)(2,1)S(1)}, bf16[512,512]{1,0:T(8,128)(2,1)S(1)}, u32[]{:S(2)}, u32[]{:S(2)}) collective-permute-start(bf16[512,512]{1,0:T(8,128)(2,1)S(1)} %get-tuple-element.38), channel_id=1, source_target_pairs={{0,4},{4,0},{8,12},{12,8},{1,5},{5,1},{9,13},{13,9},{2,6},{6,2},{1... | collective-permute-start | bytes 1572872 | tf_op jit(solution)/shard_map/ppermute | solution.py:397
  33.0 95.2 %all-to-all-start.1 = ((bf16[4,64,2,16,256]{4,3,2,1,0:T(8,128)(2,1)}), bf16[4,64,2,16,256]{4,3,2,1,0:T(8,128)(2,1)}, u32[]{:S(2)}, u32[]{:S(2)}) async-start(bf16[4,64,2,16,256]{4,3,2,1,0:T(8,128)(2,1)} %pick.1), calls=%async_computation.1 | async-start | bytes 8388608 | tf_op jit(solution)/shard_map/all_to_all | solution.py:404
  38.9 59.2 %collective-permute-start.10 = (bf16[512,512]{1,0:T(8,128)(2,1)S(1)}, bf16[512,512]{1,0:T(8,128)(2,1)}, u32[]{:S(2)}, u32[]{:S(2)}) collective-permute-start(bf16[512,512]{1,0:T(8,128)(2,1)S(1)} %collective-permute-done.1), channel_id=1, source_target_pairs={{4,0},{8,12},{5,1},{9,13},{6,2},{10,14},{7,3},{11,15},{20,16},{24,... | collective-permute-start | bytes 1572872 | tf_op jit(solution)/shard_map/ppermute | solution.py:431
  43.1 64.4 %collective-permute-start.14 = (bf16[512,512]{1,0:T(8,128)(2,1)S(1)}, bf16[512,512]{1,0:T(8,128)(2,1)}, u32[]{:S(2)}, u32[]{:S(2)}) collective-permute-start(bf16[512,512]{1,0:T(8,128)(2,1)S(1)} %collective-permute-done.3), channel_id=1, source_target_pairs={{4,0},{8,12},{5,1},{9,13},{6,2},{10,14},{7,3},{11,15},{20,16},{24,... | collective-permute-start | bytes 1572872 | tf_op jit(solution)/shard_map/ppermute | solution.py:431
  45.2 64.6 %copy-start.5 = (s32[1,384]{1,0:T(1,128)S(1)}, s32[1,384]{1,0:T(1,128)}, u32[]{:S(2)}) copy-start(s32[1,384]{1,0:T(1,128)} %param.13) | copy-start | bytes 4612
  45.2 65.0 %copy-start.6 = (s32[1,128]{1,0:T(1,128)S(1)}, s32[1,128]{1,0:T(1,128)}, u32[]{:S(2)}) copy-start(s32[1,128]{1,0:T(1,128)} %param.14) | copy-start | bytes 1540
  45.2 65.2 %copy-start.7 = (s32[1,128]{1,0:T(1,128)S(1)}, s32[1,128]{1,0:T(1,128)}, u32[]{:S(2)}) copy-start(s32[1,128]{1,0:T(1,128)} %param.15) | copy-start | bytes 1540
  45.2 64.0 %collective-permute-start.4 = (bf16[512,512]{1,0:T(8,128)(2,1)S(1)}, bf16[512,512]{1,0:T(8,128)(2,1)S(1)}, u32[]{:S(2)}, u32[]{:S(2)}) collective-permute-start(bf16[512,512]{1,0:T(8,128)(2,1)S(1)} %collective-permute-done.refs_0_), channel_id=1, source_target_pairs={{0,16},{16,0},{1,17},{17,1},{2,18},{18,2},{3,19},{19,3},{4,20},{20... | collective-permute-start | bytes 1572872 | tf_op jit(solution)/shard_map/ppermute | solution.py:430
  46.7 63.0 %collective-permute-start.7 = (bf16[512,512]{1,0:T(8,128)(2,1)S(1)}, bf16[512,512]{1,0:T(8,128)(2,1)}, u32[]{:S(2)}, u32[]{:S(2)}) collective-permute-start(bf16[512,512]{1,0:T(8,128)(2,1)S(1)} %collective-permute-done.2.refs_4_), channel_id=1, source_target_pairs={{0,16},{16,0},{1,17},{17,1},{2,18},{18,2},{3,19},{19,3},{4,20},{20... | collective-permute-start | bytes 1572872 | tf_op jit(solution)/shard_map/ppermute | solution.py:430
  98.2 30.0 %copy-start.2 = (s32[128]{0:T(128)S(1)}, s32[128]{0:T(128)}, u32[]{:S(2)}) copy-start(s32[128]{0:T(128)} %get-tuple-element.33.position) | copy-start | bytes 1540
  98.2 12.3 %collective-permute-start.11 = (bf16[512,512]{1,0:T(8,128)(2,1)S(1)}, bf16[512,512]{1,0:T(8,128)(2,1)}, u32[]{:S(2)}, u32[]{:S(2)}) collective-permute-start(bf16[512,512]{1,0:T(8,128)(2,1)S(1)} %broadcast_select_fusion.3.refs_0_), channel_id=1, source_target_pairs={{0,16},{16,0},{1,17},{17,1},{2,18},{18,2},{3,19},{19,3},{4,20},{20... | collective-permute-start | bytes 1572872 | tf_op jit(solution)/shard_map/ppermute | solution.py:432
  107.6 11.1 %collective-permute-start.15 = (bf16[512,512]{1,0:T(8,128)(2,1)S(1)}, bf16[512,512]{1,0:T(8,128)(2,1)}, u32[]{:S(2)}, u32[]{:S(2)}) collective-permute-start(bf16[512,512]{1,0:T(8,128)(2,1)S(1)} %broadcast_select_fusion.2.refs_4_), channel_id=1, source_target_pairs={{0,16},{16,0},{1,17},{17,1},{2,18},{18,2},{3,19},{19,3},{4,20},{20... | collective-permute-start | bytes 1572872 | tf_op jit(solution)/shard_map/ppermute | solution.py:432
  109.2 9.6 %collective-permute-start.5 = (bf16[512,512]{1,0:T(8,128)(2,1)S(1)}, bf16[512,512]{1,0:T(8,128)(2,1)}, u32[]{:S(2)}, u32[]{:S(2)}) collective-permute-start(bf16[512,512]{1,0:T(8,128)(2,1)S(1)} %collective-permute-done.refs_0_), channel_id=1, source_target_pairs={{0,1},{1,0},{2,3},{3,2},{4,5},{5,4},{6,7},{7,6},{8,9},{9,8},{10,11... | collective-permute-start | bytes 1572872 | tf_op jit(solution)/shard_map/ppermute | solution.py:428
  109.2 10.1 %collective-permute-start.8 = (bf16[512,512]{1,0:T(8,128)(2,1)S(1)}, bf16[512,512]{1,0:T(8,128)(2,1)}, u32[]{:S(2)}, u32[]{:S(2)}) collective-permute-start(bf16[512,512]{1,0:T(8,128)(2,1)S(1)} %collective-permute-done.2.refs_4_), channel_id=1, source_target_pairs={{0,1},{1,0},{2,3},{3,2},{4,5},{5,4},{6,7},{7,6},{8,9},{9,8},{10,11... | collective-permute-start | bytes 1572872 | tf_op jit(solution)/shard_map/ppermute | solution.py:428
  109.7 9.6 %collective-permute-start.12 = (bf16[512,512]{1,0:T(8,128)(2,1)S(1)}, bf16[512,512]{1,0:T(8,128)(2,1)S(1)}, u32[]{:S(2)}, u32[]{:S(2)}) collective-permute-start(bf16[512,512]{1,0:T(8,128)(2,1)S(1)} %broadcast_select_fusion.3.refs_0_), channel_id=1, source_target_pairs={{0,1},{1,0},{2,3},{3,2},{4,5},{5,4},{6,7},{7,6},{8,9},{9,8},{10,11... | collective-permute-start | bytes 1572872 | tf_op jit(solution)/shard_map/ppermute | solution.py:428
  110.6 10.2 %collective-permute-start.6 = (bf16[512,512]{1,0:T(8,128)(2,1)S(1)}, bf16[512,512]{1,0:T(8,128)(2,1)}, u32[]{:S(2)}, u32[]{:S(2)}) collective-permute-start(bf16[512,512]{1,0:T(8,128)(2,1)S(1)} %collective-permute-done.4.refs_1_), channel_id=1, source_target_pairs={{0,1},{1,0},{2,3},{3,2},{4,5},{5,4},{6,7},{7,6},{8,9},{9,8},{10,11... | collective-permute-start | bytes 1572872 | tf_op jit(solution)/shard_map/ppermute | solution.py:428
  118.8 5.5 %collective-permute-start.16 = (bf16[512,512]{1,0:T(8,128)(2,1)S(1)}, bf16[512,512]{1,0:T(8,128)(2,1)}, u32[]{:S(2)}, u32[]{:S(2)}) collective-permute-start(bf16[512,512]{1,0:T(8,128)(2,1)S(1)} %broadcast_select_fusion.2.refs_4_), channel_id=1, source_target_pairs={{0,1},{1,0},{2,3},{3,2},{4,5},{5,4},{6,7},{7,6},{8,9},{9,8},{10,11... | collective-permute-start | bytes 1572872 | tf_op jit(solution)/shard_map/ppermute | solution.py:428
  118.8 9.4 %collective-permute-start.9 = (bf16[512,512]{1,0:T(8,128)(2,1)}, bf16[512,512]{1,0:T(8,128)(2,1)}, u32[]{:S(2)}, u32[]{:S(2)}) collective-permute-start(bf16[512,512]{1,0:T(8,128)(2,1)} %collective-permute-done.7.refs_5_), channel_id=1, source_target_pairs={{0,1},{1,0},{2,3},{3,2},{4,5},{5,4},{6,7},{7,6},{8,9},{9,8},{10,11... | collective-permute-start | bytes 1572872 | tf_op jit(solution)/shard_map/ppermute | solution.py:428
  119.3 8.9 %collective-permute-start.13 = (bf16[512,512]{1,0:T(8,128)(2,1)}, bf16[512,512]{1,0:T(8,128)(2,1)}, u32[]{:S(2)}, u32[]{:S(2)}) collective-permute-start(bf16[512,512]{1,0:T(8,128)(2,1)} %collective-permute-done.11.refs_1_), channel_id=1, source_target_pairs={{0,1},{1,0},{2,3},{3,2},{4,5},{5,4},{6,7},{7,6},{8,9},{9,8},{10,11... | collective-permute-start | bytes 1572872 | tf_op jit(solution)/shard_map/ppermute | solution.py:428
  119.4 0.8 copy-start.3
  120.2 8.0 %collective-permute-start.17 = (bf16[512,512]{1,0:T(8,128)(2,1)}, bf16[512,512]{1,0:T(8,128)(2,1)}, u32[]{:S(2)}, u32[]{:S(2)}) collective-permute-start(bf16[512,512]{1,0:T(8,128)(2,1)} %collective-permute-done.15.refs_5_), channel_id=1, source_target_pairs={{0,1},{1,0},{2,3},{3,2},{4,5},{5,4},{6,7},{7,6},{8,9},{9,8},{10,11... | collective-permute-start | bytes 1572872 | tf_op jit(solution)/shard_map/ppermute | solution.py:428
  120.7 22.6 %collective-permute-start.18 = (bf16[512,512]{1,0:T(8,128)(2,1)S(1)}, bf16[512,512]{1,0:T(8,128)(2,1)}, u32[]{:S(2)}, u32[]{:S(2)}) collective-permute-start(bf16[512,512]{1,0:T(8,128)(2,1)S(1)} %collective-permute-done.refs_0_), channel_id=1, source_target_pairs={{4,8},{8,4},{5,9},{9,5},{6,10},{10,6},{7,11},{11,7},{20,24},{24,20... | collective-permute-start | bytes 1572872 | tf_op jit(solution)/shard_map/ppermute | solution.py:435
  124.3 34.0 %collective-permute-start.20 = (bf16[512,512]{1,0:T(8,128)(2,1)S(1)}, bf16[512,512]{1,0:T(8,128)(2,1)}, u32[]{:S(2)}, u32[]{:S(2)}) collective-permute-start(bf16[512,512]{1,0:T(8,128)(2,1)S(1)} %collective-permute-done.2.refs_4_), channel_id=1, source_target_pairs={{4,8},{8,4},{5,9},{9,5},{6,10},{10,6},{7,11},{11,7},{20,24},{24,20... | collective-permute-start | bytes 1572872 | tf_op jit(solution)/shard_map/ppermute | solution.py:435
  128.2 3.3 %copy-start = (bf16[1,384,2048]{2,1,0:T(8,128)(2,1)S(1)}, bf16[1,384,2048]{2,1,0:T(8,128)(2,1)}, u32[]{:S(2)}) copy-start(bf16[1,384,2048]{2,1,0:T(8,128)(2,1)} %param.9) | copy-start | bytes 4718596
  131.5 10.2 %copy-start.1 = (bf16[2048,1024]{1,0:T(8,128)(2,1)S(1)}, bf16[2048,1024]{1,0:T(8,128)(2,1)}, u32[]{:S(2)}) copy-start(bf16[2048,1024]{1,0:T(8,128)(2,1)} %refs_0_.3) | copy-start | bytes 12582916
  143.3 11.6 %copy-start.4 = (bf16[512,512]{1,0:T(8,128)(2,1)S(1)}, bf16[512,512]{1,0:T(8,128)(2,1)}, u32[]{:S(2)}) copy-start(bf16[512,512]{1,0:T(8,128)(2,1)} %copy-done.3) | copy-start | bytes 1572868
  143.3 16.5 %collective-permute-start.19 = (bf16[512,512]{1,0:T(8,128)(2,1)}, bf16[512,512]{1,0:T(8,128)(2,1)S(1)}, u32[]{:S(2)}, u32[]{:S(2)}) collective-permute-start(bf16[512,512]{1,0:T(8,128)(2,1)} %collective-permute-done.18), channel_id=1, source_target_pairs={{4,0},{8,12},{5,1},{9,13},{6,2},{10,14},{7,3},{11,15},{20,16},{24,... | collective-permute-start | bytes 1572872 | tf_op jit(solution)/shard_map/ppermute | solution.py:439
  152.8 21.7 %collective-permute-start.24 = (bf16[192,1024]{1,0:T(8,128)(2,1)S(1)}, bf16[192,1024]{1,0:T(8,128)(2,1)S(1)}, u32[]{:S(2)}, u32[]{:S(2)}) collective-permute-start(bf16[192,1024]{1,0:T(8,128)(2,1)S(1)} %project.6), channel_id=1, source_target_pairs={{0,2},{2,0},{1,3},{3,1},{4,6},{6,4},{5,7},{7,5},{8,10},{10,8},{9,1... | collective-permute-start | bytes 1179656 | tf_op jit(solution)/shard_map/ppermute | solution.py:446
  152.9 21.7 %collective-permute-start.25 = (bf16[192,1024]{1,0:T(8,128)(2,1)S(1)}, bf16[192,1024]{1,0:T(8,128)(2,1)S(1)}, u32[]{:S(2)}, u32[]{:S(2)}) collective-permute-start(bf16[192,1024]{1,0:T(8,128)(2,1)S(1)} %project.5), channel_id=1, source_target_pairs={{0,2},{2,0},{1,3},{3,1},{4,6},{6,4},{5,7},{7,5},{8,10},{10,8},{9,1... | collective-permute-start | bytes 1179656 | tf_op jit(solution)/shard_map/ppermute | solution.py:446
  158.1 24.4 %collective-permute-start.23 = (bf16[192,1024]{1,0:T(8,128)(2,1)S(1)}, bf16[192,1024]{1,0:T(8,128)(2,1)S(1)}, u32[]{:S(2)}, u32[]{:S(2)}) collective-permute-start(bf16[192,1024]{1,0:T(8,128)(2,1)S(1)} %project.7), channel_id=1, source_target_pairs={{0,2},{2,0},{1,3},{3,1},{4,6},{6,4},{5,7},{7,5},{8,10},{10,8},{9,1... | collective-permute-start | bytes 1179656 | tf_op jit(solution)/shard_map/ppermute | solution.py:446
  158.3 16.3 %collective-permute-start.21 = (bf16[512,512]{1,0:T(8,128)(2,1)}, bf16[512,512]{1,0:T(8,128)(2,1)S(1)}, u32[]{:S(2)}, u32[]{:S(2)}) collective-permute-start(bf16[512,512]{1,0:T(8,128)(2,1)} %collective-permute-done.20), channel_id=1, source_target_pairs={{4,0},{8,12},{5,1},{9,13},{6,2},{10,14},{7,3},{11,15},{20,16},{24,... | collective-permute-start | bytes 1572872 | tf_op jit(solution)/shard_map/ppermute | solution.py:441
  160.9 17.2 %collective-permute-start.26 = (bf16[512,512]{1,0:T(8,128)(2,1)S(1)}, bf16[512,512]{1,0:T(8,128)(2,1)S(1)}, u32[]{:S(2)}, u32[]{:S(2)}) collective-permute-start(bf16[512,512]{1,0:T(8,128)(2,1)S(1)} %broadcast_select_fusion.1.refs_0_), channel_id=1, source_target_pairs={{0,16},{16,0},{1,17},{17,1},{2,18},{18,2},{3,19},{19,3},{4,20},{20... | collective-permute-start | bytes 1572872 | tf_op jit(solution)/shard_map/ppermute | solution.py:444
  174.5 12.0 %collective-permute-start.27 = (bf16[512,512]{1,0:T(8,128)(2,1)S(1)}, bf16[512,512]{1,0:T(8,128)(2,1)S(1)}, u32[]{:S(2)}, u32[]{:S(2)}) collective-permute-start(bf16[512,512]{1,0:T(8,128)(2,1)S(1)} %broadcast_select_fusion.1.refs_0_), channel_id=1, source_target_pairs={{0,1},{1,0},{2,3},{3,2},{4,5},{5,4},{6,7},{7,6},{8,9},{9,8},{10,11... | collective-permute-start | bytes 1572872 | tf_op jit(solution)/shard_map/ppermute | solution.py:428
  175.7 14.4 %collective-permute-start.22 = (bf16[512,512]{1,0:T(8,128)(2,1)S(1)}, bf16[512,512]{1,0:T(8,128)(2,1)S(1)}, u32[]{:S(2)}, u32[]{:S(2)}) collective-permute-start(bf16[512,512]{1,0:T(8,128)(2,1)S(1)} %broadcast_select_fusion.refs_0_), channel_id=1, source_target_pairs={{0,16},{16,0},{1,17},{17,1},{2,18},{18,2},{3,19},{19,3},{4,20},{20... | collective-permute-start | bytes 1572872 | tf_op jit(solution)/shard_map/ppermute | solution.py:449
  178.1 8.4 %collective-permute-start.28 = (bf16[512,512]{1,0:T(8,128)(2,1)S(1)}, bf16[512,512]{1,0:T(8,128)(2,1)S(1)}, u32[]{:S(2)}, u32[]{:S(2)}) collective-permute-start(bf16[512,512]{1,0:T(8,128)(2,1)S(1)} %collective-permute-done.26.refs_1_), channel_id=1, source_target_pairs={{0,1},{1,0},{2,3},{3,2},{4,5},{5,4},{6,7},{7,6},{8,9},{9,8},{10,11... | collective-permute-start | bytes 1572872 | tf_op jit(solution)/shard_map/ppermute | solution.py:428
  190.1 1.9 collective-permute-start.30
  190.1 2.7 %collective-permute-start.29 = (bf16[512,512]{1,0:T(8,128)(2,1)S(1)}, bf16[512,512]{1,0:T(8,128)(2,1)S(1)}, u32[]{:S(2)}, u32[]{:S(2)}) collective-permute-start(bf16[512,512]{1,0:T(8,128)(2,1)S(1)} %broadcast_select_fusion.refs_0_), channel_id=1, source_target_pairs={{0,1},{1,0},{2,3},{3,2},{4,5},{5,4},{6,7},{7,6},{8,9},{9,8},{10,11... | collective-permute-start | bytes 1572872 | tf_op jit(solution)/shard_map/ppermute | solution.py:428
  190.6 7.5 %collective-permute-start.32 = (bf16[192,512]{1,0:T(8,128)(2,1)S(1)}, bf16[192,512]{1,0:T(8,128)(2,1)S(1)}, u32[]{:S(2)}, u32[]{:S(2)}) collective-permute-start(bf16[192,512]{1,0:T(8,128)(2,1)S(1)} %project.8), channel_id=1, source_target_pairs={{0,2},{2,0},{1,3},{3,1},{4,6},{6,4},{5,7},{7,5},{8,10},{10,8},{9,1... | collective-permute-start | bytes 589832 | tf_op jit(solution)/shard_map/ppermute | solution.py:456
  193.9 7.8 %collective-permute-start.31 = (bf16[192,512]{1,0:T(8,128)(2,1)S(1)}, bf16[192,512]{1,0:T(8,128)(2,1)S(1)}, u32[]{:S(2)}, u32[]{:S(2)}) collective-permute-start(bf16[192,512]{1,0:T(8,128)(2,1)S(1)} %project.9), channel_id=1, source_target_pairs={{0,2},{2,0},{1,3},{3,1},{4,6},{6,4},{5,7},{7,5},{8,10},{10,8},{9,1... | collective-permute-start | bytes 589832 | tf_op jit(solution)/shard_map/ppermute | solution.py:459
